TPU v7x, 32 devices: a whole 2x2x4 slice. The times are simulated.
32 devices in a mesh: ctx: 4 (over y, x), exp: 4 (over z), tp: 2 (over core).
Axes of the slice: x: 2, y: 2, z: 4, core: 2. Of those that a mesh axis runs over, the one named last changes fastest.
Arguments:
- hidden: bfloat16 [2048, 4, 1408], P(('ctx', 'exp'), None, 'tp'), may hold values from -6 to 6
- expert_ids: int32 [2048, 4], P(('ctx', 'exp')), may hold values from 0 to 7, all different within a row; in each aligned block of 128 rows (0 to 127, 128 to 255, ...) at most 72 rows name the same one
- gate_fix: int32 [2048, 4], P(('ctx', 'exp')), may hold values from 1024 to 65535
- grad_out: bfloat16 [2048, 2048], P(('ctx', 'exp'), 'tp'), may hold values from -6 to 6
- w_down: bfloat16 [8, 1408, 2048], P('ctx', 'tp'), may hold values from -0.15625 to 0.15625
Outputs:
- mixed: bfloat16 [2048, 2048], P(('ctx', 'exp'), 'tp')
- grad_hidden: bfloat16 [2048, 4, 1408], P(('ctx', 'exp'), None, 'tp')
Inputs may be any that keep to these rules, and one draw needn't show every extreme that they name: `expert_ids`: each row names 4 different experts. Within the 128 rows of one index of ctx and exp, no expert is named by more than 72 rows, a bound that some block reaches.
All inputs are finite; a program needn't handle non-finite values.
Results may differ from a plain program's by a relative error of at most 0.013.
Values may be sent and summed in bfloat16 or wider, within the bound.
No kernel may reach another device: no remote copies, remote signals or barrier semaphores. Data moves between devices by JAX's collectives and lax.ppermute only.
A program may use at most 64 MiB of HBM per device.

v0:
```python
import functools

import jax
import jax.numpy as jnp
from jax import lax
from jax.experimental import pallas as pl
from jax.experimental.pallas import tpu as pltpu
from jax.sharding import PartitionSpec as P

BF16 = jnp.bfloat16
F32 = jnp.float32
NN = (((1,), (0,)), ((), ()))
NT = (((1,), (1,)), ((), ()))
TN = (((0,), (0,)), ((), ()))
BIG = 10**11


def dot(a, b, dims):
    return lax.dot_general(a, b, dims, preferred_element_type=F32)


def iota(shape, axis):
    return lax.broadcasted_iota(jnp.int32, shape, axis)


def ones_where(mask):
    return mask.astype(F32).astype(BF16)


def earlier(tokens):
    return ones_where(iota((tokens, tokens), 0) < iota((tokens, tokens), 1))


def token_slots(ids, me, experts, local, cap, width):
    top, tokens = ids.shape
    row = iota((experts, tokens), 0)
    hits = [ids[k : k + 1, :] == row for k in range(top)]
    named = functools.reduce(jnp.logical_or, hits)
    before = dot(ones_where(named), earlier(tokens), NN)
    base = jnp.bitwise_xor(row // local, me) * width + lax.rem(row, local) * cap
    slot = before + base.astype(F32)
    return [
        jnp.sum(jnp.where(hit, slot, 0.0), axis=0, keepdims=True).astype(jnp.int32)
        for hit in hits
    ]


def named_here(ids, me, local):
    top, tokens = ids.shape
    row = iota((8, tokens), 0) + me * local
    return functools.reduce(
        jnp.logical_or, [ids[k : k + 1, :] == row for k in range(top)]
    )


def slots_by_lane(ids, me, local, cap, width):
    tokens = ids.shape[1]
    named = named_here(ids, me, local)
    before = dot(ones_where(named), earlier(tokens), NN)
    slot = before.astype(jnp.int32) + iota((8, tokens), 0) * cap
    slot = jnp.where(named, slot, -1)
    rows = iota((cap, tokens), 0)
    return [ones_where(rows + l * cap == slot[l : l + 1, :]) for l in range(local)]


def picks_of(meta, me, dims):
    experts, local, cap, width = dims
    top = meta.shape[0] // 2
    slots = token_slots(meta[:top], me, experts, local, cap, width)
    rows = iota((experts // local * width, meta.shape[1]), 0)
    picks = jnp.concatenate([ones_where(rows == slot) for slot in slots], axis=1)
    return picks, meta[top:].astype(F32) * (1.0 / 65536.0)


def dispatch_kernel(dims, place, meta_ref, hid_ref, *outs):
    width = outs[0].shape[0]
    picks, gate = picks_of(meta_ref[...], place[0], dims)
    scaled = [
        (hid_ref[k].astype(F32) * gate[k : k + 1, :]).astype(BF16)
        for k in range(hid_ref.shape[0])
    ]
    rows = jnp.concatenate(scaled, axis=1)
    spare = outs[0].shape[1] - rows.shape[0]
    tokens = hid_ref.shape[2]
    number = jnp.bitwise_and(iota((spare, rows.shape[1]), 1), tokens - 1) + 1
    number = jnp.where(iota(number.shape, 0) == 0, number.astype(F32), 0.0)
    sent = dot(picks, jnp.concatenate([rows, number.astype(BF16)], axis=0), NT)
    for s, out in enumerate(outs):
        out[...] = sent[s * width : (s + 1) * width].astype(BF16)


def by_expert(rows, local, cap):
    return [
        jnp.concatenate([r[l * cap : (l + 1) * cap] for r in rows], axis=0)
        for l in range(local)
    ]


def by_source(rows, count, cap):
    return [
        jnp.concatenate([r[s * cap : (s + 1) * cap] for r in rows], axis=0)
        for s in range(count)
    ]


def routes(dims, top, me, packed, tokens):
    experts, local, cap, width = dims
    ids = packed[tokens:, :tokens].astype(F32).astype(jnp.int32)[:top]
    return jnp.concatenate(slots_by_lane(ids, me, local, cap, width), axis=0)


def gather_rows(dims, held, halves, x_ref):
    experts, local, cap, width = dims
    tokens, half = held[0].shape[1], halves[0].shape[1]
    chunk = min(half, 512)
    for c in range(0, half, chunk):
        rows = [dot(h, ref[:tokens, c : c + chunk], NN) for h, ref in zip(held, halves)]
        for l, x in enumerate(by_expert(rows, local, cap)):
            x_ref[l, :, c : c + chunk] = x.astype(BF16)


def gather_kernel(dims, top, place, *refs):
    x_ref, held_ref = refs[-2:]
    own = refs[:-2]
    tokens = held_ref.shape[2]
    held = [routes(dims, top, place[0], ref, tokens) for ref in own]
    for s, h in enumerate(held):
        held_ref[s] = h
    gather_rows(dims, held, own, x_ref)


def products(dims, place, x_ref, x_other, w_ref):
    half = x_ref.shape[2]
    mine = pl.ds(pl.multiple_of(place[1] * half, half), half)
    theirs = pl.ds(pl.multiple_of((1 - place[1]) * half, half), half)
    return [
        dot(x_ref[l], w_ref[l, :, mine], NT) + dot(x_other[l], w_ref[l, :, theirs], NT)
        for l in range(dims[1])
    ]


def grad_kernel(dims, place, *refs):
    n = (len(refs) - 4) // 2
    other = refs[:n]
    x_ref, held_ref, w_ref = refs[n : n + 3]
    outs, x_other = refs[n + 3 : 2 * n + 3], refs[-1]
    gather_rows(dims, [held_ref[s] for s in range(n)], other, x_other)
    grads = products(dims, place, x_ref, x_other, w_ref)
    for s, rows in enumerate(by_source(grads, n, dims[2])):
        outs[s][...] = rows.astype(BF16)


def mix_rows(dims, side, hid, w_ref, tokens, half, store):
    experts, local, cap, width = dims
    n = len(hid)
    ff = w_ref.shape[1]
    chunk = min(half, 256)
    same = ones_where(iota((tokens, tokens), 0) == iota((tokens, tokens), 1))
    held = []
    for h in hid:
        number = h[:, ff : ff + 1].astype(F32).astype(jnp.int32) - 1
        slots = ones_where(iota((width, tokens), 1) == number)
        held.append(dot(same, slots, NT).astype(BF16))
    rows = [h[:, :ff].astype(F32) for h in hid]
    x = [r.astype(BF16) for r in by_expert(rows, local, cap)]
    for c in range(0, half, chunk):
        at = pl.ds(pl.multiple_of(side * half + c, chunk), chunk)
        out = [dot(x[l], w_ref[l, :, at], NN) for l in range(local)]
        for s, rows in enumerate(by_source(out, n, cap)):
            store(s, slice(c, c + chunk), dot(held[s], rows.astype(BF16), NN))


def mix_kernel(dims, sibling, place, *refs):
    hid, (w_ref, out) = refs[:-2], refs[-2:]
    tokens = out.shape[0] // len(hid)

    def store(s, columns, part):
        out[pl.ds(s * tokens, tokens), columns] = part.astype(out.dtype)

    side = 1 - place[1] if sibling else place[1]
    mix_rows(dims, side, hid, w_ref, tokens, out.shape[1], store)


def mix_add_kernel(dims, place, *refs):
    n = (len(refs) - 2) // 2
    hid, (w_ref, arrived), outs = refs[:n], refs[n : n + 2], refs[n + 2 :]
    tokens, half = outs[0].shape

    def store(s, columns, part):
        theirs = arrived[pl.ds(s * tokens, tokens), columns].astype(F32)
        outs[s][:, columns] = (part + theirs).astype(BF16)

    mix_rows(dims, place[1], hid, w_ref, tokens, half, store)


def add_split_kernel(own, arrived, mine, one, two, low, high):
    tokens, half = mine.shape
    cut = half // 2
    for s, out in enumerate((mine, one, two)):
        at = pl.ds(s * tokens, tokens)
        out[...] = own[at, :] + arrived[at, :].astype(F32)
    at = pl.ds(3 * tokens, tokens)
    far = own[at, :] + arrived[at, :].astype(F32)
    low[...] = far[:, :cut].astype(BF16)
    high[...] = far[:, cut:].astype(BF16)


def join_kernel(one, two, low, high, to_one, to_two):
    cut = one.shape[1] // 2
    to_one[:, :cut] = one[:, :cut].astype(BF16)
    to_one[:, cut:] = (one[:, cut:] + high[...].astype(F32)).astype(BF16)
    to_two[:, :cut] = (two[:, :cut] + low[...].astype(F32)).astype(BF16)
    to_two[:, cut:] = two[:, cut:].astype(BF16)


def restore_kernel(dims, place, meta_ref, *refs):
    back_refs, out = refs[:-1], refs[-1]
    top, _, tokens = out.shape
    picks, gate = picks_of(meta_ref[...], place[0], dims)
    back = jnp.concatenate([ref[...] for ref in back_refs], axis=0)
    grads = dot(back, picks, TN)
    for k in range(top):
        out[k] = (grads[:, k * tokens : (k + 1) * tokens] * gate[k : k + 1, :]).astype(BF16)


def shaped(shape, dtype=BF16):
    return jax.ShapeDtypeStruct(shape, dtype)


def call(kernel, outs, args, where=(), scratch=(), grant=24, weight=1, name=None):
    where = dict(where)
    return pl.pallas_call(
        kernel,
        out_shape=outs,
        in_specs=[
            pl.BlockSpec(memory_space=where.get(i, pltpu.VMEM)) for i in range(len(args))
        ],
        out_specs=[pl.BlockSpec(memory_space=pltpu.VMEM)] * len(outs),
        scratch_shapes=scratch,
        compiler_params=pltpu.CompilerParams(vmem_limit_bytes=grant * 1024 * 1024),
        cost_estimate=pl.CostEstimate(
            flops=weight, bytes_accessed=1, transcendentals=0
        ),
        name=name,
    )(*args)


def body(hidden, expert_ids, gate_fix, grad_out, w_down):
    tokens, top, ff = hidden.shape
    half = grad_out.shape[1]
    local, _, full = w_down.shape
    n = lax.axis_size("ctx")
    experts = n * local
    assigned = tokens * top
    cap = min(tokens, assigned // experts + max(1, assigned // (8 * experts)))
    unit = 8 if local % 2 == 0 else 16
    cap = -(-cap // unit) * unit
    width = local * cap
    dims = (experts, local, cap, width)
    run = functools.partial(call, grant=24 if n <= 4 else 56)
    place = jnp.stack([lax.axis_index("ctx"), lax.axis_index("tp")]).astype(jnp.int32)
    placed = {0: pltpu.SMEM}

    def send(x, s):
        return lax.ppermute(x, "ctx", [(i, i ^ s) for i in range(n)]) if s else x

    def swap(x):
        return lax.ppermute(x, "tp", [(0, 1), (1, 0)])

    meta = jnp.concatenate([expert_ids.T, gate_fix.T], axis=0)
    hid_t = hidden.transpose(1, 2, 0)
    named = jnp.pad(expert_ids.T.astype(BF16), ((0, 8 - top), (0, half - tokens)))
    packed = jnp.concatenate([grad_out, named], axis=0)
    forward = n == 4
    own = [send(packed, s) for s in range(n)]
    hid_sent = run(
        functools.partial(dispatch_kernel, dims), [shaped((width, -(-(ff + 1) // 128) * 128))] * n,
        [place, meta, hid_t], where=placed, name="dispatch",
    )
    hid = [send(hid_sent[s], s) for s in range(n)]
    for s in range(1, n):
        own[s], hid[0] = lax.optimization_barrier((own[s], hid[0]))
    other = [swap(x) for x in own]

    slot = shaped((width, ff))
    x, held = run(
        functools.partial(gather_kernel, dims, top),
        [shaped((local, n * cap, half)), shaped((n, width, tokens))],
        [place, *own], where=placed, name="gather", weight=BIG,
    )
    grad_sent = run(
        functools.partial(grad_kernel, dims), [slot] * n,
        [place, *other, x, held, w_down], where=placed,
        scratch=[pltpu.VMEM((local, n * cap, half), BF16)], name="grad",
    )
    hid[0], grad_own = lax.optimization_barrier((hid[0], grad_sent[0]))
    grad_back = [grad_own] + [send(grad_sent[s], s) for s in range(1, n)]

    (theirs,) = run(
        functools.partial(mix_kernel, dims, True), [shaped((n * tokens, half))],
        [place, *hid, w_down], where=placed, name="mix_sibling",
    )
    arrived = swap(theirs)
    if forward:
        (mine,) = run(
            functools.partial(mix_kernel, dims, False), [shaped((n * tokens, half), F32)],
            [place, *hid, w_down], where=placed, name="mix_own", weight=BIG,
        )
        cut = half // 2
        block, piece = shaped((tokens, half), F32), shaped((tokens, cut))
        kept, one, two, one_low, two_high = run(
            add_split_kernel, [block] * 3 + [piece] * 2, [mine, arrived], name="add"
        )
        one_low, two_high = send(one_low, 1), send(two_high, 2)
        to_one, to_two = run(
            join_kernel, [shaped((tokens, half))] * 2, [one, two, one_low, two_high],
            name="join",
        )
        parts = [kept, send(to_one, 1), send(to_two, 2)]
    else:
        sums = run(
            functools.partial(mix_add_kernel, dims), [shaped((tokens, half))] * n,
            [place, *hid, w_down, arrived], where=placed, name="mix_own",
        )
        parts = [send(sums[s], s) for s in range(n)]

    (grad_t,) = run(
        functools.partial(restore_kernel, dims), [shaped((top, ff, tokens))],
        [place, meta, *grad_back], where=placed, name="restore", weight=BIG,
    )
    mixed = sum(x.astype(F32) for x in parts).astype(BF16)
    return mixed, grad_t.transpose(2, 0, 1)


def solution(mesh):
    placed = (
        P(("ctx", "exp"), None, "tp"),
        P(("ctx", "exp"), None),
        P(("ctx", "exp"), None),
        P(("ctx", "exp"), "tp"),
        P("ctx", "tp", None),
    )
    return jax.shard_map(
        body,
        mesh=mesh,
        in_specs=placed,
        out_specs=(P(("ctx", "exp"), "tp"), P(("ctx", "exp"), None, "tp")),
        check_vma=False,
    )
```

profile of v0, /device:TPU:0, one launch (start us, length us, event | category | flops | bytes accessed | tf_op | source)
XLA Modules:
  0.0 54.4 jit_solution(6040314963331183323)
XLA Ops:
  0.6 0.7 %bitcast_convert_fusion = bf16[4,128]{1,0:T(4,128)(2,1)S(1)} fusion(s32[128,4]{0,1:T(4,128)} %param.6), kind=kLoop, calls=%fused_computation.6 | loop fusion | flops 512 | bytes 3072 | tf_op jit(solution)/shard_map/convert_element_type | solution.py:272
  1.3 1.0 %fusion.1.refs_0_ = bf16[136,1024]{1,0:T(8,128)(2,1)S(1)} fusion(bf16[4,128]{1,0:T(4,128)(2,1)S(1)} %bitcast_convert_fusion, bf16[128,1024]{1,0:T(8,128)(2,1)} %param.8), kind=kLoop, calls=%fused_computation.3 | loop fusion | flops 835584 | bytes 541696 | tf_op jit(solution)/shard_map/concatenate | solution.py:273
  2.3 3.0 %collective-permute-start.2 = (bf16[136,1024]{1,0:T(8,128)(2,1)S(1)}, bf16[136,1024]{1,0:T(8,128)(2,1)S(1)}, u32[]{:S(2)}, u32[]{:S(2)}) collective-permute-start(bf16[136,1024]{1,0:T(8,128)(2,1)S(1)} %fusion.1.refs_0_), channel_id=1, source_target_pairs={{0,8},{8,0},{16,24},{24,16},{1,9},{9,1},{17,25},{25,17},{2,10},{10... | collective-permute-start | bytes 835592 | tf_op jit(solution)/shard_map/ppermute | solution.py:265
  5.3 1.5 %collective-permute-start.1 = (bf16[136,1024]{1,0:T(8,128)(2,1)S(1)}, bf16[136,1024]{1,0:T(8,128)(2,1)S(1)}, u32[]{:S(2)}, u32[]{:S(2)}) collective-permute-start(bf16[136,1024]{1,0:T(8,128)(2,1)S(1)} %fusion.1.refs_0_), channel_id=1, source_target_pairs={{0,16},{8,24},{16,0},{24,8},{1,17},{9,25},{17,1},{25,9},{2,18},{10... | collective-permute-start | bytes 835592 | tf_op jit(solution)/shard_map/ppermute | solution.py:265
  6.8 0.0 collective-permute-start
  6.8 0.0 collective-permute-start.3
  6.8 0.1 pad_add_fusion.1.place
  6.9 0.7 %pad_add_fusion.meta_ref = s32[8,128]{1,0:T(8,128)S(1)} fusion(s32[4,128]{1,0:T(4,128)} %bitcast.9, s32[4,128]{1,0:T(4,128)} %bitcast.8), kind=kLoop, calls=%fused_computation.4 | loop fusion | flops 1024 | bytes 8192 | tf_op jit(solution)/shard_map/concatenate | solution.py:270
  7.6 1.1 %copy-done.1 = bf16[128,4,704]{0,2,1:T(8,128)(2,1)S(1)} copy-done((bf16[128,4,704]{0,2,1:T(8,128)(2,1)S(1)}, bf16[128,4,704]{0,2,1:T(8,128)(2,1)}, u32[]{:S(2)}) %copy-start.1) | copy-done | bytes 720920
  8.7 1.4 %dispatch.1 = (bf16[144,768]{1,0:T(8,128)(2,1)S(1)}, bf16[144,768]{1,0:T(8,128)(2,1)S(1)}, bf16[144,768]{1,0:T(8,128)(2,1)S(1)}, bf16[144,768]{1,0:T(8,128)(2,1)S(1)}) custom-call(s32[2]{0:T(128)S(1)} %pad_add_fusion.1.place, s32[8,128]{1,0:T(8,128)S(1)} %pad_add_fusion.meta_ref, bf16[4,704,128]{2,1,0:T(8,128)(2,1)S(1)} %bitcast.7), custom_call_target="tpu_custom_call" | custom-call | flops 1 | bytes 1 | tf_op jit(solution)/shard_map/dispatch/pallas_call | solution.py:232
  10.1 2.7 %collective-permute-done.2.refs_1_ = bf16[136,1024]{1,0:T(8,128)(2,1)S(1)} collective-permute-done((bf16[136,1024]{1,0:T(8,128)(2,1)S(1)}, bf16[136,1024]{1,0:T(8,128)(2,1)S(1)}, u32[]{:S(2)}, u32[]{:S(2)}) %collective-permute-start.2) | collective-permute-done | bytes 278560 | tf_op jit(solution)/shard_map/ppermute | solution.py:265
  12.8 6.6 %collective-permute-done.1.refs_2_ = bf16[136,1024]{1,0:T(8,128)(2,1)S(1)} collective-permute-done((bf16[136,1024]{1,0:T(8,128)(2,1)S(1)}, bf16[136,1024]{1,0:T(8,128)(2,1)S(1)}, u32[]{:S(2)}, u32[]{:S(2)}) %collective-permute-start.1) | collective-permute-done | bytes 278560 | tf_op jit(solution)/shard_map/ppermute | solution.py:265
  19.4 0.0 collective-permute-done.refs_3_
  19.4 0.0 collective-permute-start.6
  19.4 1.2 %collective-permute-start.7 = (bf16[144,768]{1,0:T(8,128)(2,1)S(1)}, bf16[144,768]{1,0:T(8,128)(2,1)S(1)}, u32[]{:S(2)}, u32[]{:S(2)}) collective-permute-start(bf16[144,768]{1,0:T(8,128)(2,1)S(1)} %get-tuple-element.38), channel_id=1, source_target_pairs={{0,8},{8,0},{16,24},{24,16},{1,9},{9,1},{17,25},{25,17},{2,10},{10... | collective-permute-start | bytes 663560 | tf_op jit(solution)/shard_map/ppermute | solution.py:265
  20.6 0.9 %collective-permute-start.8 = (bf16[144,768]{1,0:T(8,128)(2,1)S(1)}, bf16[144,768]{1,0:T(8,128)(2,1)S(1)}, u32[]{:S(2)}, u32[]{:S(2)}) collective-permute-start(bf16[144,768]{1,0:T(8,128)(2,1)S(1)} %get-tuple-element.39), channel_id=1, source_target_pairs={{0,16},{8,24},{16,0},{24,8},{1,17},{9,25},{17,1},{25,9},{2,18},{10... | collective-permute-start | bytes 663560 | tf_op jit(solution)/shard_map/ppermute | solution.py:265
  21.5 1.4 %collective-permute-start.9 = (bf16[144,768]{1,0:T(8,128)(2,1)S(1)}, bf16[144,768]{1,0:T(8,128)(2,1)S(1)}, u32[]{:S(2)}, u32[]{:S(2)}) collective-permute-start(bf16[144,768]{1,0:T(8,128)(2,1)S(1)} %get-tuple-element.40), channel_id=1, source_target_pairs={{0,24},{8,16},{16,8},{24,0},{1,25},{9,17},{17,9},{25,1},{2,26},{10... | collective-permute-start | bytes 663560 | tf_op jit(solution)/shard_map/ppermute | solution.py:265
  22.9 0.0 collective-permute-done.3.refs_0_
  22.9 0.0 collective-permute-start.5
  23.0 0.0 collective-permute-done.6.refs_3_
  23.0 0.5 collective-permute-start.4
  23.5 1.1 %gather.1 = (bf16[2,288,1024]{2,1,0:T(8,128)(2,1)S(1)}, bf16[4,144,128]{2,1,0:T(8,128)(2,1)S(1)}) custom-call(s32[2]{0:T(128)S(1)} %pad_add_fusion.1.place, bf16[136,1024]{1,0:T(8,128)(2,1)S(1)} %fusion.1.refs_0_, bf16[136,1024]{1,0:T(8,128)(2,1)S(1)} %collective-permute-done.2.refs_1_, bf16[136,1024]{1,0:T(8,128)(2,1)S(1)} %collective-permute-done.1.refs_2_, ...), custom_call_target="tpu_custom_call" | custom-call | flops 99999997952 | bytes 1 | tf_op jit(solution)/shard_map/gather/pallas_call | solution.py:232
  24.6 0.0 collective-permute-done.5.refs_2_
  24.6 0.3 collective-permute-done.4.refs_1_
  24.9 1.2 %copy-done = bf16[2,704,2048]{2,1,0:T(8,128)(2,1)S(1)} copy-done((bf16[2,704,2048]{2,1,0:T(8,128)(2,1)S(1)}, bf16[2,704,2048]{2,1,0:T(8,128)(2,1)}, u32[]{:S(2)}) %copy-start) | copy-done | bytes 5767192
  26.1 2.9 %grad.1 = (bf16[144,704]{1,0:T(8,128)(2,1)S(1)}, bf16[144,704]{1,0:T(8,128)(2,1)S(1)}, bf16[144,704]{1,0:T(8,128)(2,1)S(1)}, bf16[144,704]{1,0:T(8,128)(2,1)S(1)}) custom-call(s32[2]{0:T(128)S(1)} %pad_add_fusion.1.place, bf16[136,1024]{1,0:T(8,128)(2,1)S(1)} %collective-permute-done.3.refs_0_, bf16[136,1024]{1,0:T(8,128)(2,1)S(1)} %collective-permute-done.4.refs_1_, ...), custom_call_target="tpu_custom_call" | custom-call | flops 1 | bytes 1 | tf_op jit(solution)/shard_map/grad/pallas_call | solution.py:232
  29.0 1.2 %collective-permute-start.15 = (bf16[144,704]{1,0:T(8,128)(2,1)S(1)}, bf16[144,704]{1,0:T(8,128)(2,1)S(1)}, u32[]{:S(2)}, u32[]{:S(2)}) collective-permute-start(bf16[144,704]{1,0:T(8,128)(2,1)S(1)} %get-tuple-element.49), channel_id=1, source_target_pairs={{0,8},{8,0},{16,24},{24,16},{1,9},{9,1},{17,25},{25,17},{2,10},{10... | collective-permute-start | bytes 608264 | tf_op jit(solution)/shard_map/ppermute | solution.py:265
  30.2 0.9 %collective-permute-start.16 = (bf16[144,704]{1,0:T(8,128)(2,1)S(1)}, bf16[144,704]{1,0:T(8,128)(2,1)S(1)}, u32[]{:S(2)}, u32[]{:S(2)}) collective-permute-start(bf16[144,704]{1,0:T(8,128)(2,1)S(1)} %get-tuple-element.50), channel_id=1, source_target_pairs={{0,16},{8,24},{16,0},{24,8},{1,17},{9,25},{17,1},{25,9},{2,18},{10... | collective-permute-start | bytes 608264 | tf_op jit(solution)/shard_map/ppermute | solution.py:265
  31.1 0.0 collective-permute-done.7.refs_1_
  31.1 1.4 %collective-permute-start.17 = (bf16[144,704]{1,0:T(8,128)(2,1)S(1)}, bf16[144,704]{1,0:T(8,128)(2,1)S(1)}, u32[]{:S(2)}, u32[]{:S(2)}) collective-permute-start(bf16[144,704]{1,0:T(8,128)(2,1)S(1)} %get-tuple-element.51), channel_id=1, source_target_pairs={{0,24},{8,16},{16,8},{24,0},{1,25},{9,17},{17,9},{25,1},{2,26},{10... | collective-permute-start | bytes 608264 | tf_op jit(solution)/shard_map/ppermute | solution.py:265
  32.6 0.5 collective-permute-done.9.refs_3_
  33.1 2.5 %mix_sibling.1 = bf16[512,1024]{1,0:T(8,128)(2,1)S(1)} custom-call(s32[2]{0:T(128)S(1)} %pad_add_fusion.1.place, bf16[144,768]{1,0:T(8,128)(2,1)S(1)} %get-tuple-element.37.refs_0_, bf16[144,768]{1,0:T(8,128)(2,1)S(1)} %collective-permute-done.7.refs_1_, bf16[144,768]{1,0:T(8,128)(2,1)S(1)} %collective-permute-done.8.refs_2_, ...), custom_call_target="tpu_custom_call" | custom-call | flops 1 | bytes 1 | tf_op jit(solution)/shard_map/mix_sibling/pallas_call | solution.py:232
  35.6 0.1 collective-permute-start.10
  35.6 2.4 %mix_own.1.own = f32[512,1024]{1,0:T(8,128)S(1)} custom-call(s32[2]{0:T(128)S(1)} %pad_add_fusion.1.place, bf16[144,768]{1,0:T(8,128)(2,1)S(1)} %get-tuple-element.37.refs_0_, bf16[144,768]{1,0:T(8,128)(2,1)S(1)} %collective-permute-done.7.refs_1_, bf16[144,768]{1,0:T(8,128)(2,1)S(1)} %collective-permute-done.8.refs_2_, ...), custom_call_target="tpu_custom_call" | custom-call | flops 99999997952 | bytes 1 | tf_op jit(solution)/shard_map/mix_own/pallas_call | solution.py:232
  38.1 0.0 copy-start.3
  38.1 0.2 collective-permute-done.10.arrived
  38.3 0.2 add.17
  38.5 0.7 %collective-permute-start.11 = (bf16[128,512]{1,0:T(8,128)(2,1)S(1)}, bf16[128,512]{1,0:T(8,128)(2,1)S(1)}, u32[]{:S(2)}, u32[]{:S(2)}) collective-permute-start(bf16[128,512]{1,0:T(8,128)(2,1)S(1)} %get-tuple-element.44), channel_id=1, source_target_pairs={{0,8},{8,0},{16,24},{24,16},{1,9},{9,1},{17,25},{25,17},{2,10},{10... | collective-permute-start | bytes 393224 | tf_op jit(solution)/shard_map/ppermute | solution.py:265
  39.2 1.6 %collective-permute-start.12 = (bf16[128,512]{1,0:T(8,128)(2,1)S(1)}, bf16[128,512]{1,0:T(8,128)(2,1)S(1)}, u32[]{:S(2)}, u32[]{:S(2)}) collective-permute-start(bf16[128,512]{1,0:T(8,128)(2,1)S(1)} %get-tuple-element.45), channel_id=1, source_target_pairs={{0,16},{8,24},{16,0},{24,8},{1,17},{9,25},{17,1},{25,9},{2,18},{10... | collective-permute-start | bytes 393224 | tf_op jit(solution)/shard_map/ppermute | solution.py:265
  40.9 3.5 %collective-permute-done.11.low = bf16[128,512]{1,0:T(8,128)(2,1)S(1)} collective-permute-done((bf16[128,512]{1,0:T(8,128)(2,1)S(1)}, bf16[128,512]{1,0:T(8,128)(2,1)S(1)}, u32[]{:S(2)}, u32[]{:S(2)}) %collective-permute-start.11) | collective-permute-done | bytes 131104 | tf_op jit(solution)/shard_map/ppermute | solution.py:265
  44.4 0.9 %collective-permute-done.12.high = bf16[128,512]{1,0:T(8,128)(2,1)S(1)} collective-permute-done((bf16[128,512]{1,0:T(8,128)(2,1)S(1)}, bf16[128,512]{1,0:T(8,128)(2,1)S(1)}, u32[]{:S(2)}, u32[]{:S(2)}) %collective-permute-start.12) | collective-permute-done | bytes 131104 | tf_op jit(solution)/shard_map/ppermute | solution.py:265
  45.2 0.1 join.1
  45.3 0.9 %collective-permute-start.13 = (bf16[128,1024]{1,0:T(8,128)(2,1)S(1)}, bf16[128,1024]{1,0:T(8,128)(2,1)S(1)}, u32[]{:S(2)}, u32[]{:S(2)}) collective-permute-start(bf16[128,1024]{1,0:T(8,128)(2,1)S(1)} %get-tuple-element.46), channel_id=1, source_target_pairs={{0,8},{8,0},{16,24},{24,16},{1,9},{9,1},{17,25},{25,17},{2,10},{10... | collective-permute-start | bytes 786440 | tf_op jit(solution)/shard_map/ppermute | solution.py:265
  46.2 1.5 %collective-permute-start.14 = (bf16[128,1024]{1,0:T(8,128)(2,1)S(1)}, bf16[128,1024]{1,0:T(8,128)(2,1)S(1)}, u32[]{:S(2)}, u32[]{:S(2)}) collective-permute-start(bf16[128,1024]{1,0:T(8,128)(2,1)S(1)} %get-tuple-element.47), channel_id=1, source_target_pairs={{0,16},{8,24},{16,0},{24,8},{1,17},{9,25},{17,1},{25,9},{2,18},{10... | collective-permute-start | bytes 786440 | tf_op jit(solution)/shard_map/ppermute | solution.py:265
  47.7 2.3 %restore.1 = bf16[4,704,128]{2,1,0:T(8,128)(2,1)} custom-call(s32[2]{0:T(128)S(1)} %pad_add_fusion.1.place, s32[8,128]{1,0:T(8,128)S(1)} %copy-done.3, bf16[144,704]{1,0:T(8,128)(2,1)S(1)} %get-tuple-element.48.refs_0_, bf16[144,704]{1,0:T(8,128)(2,1)S(1)} %collective-permute-done.15.refs_1_, bf16[144,704]{1,0:T(8,128)(2,1)S(1)} %collective-permute-done.16.refs_2_, ...), custom_call_target="tpu_custom_call" | custom-call | flops 99999997952 | bytes 1 | tf_op jit(solution)/shard_map/restore/pallas_call | solution.py:232
  50.0 3.3 %collective-permute-done.13 = bf16[128,1024]{1,0:T(8,128)(2,1)S(1)} collective-permute-done((bf16[128,1024]{1,0:T(8,128)(2,1)S(1)}, bf16[128,1024]{1,0:T(8,128)(2,1)S(1)}, u32[]{:S(2)}, u32[]{:S(2)}) %collective-permute-start.13) | collective-permute-done | bytes 262176 | tf_op jit(solution)/shard_map/ppermute | solution.py:265
  53.3 0.3 collective-permute-done.14
  53.6 0.8 %add_convert_fusion = bf16[128,1024]{1,0:T(8,128)(2,1)} fusion(bf16[128,1024]{1,0:T(8,128)(2,1)S(1)} %collective-permute-done.14, f32[128,1024]{1,0:T(8,128)S(1)} %get-tuple-element.41, bf16[128,1024]{1,0:T(8,128)(2,1)S(1)} %collective-permute-done.13), kind=kLoop, calls=%fused_computation.2 | loop fusion | flops 655360 | bytes 1310720 | tf_op jit(solution)/shard_map/convert_element_type | solution.py:331
  (9 shorter events, 0.0 us)
Async XLA Ops:
  2.3 10.5 %collective-permute-start.2 = (bf16[136,1024]{1,0:T(8,128)(2,1)S(1)}, bf16[136,1024]{1,0:T(8,128)(2,1)S(1)}, u32[]{:S(2)}, u32[]{:S(2)}) collective-permute-start(bf16[136,1024]{1,0:T(8,128)(2,1)S(1)} %fusion.1.refs_0_), channel_id=1, source_target_pairs={{0,8},{8,0},{16,24},{24,16},{1,9},{9,1},{17,25},{25,17},{2,10},{10... | collective-permute-start | bytes 835592 | tf_op jit(solution)/shard_map/ppermute | solution.py:265
  5.3 14.1 %collective-permute-start.1 = (bf16[136,1024]{1,0:T(8,128)(2,1)S(1)}, bf16[136,1024]{1,0:T(8,128)(2,1)S(1)}, u32[]{:S(2)}, u32[]{:S(2)}) collective-permute-start(bf16[136,1024]{1,0:T(8,128)(2,1)S(1)} %fusion.1.refs_0_), channel_id=1, source_target_pairs={{0,16},{8,24},{16,0},{24,8},{1,17},{9,25},{17,1},{25,9},{2,18},{10... | collective-permute-start | bytes 835592 | tf_op jit(solution)/shard_map/ppermute | solution.py:265
  6.8 12.6 %collective-permute-start = (bf16[136,1024]{1,0:T(8,128)(2,1)S(1)}, bf16[136,1024]{1,0:T(8,128)(2,1)S(1)}, u32[]{:S(2)}, u32[]{:S(2)}) collective-permute-start(bf16[136,1024]{1,0:T(8,128)(2,1)S(1)} %fusion.1.refs_0_), channel_id=1, source_target_pairs={{0,24},{8,16},{16,8},{24,0},{1,25},{9,17},{17,9},{25,1},{2,26},{10... | collective-permute-start | bytes 835592 | tf_op jit(solution)/shard_map/ppermute | solution.py:265
  6.8 16.1 %collective-permute-start.3 = (bf16[136,1024]{1,0:T(8,128)(2,1)S(1)}, bf16[136,1024]{1,0:T(8,128)(2,1)S(1)}, u32[]{:S(2)}, u32[]{:S(2)}) collective-permute-start(bf16[136,1024]{1,0:T(8,128)(2,1)S(1)} %fusion.1.refs_0_), channel_id=1, source_target_pairs={{0,1},{1,0},{2,3},{3,2},{4,5},{5,4},{6,7},{7,6},{8,9},{9,8},{10,11... | collective-permute-start | bytes 835592 | tf_op jit(solution)/shard_map/ppermute | solution.py:268
  7.6 11.8 %copy-start.2 = (s32[8,128]{1,0:T(8,128)}, s32[8,128]{1,0:T(8,128)S(1)}, u32[]{:S(2)}) copy-start(s32[8,128]{1,0:T(8,128)S(1)} %pad_add_fusion.meta_ref) | copy-start | bytes 12292
  7.6 1.1 %copy-start.1 = (bf16[128,4,704]{0,2,1:T(8,128)(2,1)S(1)}, bf16[128,4,704]{0,2,1:T(8,128)(2,1)}, u32[]{:S(2)}) copy-start(bf16[128,4,704]{0,2,1:T(8,128)(2,1)} %param.5) | copy-start | bytes 2162692
  19.4 3.6 %collective-permute-start.6 = (bf16[136,1024]{1,0:T(8,128)(2,1)S(1)}, bf16[136,1024]{1,0:T(8,128)(2,1)S(1)}, u32[]{:S(2)}, u32[]{:S(2)}) collective-permute-start(bf16[136,1024]{1,0:T(8,128)(2,1)S(1)} %collective-permute-done.refs_3_), channel_id=1, source_target_pairs={{0,1},{1,0},{2,3},{3,2},{4,5},{5,4},{6,7},{7,6},{8,9},{9,8},{10,11... | collective-permute-start | bytes 835592 | tf_op jit(solution)/shard_map/ppermute | solution.py:268
  19.4 11.7 %collective-permute-start.7 = (bf16[144,768]{1,0:T(8,128)(2,1)S(1)}, bf16[144,768]{1,0:T(8,128)(2,1)S(1)}, u32[]{:S(2)}, u32[]{:S(2)}) collective-permute-start(bf16[144,768]{1,0:T(8,128)(2,1)S(1)} %get-tuple-element.38), channel_id=1, source_target_pairs={{0,8},{8,0},{16,24},{24,16},{1,9},{9,1},{17,25},{25,17},{2,10},{10... | collective-permute-start | bytes 663560 | tf_op jit(solution)/shard_map/ppermute | solution.py:265
  20.6 11.9 %collective-permute-start.8 = (bf16[144,768]{1,0:T(8,128)(2,1)S(1)}, bf16[144,768]{1,0:T(8,128)(2,1)S(1)}, u32[]{:S(2)}, u32[]{:S(2)}) collective-permute-start(bf16[144,768]{1,0:T(8,128)(2,1)S(1)} %get-tuple-element.39), channel_id=1, source_target_pairs={{0,16},{8,24},{16,0},{24,8},{1,17},{9,25},{17,1},{25,9},{2,18},{10... | collective-permute-start | bytes 663560 | tf_op jit(solution)/shard_map/ppermute | solution.py:265
  21.5 11.6 %collective-permute-start.9 = (bf16[144,768]{1,0:T(8,128)(2,1)S(1)}, bf16[144,768]{1,0:T(8,128)(2,1)S(1)}, u32[]{:S(2)}, u32[]{:S(2)}) collective-permute-start(bf16[144,768]{1,0:T(8,128)(2,1)S(1)} %get-tuple-element.40), channel_id=1, source_target_pairs={{0,24},{8,16},{16,8},{24,0},{1,25},{9,17},{17,9},{25,1},{2,26},{10... | collective-permute-start | bytes 663560 | tf_op jit(solution)/shard_map/ppermute | solution.py:265
  22.9 1.7 %collective-permute-start.5 = (bf16[136,1024]{1,0:T(8,128)(2,1)S(1)}, bf16[136,1024]{1,0:T(8,128)(2,1)S(1)}, u32[]{:S(2)}, u32[]{:S(2)}) collective-permute-start(bf16[136,1024]{1,0:T(8,128)(2,1)S(1)} %collective-permute-done.1.refs_2_), channel_id=1, source_target_pairs={{0,1},{1,0},{2,3},{3,2},{4,5},{5,4},{6,7},{7,6},{8,9},{9,8},{10,11... | collective-permute-start | bytes 835592 | tf_op jit(solution)/shard_map/ppermute | solution.py:268
  23.0 1.9 %collective-permute-start.4 = (bf16[136,1024]{1,0:T(8,128)(2,1)S(1)}, bf16[136,1024]{1,0:T(8,128)(2,1)S(1)}, u32[]{:S(2)}, u32[]{:S(2)}) collective-permute-start(bf16[136,1024]{1,0:T(8,128)(2,1)S(1)} %collective-permute-done.2.refs_1_), channel_id=1, source_target_pairs={{0,1},{1,0},{2,3},{3,2},{4,5},{5,4},{6,7},{7,6},{8,9},{9,8},{10,11... | collective-permute-start | bytes 835592 | tf_op jit(solution)/shard_map/ppermute | solution.py:268
  23.5 2.6 %copy-start = (bf16[2,704,2048]{2,1,0:T(8,128)(2,1)S(1)}, bf16[2,704,2048]{2,1,0:T(8,128)(2,1)}, u32[]{:S(2)}) copy-start(bf16[2,704,2048]{2,1,0:T(8,128)(2,1)} %refs_4_.3) | copy-start | bytes 17301508
  29.0 18.7 %collective-permute-start.15 = (bf16[144,704]{1,0:T(8,128)(2,1)S(1)}, bf16[144,704]{1,0:T(8,128)(2,1)S(1)}, u32[]{:S(2)}, u32[]{:S(2)}) collective-permute-start(bf16[144,704]{1,0:T(8,128)(2,1)S(1)} %get-tuple-element.49), channel_id=1, source_target_pairs={{0,8},{8,0},{16,24},{24,16},{1,9},{9,1},{17,25},{25,17},{2,10},{10... | collective-permute-start | bytes 608264 | tf_op jit(solution)/shard_map/ppermute | solution.py:265
  30.2 17.4 %collective-permute-start.16 = (bf16[144,704]{1,0:T(8,128)(2,1)S(1)}, bf16[144,704]{1,0:T(8,128)(2,1)S(1)}, u32[]{:S(2)}, u32[]{:S(2)}) collective-permute-start(bf16[144,704]{1,0:T(8,128)(2,1)S(1)} %get-tuple-element.50), channel_id=1, source_target_pairs={{0,16},{8,24},{16,0},{24,8},{1,17},{9,25},{17,1},{25,9},{2,18},{10... | collective-permute-start | bytes 608264 | tf_op jit(solution)/shard_map/ppermute | solution.py:265
  31.1 16.6 %collective-permute-start.17 = (bf16[144,704]{1,0:T(8,128)(2,1)S(1)}, bf16[144,704]{1,0:T(8,128)(2,1)S(1)}, u32[]{:S(2)}, u32[]{:S(2)}) collective-permute-start(bf16[144,704]{1,0:T(8,128)(2,1)S(1)} %get-tuple-element.51), channel_id=1, source_target_pairs={{0,24},{8,16},{16,8},{24,0},{1,25},{9,17},{17,9},{25,1},{2,26},{10... | collective-permute-start | bytes 608264 | tf_op jit(solution)/shard_map/ppermute | solution.py:265
  35.6 2.7 %collective-permute-start.10 = (bf16[512,1024]{1,0:T(8,128)(2,1)S(1)}, bf16[512,1024]{1,0:T(8,128)(2,1)S(1)}, u32[]{:S(2)}, u32[]{:S(2)}) collective-permute-start(bf16[512,1024]{1,0:T(8,128)(2,1)S(1)} %mix_sibling.1), channel_id=1, source_target_pairs={{0,1},{1,0},{2,3},{3,2},{4,5},{5,4},{6,7},{7,6},{8,9},{9,8},{10,11... | collective-permute-start | bytes 3145736 | tf_op jit(solution)/shard_map/ppermute | solution.py:268
  38.1 9.6 %copy-start.3 = (s32[8,128]{1,0:T(8,128)S(1)}, s32[8,128]{1,0:T(8,128)}, u32[]{:S(2)}) copy-start(s32[8,128]{1,0:T(8,128)} %copy-done.2) | copy-start | bytes 12292
  38.5 5.9 %collective-permute-start.11 = (bf16[128,512]{1,0:T(8,128)(2,1)S(1)}, bf16[128,512]{1,0:T(8,128)(2,1)S(1)}, u32[]{:S(2)}, u32[]{:S(2)}) collective-permute-start(bf16[128,512]{1,0:T(8,128)(2,1)S(1)} %get-tuple-element.44), channel_id=1, source_target_pairs={{0,8},{8,0},{16,24},{24,16},{1,9},{9,1},{17,25},{25,17},{2,10},{10... | collective-permute-start | bytes 393224 | tf_op jit(solution)/shard_map/ppermute | solution.py:265
  39.2 6.0 %collective-permute-start.12 = (bf16[128,512]{1,0:T(8,128)(2,1)S(1)}, bf16[128,512]{1,0:T(8,128)(2,1)S(1)}, u32[]{:S(2)}, u32[]{:S(2)}) collective-permute-start(bf16[128,512]{1,0:T(8,128)(2,1)S(1)} %get-tuple-element.45), channel_id=1, source_target_pairs={{0,16},{8,24},{16,0},{24,8},{1,17},{9,25},{17,1},{25,9},{2,18},{10... | collective-permute-start | bytes 393224 | tf_op jit(solution)/shard_map/ppermute | solution.py:265
  45.3 8.0 %collective-permute-start.13 = (bf16[128,1024]{1,0:T(8,128)(2,1)S(1)}, bf16[128,1024]{1,0:T(8,128)(2,1)S(1)}, u32[]{:S(2)}, u32[]{:S(2)}) collective-permute-start(bf16[128,1024]{1,0:T(8,128)(2,1)S(1)} %get-tuple-element.46), channel_id=1, source_target_pairs={{0,8},{8,0},{16,24},{24,16},{1,9},{9,1},{17,25},{25,17},{2,10},{10... | collective-permute-start | bytes 786440 | tf_op jit(solution)/shard_map/ppermute | solution.py:265
  46.2 7.4 %collective-permute-start.14 = (bf16[128,1024]{1,0:T(8,128)(2,1)S(1)}, bf16[128,1024]{1,0:T(8,128)(2,1)S(1)}, u32[]{:S(2)}, u32[]{:S(2)}) collective-permute-start(bf16[128,1024]{1,0:T(8,128)(2,1)S(1)} %get-tuple-element.47), channel_id=1, source_target_pairs={{0,16},{8,24},{16,0},{24,8},{1,17},{9,25},{17,1},{25,9},{2,18},{10... | collective-permute-start | bytes 786440 | tf_op jit(solution)/shard_map/ppermute | solution.py:265
where the time goes:
time: 54.6 us; the launch traced here: 54.4 us
  waiting for transfers between devices  18.3 us (34%)
  starting transfers between devices  17 us (31%)
  Pallas kernels  12.8 us (23%)
  other arithmetic  3.24 us (6%)
  local copies, waits for them, and re-layouts  2.31 us (4%)
  between operations  0.73 us (1%)
    ppermute x13, waiting for transfers between devices, send(): return lax.ppermute(x, 'ctx', [(i, i ^ s) for i in range(n)]) if s else x  17.8 us
    ppermute x13, starting transfers between devices, send(): return lax.ppermute(x, 'ctx', [(i, i ^ s) for i in range(n)]) if s else x  16.4 us
    pallas_call x8, Pallas kernels, call(): pl.pallas_call(kernel, out_shape=outs, in_specs=[pl.BlockSpec(memory_spac...  12.8 us
    unnamed x8, local copies, waits for them, and re-layouts  2.31 us
  transfers between devices with their start and end apart: 18, of which 9 were waited for; matrix products, arithmetic and copies ran while one was open for 1% of the time, Pallas kernels for 24%

commit v1 on v0

--- a/solution.py
+++ b/solution.py
@@ -13,6 +13,7 @@
 NT = (((1,), (1,)), ((), ()))
 TN = (((0,), (0,)), ((), ()))
 BIG = 10**11
+W_GATHER, W_GRAD, W_FAR, FAR_LATE = 1, 1, 1, False
 
 
 def dot(a, b, dims):
@@ -73,7 +74,8 @@
 
 
 def dispatch_kernel(dims, place, meta_ref, hid_ref, *outs):
-    width = outs[0].shape[0]
+    experts, local, cap, width = dims
+    count = experts // local
     picks, gate = picks_of(meta_ref[...], place[0], dims)
     scaled = [
         (hid_ref[k].astype(F32) * gate[k : k + 1, :]).astype(BF16)
@@ -85,8 +87,23 @@
     number = jnp.bitwise_and(iota((spare, rows.shape[1]), 1), tokens - 1) + 1
     number = jnp.where(iota(number.shape, 0) == 0, number.astype(F32), 0.0)
     sent = dot(picks, jnp.concatenate([rows, number.astype(BF16)], axis=0), NT)
-    for s, out in enumerate(outs):
-        out[...] = sent[s * width : (s + 1) * width].astype(BF16)
+    sent = [sent[s * width : (s + 1) * width] for s in range(count)]
+    if len(outs) < count:
+        mine, one, two, far = sent
+        first = outs[1].shape[0] - width
+        sent = [
+            mine,
+            jnp.concatenate([one, far[:first]], axis=0),
+            jnp.concatenate([two, far[first:]], axis=0),
+        ]
+    for rows, out in zip(sent, outs):
+        out[...] = rows.astype(BF16)
+
+
+def pass_rows_kernel(one, two, to_two, to_one):
+    first, second = to_two.shape[0], to_one.shape[0]
+    to_two[...] = one[one.shape[0] - first :]
+    to_one[...] = two[two.shape[0] - second :]
 
 
 def by_expert(rows, local, cap):
@@ -127,6 +144,14 @@
     for s, h in enumerate(held):
         held_ref[s] = h
     gather_rows(dims, held, own, x_ref)
+
+
+def gather_pass_kernel(dims, top, place, *refs):
+    own, (x_ref, held_ref, low, high) = refs[:3], refs[3:]
+    cut = low.shape[1]
+    low[...] = own[1][:, :cut]
+    high[...] = own[2][:, cut:]
+    gather_kernel(dims, top, place, *own, x_ref, held_ref)
 
 
 def products(dims, place, x_ref, x_other, w_ref):
@@ -150,18 +175,40 @@
         outs[s][...] = rows.astype(BF16)
 
 
+def grad_far_kernel(dims, top, place, low, high, low_other, high_other, w_ref, out, x_ref, x_other):
+    experts, local, cap, width = dims
+    cut = low.shape[1]
+    tokens = low.shape[0] - 8
+    held = [routes(dims, top, place[0], low, tokens)]
+    for ref, at, x in (
+        (low, 0, x_ref), (high, cut, x_ref), (low_other, 0, x_other), (high_other, cut, x_other)
+    ):
+        gather_rows(dims, held, [ref], x.at[:, :, pl.ds(at, cut)])
+    grads = products(dims, place, x_ref, x_other, w_ref)
+    out[...] = jnp.concatenate(grads, axis=0).astype(BF16)
+
+
+def whole_rows(dims, hid):
+    experts, local, cap, width = dims
+    if len(hid) <= experts // local:
+        return [h[...].astype(F32) for h in hid]
+    mine, one, two, first, second = [h[...].astype(F32) for h in hid]
+    return [mine, one[:width], two[:width], jnp.concatenate([first, second], axis=0)]
+
+
 def mix_rows(dims, side, hid, w_ref, tokens, half, store):
     experts, local, cap, width = dims
-    n = len(hid)
+    n = dims[0] // dims[1]
     ff = w_ref.shape[1]
     chunk = min(half, 256)
     same = ones_where(iota((tokens, tokens), 0) == iota((tokens, tokens), 1))
+    hid = whole_rows(dims, hid)
     held = []
     for h in hid:
-        number = h[:, ff : ff + 1].astype(F32).astype(jnp.int32) - 1
+        number = h[:, ff : ff + 1].astype(jnp.int32) - 1
         slots = ones_where(iota((width, tokens), 1) == number)
         held.append(dot(same, slots, NT).astype(BF16))
-    rows = [h[:, :ff].astype(F32) for h in hid]
+    rows = [h[:, :ff] for h in hid]
     x = [r.astype(BF16) for r in by_expert(rows, local, cap)]
     for c in range(0, half, chunk):
         at = pl.ds(pl.multiple_of(side * half + c, chunk), chunk)
@@ -172,7 +219,7 @@
 
 def mix_kernel(dims, sibling, place, *refs):
     hid, (w_ref, out) = refs[:-2], refs[-2:]
-    tokens = out.shape[0] // len(hid)
+    tokens = out.shape[0] // (dims[0] // dims[1])
 
     def store(s, columns, part):
         out[pl.ds(s * tokens, tokens), columns] = part.astype(out.dtype)
@@ -272,29 +319,54 @@
     named = jnp.pad(expert_ids.T.astype(BF16), ((0, 8 - top), (0, half - tokens)))
     packed = jnp.concatenate([grad_out, named], axis=0)
     forward = n == 4
-    own = [send(packed, s) for s in range(n)]
+    near = 3 if forward else n
+    own = [send(packed, s) for s in range(near)]
+    swapped = swap(packed)
+    lanes = -(-(ff + 1) // 128) * 128
+    first = -(-(width // 2) // 16) * 16
+    rows = [width, width + first, 2 * width - first] if forward else [width] * n
     hid_sent = run(
-        functools.partial(dispatch_kernel, dims), [shaped((width, -(-(ff + 1) // 128) * 128))] * n,
+        functools.partial(dispatch_kernel, dims), [shaped((r, lanes)) for r in rows],
         [place, meta, hid_t], where=placed, name="dispatch",
     )
-    hid = [send(hid_sent[s], s) for s in range(n)]
-    for s in range(1, n):
+    hid = [send(hid_sent[s], s) for s in range(near)]
+    for s in range(1, near):
         own[s], hid[0] = lax.optimization_barrier((own[s], hid[0]))
-    other = [swap(x) for x in own]
+    other = [swapped] + [swap(x) for x in own[1:]]
 
     slot = shaped((width, ff))
-    x, held = run(
-        functools.partial(gather_kernel, dims, top),
-        [shaped((local, n * cap, half)), shaped((n, width, tokens))],
-        [place, *own], where=placed, name="gather", weight=BIG,
-    )
+    x_near = shaped((local, near * cap, half))
+    held_near = shaped((near, width, tokens))
+    if forward:
+        cut = half // 2
+        passed = shaped((tokens + 8, cut))
+        x, held, low, high = run(
+            functools.partial(gather_pass_kernel, dims, top),
+            [x_near, held_near, passed, passed], [place, *own],
+            where=placed, name="gather", weight=W_GATHER,
+        )
+        low, high = send(low, 2), send(high, 1)
+    else:
+        x, held = run(
+            functools.partial(gather_kernel, dims, top), [x_near, held_near],
+            [place, *own], where=placed, name="gather",
+        )
     grad_sent = run(
-        functools.partial(grad_kernel, dims), [slot] * n,
+        functools.partial(grad_kernel, dims), [slot] * near,
         [place, *other, x, held, w_down], where=placed,
-        scratch=[pltpu.VMEM((local, n * cap, half), BF16)], name="grad",
-    )
-    hid[0], grad_own = lax.optimization_barrier((hid[0], grad_sent[0]))
-    grad_back = [grad_own] + [send(grad_sent[s], s) for s in range(1, n)]
+        scratch=[pltpu.VMEM(x_near.shape, BF16)], name="grad", weight=W_GRAD,
+    )
+    if forward:
+        hid[1], hid[2], grad_own = lax.optimization_barrier((hid[1], hid[2], grad_sent[0]))
+        to_two, to_one = run(
+            pass_rows_kernel, [shaped((first, lanes)), shaped((width - first, lanes))],
+            hid[1:], name="pass_rows", weight=BIG,
+        )
+        hid += [send(to_two, 2), send(to_one, 1)]
+        low, high, *hid[3:] = lax.optimization_barrier((low, high, *hid[3:]))
+    else:
+        hid[0], grad_own = lax.optimization_barrier((hid[0], grad_sent[0]))
+    grad_back = [grad_own] + [send(grad_sent[s], s) for s in range(1, near)]
 
     (theirs,) = run(
         functools.partial(mix_kernel, dims, True), [shaped((n * tokens, half))],
@@ -306,11 +378,19 @@
             functools.partial(mix_kernel, dims, False), [shaped((n * tokens, half), F32)],
             [place, *hid, w_down], where=placed, name="mix_own", weight=BIG,
         )
-        cut = half // 2
         block, piece = shaped((tokens, half), F32), shaped((tokens, cut))
         kept, one, two, one_low, two_high = run(
             add_split_kernel, [block] * 3 + [piece] * 2, [mine, arrived], name="add"
         )
+        if FAR_LATE:
+            low, kept = lax.optimization_barrier((low, kept))
+        x_far = pltpu.VMEM((local, cap, half), BF16)
+        (grad_far,) = run(
+            functools.partial(grad_far_kernel, dims, top), [slot],
+            [place, low, high, swap(low), swap(high), w_down], where=placed,
+            scratch=[x_far, x_far], name="grad_far", weight=W_FAR,
+        )
+        grad_back.append(send(grad_far, 3))
         one_low, two_high = send(one_low, 1), send(two_high, 2)
         to_one, to_two = run(
             join_kernel, [shaped((tokens, half))] * 2, [one, two, one_low, two_high],

time: 54.6 us -> 58.9 us (1.079)
  Pallas kernels: 12.8 us -> 15.1 us
  starting transfers between devices: 17 us -> 18.6 us
  local copies, waits for them, and re-layouts: 2.31 us -> 3.77 us
  waiting for transfers between devices: 18.3 us -> 17.2 us
    pallas_call x8 -> x10, Pallas kernels: 12.8 us -> 15.1 us  [call(): pl.pallas_call(kernel, out_shape=outs, in_specs=[pl.BlockSpec(memory_spac...]
    unnamed x8 -> x12, local copies, waits for them, and re-layouts: 2.31 us -> 3.77 us
    ppermute x13 -> x15, starting transfers between devices: 16.4 us -> 17.5 us  [send(): return lax.ppermute(x, 'ctx', [(i, i ^ s) for i in range(n)]) if s else x]
    ppermute x13 -> x15, waiting for transfers between devices: 17.8 us -> 17.2 us  [send(): return lax.ppermute(x, 'ctx', [(i, i ^ s) for i in range(n)]) if s else x]
  transfers between devices with their start and end apart: 18 -> 21, of which waited for: 9 -> 8; matrix products, arithmetic and copies ran while one was open for 1% -> 1% of each run, Pallas kernels for 24% -> 26%
where the time goes in v1:
time: 58.9 us; the launch traced here: 58.6 us
  starting transfers between devices  18.6 us (32%)
  waiting for transfers between devices  17.2 us (29%)
  Pallas kernels  15.1 us (26%)
  local copies, waits for them, and re-layouts  3.77 us (6%)
  other arithmetic  3.23 us (5%)
  between operations  0.8 us (1%)
    ppermute x15, starting transfers between devices, send(): return lax.ppermute(x, 'ctx', [(i, i ^ s) for i in range(n)]) if s else x  17.5 us
    ppermute x15, waiting for transfers between devices, send(): return lax.ppermute(x, 'ctx', [(i, i ^ s) for i in range(n)]) if s else x  17.2 us
    pallas_call x10, Pallas kernels, call(): pl.pallas_call(kernel, out_shape=outs, in_specs=[pl.BlockSpec(memory_spac...  15.1 us
    unnamed x12, local copies, waits for them, and re-layouts  3.77 us
  transfers between devices with their start and end apart: 21, of which 8 were waited for; matrix products, arithmetic and copies ran while one was open for 1% of the time, Pallas kernels for 26%

profile of v1, /device:TPU:0, one launch (start us, length us, event | category | flops | bytes accessed | tf_op | source)
XLA Modules:
  0.0 58.6 jit_solution(845837418770890197)
XLA Ops:
  0.6 0.7 %bitcast_convert_fusion = bf16[4,128]{1,0:T(4,128)(2,1)S(1)} fusion(s32[128,4]{0,1:T(4,128)} %param.6), kind=kLoop, calls=%fused_computation.6 | loop fusion | flops 512 | bytes 3072 | tf_op jit(solution)/shard_map/convert_element_type | solution.py:319
  1.3 1.0 %fusion.1.refs_0_ = bf16[136,1024]{1,0:T(8,128)(2,1)S(1)} fusion(bf16[4,128]{1,0:T(4,128)(2,1)S(1)} %bitcast_convert_fusion, bf16[128,1024]{1,0:T(8,128)(2,1)} %param.8), kind=kLoop, calls=%fused_computation.3 | loop fusion | flops 835584 | bytes 541696 | tf_op jit(solution)/shard_map/concatenate | solution.py:320
  2.3 3.0 %collective-permute-start.1 = (bf16[136,1024]{1,0:T(8,128)(2,1)S(1)}, bf16[136,1024]{1,0:T(8,128)(2,1)S(1)}, u32[]{:S(2)}, u32[]{:S(2)}) collective-permute-start(bf16[136,1024]{1,0:T(8,128)(2,1)S(1)} %fusion.1.refs_0_), channel_id=1, source_target_pairs={{0,8},{8,0},{16,24},{24,16},{1,9},{9,1},{17,25},{25,17},{2,10},{10... | collective-permute-start | bytes 835592 | tf_op jit(solution)/shard_map/ppermute | solution.py:312
  5.3 1.5 %collective-permute-start = (bf16[136,1024]{1,0:T(8,128)(2,1)S(1)}, bf16[136,1024]{1,0:T(8,128)(2,1)S(1)}, u32[]{:S(2)}, u32[]{:S(2)}) collective-permute-start(bf16[136,1024]{1,0:T(8,128)(2,1)S(1)} %fusion.1.refs_0_), channel_id=1, source_target_pairs={{0,16},{8,24},{16,0},{24,8},{1,17},{9,25},{17,1},{25,9},{2,18},{10... | collective-permute-start | bytes 835592 | tf_op jit(solution)/shard_map/ppermute | solution.py:312
  6.8 0.1 pad_add_fusion.1.place
  6.9 0.7 %pad_add_fusion.meta_ref = s32[8,128]{1,0:T(8,128)S(1)} fusion(s32[4,128]{1,0:T(4,128)} %bitcast.11, s32[4,128]{1,0:T(4,128)} %bitcast.10), kind=kLoop, calls=%fused_computation.4 | loop fusion | flops 1024 | bytes 8192 | tf_op jit(solution)/shard_map/concatenate | solution.py:317
  7.6 1.1 %copy-done.1 = bf16[128,4,704]{0,2,1:T(8,128)(2,1)S(1)} copy-done((bf16[128,4,704]{0,2,1:T(8,128)(2,1)S(1)}, bf16[128,4,704]{0,2,1:T(8,128)(2,1)}, u32[]{:S(2)}) %copy-start.1) | copy-done | bytes 720920
  8.7 1.4 %dispatch.1 = (bf16[144,768]{1,0:T(8,128)(2,1)S(1)}, bf16[224,768]{1,0:T(8,128)(2,1)S(1)}, bf16[208,768]{1,0:T(8,128)(2,1)S(1)}) custom-call(s32[2]{0:T(128)S(1)} %pad_add_fusion.1.place, s32[8,128]{1,0:T(8,128)S(1)} %pad_add_fusion.meta_ref, bf16[4,704,128]{2,1,0:T(8,128)(2,1)S(1)} %bitcast.9), custom_call_target="tpu_custom_call" | custom-call | flops 1 | bytes 1 | tf_op jit(solution)/shard_map/dispatch/pallas_call | solution.py:279
  10.1 0.6 %collective-permute-start.2 = (bf16[224,768]{1,0:T(8,128)(2,1)S(1)}, bf16[224,768]{1,0:T(8,128)(2,1)S(1)}, u32[]{:S(2)}, u32[]{:S(2)}) collective-permute-start(bf16[224,768]{1,0:T(8,128)(2,1)S(1)} %get-tuple-element.35), channel_id=1, source_target_pairs={{0,8},{8,0},{16,24},{24,16},{1,9},{9,1},{17,25},{25,17},{2,10},{10... | collective-permute-start | bytes 1032200 | tf_op jit(solution)/shard_map/ppermute | solution.py:312
  10.7 0.1 collective-permute-start.3
  10.7 0.0 collective-permute-start.4
  10.7 1.6 %collective-permute-done.1.refs_1_ = bf16[136,1024]{1,0:T(8,128)(2,1)S(1)} collective-permute-done((bf16[136,1024]{1,0:T(8,128)(2,1)S(1)}, bf16[136,1024]{1,0:T(8,128)(2,1)S(1)}, u32[]{:S(2)}, u32[]{:S(2)}) %collective-permute-start.1) | collective-permute-done | bytes 278560 | tf_op jit(solution)/shard_map/ppermute | solution.py:312
  12.3 2.2 %collective-permute-done.refs_2_ = bf16[136,1024]{1,0:T(8,128)(2,1)S(1)} collective-permute-done((bf16[136,1024]{1,0:T(8,128)(2,1)S(1)}, bf16[136,1024]{1,0:T(8,128)(2,1)S(1)}, u32[]{:S(2)}, u32[]{:S(2)}) %collective-permute-start) | collective-permute-done | bytes 278560 | tf_op jit(solution)/shard_map/ppermute | solution.py:312
  14.5 0.0 collective-permute-start.6
  14.5 0.5 collective-permute-start.5
  15.0 1.1 %gather.1 = (bf16[2,216,1024]{2,1,0:T(8,128)(2,1)S(1)}, bf16[3,144,128]{2,1,0:T(8,128)(2,1)S(1)}, bf16[136,512]{1,0:T(8,128)(2,1)S(1)}, bf16[136,512]{1,0:T(8,128)(2,1)S(1)}) custom-call(s32[2]{0:T(128)S(1)} %pad_add_fusion.1.place, bf16[136,1024]{1,0:T(8,128)(2,1)S(1)} %fusion.1.refs_0_, bf16[136,1024]{1,0:T(8,128)(2,1)S(1)} %collective-permute-done.1.refs_1_, ...), custom_call_target="tpu_custom_call" | custom-call | flops 1 | bytes 1 | tf_op jit(solution)/shard_map/gather/pallas_call | solution.py:279
  16.1 2.0 %collective-permute-start.7 = (bf16[136,512]{1,0:T(8,128)(2,1)S(1)}, bf16[136,512]{1,0:T(8,128)(2,1)S(1)}, u32[]{:S(2)}, u32[]{:S(2)}) collective-permute-start(bf16[136,512]{1,0:T(8,128)(2,1)S(1)} %get-tuple-element.44), channel_id=1, source_target_pairs={{0,16},{8,24},{16,0},{24,8},{1,17},{9,25},{17,1},{25,9},{2,18},{10... | collective-permute-start | bytes 417800 | tf_op jit(solution)/shard_map/ppermute | solution.py:312
  18.1 0.0 collective-permute-done.6.refs_2_
  18.1 0.2 collective-permute-start.8
  18.3 0.0 collective-permute-done.5.refs_1_
  18.3 2.6 %copy-done = bf16[2,704,2048]{2,1,0:T(8,128)(2,1)S(1)} copy-done((bf16[2,704,2048]{2,1,0:T(8,128)(2,1)S(1)}, bf16[2,704,2048]{2,1,0:T(8,128)(2,1)}, u32[]{:S(2)}) %copy-start) | copy-done | bytes 5767192
  20.9 2.6 %grad.1 = (bf16[144,704]{1,0:T(8,128)(2,1)S(1)}, bf16[144,704]{1,0:T(8,128)(2,1)S(1)}, bf16[144,704]{1,0:T(8,128)(2,1)S(1)}) custom-call(s32[2]{0:T(128)S(1)} %pad_add_fusion.1.place, bf16[136,1024]{1,0:T(8,128)(2,1)S(1)} %collective-permute-done.4.refs_0_, bf16[136,1024]{1,0:T(8,128)(2,1)S(1)} %collective-permute-done.5.refs_1_, ...), custom_call_target="tpu_custom_call" | custom-call | flops 1 | bytes 1 | tf_op jit(solution)/shard_map/grad/pallas_call | solution.py:279
  23.5 0.0 slice-start.1
  23.6 0.3 collective-permute-start.9
  23.8 1.7 %collective-permute-start.10 = (bf16[64,768]{1,0:T(8,128)(2,1)S(1)}, bf16[64,768]{1,0:T(8,128)(2,1)S(1)}, u32[]{:S(2)}, u32[]{:S(2)}) collective-permute-start(bf16[64,768]{1,0:T(8,128)(2,1)S(1)} %get-tuple-element.47), channel_id=1, source_target_pairs={{0,8},{8,0},{16,24},{24,16},{1,9},{9,1},{17,25},{25,17},{2,10},{10... | collective-permute-start | bytes 294920 | tf_op jit(solution)/shard_map/ppermute | solution.py:312
  25.6 2.9 %collective-permute-done.10.refs_4_ = bf16[64,768]{1,0:T(8,128)(2,1)S(1)} collective-permute-done((bf16[64,768]{1,0:T(8,128)(2,1)S(1)}, bf16[64,768]{1,0:T(8,128)(2,1)S(1)}, u32[]{:S(2)}, u32[]{:S(2)}) %collective-permute-start.10) | collective-permute-done | bytes 98336 | tf_op jit(solution)/shard_map/ppermute | solution.py:312
  28.5 0.1 collective-permute-done.9.refs_3_
  28.5 0.5 collective-permute-start.19
  29.0 1.8 %collective-permute-start.16 = (bf16[144,704]{1,0:T(8,128)(2,1)S(1)}, bf16[144,704]{1,0:T(8,128)(2,1)S(1)}, u32[]{:S(2)}, u32[]{:S(2)}) collective-permute-start(bf16[144,704]{1,0:T(8,128)(2,1)S(1)} %get-tuple-element.58), channel_id=1, source_target_pairs={{0,8},{8,0},{16,24},{24,16},{1,9},{9,1},{17,25},{25,17},{2,10},{10... | collective-permute-start | bytes 608264 | tf_op jit(solution)/shard_map/ppermute | solution.py:312
  30.8 1.8 %collective-permute-start.17 = (bf16[144,704]{1,0:T(8,128)(2,1)S(1)}, bf16[144,704]{1,0:T(8,128)(2,1)S(1)}, u32[]{:S(2)}, u32[]{:S(2)}) collective-permute-start(bf16[144,704]{1,0:T(8,128)(2,1)S(1)} %get-tuple-element.59), channel_id=1, source_target_pairs={{0,16},{8,24},{16,0},{24,8},{1,17},{9,25},{17,1},{25,9},{2,18},{10... | collective-permute-start | bytes 608264 | tf_op jit(solution)/shard_map/ppermute | solution.py:312
  32.6 2.5 %mix_sibling.1 = bf16[512,1024]{1,0:T(8,128)(2,1)S(1)} custom-call(s32[2]{0:T(128)S(1)} %pad_add_fusion.1.place, bf16[144,768]{1,0:T(8,128)(2,1)S(1)} %get-tuple-element.34.refs_0_, bf16[224,768]{1,0:T(8,128)(2,1)S(1)} %collective-permute-done.2.one.refs_1_, bf16[208,768]{1,0:T(8,128)(2,1)S(1)} %collective-permute-done.3.two.refs_2_, ...), custom_call_target="tpu_custom_call" | custom-call | flops 1 | bytes 1 | tf_op jit(solution)/shard_map/mix_sibling/pallas_call | solution.py:279
  35.1 0.1 collective-permute-start.11
  35.2 2.6 %grad_far.1 = bf16[144,704]{1,0:T(8,128)(2,1)S(1)} custom-call(s32[2]{0:T(128)S(1)} %pad_add_fusion.1.place, bf16[136,512]{1,0:T(8,128)(2,1)S(1)} %collective-permute-done.7.low, bf16[136,512]{1,0:T(8,128)(2,1)S(1)} %collective-permute-done.8.high, bf16[136,512]{1,0:T(8,128)(2,1)S(1)} %collective-permute-done.18.low_other, ...), custom_call_target="tpu_custom_call" | custom-call | flops 1 | bytes 1 | tf_op jit(solution)/shard_map/grad_far/pallas_call | solution.py:279
  37.8 0.0 copy-start.3
  37.8 0.1 collective-permute-start.20
  37.9 2.4 %mix_own.1.own = f32[512,1024]{1,0:T(8,128)S(1)} custom-call(s32[2]{0:T(128)S(1)} %pad_add_fusion.1.place, bf16[144,768]{1,0:T(8,128)(2,1)S(1)} %get-tuple-element.34.refs_0_, bf16[224,768]{1,0:T(8,128)(2,1)S(1)} %collective-permute-done.2.one.refs_1_, bf16[208,768]{1,0:T(8,128)(2,1)S(1)} %collective-permute-done.3.two.refs_2_, ...), custom_call_target="tpu_custom_call" | custom-call | flops 99999997952 | bytes 1 | tf_op jit(solution)/shard_map/mix_own/pallas_call | solution.py:279
  40.3 0.2 add.17
  40.5 1.8 %collective-permute-start.12 = (bf16[128,512]{1,0:T(8,128)(2,1)S(1)}, bf16[128,512]{1,0:T(8,128)(2,1)S(1)}, u32[]{:S(2)}, u32[]{:S(2)}) collective-permute-start(bf16[128,512]{1,0:T(8,128)(2,1)S(1)} %get-tuple-element.53), channel_id=1, source_target_pairs={{0,8},{8,0},{16,24},{24,16},{1,9},{9,1},{17,25},{25,17},{2,10},{10... | collective-permute-start | bytes 393224 | tf_op jit(solution)/shard_map/ppermute | solution.py:312
  42.3 1.8 %collective-permute-start.13 = (bf16[128,512]{1,0:T(8,128)(2,1)S(1)}, bf16[128,512]{1,0:T(8,128)(2,1)S(1)}, u32[]{:S(2)}, u32[]{:S(2)}) collective-permute-start(bf16[128,512]{1,0:T(8,128)(2,1)S(1)} %get-tuple-element.54), channel_id=1, source_target_pairs={{0,16},{8,24},{16,0},{24,8},{1,17},{9,25},{17,1},{25,9},{2,18},{10... | collective-permute-start | bytes 393224 | tf_op jit(solution)/shard_map/ppermute | solution.py:312
  44.0 4.1 %collective-permute-done.12.low = bf16[128,512]{1,0:T(8,128)(2,1)S(1)} collective-permute-done((bf16[128,512]{1,0:T(8,128)(2,1)S(1)}, bf16[128,512]{1,0:T(8,128)(2,1)S(1)}, u32[]{:S(2)}, u32[]{:S(2)}) %collective-permute-start.12) | collective-permute-done | bytes 131104 | tf_op jit(solution)/shard_map/ppermute | solution.py:312
  48.2 1.2 %collective-permute-done.13.high = bf16[128,512]{1,0:T(8,128)(2,1)S(1)} collective-permute-done((bf16[128,512]{1,0:T(8,128)(2,1)S(1)}, bf16[128,512]{1,0:T(8,128)(2,1)S(1)}, u32[]{:S(2)}, u32[]{:S(2)}) %collective-permute-start.13) | collective-permute-done | bytes 131104 | tf_op jit(solution)/shard_map/ppermute | solution.py:312
  49.4 0.1 join.1
  49.5 0.3 collective-permute-start.14
  49.7 0.6 %collective-permute-start.15 = (bf16[128,1024]{1,0:T(8,128)(2,1)S(1)}, bf16[128,1024]{1,0:T(8,128)(2,1)S(1)}, u32[]{:S(2)}, u32[]{:S(2)}) collective-permute-start(bf16[128,1024]{1,0:T(8,128)(2,1)S(1)} %get-tuple-element.56), channel_id=1, source_target_pairs={{0,16},{8,24},{16,0},{24,8},{1,17},{9,25},{17,1},{25,9},{2,18},{10... | collective-permute-start | bytes 786440 | tf_op jit(solution)/shard_map/ppermute | solution.py:312
  50.4 2.3 %restore.1 = bf16[4,704,128]{2,1,0:T(8,128)(2,1)} custom-call(s32[2]{0:T(128)S(1)} %pad_add_fusion.1.place, s32[8,128]{1,0:T(8,128)S(1)} %copy-done.3, bf16[144,704]{1,0:T(8,128)(2,1)S(1)} %get-tuple-element.57.refs_0_, bf16[144,704]{1,0:T(8,128)(2,1)S(1)} %collective-permute-done.16.refs_1_, bf16[144,704]{1,0:T(8,128)(2,1)S(1)} %collective-permute-done.17.refs_2_, ...), custom_call_target="tpu_custom_call" | custom-call | flops 99999997952 | bytes 1 | tf_op jit(solution)/shard_map/restore/pallas_call | solution.py:279
  52.7 5.1 %collective-permute-done.14 = bf16[128,1024]{1,0:T(8,128)(2,1)S(1)} collective-permute-done((bf16[128,1024]{1,0:T(8,128)(2,1)S(1)}, bf16[128,1024]{1,0:T(8,128)(2,1)S(1)}, u32[]{:S(2)}, u32[]{:S(2)}) %collective-permute-start.14) | collective-permute-done | bytes 262176 | tf_op jit(solution)/shard_map/ppermute | solution.py:312
  57.7 0.1 collective-permute-done.15
  57.8 0.8 %add_convert_fusion = bf16[128,1024]{1,0:T(8,128)(2,1)} fusion(bf16[128,1024]{1,0:T(8,128)(2,1)S(1)} %collective-permute-done.15, f32[128,1024]{1,0:T(8,128)S(1)} %get-tuple-element.50, bf16[128,1024]{1,0:T(8,128)(2,1)S(1)} %collective-permute-done.14), kind=kLoop, calls=%fused_computation.2 | loop fusion | flops 655360 | bytes 1310720 | tf_op jit(solution)/shard_map/convert_element_type | solution.py:411
  (22 shorter events, 0.1 us)
Async XLA Ops:
  2.3 10.0 %collective-permute-start.1 = (bf16[136,1024]{1,0:T(8,128)(2,1)S(1)}, bf16[136,1024]{1,0:T(8,128)(2,1)S(1)}, u32[]{:S(2)}, u32[]{:S(2)}) collective-permute-start(bf16[136,1024]{1,0:T(8,128)(2,1)S(1)} %fusion.1.refs_0_), channel_id=1, source_target_pairs={{0,8},{8,0},{16,24},{24,16},{1,9},{9,1},{17,25},{25,17},{2,10},{10... | collective-permute-start | bytes 835592 | tf_op jit(solution)/shard_map/ppermute | solution.py:312
  5.3 9.2 %collective-permute-start = (bf16[136,1024]{1,0:T(8,128)(2,1)S(1)}, bf16[136,1024]{1,0:T(8,128)(2,1)S(1)}, u32[]{:S(2)}, u32[]{:S(2)}) collective-permute-start(bf16[136,1024]{1,0:T(8,128)(2,1)S(1)} %fusion.1.refs_0_), channel_id=1, source_target_pairs={{0,16},{8,24},{16,0},{24,8},{1,17},{9,25},{17,1},{25,9},{2,18},{10... | collective-permute-start | bytes 835592 | tf_op jit(solution)/shard_map/ppermute | solution.py:312
  7.6 10.7 %copy-start.2 = (s32[8,128]{1,0:T(8,128)}, s32[8,128]{1,0:T(8,128)S(1)}, u32[]{:S(2)}) copy-start(s32[8,128]{1,0:T(8,128)S(1)} %pad_add_fusion.meta_ref) | copy-start | bytes 12292
  7.6 1.1 %copy-start.1 = (bf16[128,4,704]{0,2,1:T(8,128)(2,1)S(1)}, bf16[128,4,704]{0,2,1:T(8,128)(2,1)}, u32[]{:S(2)}) copy-start(bf16[128,4,704]{0,2,1:T(8,128)(2,1)} %param.5) | copy-start | bytes 2162692
  10.1 13.5 %collective-permute-start.2 = (bf16[224,768]{1,0:T(8,128)(2,1)S(1)}, bf16[224,768]{1,0:T(8,128)(2,1)S(1)}, u32[]{:S(2)}, u32[]{:S(2)}) collective-permute-start(bf16[224,768]{1,0:T(8,128)(2,1)S(1)} %get-tuple-element.35), channel_id=1, source_target_pairs={{0,8},{8,0},{16,24},{24,16},{1,9},{9,1},{17,25},{25,17},{2,10},{10... | collective-permute-start | bytes 1032200 | tf_op jit(solution)/shard_map/ppermute | solution.py:312
  10.7 12.8 %collective-permute-start.3 = (bf16[208,768]{1,0:T(8,128)(2,1)S(1)}, bf16[208,768]{1,0:T(8,128)(2,1)S(1)}, u32[]{:S(2)}, u32[]{:S(2)}) collective-permute-start(bf16[208,768]{1,0:T(8,128)(2,1)S(1)} %get-tuple-element.36), channel_id=1, source_target_pairs={{0,16},{8,24},{16,0},{24,8},{1,17},{9,25},{17,1},{25,9},{2,18},{10... | collective-permute-start | bytes 958472 | tf_op jit(solution)/shard_map/ppermute | solution.py:312
  10.7 5.4 %collective-permute-start.4 = (bf16[136,1024]{1,0:T(8,128)(2,1)S(1)}, bf16[136,1024]{1,0:T(8,128)(2,1)S(1)}, u32[]{:S(2)}, u32[]{:S(2)}) collective-permute-start(bf16[136,1024]{1,0:T(8,128)(2,1)S(1)} %fusion.1.refs_0_), channel_id=1, source_target_pairs={{0,1},{1,0},{2,3},{3,2},{4,5},{5,4},{6,7},{7,6},{8,9},{9,8},{10,11... | collective-permute-start | bytes 835592 | tf_op jit(solution)/shard_map/ppermute | solution.py:315
  14.5 3.6 %collective-permute-start.6 = (bf16[136,1024]{1,0:T(8,128)(2,1)S(1)}, bf16[136,1024]{1,0:T(8,128)(2,1)S(1)}, u32[]{:S(2)}, u32[]{:S(2)}) collective-permute-start(bf16[136,1024]{1,0:T(8,128)(2,1)S(1)} %collective-permute-done.refs_2_), channel_id=1, source_target_pairs={{0,1},{1,0},{2,3},{3,2},{4,5},{5,4},{6,7},{7,6},{8,9},{9,8},{10,11... | collective-permute-start | bytes 835592 | tf_op jit(solution)/shard_map/ppermute | solution.py:315
  14.5 3.8 %collective-permute-start.5 = (bf16[136,1024]{1,0:T(8,128)(2,1)S(1)}, bf16[136,1024]{1,0:T(8,128)(2,1)S(1)}, u32[]{:S(2)}, u32[]{:S(2)}) collective-permute-start(bf16[136,1024]{1,0:T(8,128)(2,1)S(1)} %collective-permute-done.1.refs_1_), channel_id=1, source_target_pairs={{0,1},{1,0},{2,3},{3,2},{4,5},{5,4},{6,7},{7,6},{8,9},{9,8},{10,11... | collective-permute-start | bytes 835592 | tf_op jit(solution)/shard_map/ppermute | solution.py:315
  16.1 9.5 %collective-permute-start.7 = (bf16[136,512]{1,0:T(8,128)(2,1)S(1)}, bf16[136,512]{1,0:T(8,128)(2,1)S(1)}, u32[]{:S(2)}, u32[]{:S(2)}) collective-permute-start(bf16[136,512]{1,0:T(8,128)(2,1)S(1)} %get-tuple-element.44), channel_id=1, source_target_pairs={{0,16},{8,24},{16,0},{24,8},{1,17},{9,25},{17,1},{25,9},{2,18},{10... | collective-permute-start | bytes 417800 | tf_op jit(solution)/shard_map/ppermute | solution.py:312
  18.1 7.5 %collective-permute-start.8 = (bf16[136,512]{1,0:T(8,128)(2,1)S(1)}, bf16[136,512]{1,0:T(8,128)(2,1)S(1)}, u32[]{:S(2)}, u32[]{:S(2)}) collective-permute-start(bf16[136,512]{1,0:T(8,128)(2,1)S(1)} %get-tuple-element.45), channel_id=1, source_target_pairs={{0,8},{8,0},{16,24},{24,16},{1,9},{9,1},{17,25},{25,17},{2,10},{10... | collective-permute-start | bytes 417800 | tf_op jit(solution)/shard_map/ppermute | solution.py:312
  18.3 2.6 %copy-start = (bf16[2,704,2048]{2,1,0:T(8,128)(2,1)S(1)}, bf16[2,704,2048]{2,1,0:T(8,128)(2,1)}, u32[]{:S(2)}) copy-start(bf16[2,704,2048]{2,1,0:T(8,128)(2,1)} %w_ref.1) | copy-start | bytes 17301508
  20.9 11.7 %slice-start = ((s8[5767168]{0:T(1024)(128)(4,1)}), s8[4194304]{0:T(1024)(128)(4,1)S(1)}, s32[]{:S(2)}) async-start(s8[5767168]{0:T(1024)(128)(4,1)} %bitcast.7), calls=%async_computation | async-start | bytes 8388608
  23.5 9.1 %slice-start.1 = ((s8[5767168]{0:T(1024)(128)(4,1)}), s8[1572864]{0:T(1024)(128)(4,1)S(1)}, s32[]{:S(2)}) async-start(s8[5767168]{0:T(1024)(128)(4,1)} %bitcast.7), calls=%async_computation.1 | async-start | bytes 3145728
  23.6 4.9 %collective-permute-start.9 = (bf16[80,768]{1,0:T(8,128)(2,1)S(1)}, bf16[80,768]{1,0:T(8,128)(2,1)S(1)}, u32[]{:S(2)}, u32[]{:S(2)}) collective-permute-start(bf16[80,768]{1,0:T(8,128)(2,1)S(1)} %get-tuple-element.46), channel_id=1, source_target_pairs={{0,16},{8,24},{16,0},{24,8},{1,17},{9,25},{17,1},{25,9},{2,18},{10... | collective-permute-start | bytes 368648 | tf_op jit(solution)/shard_map/ppermute | solution.py:312
  23.8 4.6 %collective-permute-start.10 = (bf16[64,768]{1,0:T(8,128)(2,1)S(1)}, bf16[64,768]{1,0:T(8,128)(2,1)S(1)}, u32[]{:S(2)}, u32[]{:S(2)}) collective-permute-start(bf16[64,768]{1,0:T(8,128)(2,1)S(1)} %get-tuple-element.47), channel_id=1, source_target_pairs={{0,8},{8,0},{16,24},{24,16},{1,9},{9,1},{17,25},{25,17},{2,10},{10... | collective-permute-start | bytes 294920 | tf_op jit(solution)/shard_map/ppermute | solution.py:312
  28.5 6.6 %collective-permute-start.18 = (bf16[136,512]{1,0:T(8,128)(2,1)S(1)}, bf16[136,512]{1,0:T(8,128)(2,1)S(1)}, u32[]{:S(2)}, u32[]{:S(2)}) collective-permute-start(bf16[136,512]{1,0:T(8,128)(2,1)S(1)} %collective-permute-done.7.low), channel_id=1, source_target_pairs={{0,1},{1,0},{2,3},{3,2},{4,5},{5,4},{6,7},{7,6},{8,9},{9,8},{10,11... | collective-permute-start | bytes 417800 | tf_op jit(solution)/shard_map/ppermute | solution.py:315
  28.5 6.7 %collective-permute-start.19 = (bf16[136,512]{1,0:T(8,128)(2,1)S(1)}, bf16[136,512]{1,0:T(8,128)(2,1)S(1)}, u32[]{:S(2)}, u32[]{:S(2)}) collective-permute-start(bf16[136,512]{1,0:T(8,128)(2,1)S(1)} %collective-permute-done.8.high), channel_id=1, source_target_pairs={{0,1},{1,0},{2,3},{3,2},{4,5},{5,4},{6,7},{7,6},{8,9},{9,8},{10,11... | collective-permute-start | bytes 417800 | tf_op jit(solution)/shard_map/ppermute | solution.py:315
  29.0 21.3 %collective-permute-start.16 = (bf16[144,704]{1,0:T(8,128)(2,1)S(1)}, bf16[144,704]{1,0:T(8,128)(2,1)S(1)}, u32[]{:S(2)}, u32[]{:S(2)}) collective-permute-start(bf16[144,704]{1,0:T(8,128)(2,1)S(1)} %get-tuple-element.58), channel_id=1, source_target_pairs={{0,8},{8,0},{16,24},{24,16},{1,9},{9,1},{17,25},{25,17},{2,10},{10... | collective-permute-start | bytes 608264 | tf_op jit(solution)/shard_map/ppermute | solution.py:312
  30.8 19.5 %collective-permute-start.17 = (bf16[144,704]{1,0:T(8,128)(2,1)S(1)}, bf16[144,704]{1,0:T(8,128)(2,1)S(1)}, u32[]{:S(2)}, u32[]{:S(2)}) collective-permute-start(bf16[144,704]{1,0:T(8,128)(2,1)S(1)} %get-tuple-element.59), channel_id=1, source_target_pairs={{0,16},{8,24},{16,0},{24,8},{1,17},{9,25},{17,1},{25,9},{2,18},{10... | collective-permute-start | bytes 608264 | tf_op jit(solution)/shard_map/ppermute | solution.py:312
  35.1 5.2 %collective-permute-start.11 = (bf16[512,1024]{1,0:T(8,128)(2,1)S(1)}, bf16[512,1024]{1,0:T(8,128)(2,1)S(1)}, u32[]{:S(2)}, u32[]{:S(2)}) collective-permute-start(bf16[512,1024]{1,0:T(8,128)(2,1)S(1)} %mix_sibling.1), channel_id=1, source_target_pairs={{0,1},{1,0},{2,3},{3,2},{4,5},{5,4},{6,7},{7,6},{8,9},{9,8},{10,11... | collective-permute-start | bytes 3145736 | tf_op jit(solution)/shard_map/ppermute | solution.py:315
  37.8 12.6 %copy-start.3 = (s32[8,128]{1,0:T(8,128)S(1)}, s32[8,128]{1,0:T(8,128)}, u32[]{:S(2)}) copy-start(s32[8,128]{1,0:T(8,128)} %copy-done.2) | copy-start | bytes 12292
  37.8 12.6 %collective-permute-start.20 = (bf16[144,704]{1,0:T(8,128)(2,1)S(1)}, bf16[144,704]{1,0:T(8,128)(2,1)S(1)}, u32[]{:S(2)}, u32[]{:S(2)}) collective-permute-start(bf16[144,704]{1,0:T(8,128)(2,1)S(1)} %grad_far.1), channel_id=1, source_target_pairs={{0,24},{8,16},{16,8},{24,0},{1,25},{9,17},{17,9},{25,1},{2,26},{10... | collective-permute-start | bytes 608264 | tf_op jit(solution)/shard_map/ppermute | solution.py:312
  40.5 7.7 %collective-permute-start.12 = (bf16[128,512]{1,0:T(8,128)(2,1)S(1)}, bf16[128,512]{1,0:T(8,128)(2,1)S(1)}, u32[]{:S(2)}, u32[]{:S(2)}) collective-permute-start(bf16[128,512]{1,0:T(8,128)(2,1)S(1)} %get-tuple-element.53), channel_id=1, source_target_pairs={{0,8},{8,0},{16,24},{24,16},{1,9},{9,1},{17,25},{25,17},{2,10},{10... | collective-permute-start | bytes 393224 | tf_op jit(solution)/shard_map/ppermute | solution.py:312
  42.3 7.1 %collective-permute-start.13 = (bf16[128,512]{1,0:T(8,128)(2,1)S(1)}, bf16[128,512]{1,0:T(8,128)(2,1)S(1)}, u32[]{:S(2)}, u32[]{:S(2)}) collective-permute-start(bf16[128,512]{1,0:T(8,128)(2,1)S(1)} %get-tuple-element.54), channel_id=1, source_target_pairs={{0,16},{8,24},{16,0},{24,8},{1,17},{9,25},{17,1},{25,9},{2,18},{10... | collective-permute-start | bytes 393224 | tf_op jit(solution)/shard_map/ppermute | solution.py:312
  49.5 8.3 %collective-permute-start.14 = (bf16[128,1024]{1,0:T(8,128)(2,1)S(1)}, bf16[128,1024]{1,0:T(8,128)(2,1)S(1)}, u32[]{:S(2)}, u32[]{:S(2)}) collective-permute-start(bf16[128,1024]{1,0:T(8,128)(2,1)S(1)} %get-tuple-element.55), channel_id=1, source_target_pairs={{0,8},{8,0},{16,24},{24,16},{1,9},{9,1},{17,25},{25,17},{2,10},{10... | collective-permute-start | bytes 786440 | tf_op jit(solution)/shard_map/ppermute | solution.py:312
  49.7 8.1 %collective-permute-start.15 = (bf16[128,1024]{1,0:T(8,128)(2,1)S(1)}, bf16[128,1024]{1,0:T(8,128)(2,1)S(1)}, u32[]{:S(2)}, u32[]{:S(2)}) collective-permute-start(bf16[128,1024]{1,0:T(8,128)(2,1)S(1)} %get-tuple-element.56), channel_id=1, source_target_pairs={{0,16},{8,24},{16,0},{24,8},{1,17},{9,25},{17,1},{25,9},{2,18},{10... | collective-permute-start | bytes 786440 | tf_op jit(solution)/shard_map/ppermute | solution.py:312

commit v2 on v0

--- a/solution.py
+++ b/solution.py
@@ -13,6 +13,7 @@
 NT = (((1,), (1,)), ((), ()))
 TN = (((0,), (0,)), ((), ()))
 BIG = 10**11
+W_GATHER, TIE_OWN = BIG, True
 
 
 def dot(a, b, dims):
@@ -119,35 +120,62 @@
             x_ref[l, :, c : c + chunk] = x.astype(BF16)
 
 
+def join_far(refs, n, tokens):
+    blocks = [[ref] for ref in refs[:n]]
+    if len(refs) > n:
+        blocks = blocks[: n - 1] + [list(refs[n - 1 :])]
+    return blocks
+
+
+def gather_rows(dims, held, blocks, x_ref):
+    experts, local, cap, width = dims
+    tokens, half = held[0].shape[1], x_ref.shape[2]
+    chunk = min(half, 512)
+    for c in range(0, half, chunk):
+        rows = []
+        for h, block in zip(held, blocks):
+            size = half // len(block)
+            ref, at = block[c // size], c % size
+            rows.append(dot(h, ref[:tokens, at : at + chunk], NN))
+        for l, x in enumerate(by_expert(rows, local, cap)):
+            x_ref[l, :, c : c + chunk] = x.astype(BF16)
+
+
 def gather_kernel(dims, top, place, *refs):
-    x_ref, held_ref = refs[-2:]
-    own = refs[:-2]
-    tokens = held_ref.shape[2]
-    held = [routes(dims, top, place[0], ref, tokens) for ref in own]
-    for s, h in enumerate(held):
-        held_ref[s] = h
-    gather_rows(dims, held, own, x_ref)
-
-
-def products(dims, place, x_ref, x_other, w_ref):
+    experts, local, cap, width = dims
+    own, (x_ref, held_ref) = refs[:-2], refs[-2:]
+    n, _, tokens = held_ref.shape
+    blocks = join_far(own, n, tokens)
+    for s, block in enumerate(blocks):
+        ids = block[0][tokens:, :tokens].astype(F32).astype(jnp.int32)[:top]
+        held_ref[s] = jnp.concatenate(
+            slots_by_lane(ids, place[0], local, cap, width), axis=0
+        )
+    gather_rows(dims, [held_ref[s] for s in range(n)], blocks, x_ref)
+
+
+def grad_kernel(dims, place, *refs):
+    experts, local, cap, width = dims
+    n = experts // local
+    x_other, outs, (x_ref, held_ref, w_ref) = refs[-1], refs[-1 - n : -1], refs[-4 - n : -1 - n]
+    other = refs[: -4 - n]
     half = x_ref.shape[2]
+    blocks = join_far(other, n, held_ref.shape[2])
+    gather_rows(dims, [held_ref[s] for s in range(n)], blocks, x_other)
     mine = pl.ds(pl.multiple_of(place[1] * half, half), half)
     theirs = pl.ds(pl.multiple_of((1 - place[1]) * half, half), half)
-    return [
+    grads = [
         dot(x_ref[l], w_ref[l, :, mine], NT) + dot(x_other[l], w_ref[l, :, theirs], NT)
-        for l in range(dims[1])
-    ]
-
-
-def grad_kernel(dims, place, *refs):
-    n = (len(refs) - 4) // 2
-    other = refs[:n]
-    x_ref, held_ref, w_ref = refs[n : n + 3]
-    outs, x_other = refs[n + 3 : 2 * n + 3], refs[-1]
-    gather_rows(dims, [held_ref[s] for s in range(n)], other, x_other)
-    grads = products(dims, place, x_ref, x_other, w_ref)
-    for s, rows in enumerate(by_source(grads, n, dims[2])):
+        for l in range(local)
+    ]
+    for s, rows in enumerate(by_source(grads, n, cap)):
         outs[s][...] = rows.astype(BF16)
+
+
+def pass_kernel(one, two, low, high):
+    cut = low.shape[1]
+    low[...] = one[:, :cut]
+    high[...] = two[:, cut:]
 
 
 def mix_rows(dims, side, hid, w_ref, tokens, half, store):
@@ -272,21 +300,32 @@
     named = jnp.pad(expert_ids.T.astype(BF16), ((0, 8 - top), (0, half - tokens)))
     packed = jnp.concatenate([grad_out, named], axis=0)
     forward = n == 4
-    own = [send(packed, s) for s in range(n)]
+    near = 3 if forward else n
+    own = [send(packed, s) for s in range(near)]
+    swapped = swap(packed)
+    if TIE_OWN:
+        meta, swapped = lax.optimization_barrier((meta, swapped))
     hid_sent = run(
         functools.partial(dispatch_kernel, dims), [shaped((width, -(-(ff + 1) // 128) * 128))] * n,
         [place, meta, hid_t], where=placed, name="dispatch",
     )
     hid = [send(hid_sent[s], s) for s in range(n)]
-    for s in range(1, n):
+    for s in range(1, near):
         own[s], hid[0] = lax.optimization_barrier((own[s], hid[0]))
-    other = [swap(x) for x in own]
+    if forward:
+        cut = half // 2
+        low, high = run(pass_kernel, [shaped((tokens + 8, cut))] * 2, own[1:], name="pass")
+        own += [send(low, 2), send(high, 1)]
+    other = [swapped] + [swap(x) for x in own[1:near]]
+    if forward:
+        *own[3:], other[1], other[2] = lax.optimization_barrier((*own[3:], other[1], other[2]))
+        other += [swap(x) for x in own[3:]]
 
     slot = shaped((width, ff))
     x, held = run(
         functools.partial(gather_kernel, dims, top),
         [shaped((local, n * cap, half)), shaped((n, width, tokens))],
-        [place, *own], where=placed, name="gather", weight=BIG,
+        [place, *own], where=placed, name="gather", weight=W_GATHER,
     )
     grad_sent = run(
         functools.partial(grad_kernel, dims), [slot] * n,
@@ -306,7 +345,6 @@
             functools.partial(mix_kernel, dims, False), [shaped((n * tokens, half), F32)],
             [place, *hid, w_down], where=placed, name="mix_own", weight=BIG,
         )
-        cut = half // 2
         block, piece = shaped((tokens, half), F32), shaped((tokens, cut))
         kept, one, two, one_low, two_high = run(
             add_split_kernel, [block] * 3 + [piece] * 2, [mine, arrived], name="add"

time: 54.6 us -> 56 us (1.026)
  starting transfers between devices: 17 us -> 20 us
  waiting for transfers between devices: 18.3 us -> 16.2 us
    ppermute x13 -> x14, starting transfers between devices: 16.4 us -> 18.4 us  [send(): return lax.ppermute(x, 'ctx', [(i, i ^ s) for i in range(n)]) if s else x]
    ppermute x13 -> x14, waiting for transfers between devices: 17.8 us -> 16 us  [send(): return lax.ppermute(x, 'ctx', [(i, i ^ s) for i in range(n)]) if s else x]
    ppermute x5 -> x6, starting transfers between devices: 0.58 us -> 1.6 us  [swap(): return lax.ppermute(x, 'tp', [(0, 1), (1, 0)])]
    pallas_call x8 -> x9, Pallas kernels: 12.8 us -> 12.9 us  [call(): pl.pallas_call(kernel, out_shape=outs, in_specs=[pl.BlockSpec(memory_spac...]
  transfers between devices with their start and end apart: 18 -> 20, of which waited for: 9 -> 9; matrix products, arithmetic and copies ran while one was open for 1% -> 1% of each run, Pallas kernels for 24% -> 23%
where the time goes in v2:
time: 56 us; the launch traced here: 55.7 us
  starting transfers between devices  20 us (36%)
  waiting for transfers between devices  16.2 us (29%)
  Pallas kernels  12.9 us (23%)
  other arithmetic  3.24 us (6%)
  local copies, waits for them, and re-layouts  2.58 us (5%)
  between operations  0.75 us (1%)
    ppermute x14, starting transfers between devices, send(): return lax.ppermute(x, 'ctx', [(i, i ^ s) for i in range(n)]) if s else x  18.4 us
    ppermute x14, waiting for transfers between devices, send(): return lax.ppermute(x, 'ctx', [(i, i ^ s) for i in range(n)]) if s else x  16 us
    pallas_call x9, Pallas kernels, call(): pl.pallas_call(kernel, out_shape=outs, in_specs=[pl.BlockSpec(memory_spac...  12.9 us
    unnamed x8, local copies, waits for them, and re-layouts  2.58 us
    ppermute x6, starting transfers between devices, swap(): return lax.ppermute(x, 'tp', [(0, 1), (1, 0)])  1.6 us
  transfers between devices with their start and end apart: 20, of which 9 were waited for; matrix products, arithmetic and copies ran while one was open for 1% of the time, Pallas kernels for 23%

profile of v2, /device:TPU:0, one launch (start us, length us, event | category | flops | bytes accessed | tf_op | source)
XLA Modules:
  0.0 55.7 jit_solution(15017431948984883483)
XLA Ops:
  0.6 0.7 %bitcast_convert_fusion = bf16[4,128]{1,0:T(4,128)(2,1)S(1)} fusion(s32[128,4]{0,1:T(4,128)} %param.6), kind=kLoop, calls=%fused_computation.6 | loop fusion | flops 512 | bytes 3072 | tf_op jit(solution)/shard_map/convert_element_type | solution.py:300
  1.3 1.0 %fusion.1.refs_0_ = bf16[136,1024]{1,0:T(8,128)(2,1)S(1)} fusion(bf16[4,128]{1,0:T(4,128)(2,1)S(1)} %bitcast_convert_fusion, bf16[128,1024]{1,0:T(8,128)(2,1)} %param.8), kind=kLoop, calls=%fused_computation.3 | loop fusion | flops 835584 | bytes 541696 | tf_op jit(solution)/shard_map/concatenate | solution.py:301
  2.3 0.5 collective-permute-start.2
  2.8 2.6 %collective-permute-start.1 = (bf16[136,1024]{1,0:T(8,128)(2,1)S(1)}, bf16[136,1024]{1,0:T(8,128)(2,1)S(1)}, u32[]{:S(2)}, u32[]{:S(2)}) collective-permute-start(bf16[136,1024]{1,0:T(8,128)(2,1)S(1)} %fusion.1.refs_0_), channel_id=1, source_target_pairs={{0,8},{8,0},{16,24},{24,16},{1,9},{9,1},{17,25},{25,17},{2,10},{10... | collective-permute-start | bytes 835592 | tf_op jit(solution)/shard_map/ppermute | solution.py:293
  5.4 1.5 %collective-permute-start = (bf16[136,1024]{1,0:T(8,128)(2,1)S(1)}, bf16[136,1024]{1,0:T(8,128)(2,1)S(1)}, u32[]{:S(2)}, u32[]{:S(2)}) collective-permute-start(bf16[136,1024]{1,0:T(8,128)(2,1)S(1)} %fusion.1.refs_0_), channel_id=1, source_target_pairs={{0,16},{8,24},{16,0},{24,8},{1,17},{9,25},{17,1},{25,9},{2,18},{10... | collective-permute-start | bytes 835592 | tf_op jit(solution)/shard_map/ppermute | solution.py:293
  6.9 0.1 pad_add_fusion.1.place
  7.0 0.7 %pad_add_fusion.meta_ref = s32[8,128]{1,0:T(8,128)S(1)} fusion(s32[4,128]{1,0:T(4,128)} %bitcast.9, s32[4,128]{1,0:T(4,128)} %bitcast.8), kind=kLoop, calls=%fused_computation.4 | loop fusion | flops 1024 | bytes 8192 | tf_op jit(solution)/shard_map/concatenate | solution.py:298
  7.7 0.0 copy-start.1
  7.7 1.1 %copy-done.1 = bf16[128,4,704]{0,2,1:T(8,128)(2,1)S(1)} copy-done((bf16[128,4,704]{0,2,1:T(8,128)(2,1)S(1)}, bf16[128,4,704]{0,2,1:T(8,128)(2,1)}, u32[]{:S(2)}) %copy-start.1) | copy-done | bytes 720920
  8.8 1.4 %dispatch.1 = (bf16[144,768]{1,0:T(8,128)(2,1)S(1)}, bf16[144,768]{1,0:T(8,128)(2,1)S(1)}, bf16[144,768]{1,0:T(8,128)(2,1)S(1)}, bf16[144,768]{1,0:T(8,128)(2,1)S(1)}) custom-call(s32[2]{0:T(128)S(1)} %pad_add_fusion.1.place, s32[8,128]{1,0:T(8,128)S(1)} %pad_add_fusion.meta_ref, bf16[4,704,128]{2,1,0:T(8,128)(2,1)S(1)} %bitcast.7), custom_call_target="tpu_custom_call" | custom-call | flops 1 | bytes 1 | tf_op jit(solution)/shard_map/dispatch/pallas_call | solution.py:260
  10.2 2.5 %collective-permute-done.1.one.refs_1_ = bf16[136,1024]{1,0:T(8,128)(2,1)S(1)} collective-permute-done((bf16[136,1024]{1,0:T(8,128)(2,1)S(1)}, bf16[136,1024]{1,0:T(8,128)(2,1)S(1)}, u32[]{:S(2)}, u32[]{:S(2)}) %collective-permute-start.1) | collective-permute-done | bytes 278560 | tf_op jit(solution)/shard_map/ppermute | solution.py:293
  12.6 1.5 %collective-permute-done.two.refs_2_ = bf16[136,1024]{1,0:T(8,128)(2,1)S(1)} collective-permute-done((bf16[136,1024]{1,0:T(8,128)(2,1)S(1)}, bf16[136,1024]{1,0:T(8,128)(2,1)S(1)}, u32[]{:S(2)}, u32[]{:S(2)}) %collective-permute-start) | collective-permute-done | bytes 278560 | tf_op jit(solution)/shard_map/ppermute | solution.py:293
  14.1 0.5 collective-permute-start.5
  14.6 1.6 %collective-permute-start.3 = (bf16[136,512]{1,0:T(8,128)(2,1)S(1)}, bf16[136,512]{1,0:T(8,128)(2,1)S(1)}, u32[]{:S(2)}, u32[]{:S(2)}) collective-permute-start(bf16[136,512]{1,0:T(8,128)(2,1)S(1)} %get-tuple-element.40), channel_id=1, source_target_pairs={{0,16},{8,24},{16,0},{24,8},{1,17},{9,25},{17,1},{25,9},{2,18},{10... | collective-permute-start | bytes 417800 | tf_op jit(solution)/shard_map/ppermute | solution.py:293
  16.2 0.5 collective-permute-start.4
  16.8 1.5 %collective-permute-start.9 = (bf16[144,768]{1,0:T(8,128)(2,1)S(1)}, bf16[144,768]{1,0:T(8,128)(2,1)S(1)}, u32[]{:S(2)}, u32[]{:S(2)}) collective-permute-start(bf16[144,768]{1,0:T(8,128)(2,1)S(1)} %get-tuple-element.50), channel_id=1, source_target_pairs={{0,8},{8,0},{16,24},{24,16},{1,9},{9,1},{17,25},{25,17},{2,10},{10... | collective-permute-start | bytes 663560 | tf_op jit(solution)/shard_map/ppermute | solution.py:293
  18.2 2.0 %collective-permute-done.3.refs_3_ = bf16[136,512]{1,0:T(8,128)(2,1)S(1)} collective-permute-done((bf16[136,512]{1,0:T(8,128)(2,1)S(1)}, bf16[136,512]{1,0:T(8,128)(2,1)S(1)}, u32[]{:S(2)}, u32[]{:S(2)}) %collective-permute-start.3) | collective-permute-done | bytes 139296 | tf_op jit(solution)/shard_map/ppermute | solution.py:293
  20.3 1.5 %collective-permute-start.10 = (bf16[144,768]{1,0:T(8,128)(2,1)S(1)}, bf16[144,768]{1,0:T(8,128)(2,1)S(1)}, u32[]{:S(2)}, u32[]{:S(2)}) collective-permute-start(bf16[144,768]{1,0:T(8,128)(2,1)S(1)} %get-tuple-element.51), channel_id=1, source_target_pairs={{0,16},{8,24},{16,0},{24,8},{1,17},{9,25},{17,1},{25,9},{2,18},{10... | collective-permute-start | bytes 663560 | tf_op jit(solution)/shard_map/ppermute | solution.py:293
  21.8 1.0 %collective-permute-done.4.refs_4_ = bf16[136,512]{1,0:T(8,128)(2,1)S(1)} collective-permute-done((bf16[136,512]{1,0:T(8,128)(2,1)S(1)}, bf16[136,512]{1,0:T(8,128)(2,1)S(1)}, u32[]{:S(2)}, u32[]{:S(2)}) %collective-permute-start.4) | collective-permute-done | bytes 139296 | tf_op jit(solution)/shard_map/ppermute | solution.py:293
  22.8 0.2 collective-permute-start.11
  23.0 0.0 collective-permute-done.6.refs_2_
  23.0 0.0 collective-permute-done.5.refs_1_
  23.0 0.0 collective-permute-start.7
  23.1 0.5 collective-permute-start.8
  23.6 1.1 %gather.1 = (bf16[2,288,1024]{2,1,0:T(8,128)(2,1)S(1)}, bf16[4,144,128]{2,1,0:T(8,128)(2,1)S(1)}) custom-call(s32[2]{0:T(128)S(1)} %pad_add_fusion.1.place, bf16[136,1024]{1,0:T(8,128)(2,1)S(1)} %fusion.1.refs_0_, bf16[136,1024]{1,0:T(8,128)(2,1)S(1)} %collective-permute-done.1.one.refs_1_, bf16[136,1024]{1,0:T(8,128)(2,1)S(1)} %collective-permute-done.two.refs_2_, ...), custom_call_target="tpu_custom_call" | custom-call | flops 99999997952 | bytes 1 | tf_op jit(solution)/shard_map/gather/pallas_call | solution.py:260
  24.7 0.0 collective-permute-done.8.refs_4_
  24.7 1.5 %copy-done = bf16[2,704,2048]{2,1,0:T(8,128)(2,1)S(1)} copy-done((bf16[2,704,2048]{2,1,0:T(8,128)(2,1)S(1)}, bf16[2,704,2048]{2,1,0:T(8,128)(2,1)}, u32[]{:S(2)}) %copy-start) | copy-done | bytes 5767192
  26.2 2.9 %grad.1 = (bf16[144,704]{1,0:T(8,128)(2,1)S(1)}, bf16[144,704]{1,0:T(8,128)(2,1)S(1)}, bf16[144,704]{1,0:T(8,128)(2,1)S(1)}, bf16[144,704]{1,0:T(8,128)(2,1)S(1)}) custom-call(s32[2]{0:T(128)S(1)} %pad_add_fusion.1.place, bf16[136,1024]{1,0:T(8,128)(2,1)S(1)} %collective-permute-done.2.refs_0_, bf16[136,1024]{1,0:T(8,128)(2,1)S(1)} %collective-permute-done.5.refs_1_, ...), custom_call_target="tpu_custom_call" | custom-call | flops 1 | bytes 1 | tf_op jit(solution)/shard_map/grad/pallas_call | solution.py:260
  29.1 1.8 %collective-permute-start.17 = (bf16[144,704]{1,0:T(8,128)(2,1)S(1)}, bf16[144,704]{1,0:T(8,128)(2,1)S(1)}, u32[]{:S(2)}, u32[]{:S(2)}) collective-permute-start(bf16[144,704]{1,0:T(8,128)(2,1)S(1)} %get-tuple-element.61), channel_id=1, source_target_pairs={{0,8},{8,0},{16,24},{24,16},{1,9},{9,1},{17,25},{25,17},{2,10},{10... | collective-permute-start | bytes 608264 | tf_op jit(solution)/shard_map/ppermute | solution.py:293
  30.9 1.5 %collective-permute-start.18 = (bf16[144,704]{1,0:T(8,128)(2,1)S(1)}, bf16[144,704]{1,0:T(8,128)(2,1)S(1)}, u32[]{:S(2)}, u32[]{:S(2)}) collective-permute-start(bf16[144,704]{1,0:T(8,128)(2,1)S(1)} %get-tuple-element.62), channel_id=1, source_target_pairs={{0,16},{8,24},{16,0},{24,8},{1,17},{9,25},{17,1},{25,9},{2,18},{10... | collective-permute-start | bytes 608264 | tf_op jit(solution)/shard_map/ppermute | solution.py:293
  32.4 0.2 collective-permute-start.19
  32.7 2.5 %mix_sibling.1 = bf16[512,1024]{1,0:T(8,128)(2,1)S(1)} custom-call(s32[2]{0:T(128)S(1)} %pad_add_fusion.1.place, bf16[144,768]{1,0:T(8,128)(2,1)S(1)} %get-tuple-element.49.refs_0_, bf16[144,768]{1,0:T(8,128)(2,1)S(1)} %collective-permute-done.9.refs_1_, bf16[144,768]{1,0:T(8,128)(2,1)S(1)} %collective-permute-done.10.refs_2_, ...), custom_call_target="tpu_custom_call" | custom-call | flops 1 | bytes 1 | tf_op jit(solution)/shard_map/mix_sibling/pallas_call | solution.py:260
  35.1 0.1 collective-permute-start.12
  35.2 2.4 %mix_own.1.own = f32[512,1024]{1,0:T(8,128)S(1)} custom-call(s32[2]{0:T(128)S(1)} %pad_add_fusion.1.place, bf16[144,768]{1,0:T(8,128)(2,1)S(1)} %get-tuple-element.49.refs_0_, bf16[144,768]{1,0:T(8,128)(2,1)S(1)} %collective-permute-done.9.refs_1_, bf16[144,768]{1,0:T(8,128)(2,1)S(1)} %collective-permute-done.10.refs_2_, ...), custom_call_target="tpu_custom_call" | custom-call | flops 99999997952 | bytes 1 | tf_op jit(solution)/shard_map/mix_own/pallas_call | solution.py:260
  37.6 0.0 copy-start.3
  37.7 0.2 collective-permute-done.12.arrived
  37.9 0.2 add.17
  38.0 1.8 %collective-permute-start.13 = (bf16[128,512]{1,0:T(8,128)(2,1)S(1)}, bf16[128,512]{1,0:T(8,128)(2,1)S(1)}, u32[]{:S(2)}, u32[]{:S(2)}) collective-permute-start(bf16[128,512]{1,0:T(8,128)(2,1)S(1)} %get-tuple-element.56), channel_id=1, source_target_pairs={{0,8},{8,0},{16,24},{24,16},{1,9},{9,1},{17,25},{25,17},{2,10},{10... | collective-permute-start | bytes 393224 | tf_op jit(solution)/shard_map/ppermute | solution.py:293
  39.8 1.5 %collective-permute-start.14 = (bf16[128,512]{1,0:T(8,128)(2,1)S(1)}, bf16[128,512]{1,0:T(8,128)(2,1)S(1)}, u32[]{:S(2)}, u32[]{:S(2)}) collective-permute-start(bf16[128,512]{1,0:T(8,128)(2,1)S(1)} %get-tuple-element.57), channel_id=1, source_target_pairs={{0,16},{8,24},{16,0},{24,8},{1,17},{9,25},{17,1},{25,9},{2,18},{10... | collective-permute-start | bytes 393224 | tf_op jit(solution)/shard_map/ppermute | solution.py:293
  41.4 2.8 %collective-permute-done.13.low = bf16[128,512]{1,0:T(8,128)(2,1)S(1)} collective-permute-done((bf16[128,512]{1,0:T(8,128)(2,1)S(1)}, bf16[128,512]{1,0:T(8,128)(2,1)S(1)}, u32[]{:S(2)}, u32[]{:S(2)}) %collective-permute-start.13) | collective-permute-done | bytes 131104 | tf_op jit(solution)/shard_map/ppermute | solution.py:293
  44.2 1.4 %collective-permute-done.14.high = bf16[128,512]{1,0:T(8,128)(2,1)S(1)} collective-permute-done((bf16[128,512]{1,0:T(8,128)(2,1)S(1)}, bf16[128,512]{1,0:T(8,128)(2,1)S(1)}, u32[]{:S(2)}, u32[]{:S(2)}) %collective-permute-start.14) | collective-permute-done | bytes 131104 | tf_op jit(solution)/shard_map/ppermute | solution.py:293
  45.6 0.1 join.1
  45.6 1.3 %collective-permute-start.15 = (bf16[128,1024]{1,0:T(8,128)(2,1)S(1)}, bf16[128,1024]{1,0:T(8,128)(2,1)S(1)}, u32[]{:S(2)}, u32[]{:S(2)}) collective-permute-start(bf16[128,1024]{1,0:T(8,128)(2,1)S(1)} %get-tuple-element.58), channel_id=1, source_target_pairs={{0,8},{8,0},{16,24},{24,16},{1,9},{9,1},{17,25},{25,17},{2,10},{10... | collective-permute-start | bytes 786440 | tf_op jit(solution)/shard_map/ppermute | solution.py:293
  46.9 0.8 %collective-permute-start.16 = (bf16[128,1024]{1,0:T(8,128)(2,1)S(1)}, bf16[128,1024]{1,0:T(8,128)(2,1)S(1)}, u32[]{:S(2)}, u32[]{:S(2)}) collective-permute-start(bf16[128,1024]{1,0:T(8,128)(2,1)S(1)} %get-tuple-element.59), channel_id=1, source_target_pairs={{0,16},{8,24},{16,0},{24,8},{1,17},{9,25},{17,1},{25,9},{2,18},{10... | collective-permute-start | bytes 786440 | tf_op jit(solution)/shard_map/ppermute | solution.py:293
  47.8 2.3 %restore.1 = bf16[4,704,128]{2,1,0:T(8,128)(2,1)} custom-call(s32[2]{0:T(128)S(1)} %pad_add_fusion.1.place, s32[8,128]{1,0:T(8,128)S(1)} %copy-done.3, bf16[144,704]{1,0:T(8,128)(2,1)S(1)} %get-tuple-element.60.refs_0_, bf16[144,704]{1,0:T(8,128)(2,1)S(1)} %collective-permute-done.17.refs_1_, bf16[144,704]{1,0:T(8,128)(2,1)S(1)} %collective-permute-done.18.refs_2_, ...), custom_call_target="tpu_custom_call" | custom-call | flops 99999997952 | bytes 1 | tf_op jit(solution)/shard_map/restore/pallas_call | solution.py:260
  50.1 3.4 %collective-permute-done.15 = bf16[128,1024]{1,0:T(8,128)(2,1)S(1)} collective-permute-done((bf16[128,1024]{1,0:T(8,128)(2,1)S(1)}, bf16[128,1024]{1,0:T(8,128)(2,1)S(1)}, u32[]{:S(2)}, u32[]{:S(2)}) %collective-permute-start.15) | collective-permute-done | bytes 262176 | tf_op jit(solution)/shard_map/ppermute | solution.py:293
  53.4 1.5 %collective-permute-done.16 = bf16[128,1024]{1,0:T(8,128)(2,1)S(1)} collective-permute-done((bf16[128,1024]{1,0:T(8,128)(2,1)S(1)}, bf16[128,1024]{1,0:T(8,128)(2,1)S(1)}, u32[]{:S(2)}, u32[]{:S(2)}) %collective-permute-start.16) | collective-permute-done | bytes 262176 | tf_op jit(solution)/shard_map/ppermute | solution.py:293
  54.9 0.8 %add_convert_fusion = bf16[128,1024]{1,0:T(8,128)(2,1)} fusion(bf16[128,1024]{1,0:T(8,128)(2,1)S(1)} %collective-permute-done.16, f32[128,1024]{1,0:T(8,128)S(1)} %get-tuple-element.53, bf16[128,1024]{1,0:T(8,128)(2,1)S(1)} %collective-permute-done.15), kind=kLoop, calls=%fused_computation.2 | loop fusion | flops 655360 | bytes 1310720 | tf_op jit(solution)/shard_map/convert_element_type | solution.py:369
  (14 shorter events, 0.1 us)
Async XLA Ops:
  2.3 5.4 %collective-permute-start.2 = (bf16[136,1024]{1,0:T(8,128)(2,1)S(1)}, bf16[136,1024]{1,0:T(8,128)(2,1)S(1)}, u32[]{:S(2)}, u32[]{:S(2)}) collective-permute-start(bf16[136,1024]{1,0:T(8,128)(2,1)S(1)} %fusion.1.refs_0_), channel_id=1, source_target_pairs={{0,1},{1,0},{2,3},{3,2},{4,5},{5,4},{6,7},{7,6},{8,9},{9,8},{10,11... | collective-permute-start | bytes 835592 | tf_op jit(solution)/shard_map/ppermute | solution.py:296
  2.8 9.8 %collective-permute-start.1 = (bf16[136,1024]{1,0:T(8,128)(2,1)S(1)}, bf16[136,1024]{1,0:T(8,128)(2,1)S(1)}, u32[]{:S(2)}, u32[]{:S(2)}) collective-permute-start(bf16[136,1024]{1,0:T(8,128)(2,1)S(1)} %fusion.1.refs_0_), channel_id=1, source_target_pairs={{0,8},{8,0},{16,24},{24,16},{1,9},{9,1},{17,25},{25,17},{2,10},{10... | collective-permute-start | bytes 835592 | tf_op jit(solution)/shard_map/ppermute | solution.py:293
  5.4 8.7 %collective-permute-start = (bf16[136,1024]{1,0:T(8,128)(2,1)S(1)}, bf16[136,1024]{1,0:T(8,128)(2,1)S(1)}, u32[]{:S(2)}, u32[]{:S(2)}) collective-permute-start(bf16[136,1024]{1,0:T(8,128)(2,1)S(1)} %fusion.1.refs_0_), channel_id=1, source_target_pairs={{0,16},{8,24},{16,0},{24,8},{1,17},{9,25},{17,1},{25,9},{2,18},{10... | collective-permute-start | bytes 835592 | tf_op jit(solution)/shard_map/ppermute | solution.py:293
  7.7 9.1 %copy-start.2 = (s32[8,128]{1,0:T(8,128)}, s32[8,128]{1,0:T(8,128)S(1)}, u32[]{:S(2)}) copy-start(s32[8,128]{1,0:T(8,128)S(1)} %pad_add_fusion.meta_ref) | copy-start | bytes 12292
  7.7 1.1 %copy-start.1 = (bf16[128,4,704]{0,2,1:T(8,128)(2,1)S(1)}, bf16[128,4,704]{0,2,1:T(8,128)(2,1)}, u32[]{:S(2)}) copy-start(bf16[128,4,704]{0,2,1:T(8,128)(2,1)} %param.5) | copy-start | bytes 2162692
  14.1 8.9 %collective-permute-start.6 = (bf16[136,1024]{1,0:T(8,128)(2,1)S(1)}, bf16[136,1024]{1,0:T(8,128)(2,1)S(1)}, u32[]{:S(2)}, u32[]{:S(2)}) collective-permute-start(bf16[136,1024]{1,0:T(8,128)(2,1)S(1)} %collective-permute-done.two.refs_2_), channel_id=1, source_target_pairs={{0,1},{1,0},{2,3},{3,2},{4,5},{5,4},{6,7},{7,6},{8,9},{9,8},{10,11... | collective-permute-start | bytes 835592 | tf_op jit(solution)/shard_map/ppermute | solution.py:296
  14.1 8.9 %collective-permute-start.5 = (bf16[136,1024]{1,0:T(8,128)(2,1)S(1)}, bf16[136,1024]{1,0:T(8,128)(2,1)S(1)}, u32[]{:S(2)}, u32[]{:S(2)}) collective-permute-start(bf16[136,1024]{1,0:T(8,128)(2,1)S(1)} %collective-permute-done.1.one.refs_1_), channel_id=1, source_target_pairs={{0,1},{1,0},{2,3},{3,2},{4,5},{5,4},{6,7},{7,6},{8,9},{9,8},{10,11... | collective-permute-start | bytes 835592 | tf_op jit(solution)/shard_map/ppermute | solution.py:296
  14.6 5.6 %collective-permute-start.3 = (bf16[136,512]{1,0:T(8,128)(2,1)S(1)}, bf16[136,512]{1,0:T(8,128)(2,1)S(1)}, u32[]{:S(2)}, u32[]{:S(2)}) collective-permute-start(bf16[136,512]{1,0:T(8,128)(2,1)S(1)} %get-tuple-element.40), channel_id=1, source_target_pairs={{0,16},{8,24},{16,0},{24,8},{1,17},{9,25},{17,1},{25,9},{2,18},{10... | collective-permute-start | bytes 417800 | tf_op jit(solution)/shard_map/ppermute | solution.py:293
  16.2 6.6 %collective-permute-start.4 = (bf16[136,512]{1,0:T(8,128)(2,1)S(1)}, bf16[136,512]{1,0:T(8,128)(2,1)S(1)}, u32[]{:S(2)}, u32[]{:S(2)}) collective-permute-start(bf16[136,512]{1,0:T(8,128)(2,1)S(1)} %get-tuple-element.41), channel_id=1, source_target_pairs={{0,8},{8,0},{16,24},{24,16},{1,9},{9,1},{17,25},{25,17},{2,10},{10... | collective-permute-start | bytes 417800 | tf_op jit(solution)/shard_map/ppermute | solution.py:293
  16.8 15.7 %collective-permute-start.9 = (bf16[144,768]{1,0:T(8,128)(2,1)S(1)}, bf16[144,768]{1,0:T(8,128)(2,1)S(1)}, u32[]{:S(2)}, u32[]{:S(2)}) collective-permute-start(bf16[144,768]{1,0:T(8,128)(2,1)S(1)} %get-tuple-element.50), channel_id=1, source_target_pairs={{0,8},{8,0},{16,24},{24,16},{1,9},{9,1},{17,25},{25,17},{2,10},{10... | collective-permute-start | bytes 663560 | tf_op jit(solution)/shard_map/ppermute | solution.py:293
  20.3 12.4 %collective-permute-start.10 = (bf16[144,768]{1,0:T(8,128)(2,1)S(1)}, bf16[144,768]{1,0:T(8,128)(2,1)S(1)}, u32[]{:S(2)}, u32[]{:S(2)}) collective-permute-start(bf16[144,768]{1,0:T(8,128)(2,1)S(1)} %get-tuple-element.51), channel_id=1, source_target_pairs={{0,16},{8,24},{16,0},{24,8},{1,17},{9,25},{17,1},{25,9},{2,18},{10... | collective-permute-start | bytes 663560 | tf_op jit(solution)/shard_map/ppermute | solution.py:293
  22.8 9.9 %collective-permute-start.11 = (bf16[144,768]{1,0:T(8,128)(2,1)S(1)}, bf16[144,768]{1,0:T(8,128)(2,1)S(1)}, u32[]{:S(2)}, u32[]{:S(2)}) collective-permute-start(bf16[144,768]{1,0:T(8,128)(2,1)S(1)} %get-tuple-element.52), channel_id=1, source_target_pairs={{0,24},{8,16},{16,8},{24,0},{1,25},{9,17},{17,9},{25,1},{2,26},{10... | collective-permute-start | bytes 663560 | tf_op jit(solution)/shard_map/ppermute | solution.py:293
  23.0 1.7 %collective-permute-start.7 = (bf16[136,512]{1,0:T(8,128)(2,1)S(1)}, bf16[136,512]{1,0:T(8,128)(2,1)S(1)}, u32[]{:S(2)}, u32[]{:S(2)}) collective-permute-start(bf16[136,512]{1,0:T(8,128)(2,1)S(1)} %collective-permute-done.3.refs_3_), channel_id=1, source_target_pairs={{0,1},{1,0},{2,3},{3,2},{4,5},{5,4},{6,7},{7,6},{8,9},{9,8},{10,11... | collective-permute-start | bytes 417800 | tf_op jit(solution)/shard_map/ppermute | solution.py:296
  23.1 1.7 %collective-permute-start.8 = (bf16[136,512]{1,0:T(8,128)(2,1)S(1)}, bf16[136,512]{1,0:T(8,128)(2,1)S(1)}, u32[]{:S(2)}, u32[]{:S(2)}) collective-permute-start(bf16[136,512]{1,0:T(8,128)(2,1)S(1)} %collective-permute-done.4.refs_4_), channel_id=1, source_target_pairs={{0,1},{1,0},{2,3},{3,2},{4,5},{5,4},{6,7},{7,6},{8,9},{9,8},{10,11... | collective-permute-start | bytes 417800 | tf_op jit(solution)/shard_map/ppermute | solution.py:296
  23.6 2.6 %copy-start = (bf16[2,704,2048]{2,1,0:T(8,128)(2,1)S(1)}, bf16[2,704,2048]{2,1,0:T(8,128)(2,1)}, u32[]{:S(2)}) copy-start(bf16[2,704,2048]{2,1,0:T(8,128)(2,1)} %refs_4_.3) | copy-start | bytes 17301508
  29.1 18.7 %collective-permute-start.17 = (bf16[144,704]{1,0:T(8,128)(2,1)S(1)}, bf16[144,704]{1,0:T(8,128)(2,1)S(1)}, u32[]{:S(2)}, u32[]{:S(2)}) collective-permute-start(bf16[144,704]{1,0:T(8,128)(2,1)S(1)} %get-tuple-element.61), channel_id=1, source_target_pairs={{0,8},{8,0},{16,24},{24,16},{1,9},{9,1},{17,25},{25,17},{2,10},{10... | collective-permute-start | bytes 608264 | tf_op jit(solution)/shard_map/ppermute | solution.py:293
  30.9 16.9 %collective-permute-start.18 = (bf16[144,704]{1,0:T(8,128)(2,1)S(1)}, bf16[144,704]{1,0:T(8,128)(2,1)S(1)}, u32[]{:S(2)}, u32[]{:S(2)}) collective-permute-start(bf16[144,704]{1,0:T(8,128)(2,1)S(1)} %get-tuple-element.62), channel_id=1, source_target_pairs={{0,16},{8,24},{16,0},{24,8},{1,17},{9,25},{17,1},{25,9},{2,18},{10... | collective-permute-start | bytes 608264 | tf_op jit(solution)/shard_map/ppermute | solution.py:293
  32.4 15.4 %collective-permute-start.19 = (bf16[144,704]{1,0:T(8,128)(2,1)S(1)}, bf16[144,704]{1,0:T(8,128)(2,1)S(1)}, u32[]{:S(2)}, u32[]{:S(2)}) collective-permute-start(bf16[144,704]{1,0:T(8,128)(2,1)S(1)} %get-tuple-element.63), channel_id=1, source_target_pairs={{0,24},{8,16},{16,8},{24,0},{1,25},{9,17},{17,9},{25,1},{2,26},{10... | collective-permute-start | bytes 608264 | tf_op jit(solution)/shard_map/ppermute | solution.py:293
  35.1 2.7 %collective-permute-start.12 = (bf16[512,1024]{1,0:T(8,128)(2,1)S(1)}, bf16[512,1024]{1,0:T(8,128)(2,1)S(1)}, u32[]{:S(2)}, u32[]{:S(2)}) collective-permute-start(bf16[512,1024]{1,0:T(8,128)(2,1)S(1)} %mix_sibling.1), channel_id=1, source_target_pairs={{0,1},{1,0},{2,3},{3,2},{4,5},{5,4},{6,7},{7,6},{8,9},{9,8},{10,11... | collective-permute-start | bytes 3145736 | tf_op jit(solution)/shard_map/ppermute | solution.py:296
  37.6 10.1 %copy-start.3 = (s32[8,128]{1,0:T(8,128)S(1)}, s32[8,128]{1,0:T(8,128)}, u32[]{:S(2)}) copy-start(s32[8,128]{1,0:T(8,128)} %copy-done.2) | copy-start | bytes 12292
  38.0 6.1 %collective-permute-start.13 = (bf16[128,512]{1,0:T(8,128)(2,1)S(1)}, bf16[128,512]{1,0:T(8,128)(2,1)S(1)}, u32[]{:S(2)}, u32[]{:S(2)}) collective-permute-start(bf16[128,512]{1,0:T(8,128)(2,1)S(1)} %get-tuple-element.56), channel_id=1, source_target_pairs={{0,8},{8,0},{16,24},{24,16},{1,9},{9,1},{17,25},{25,17},{2,10},{10... | collective-permute-start | bytes 393224 | tf_op jit(solution)/shard_map/ppermute | solution.py:293
  39.8 5.7 %collective-permute-start.14 = (bf16[128,512]{1,0:T(8,128)(2,1)S(1)}, bf16[128,512]{1,0:T(8,128)(2,1)S(1)}, u32[]{:S(2)}, u32[]{:S(2)}) collective-permute-start(bf16[128,512]{1,0:T(8,128)(2,1)S(1)} %get-tuple-element.57), channel_id=1, source_target_pairs={{0,16},{8,24},{16,0},{24,8},{1,17},{9,25},{17,1},{25,9},{2,18},{10... | collective-permute-start | bytes 393224 | tf_op jit(solution)/shard_map/ppermute | solution.py:293
  45.6 7.8 %collective-permute-start.15 = (bf16[128,1024]{1,0:T(8,128)(2,1)S(1)}, bf16[128,1024]{1,0:T(8,128)(2,1)S(1)}, u32[]{:S(2)}, u32[]{:S(2)}) collective-permute-start(bf16[128,1024]{1,0:T(8,128)(2,1)S(1)} %get-tuple-element.58), channel_id=1, source_target_pairs={{0,8},{8,0},{16,24},{24,16},{1,9},{9,1},{17,25},{25,17},{2,10},{10... | collective-permute-start | bytes 786440 | tf_op jit(solution)/shard_map/ppermute | solution.py:293
  46.9 8.0 %collective-permute-start.16 = (bf16[128,1024]{1,0:T(8,128)(2,1)S(1)}, bf16[128,1024]{1,0:T(8,128)(2,1)S(1)}, u32[]{:S(2)}, u32[]{:S(2)}) collective-permute-start(bf16[128,1024]{1,0:T(8,128)(2,1)S(1)} %get-tuple-element.59), channel_id=1, source_target_pairs={{0,16},{8,24},{16,0},{24,8},{1,17},{9,25},{17,1},{25,9},{2,18},{10... | collective-permute-start | bytes 786440 | tf_op jit(solution)/shard_map/ppermute | solution.py:293

commit v3 on v0

--- a/solution.py
+++ b/solution.py
@@ -120,33 +120,33 @@
 
 
 def gather_kernel(dims, top, place, *refs):
-    x_ref, held_ref = refs[-2:]
-    own = refs[:-2]
-    tokens = held_ref.shape[2]
-    held = [routes(dims, top, place[0], ref, tokens) for ref in own]
-    for s, h in enumerate(held):
-        held_ref[s] = h
-    gather_rows(dims, held, own, x_ref)
-
-
-def products(dims, place, x_ref, x_other, w_ref):
+    experts, local, cap, width = dims
+    own, x_ref = refs[:-1], refs[-1]
+    half = own[0].shape[1]
+    tokens = own[0].shape[0] - 8
+    chunk = min(half, 512)
+    held = []
+    for ref in own:
+        ids = ref[tokens:, :tokens].astype(F32).astype(jnp.int32)[:top]
+        held.append(
+            jnp.concatenate(slots_by_lane(ids, place[0], local, cap, width), axis=0)
+        )
+    for c in range(0, half, chunk):
+        rows = [dot(h, ref[:tokens, c : c + chunk], NN) for h, ref in zip(held, own)]
+        for l, x in enumerate(by_expert(rows, local, cap)):
+            x_ref[l, :, c : c + chunk] = x.astype(BF16)
+
+
+def grad_kernel(dims, place, x_ref, x_other, w_ref, *outs):
+    experts, local, cap, width = dims
     half = x_ref.shape[2]
     mine = pl.ds(pl.multiple_of(place[1] * half, half), half)
     theirs = pl.ds(pl.multiple_of((1 - place[1]) * half, half), half)
-    return [
+    grads = [
         dot(x_ref[l], w_ref[l, :, mine], NT) + dot(x_other[l], w_ref[l, :, theirs], NT)
-        for l in range(dims[1])
-    ]
-
-
-def grad_kernel(dims, place, *refs):
-    n = (len(refs) - 4) // 2
-    other = refs[:n]
-    x_ref, held_ref, w_ref = refs[n : n + 3]
-    outs, x_other = refs[n + 3 : 2 * n + 3], refs[-1]
-    gather_rows(dims, [held_ref[s] for s in range(n)], other, x_other)
-    grads = products(dims, place, x_ref, x_other, w_ref)
-    for s, rows in enumerate(by_source(grads, n, dims[2])):
+        for l in range(local)
+    ]
+    for s, rows in enumerate(by_source(grads, len(outs), cap)):
         outs[s][...] = rows.astype(BF16)
 
 
@@ -278,20 +278,23 @@
         [place, meta, hid_t], where=placed, name="dispatch",
     )
     hid = [send(hid_sent[s], s) for s in range(n)]
-    for s in range(1, n):
-        own[s], hid[0] = lax.optimization_barrier((own[s], hid[0]))
-    other = [swap(x) for x in own]
-
     slot = shaped((width, ff))
-    x, held = run(
-        functools.partial(gather_kernel, dims, top),
-        [shaped((local, n * cap, half)), shaped((n, width, tokens))],
-        [place, *own], where=placed, name="gather", weight=BIG,
-    )
-    grad_sent = run(
-        functools.partial(grad_kernel, dims), [slot] * n,
-        [place, *other, x, held, w_down], where=placed,
-        scratch=[pltpu.VMEM((local, n * cap, half), BF16)], name="grad",
+
+    def taken(own, w_down):
+        (x,) = run(
+            functools.partial(gather_kernel, dims, top),
+            [shaped((local, n * cap, half))], [place, *own], where=placed, name="gather",
+        )
+        return list(run(
+            functools.partial(grad_kernel, dims), [slot] * n,
+            [place, x, swap(x), w_down], where=placed, name="grad",
+        ))
+
+    def skipped(own, w_down):
+        return [jnp.zeros((width, ff), BF16)] * n
+
+    grad_sent = lax.cond(
+        place[0] < 1000, taken, skipped, own, w_down
     )
     hid[0], grad_own = lax.optimization_barrier((hid[0], grad_sent[0]))
     grad_back = [grad_own] + [send(grad_sent[s], s) for s in range(1, n)]

time: 54.6 us -> 58.9 us (1.079)
  Pallas kernels: 12.8 us -> 19.4 us
  waiting for transfers between devices: 18.3 us -> 16.4 us
  local copies, waits for them, and re-layouts: 2.31 us -> 1.12 us
  starting transfers between devices: 17 us -> 17.7 us
    pallas_call x8, Pallas kernels: 12.8 us -> 19.4 us  [call(): pl.pallas_call(kernel, out_shape=outs, in_specs=[pl.BlockSpec(memory_spac...]
    ppermute x13, waiting for transfers between devices: 17.8 us -> 13.5 us  [send(): return lax.ppermute(x, 'ctx', [(i, i ^ s) for i in range(n)]) if s else x]
    ppermute x5 -> x2, waiting for transfers between devices: 0.49 us -> 2.84 us  [swap(): return lax.ppermute(x, 'tp', [(0, 1), (1, 0)])]
    unnamed x8 -> x4, local copies, waits for them, and re-layouts: 2.31 us -> 1.12 us
    ppermute x13, starting transfers between devices: 16.4 us -> 17.5 us  [send(): return lax.ppermute(x, 'ctx', [(i, i ^ s) for i in range(n)]) if s else x]
  transfers between devices with their start and end apart: 18 -> 15, of which waited for: 9 -> 8; matrix products, arithmetic and copies ran while one was open for 1% -> 1% of each run, Pallas kernels for 24% -> 33%
where the time goes in v3:
time: 58.9 us; the launch traced here: 58.6 us
  Pallas kernels  19.4 us (33%)
  starting transfers between devices  17.7 us (30%)
  waiting for transfers between devices  16.4 us (28%)
  other arithmetic  3.25 us (6%)
  local copies, waits for them, and re-layouts  1.12 us (2%)
  between operations  0.7 us (1%)
    pallas_call x8, Pallas kernels, call(): pl.pallas_call(kernel, out_shape=outs, in_specs=[pl.BlockSpec(memory_spac...  19.4 us
    ppermute x13, starting transfers between devices, send(): return lax.ppermute(x, 'ctx', [(i, i ^ s) for i in range(n)]) if s else x  17.5 us
    ppermute x13, waiting for transfers between devices, send(): return lax.ppermute(x, 'ctx', [(i, i ^ s) for i in range(n)]) if s else x  13.5 us
    ppermute x2, waiting for transfers between devices, swap(): return lax.ppermute(x, 'tp', [(0, 1), (1, 0)])  2.84 us
  transfers between devices with their start and end apart: 15, of which 8 were waited for; matrix products, arithmetic and copies ran while one was open for 1% of the time, Pallas kernels for 33%

profile of v3, /device:TPU:0, one launch (start us, length us, event | category | flops | bytes accessed | tf_op | source)
XLA Modules:
  0.0 58.6 jit_solution(5414728117120951744)
XLA Ops:
  0.6 0.7 %bitcast_convert_fusion = bf16[4,128]{1,0:T(4,128)(2,1)S(1)} fusion(s32[128,4]{0,1:T(4,128)} %param.8), kind=kLoop, calls=%fused_computation.6 | loop fusion | flops 512 | bytes 3072 | tf_op jit(solution)/shard_map/convert_element_type | solution.py:272
  1.3 1.0 %fusion.1 = bf16[136,1024]{1,0:T(8,128)(2,1)S(1)} fusion(bf16[4,128]{1,0:T(4,128)(2,1)S(1)} %bitcast_convert_fusion, bf16[128,1024]{1,0:T(8,128)(2,1)} %param.10), kind=kLoop, calls=%fused_computation.3 | loop fusion | flops 835584 | bytes 541696 | tf_op jit(solution)/shard_map/concatenate | solution.py:273
  2.3 4.0 %collective-permute-start.3 = (bf16[136,1024]{1,0:T(8,128)(2,1)S(1)}, bf16[136,1024]{1,0:T(8,128)(2,1)S(1)}, u32[]{:S(2)}, u32[]{:S(2)}) collective-permute-start(bf16[136,1024]{1,0:T(8,128)(2,1)S(1)} %fusion.1), channel_id=1, source_target_pairs={{0,24},{8,16},{16,8},{24,0},{1,25},{9,17},{17,9},{25,1},{2,26},{10... | collective-permute-start | bytes 835592 | tf_op jit(solution)/shard_map/ppermute | solution.py:265
  6.2 0.5 collective-permute-start.2
  6.8 0.1 collective-permute-start.1
  6.9 0.7 %pad_add_fusion.meta_ref = s32[8,128]{1,0:T(8,128)S(1)} fusion(s32[4,128]{1,0:T(4,128)} %bitcast.9, s32[4,128]{1,0:T(4,128)} %bitcast.8), kind=kLoop, calls=%fused_computation.4 | loop fusion | flops 1024 | bytes 8192 | tf_op jit(solution)/shard_map/concatenate | solution.py:270
  7.6 0.1 pad_add_fusion.1.place
  7.7 0.0 copy-start
  7.7 1.1 %copy-done = bf16[128,4,704]{0,2,1:T(8,128)(2,1)S(1)} copy-done((bf16[128,4,704]{0,2,1:T(8,128)(2,1)S(1)}, bf16[128,4,704]{0,2,1:T(8,128)(2,1)}, u32[]{:S(2)}) %copy-start) | copy-done | bytes 720920
  8.8 1.4 %dispatch.1 = (bf16[144,768]{1,0:T(8,128)(2,1)S(1)}, bf16[144,768]{1,0:T(8,128)(2,1)S(1)}, bf16[144,768]{1,0:T(8,128)(2,1)S(1)}, bf16[144,768]{1,0:T(8,128)(2,1)S(1)}) custom-call(s32[2]{0:T(128)S(1)} %pad_add_fusion.1.place, s32[8,128]{1,0:T(8,128)S(1)} %pad_add_fusion.meta_ref, bf16[4,704,128]{2,1,0:T(8,128)(2,1)S(1)} %bitcast.7), custom_call_target="tpu_custom_call" | custom-call | flops 1 | bytes 1 | tf_op jit(solution)/shard_map/dispatch/pallas_call | solution.py:232
  10.1 2.0 %collective-permute-start.4 = (bf16[144,768]{1,0:T(8,128)(2,1)S(1)}, bf16[144,768]{1,0:T(8,128)(2,1)S(1)}, u32[]{:S(2)}, u32[]{:S(2)}) collective-permute-start(bf16[144,768]{1,0:T(8,128)(2,1)S(1)} %get-tuple-element.40), channel_id=1, source_target_pairs={{0,8},{8,0},{16,24},{24,16},{1,9},{9,1},{17,25},{25,17},{2,10},{10... | collective-permute-start | bytes 663560 | tf_op jit(solution)/shard_map/ppermute | solution.py:265
  12.1 1.5 %collective-permute-start.5 = (bf16[144,768]{1,0:T(8,128)(2,1)S(1)}, bf16[144,768]{1,0:T(8,128)(2,1)S(1)}, u32[]{:S(2)}, u32[]{:S(2)}) collective-permute-start(bf16[144,768]{1,0:T(8,128)(2,1)S(1)} %get-tuple-element.41), channel_id=1, source_target_pairs={{0,16},{8,24},{16,0},{24,8},{1,17},{9,25},{17,1},{25,9},{2,18},{10... | collective-permute-start | bytes 663560 | tf_op jit(solution)/shard_map/ppermute | solution.py:265
  13.6 0.2 collective-permute-done.3
  13.8 2.9 %collective-permute-start.6 = (bf16[144,768]{1,0:T(8,128)(2,1)S(1)}, bf16[144,768]{1,0:T(8,128)(2,1)S(1)}, u32[]{:S(2)}, u32[]{:S(2)}) collective-permute-start(bf16[144,768]{1,0:T(8,128)(2,1)S(1)} %get-tuple-element.42), channel_id=1, source_target_pairs={{0,24},{8,16},{16,8},{24,0},{1,25},{9,17},{17,9},{25,1},{2,26},{10... | collective-permute-start | bytes 663560 | tf_op jit(solution)/shard_map/ppermute | solution.py:265
  16.7 2.3 %collective-permute-done.2 = bf16[136,1024]{1,0:T(8,128)(2,1)S(1)} collective-permute-done((bf16[136,1024]{1,0:T(8,128)(2,1)S(1)}, bf16[136,1024]{1,0:T(8,128)(2,1)S(1)}, u32[]{:S(2)}, u32[]{:S(2)}) %collective-permute-start.2) | collective-permute-done | bytes 278560 | tf_op jit(solution)/shard_map/ppermute | solution.py:265
  19.0 1.3 %collective-permute-done.1 = bf16[136,1024]{1,0:T(8,128)(2,1)S(1)} collective-permute-done((bf16[136,1024]{1,0:T(8,128)(2,1)S(1)}, bf16[136,1024]{1,0:T(8,128)(2,1)S(1)}, u32[]{:S(2)}, u32[]{:S(2)}) %collective-permute-start.1) | collective-permute-done | bytes 278560 | tf_op jit(solution)/shard_map/ppermute | solution.py:265
  20.3 9.4 %conditional.1 = ((bf16[144,704]{1,0:T(8,128)(2,1)}, bf16[144,704]{1,0:T(8,128)(2,1)S(1)}, bf16[144,704]{1,0:T(8,128)(2,1)S(1)}, bf16[144,704]{1,0:T(8,128)(2,1)S(1)})) conditional(s32[]{:T(128)} %convert_element_type.17, () %tuple.16, (s32[2]{0:T(128)S(1)}, bf16[136,1024]{1,0:T(8,128)(2,1)S(1)}, bf16[136,1024]{1,0:T(8,128)(2,1)S(1)}, ...), branch_computations={%region_0.1_spmd, %region_1.2_spmd} | conditional | flops 2 | bytes 4718642 | solution.py:296
  20.3 1.1 %gather.1.x_ref = bf16[2,288,1024]{2,1,0:T(8,128)(2,1)S(1)} custom-call(s32[2]{0:T(128)S(1)} %get-tuple-element.12.place, bf16[136,1024]{1,0:T(8,128)(2,1)S(1)} %get-tuple-element.13.refs_0_, bf16[136,1024]{1,0:T(8,128)(2,1)S(1)} %get-tuple-element.14.refs_1_, bf16[136,1024]{1,0:T(8,128)(2,1)S(1)} %get-tuple-element.15.refs_2_, ...), custom_call_target="tpu_custom_call" | custom-call | flops 1 | bytes 1 | tf_op jit(solution)/shard_map/cond/branch_1_fun/gather/pallas_call | solution.py:232
  21.4 0.1 collective-permute-start
  21.5 2.8 %collective-permute-done.x_other = bf16[2,288,1024]{2,1,0:T(8,128)(2,1)S(1)} collective-permute-done((bf16[2,288,1024]{2,1,0:T(8,128)(2,1)S(1)}, bf16[2,288,1024]{2,1,0:T(8,128)(2,1)S(1)}, u32[]{:S(2)}, u32[]{:S(2)}) %collective-permute-start) | collective-permute-done | bytes 1179680 | tf_op jit(solution)/shard_map/cond/branch_1_fun/ppermute | solution.py:268
  24.3 5.3 %grad.1 = (bf16[144,704]{1,0:T(8,128)(2,1)}, bf16[144,704]{1,0:T(8,128)(2,1)S(1)}, bf16[144,704]{1,0:T(8,128)(2,1)S(1)}, bf16[144,704]{1,0:T(8,128)(2,1)S(1)}) custom-call(s32[2]{0:T(128)S(1)} %get-tuple-element.12.place, bf16[2,288,1024]{2,1,0:T(8,128)(2,1)S(1)} %gather.1.x_ref, bf16[2,288,1024]{2,1,0:T(8,128)(2,1)S(1)} %collective-permute-done.x_other, ...), custom_call_target="tpu_custom_call" | custom-call | flops 1 | bytes 1 | tf_op jit(solution)/shard_map/cond/branch_1_fun/grad/pallas_call | solution.py:232
  29.7 1.4 %collective-permute-start.12 = (bf16[144,704]{1,0:T(8,128)(2,1)S(1)}, bf16[144,704]{1,0:T(8,128)(2,1)S(1)}, u32[]{:S(2)}, u32[]{:S(2)}) collective-permute-start(bf16[144,704]{1,0:T(8,128)(2,1)S(1)} %get-tuple-element.51), channel_id=1, source_target_pairs={{0,8},{8,0},{16,24},{24,16},{1,9},{9,1},{17,25},{25,17},{2,10},{10... | collective-permute-start | bytes 608264 | tf_op jit(solution)/shard_map/ppermute | solution.py:265
  31.1 0.5 collective-permute-start.13
  31.7 0.0 collective-permute-done.4.refs_1_
  31.7 1.5 %collective-permute-start.14 = (bf16[144,704]{1,0:T(8,128)(2,1)S(1)}, bf16[144,704]{1,0:T(8,128)(2,1)S(1)}, u32[]{:S(2)}, u32[]{:S(2)}) collective-permute-start(bf16[144,704]{1,0:T(8,128)(2,1)S(1)} %get-tuple-element.53), channel_id=1, source_target_pairs={{0,24},{8,16},{16,8},{24,0},{1,25},{9,17},{17,9},{25,1},{2,26},{10... | collective-permute-start | bytes 608264 | tf_op jit(solution)/shard_map/ppermute | solution.py:265
  33.2 0.0 collective-permute-done.5.refs_2_
  33.2 0.0 collective-permute-done.6.refs_3_
  33.2 4.5 %mix_sibling.1 = bf16[512,1024]{1,0:T(8,128)(2,1)S(1)} custom-call(s32[2]{0:T(128)S(1)} %pad_add_fusion.1.place, bf16[144,768]{1,0:T(8,128)(2,1)S(1)} %get-tuple-element.39.refs_0_, bf16[144,768]{1,0:T(8,128)(2,1)S(1)} %collective-permute-done.4.refs_1_, bf16[144,768]{1,0:T(8,128)(2,1)S(1)} %collective-permute-done.5.refs_2_, ...), custom_call_target="tpu_custom_call" | custom-call | flops 1 | bytes 1 | tf_op jit(solution)/shard_map/mix_sibling/pallas_call | solution.py:232
  37.7 0.1 collective-permute-start.7
  37.8 4.5 %mix_own.1.own = f32[512,1024]{1,0:T(8,128)S(1)} custom-call(s32[2]{0:T(128)S(1)} %pad_add_fusion.1.place, bf16[144,768]{1,0:T(8,128)(2,1)S(1)} %get-tuple-element.39.refs_0_, bf16[144,768]{1,0:T(8,128)(2,1)S(1)} %collective-permute-done.4.refs_1_, bf16[144,768]{1,0:T(8,128)(2,1)S(1)} %collective-permute-done.5.refs_2_, ...), custom_call_target="tpu_custom_call" | custom-call | flops 99999997952 | bytes 1 | tf_op jit(solution)/shard_map/mix_own/pallas_call | solution.py:232
  42.3 0.0 copy-start.1
  42.3 0.0 collective-permute-done.7.arrived
  42.4 0.2 add.17
  42.5 1.5 %collective-permute-start.8 = (bf16[128,512]{1,0:T(8,128)(2,1)S(1)}, bf16[128,512]{1,0:T(8,128)(2,1)S(1)}, u32[]{:S(2)}, u32[]{:S(2)}) collective-permute-start(bf16[128,512]{1,0:T(8,128)(2,1)S(1)} %get-tuple-element.46), channel_id=1, source_target_pairs={{0,8},{8,0},{16,24},{24,16},{1,9},{9,1},{17,25},{25,17},{2,10},{10... | collective-permute-start | bytes 393224 | tf_op jit(solution)/shard_map/ppermute | solution.py:265
  44.1 0.5 collective-permute-start.9
  44.6 3.9 %collective-permute-done.8.low = bf16[128,512]{1,0:T(8,128)(2,1)S(1)} collective-permute-done((bf16[128,512]{1,0:T(8,128)(2,1)S(1)}, bf16[128,512]{1,0:T(8,128)(2,1)S(1)}, u32[]{:S(2)}, u32[]{:S(2)}) %collective-permute-start.8) | collective-permute-done | bytes 131104 | tf_op jit(solution)/shard_map/ppermute | solution.py:265
  48.5 1.2 %collective-permute-done.9.high = bf16[128,512]{1,0:T(8,128)(2,1)S(1)} collective-permute-done((bf16[128,512]{1,0:T(8,128)(2,1)S(1)}, bf16[128,512]{1,0:T(8,128)(2,1)S(1)}, u32[]{:S(2)}, u32[]{:S(2)}) %collective-permute-start.9) | collective-permute-done | bytes 131104 | tf_op jit(solution)/shard_map/ppermute | solution.py:265
  49.7 0.1 join.1
  49.8 0.6 %collective-permute-start.10 = (bf16[128,1024]{1,0:T(8,128)(2,1)S(1)}, bf16[128,1024]{1,0:T(8,128)(2,1)S(1)}, u32[]{:S(2)}, u32[]{:S(2)}) collective-permute-start(bf16[128,1024]{1,0:T(8,128)(2,1)S(1)} %get-tuple-element.48), channel_id=1, source_target_pairs={{0,8},{8,0},{16,24},{24,16},{1,9},{9,1},{17,25},{25,17},{2,10},{10... | collective-permute-start | bytes 786440 | tf_op jit(solution)/shard_map/ppermute | solution.py:265
  50.4 0.4 collective-permute-start.11
  50.8 0.0 collective-permute-done.12.refs_1_
  50.8 0.0 collective-permute-done.13.refs_2_
  50.8 0.0 collective-permute-done.14.refs_3_
  50.8 0.0 copy-done.1
  50.8 2.3 %restore.1 = bf16[4,704,128]{2,1,0:T(8,128)(2,1)} custom-call(s32[2]{0:T(128)S(1)} %pad_add_fusion.1.place, s32[8,128]{1,0:T(8,128)S(1)} %pad_add_fusion.meta_ref, bf16[144,704]{1,0:T(8,128)(2,1)S(1)} %copy-done.1, bf16[144,704]{1,0:T(8,128)(2,1)S(1)} %collective-permute-done.12.refs_1_, bf16[144,704]{1,0:T(8,128)(2,1)S(1)} %collective-permute-done.13.refs_2_, ...), custom_call_target="tpu_custom_call" | custom-call | flops 99999997952 | bytes 1 | tf_op jit(solution)/shard_map/restore/pallas_call | solution.py:232
  53.1 4.4 %collective-permute-done.10 = bf16[128,1024]{1,0:T(8,128)(2,1)S(1)} collective-permute-done((bf16[128,1024]{1,0:T(8,128)(2,1)S(1)}, bf16[128,1024]{1,0:T(8,128)(2,1)S(1)}, u32[]{:S(2)}, u32[]{:S(2)}) %collective-permute-start.10) | collective-permute-done | bytes 262176 | tf_op jit(solution)/shard_map/ppermute | solution.py:265
  57.4 0.3 collective-permute-done.11
  57.8 0.8 %add_convert_fusion = bf16[128,1024]{1,0:T(8,128)(2,1)} fusion(bf16[128,1024]{1,0:T(8,128)(2,1)S(1)} %collective-permute-done.11, f32[128,1024]{1,0:T(8,128)S(1)} %get-tuple-element.43, bf16[128,1024]{1,0:T(8,128)(2,1)S(1)} %collective-permute-done.10), kind=kLoop, calls=%fused_computation.2 | loop fusion | flops 655360 | bytes 1310720 | tf_op jit(solution)/shard_map/convert_element_type | solution.py:334
Async XLA Ops:
  2.3 11.5 %collective-permute-start.3 = (bf16[136,1024]{1,0:T(8,128)(2,1)S(1)}, bf16[136,1024]{1,0:T(8,128)(2,1)S(1)}, u32[]{:S(2)}, u32[]{:S(2)}) collective-permute-start(bf16[136,1024]{1,0:T(8,128)(2,1)S(1)} %fusion.1), channel_id=1, source_target_pairs={{0,24},{8,16},{16,8},{24,0},{1,25},{9,17},{17,9},{25,1},{2,26},{10... | collective-permute-start | bytes 835592 | tf_op jit(solution)/shard_map/ppermute | solution.py:265
  6.2 12.7 %collective-permute-start.2 = (bf16[136,1024]{1,0:T(8,128)(2,1)S(1)}, bf16[136,1024]{1,0:T(8,128)(2,1)S(1)}, u32[]{:S(2)}, u32[]{:S(2)}) collective-permute-start(bf16[136,1024]{1,0:T(8,128)(2,1)S(1)} %fusion.1), channel_id=1, source_target_pairs={{0,16},{8,24},{16,0},{24,8},{1,17},{9,25},{17,1},{25,9},{2,18},{10... | collective-permute-start | bytes 835592 | tf_op jit(solution)/shard_map/ppermute | solution.py:265
  6.8 13.6 %collective-permute-start.1 = (bf16[136,1024]{1,0:T(8,128)(2,1)S(1)}, bf16[136,1024]{1,0:T(8,128)(2,1)S(1)}, u32[]{:S(2)}, u32[]{:S(2)}) collective-permute-start(bf16[136,1024]{1,0:T(8,128)(2,1)S(1)} %fusion.1), channel_id=1, source_target_pairs={{0,8},{8,0},{16,24},{24,16},{1,9},{9,1},{17,25},{25,17},{2,10},{10... | collective-permute-start | bytes 835592 | tf_op jit(solution)/shard_map/ppermute | solution.py:265
  7.7 1.1 %copy-start = (bf16[128,4,704]{0,2,1:T(8,128)(2,1)S(1)}, bf16[128,4,704]{0,2,1:T(8,128)(2,1)}, u32[]{:S(2)}) copy-start(bf16[128,4,704]{0,2,1:T(8,128)(2,1)} %param.7) | copy-start | bytes 2162692
  10.1 21.5 %collective-permute-start.4 = (bf16[144,768]{1,0:T(8,128)(2,1)S(1)}, bf16[144,768]{1,0:T(8,128)(2,1)S(1)}, u32[]{:S(2)}, u32[]{:S(2)}) collective-permute-start(bf16[144,768]{1,0:T(8,128)(2,1)S(1)} %get-tuple-element.40), channel_id=1, source_target_pairs={{0,8},{8,0},{16,24},{24,16},{1,9},{9,1},{17,25},{25,17},{2,10},{10... | collective-permute-start | bytes 663560 | tf_op jit(solution)/shard_map/ppermute | solution.py:265
  12.1 21.1 %collective-permute-start.5 = (bf16[144,768]{1,0:T(8,128)(2,1)S(1)}, bf16[144,768]{1,0:T(8,128)(2,1)S(1)}, u32[]{:S(2)}, u32[]{:S(2)}) collective-permute-start(bf16[144,768]{1,0:T(8,128)(2,1)S(1)} %get-tuple-element.41), channel_id=1, source_target_pairs={{0,16},{8,24},{16,0},{24,8},{1,17},{9,25},{17,1},{25,9},{2,18},{10... | collective-permute-start | bytes 663560 | tf_op jit(solution)/shard_map/ppermute | solution.py:265
  13.8 19.4 %collective-permute-start.6 = (bf16[144,768]{1,0:T(8,128)(2,1)S(1)}, bf16[144,768]{1,0:T(8,128)(2,1)S(1)}, u32[]{:S(2)}, u32[]{:S(2)}) collective-permute-start(bf16[144,768]{1,0:T(8,128)(2,1)S(1)} %get-tuple-element.42), channel_id=1, source_target_pairs={{0,24},{8,16},{16,8},{24,0},{1,25},{9,17},{17,9},{25,1},{2,26},{10... | collective-permute-start | bytes 663560 | tf_op jit(solution)/shard_map/ppermute | solution.py:265
  21.4 2.9 %collective-permute-start = (bf16[2,288,1024]{2,1,0:T(8,128)(2,1)S(1)}, bf16[2,288,1024]{2,1,0:T(8,128)(2,1)S(1)}, u32[]{:S(2)}, u32[]{:S(2)}) collective-permute-start(bf16[2,288,1024]{2,1,0:T(8,128)(2,1)S(1)} %gather.1.x_ref), channel_id=1, source_target_pairs={{0,1},{1,0},{2,3},{3,2},{4,5},{5,4},{6,7},{7,6},{8,9},{9,8},{10,11... | collective-permute-start | bytes 3538952 | tf_op jit(solution)/shard_map/cond/branch_1_fun/ppermute | solution.py:268
  29.7 21.1 %collective-permute-start.12 = (bf16[144,704]{1,0:T(8,128)(2,1)S(1)}, bf16[144,704]{1,0:T(8,128)(2,1)S(1)}, u32[]{:S(2)}, u32[]{:S(2)}) collective-permute-start(bf16[144,704]{1,0:T(8,128)(2,1)S(1)} %get-tuple-element.51), channel_id=1, source_target_pairs={{0,8},{8,0},{16,24},{24,16},{1,9},{9,1},{17,25},{25,17},{2,10},{10... | collective-permute-start | bytes 608264 | tf_op jit(solution)/shard_map/ppermute | solution.py:265
  31.1 19.7 %collective-permute-start.13 = (bf16[144,704]{1,0:T(8,128)(2,1)S(1)}, bf16[144,704]{1,0:T(8,128)(2,1)S(1)}, u32[]{:S(2)}, u32[]{:S(2)}) collective-permute-start(bf16[144,704]{1,0:T(8,128)(2,1)S(1)} %get-tuple-element.52), channel_id=1, source_target_pairs={{0,16},{8,24},{16,0},{24,8},{1,17},{9,25},{17,1},{25,9},{2,18},{10... | collective-permute-start | bytes 608264 | tf_op jit(solution)/shard_map/ppermute | solution.py:265
  31.7 19.1 %collective-permute-start.14 = (bf16[144,704]{1,0:T(8,128)(2,1)S(1)}, bf16[144,704]{1,0:T(8,128)(2,1)S(1)}, u32[]{:S(2)}, u32[]{:S(2)}) collective-permute-start(bf16[144,704]{1,0:T(8,128)(2,1)S(1)} %get-tuple-element.53), channel_id=1, source_target_pairs={{0,24},{8,16},{16,8},{24,0},{1,25},{9,17},{17,9},{25,1},{2,26},{10... | collective-permute-start | bytes 608264 | tf_op jit(solution)/shard_map/ppermute | solution.py:265
  37.7 4.6 %collective-permute-start.7 = (bf16[512,1024]{1,0:T(8,128)(2,1)S(1)}, bf16[512,1024]{1,0:T(8,128)(2,1)S(1)}, u32[]{:S(2)}, u32[]{:S(2)}) collective-permute-start(bf16[512,1024]{1,0:T(8,128)(2,1)S(1)} %mix_sibling.1), channel_id=1, source_target_pairs={{0,1},{1,0},{2,3},{3,2},{4,5},{5,4},{6,7},{7,6},{8,9},{9,8},{10,11... | collective-permute-start | bytes 3145736 | tf_op jit(solution)/shard_map/ppermute | solution.py:268
  42.3 8.4 %copy-start.1 = (bf16[144,704]{1,0:T(8,128)(2,1)S(1)}, bf16[144,704]{1,0:T(8,128)(2,1)}, u32[]{:S(2)}) copy-start(bf16[144,704]{1,0:T(8,128)(2,1)} %get-tuple-element.50.refs_0_) | copy-start | bytes 608260
  42.5 6.0 %collective-permute-start.8 = (bf16[128,512]{1,0:T(8,128)(2,1)S(1)}, bf16[128,512]{1,0:T(8,128)(2,1)S(1)}, u32[]{:S(2)}, u32[]{:S(2)}) collective-permute-start(bf16[128,512]{1,0:T(8,128)(2,1)S(1)} %get-tuple-element.46), channel_id=1, source_target_pairs={{0,8},{8,0},{16,24},{24,16},{1,9},{9,1},{17,25},{25,17},{2,10},{10... | collective-permute-start | bytes 393224 | tf_op jit(solution)/shard_map/ppermute | solution.py:265
  44.1 5.6 %collective-permute-start.9 = (bf16[128,512]{1,0:T(8,128)(2,1)S(1)}, bf16[128,512]{1,0:T(8,128)(2,1)S(1)}, u32[]{:S(2)}, u32[]{:S(2)}) collective-permute-start(bf16[128,512]{1,0:T(8,128)(2,1)S(1)} %get-tuple-element.47), channel_id=1, source_target_pairs={{0,16},{8,24},{16,0},{24,8},{1,17},{9,25},{17,1},{25,9},{2,18},{10... | collective-permute-start | bytes 393224 | tf_op jit(solution)/shard_map/ppermute | solution.py:265
  49.8 7.7 %collective-permute-start.10 = (bf16[128,1024]{1,0:T(8,128)(2,1)S(1)}, bf16[128,1024]{1,0:T(8,128)(2,1)S(1)}, u32[]{:S(2)}, u32[]{:S(2)}) collective-permute-start(bf16[128,1024]{1,0:T(8,128)(2,1)S(1)} %get-tuple-element.48), channel_id=1, source_target_pairs={{0,8},{8,0},{16,24},{24,16},{1,9},{9,1},{17,25},{25,17},{2,10},{10... | collective-permute-start | bytes 786440 | tf_op jit(solution)/shard_map/ppermute | solution.py:265
  50.4 7.4 %collective-permute-start.11 = (bf16[128,1024]{1,0:T(8,128)(2,1)S(1)}, bf16[128,1024]{1,0:T(8,128)(2,1)S(1)}, u32[]{:S(2)}, u32[]{:S(2)}) collective-permute-start(bf16[128,1024]{1,0:T(8,128)(2,1)S(1)} %get-tuple-element.49), channel_id=1, source_target_pairs={{0,16},{8,24},{16,0},{24,8},{1,17},{9,25},{17,1},{25,9},{2,18},{10... | collective-permute-start | bytes 786440 | tf_op jit(solution)/shard_map/ppermute | solution.py:265

commit v4 on v3

--- a/solution.py
+++ b/solution.py
@@ -87,6 +87,14 @@
     sent = dot(picks, jnp.concatenate([rows, number.astype(BF16)], axis=0), NT)
     for s, out in enumerate(outs):
         out[...] = sent[s * width : (s + 1) * width].astype(BF16)
+
+
+def load_kernel(w_in, w_ref):
+    local, ff, _ = w_in.shape
+    step = 64 if ff % 64 == 0 else ff
+    for l in range(local):
+        for i in range(0, ff, step):
+            w_ref[l, i : i + step, :] = w_in[l, i : i + step, :]
 
 
 def by_expert(rows, local, cap):
@@ -279,6 +287,11 @@
     )
     hid = [send(hid_sent[s], s) for s in range(n)]
     slot = shaped((width, ff))
+    if n == 4:
+        w_down, hid[0] = lax.optimization_barrier((w_down, hid[0]))
+        (w_down,) = run(
+            load_kernel, [shaped(w_down.shape)], [w_down], name="load"
+        )
 
     def taken(own, w_down):
         (x,) = run(

time: 58.9 us -> 58.5 us (level)
  waiting for transfers between devices: 16.4 us -> 12.6 us
  local copies, waits for them, and re-layouts: 1.12 us -> 3.75 us
  Pallas kernels: 19.4 us -> 20.2 us
    ppermute x13, waiting for transfers between devices: 13.5 us -> 9.54 us  [send(): return lax.ppermute(x, 'ctx', [(i, i ^ s) for i in range(n)]) if s else x]
    unnamed x4 -> x8, local copies, waits for them, and re-layouts: 1.12 us -> 3.75 us
    pallas_call x8 -> x9, Pallas kernels: 19.4 us -> 20.2 us  [call(): pl.pallas_call(kernel, out_shape=outs, in_specs=[pl.BlockSpec(memory_spac...]
  transfers between devices with their start and end apart: 15 -> 15, of which waited for: 8 -> 7; matrix products, arithmetic and copies ran while one was open for 1% -> 1% of each run, Pallas kernels for 33% -> 35%
where the time goes in v4:
time: 58.5 us; the launch traced here: 58.1 us
  Pallas kernels  20.2 us (35%)
  starting transfers between devices  17.7 us (30%)
  waiting for transfers between devices  12.6 us (22%)
  local copies, waits for them, and re-layouts  3.75 us (6%)
  other arithmetic  3.25 us (6%)
  between operations  0.71 us (1%)
    pallas_call x9, Pallas kernels, call(): pl.pallas_call(kernel, out_shape=outs, in_specs=[pl.BlockSpec(memory_spac...  20.2 us
    ppermute x13, starting transfers between devices, send(): return lax.ppermute(x, 'ctx', [(i, i ^ s) for i in range(n)]) if s else x  17.5 us
    ppermute x13, waiting for transfers between devices, send(): return lax.ppermute(x, 'ctx', [(i, i ^ s) for i in range(n)]) if s else x  9.54 us
    unnamed x8, local copies, waits for them, and re-layouts  3.75 us
    ppermute x2, waiting for transfers between devices, swap(): return lax.ppermute(x, 'tp', [(0, 1), (1, 0)])  3.02 us
  transfers between devices with their start and end apart: 15, of which 7 were waited for; matrix products, arithmetic and copies ran while one was open for 1% of the time, Pallas kernels for 35%

profile of v4, /device:TPU:0, one launch (start us, length us, event | category | flops | bytes accessed | tf_op | source)
XLA Modules:
  0.0 58.1 jit_solution(15901008309634331663)
XLA Ops:
  0.6 0.7 %bitcast_convert_fusion = bf16[4,128]{1,0:T(4,128)(2,1)S(1)} fusion(s32[128,4]{0,1:T(4,128)} %param.8), kind=kLoop, calls=%fused_computation.6 | loop fusion | flops 512 | bytes 3072 | tf_op jit(solution)/shard_map/convert_element_type | solution.py:280
  1.3 1.0 %fusion.1 = bf16[136,1024]{1,0:T(8,128)(2,1)S(1)} fusion(bf16[4,128]{1,0:T(4,128)(2,1)S(1)} %bitcast_convert_fusion, bf16[128,1024]{1,0:T(8,128)(2,1)} %param.10), kind=kLoop, calls=%fused_computation.3 | loop fusion | flops 835584 | bytes 541696 | tf_op jit(solution)/shard_map/concatenate | solution.py:281
  2.3 4.0 %collective-permute-start.3 = (bf16[136,1024]{1,0:T(8,128)(2,1)S(1)}, bf16[136,1024]{1,0:T(8,128)(2,1)S(1)}, u32[]{:S(2)}, u32[]{:S(2)}) collective-permute-start(bf16[136,1024]{1,0:T(8,128)(2,1)S(1)} %fusion.1), channel_id=1, source_target_pairs={{0,24},{8,16},{16,8},{24,0},{1,25},{9,17},{17,9},{25,1},{2,26},{10... | collective-permute-start | bytes 835592 | tf_op jit(solution)/shard_map/ppermute | solution.py:273
  6.2 0.5 collective-permute-start.2
  6.8 0.1 collective-permute-start.1
  6.9 0.7 %pad_add_fusion.meta_ref = s32[8,128]{1,0:T(8,128)S(1)} fusion(s32[4,128]{1,0:T(4,128)} %bitcast.9, s32[4,128]{1,0:T(4,128)} %bitcast.8), kind=kLoop, calls=%fused_computation.4 | loop fusion | flops 1024 | bytes 8192 | tf_op jit(solution)/shard_map/concatenate | solution.py:278
  7.6 0.1 pad_add_fusion.1.place
  7.7 1.1 %copy-done.1 = bf16[128,4,704]{0,2,1:T(8,128)(2,1)S(1)} copy-done((bf16[128,4,704]{0,2,1:T(8,128)(2,1)S(1)}, bf16[128,4,704]{0,2,1:T(8,128)(2,1)}, u32[]{:S(2)}) %copy-start.1) | copy-done | bytes 720920
  8.8 1.4 %dispatch.1 = (bf16[144,768]{1,0:T(8,128)(2,1)S(1)}, bf16[144,768]{1,0:T(8,128)(2,1)S(1)}, bf16[144,768]{1,0:T(8,128)(2,1)S(1)}, bf16[144,768]{1,0:T(8,128)(2,1)S(1)}) custom-call(s32[2]{0:T(128)S(1)} %pad_add_fusion.1.place, s32[8,128]{1,0:T(8,128)S(1)} %pad_add_fusion.meta_ref, bf16[4,704,128]{2,1,0:T(8,128)(2,1)S(1)} %bitcast.7), custom_call_target="tpu_custom_call" | custom-call | flops 1 | bytes 1 | tf_op jit(solution)/shard_map/dispatch/pallas_call | solution.py:240
  10.1 2.0 %collective-permute-start.4 = (bf16[144,768]{1,0:T(8,128)(2,1)S(1)}, bf16[144,768]{1,0:T(8,128)(2,1)S(1)}, u32[]{:S(2)}, u32[]{:S(2)}) collective-permute-start(bf16[144,768]{1,0:T(8,128)(2,1)S(1)} %get-tuple-element.44), channel_id=1, source_target_pairs={{0,8},{8,0},{16,24},{24,16},{1,9},{9,1},{17,25},{25,17},{2,10},{10... | collective-permute-start | bytes 663560 | tf_op jit(solution)/shard_map/ppermute | solution.py:273
  12.1 1.5 %collective-permute-start.5 = (bf16[144,768]{1,0:T(8,128)(2,1)S(1)}, bf16[144,768]{1,0:T(8,128)(2,1)S(1)}, u32[]{:S(2)}, u32[]{:S(2)}) collective-permute-start(bf16[144,768]{1,0:T(8,128)(2,1)S(1)} %get-tuple-element.45), channel_id=1, source_target_pairs={{0,16},{8,24},{16,0},{24,8},{1,17},{9,25},{17,1},{25,9},{2,18},{10... | collective-permute-start | bytes 663560 | tf_op jit(solution)/shard_map/ppermute | solution.py:273
  13.6 0.2 collective-permute-done.3
  13.8 2.9 %collective-permute-start.6 = (bf16[144,768]{1,0:T(8,128)(2,1)S(1)}, bf16[144,768]{1,0:T(8,128)(2,1)S(1)}, u32[]{:S(2)}, u32[]{:S(2)}) collective-permute-start(bf16[144,768]{1,0:T(8,128)(2,1)S(1)} %get-tuple-element.46), channel_id=1, source_target_pairs={{0,24},{8,16},{16,8},{24,0},{1,25},{9,17},{17,9},{25,1},{2,26},{10... | collective-permute-start | bytes 663560 | tf_op jit(solution)/shard_map/ppermute | solution.py:273
  16.7 2.6 %copy-done = bf16[2,704,2048]{2,1,0:T(8,128)(2,1)S(1)} copy-done((bf16[2,704,2048]{2,1,0:T(8,128)(2,1)S(1)}, bf16[2,704,2048]{2,1,0:T(8,128)(2,1)}, u32[]{:S(2)}) %copy-start) | copy-done | bytes 5767192
  19.3 2.9 %load.1.refs_4_ = bf16[2,704,2048]{2,1,0:T(8,128)(2,1)} custom-call(bf16[2,704,2048]{2,1,0:T(8,128)(2,1)S(1)} %copy-done), custom_call_target="tpu_custom_call" | custom-call | flops 1 | bytes 1 | tf_op jit(solution)/shard_map/load/pallas_call | solution.py:240
  22.2 0.0 collective-permute-done.2
  22.2 0.0 collective-permute-done.1
  22.2 9.4 %conditional.1 = ((bf16[144,704]{1,0:T(8,128)(2,1)}, bf16[144,704]{1,0:T(8,128)(2,1)S(1)}, bf16[144,704]{1,0:T(8,128)(2,1)S(1)}, bf16[144,704]{1,0:T(8,128)(2,1)S(1)})) conditional(s32[]{:T(128)} %convert_element_type.17, () %tuple.18, (s32[2]{0:T(128)S(1)}, bf16[136,1024]{1,0:T(8,128)(2,1)S(1)}, bf16[136,1024]{1,0:T(8,128)(2,1)S(1)}, ...), branch_computations={%region_0.1_spmd, %region_1.2_spmd} | conditional | flops 2 | bytes 4718642 | solution.py:309
  22.2 1.1 %gather.1.x_ref = bf16[2,288,1024]{2,1,0:T(8,128)(2,1)S(1)} custom-call(s32[2]{0:T(128)S(1)} %get-tuple-element.12.place, bf16[136,1024]{1,0:T(8,128)(2,1)S(1)} %get-tuple-element.13.refs_0_, bf16[136,1024]{1,0:T(8,128)(2,1)S(1)} %get-tuple-element.14.refs_1_, bf16[136,1024]{1,0:T(8,128)(2,1)S(1)} %get-tuple-element.15.refs_2_, ...), custom_call_target="tpu_custom_call" | custom-call | flops 1 | bytes 1 | tf_op jit(solution)/shard_map/cond/branch_1_fun/gather/pallas_call | solution.py:240
  23.3 0.1 collective-permute-start
  23.4 2.8 %collective-permute-done.x_other = bf16[2,288,1024]{2,1,0:T(8,128)(2,1)S(1)} collective-permute-done((bf16[2,288,1024]{2,1,0:T(8,128)(2,1)S(1)}, bf16[2,288,1024]{2,1,0:T(8,128)(2,1)S(1)}, u32[]{:S(2)}, u32[]{:S(2)}) %collective-permute-start) | collective-permute-done | bytes 1179680 | tf_op jit(solution)/shard_map/cond/branch_1_fun/ppermute | solution.py:276
  26.2 5.3 %grad.1 = (bf16[144,704]{1,0:T(8,128)(2,1)}, bf16[144,704]{1,0:T(8,128)(2,1)S(1)}, bf16[144,704]{1,0:T(8,128)(2,1)S(1)}, bf16[144,704]{1,0:T(8,128)(2,1)S(1)}) custom-call(s32[2]{0:T(128)S(1)} %get-tuple-element.12.place, bf16[2,288,1024]{2,1,0:T(8,128)(2,1)S(1)} %gather.1.x_ref, bf16[2,288,1024]{2,1,0:T(8,128)(2,1)S(1)} %collective-permute-done.x_other, ...), custom_call_target="tpu_custom_call" | custom-call | flops 1 | bytes 1 | tf_op jit(solution)/shard_map/cond/branch_1_fun/grad/pallas_call | solution.py:240
  31.5 0.6 collective-permute-start.12
  32.1 0.0 collective-permute-start.13
  32.1 0.0 collective-permute-done.4.refs_1_
  32.1 2.9 %collective-permute-start.14 = (bf16[144,704]{1,0:T(8,128)(2,1)S(1)}, bf16[144,704]{1,0:T(8,128)(2,1)S(1)}, u32[]{:S(2)}, u32[]{:S(2)}) collective-permute-start(bf16[144,704]{1,0:T(8,128)(2,1)S(1)} %get-tuple-element.57), channel_id=1, source_target_pairs={{0,24},{8,16},{16,8},{24,0},{1,25},{9,17},{17,9},{25,1},{2,26},{10... | collective-permute-start | bytes 608264 | tf_op jit(solution)/shard_map/ppermute | solution.py:273
  35.0 0.0 collective-permute-done.5.refs_2_
  35.0 0.0 collective-permute-done.6.refs_3_
  35.0 4.5 %mix_sibling.1 = bf16[512,1024]{1,0:T(8,128)(2,1)S(1)} custom-call(s32[2]{0:T(128)S(1)} %pad_add_fusion.1.place, bf16[144,768]{1,0:T(8,128)(2,1)S(1)} %get-tuple-element.43.refs_0_, bf16[144,768]{1,0:T(8,128)(2,1)S(1)} %collective-permute-done.4.refs_1_, bf16[144,768]{1,0:T(8,128)(2,1)S(1)} %collective-permute-done.5.refs_2_, ...), custom_call_target="tpu_custom_call" | custom-call | flops 1 | bytes 1 | tf_op jit(solution)/shard_map/mix_sibling/pallas_call | solution.py:240
  39.6 0.1 collective-permute-start.7
  39.7 2.4 %mix_own.1.own = f32[512,1024]{1,0:T(8,128)S(1)} custom-call(s32[2]{0:T(128)S(1)} %pad_add_fusion.1.place, bf16[144,768]{1,0:T(8,128)(2,1)S(1)} %get-tuple-element.43.refs_0_, bf16[144,768]{1,0:T(8,128)(2,1)S(1)} %collective-permute-done.4.refs_1_, bf16[144,768]{1,0:T(8,128)(2,1)S(1)} %collective-permute-done.5.refs_2_, ...), custom_call_target="tpu_custom_call" | custom-call | flops 99999997952 | bytes 1 | tf_op jit(solution)/shard_map/mix_own/pallas_call | solution.py:240
  42.1 0.0 copy-start.3
  42.1 0.2 collective-permute-done.7.arrived
  42.3 0.2 add.17
  42.5 0.8 %collective-permute-start.8 = (bf16[128,512]{1,0:T(8,128)(2,1)S(1)}, bf16[128,512]{1,0:T(8,128)(2,1)S(1)}, u32[]{:S(2)}, u32[]{:S(2)}) collective-permute-start(bf16[128,512]{1,0:T(8,128)(2,1)S(1)} %get-tuple-element.50), channel_id=1, source_target_pairs={{0,8},{8,0},{16,24},{24,16},{1,9},{9,1},{17,25},{25,17},{2,10},{10... | collective-permute-start | bytes 393224 | tf_op jit(solution)/shard_map/ppermute | solution.py:273
  43.3 0.1 collective-permute-start.9
  43.4 4.9 %collective-permute-done.8.low = bf16[128,512]{1,0:T(8,128)(2,1)S(1)} collective-permute-done((bf16[128,512]{1,0:T(8,128)(2,1)S(1)}, bf16[128,512]{1,0:T(8,128)(2,1)S(1)}, u32[]{:S(2)}, u32[]{:S(2)}) %collective-permute-start.8) | collective-permute-done | bytes 131104 | tf_op jit(solution)/shard_map/ppermute | solution.py:273
  48.3 0.5 collective-permute-done.9.high
  48.8 0.1 join.1
  48.8 1.3 %collective-permute-start.10 = (bf16[128,1024]{1,0:T(8,128)(2,1)S(1)}, bf16[128,1024]{1,0:T(8,128)(2,1)S(1)}, u32[]{:S(2)}, u32[]{:S(2)}) collective-permute-start(bf16[128,1024]{1,0:T(8,128)(2,1)S(1)} %get-tuple-element.52), channel_id=1, source_target_pairs={{0,8},{8,0},{16,24},{24,16},{1,9},{9,1},{17,25},{25,17},{2,10},{10... | collective-permute-start | bytes 786440 | tf_op jit(solution)/shard_map/ppermute | solution.py:273
  50.2 0.8 %collective-permute-start.11 = (bf16[128,1024]{1,0:T(8,128)(2,1)S(1)}, bf16[128,1024]{1,0:T(8,128)(2,1)S(1)}, u32[]{:S(2)}, u32[]{:S(2)}) collective-permute-start(bf16[128,1024]{1,0:T(8,128)(2,1)S(1)} %get-tuple-element.53), channel_id=1, source_target_pairs={{0,16},{8,24},{16,0},{24,8},{1,17},{9,25},{17,1},{25,9},{2,18},{10... | collective-permute-start | bytes 786440 | tf_op jit(solution)/shard_map/ppermute | solution.py:273
  51.0 0.0 collective-permute-done.12.refs_1_
  51.0 0.0 collective-permute-done.13.refs_2_
  51.0 0.0 collective-permute-done.14.refs_3_
  51.0 2.3 %restore.1 = bf16[4,704,128]{2,1,0:T(8,128)(2,1)} custom-call(s32[2]{0:T(128)S(1)} %pad_add_fusion.1.place, s32[8,128]{1,0:T(8,128)S(1)} %pad_add_fusion.meta_ref, bf16[144,704]{1,0:T(8,128)(2,1)S(1)} %copy-done.3, bf16[144,704]{1,0:T(8,128)(2,1)S(1)} %collective-permute-done.12.refs_1_, bf16[144,704]{1,0:T(8,128)(2,1)S(1)} %collective-permute-done.13.refs_2_, ...), custom_call_target="tpu_custom_call" | custom-call | flops 99999997952 | bytes 1 | tf_op jit(solution)/shard_map/restore/pallas_call | solution.py:240
  53.3 3.0 %collective-permute-done.10 = bf16[128,1024]{1,0:T(8,128)(2,1)S(1)} collective-permute-done((bf16[128,1024]{1,0:T(8,128)(2,1)S(1)}, bf16[128,1024]{1,0:T(8,128)(2,1)S(1)}, u32[]{:S(2)}, u32[]{:S(2)}) %collective-permute-start.10) | collective-permute-done | bytes 262176 | tf_op jit(solution)/shard_map/ppermute | solution.py:273
  56.3 1.0 %collective-permute-done.11 = bf16[128,1024]{1,0:T(8,128)(2,1)S(1)} collective-permute-done((bf16[128,1024]{1,0:T(8,128)(2,1)S(1)}, bf16[128,1024]{1,0:T(8,128)(2,1)S(1)}, u32[]{:S(2)}, u32[]{:S(2)}) %collective-permute-start.11) | collective-permute-done | bytes 262176 | tf_op jit(solution)/shard_map/ppermute | solution.py:273
  57.3 0.8 %add_convert_fusion = bf16[128,1024]{1,0:T(8,128)(2,1)} fusion(bf16[128,1024]{1,0:T(8,128)(2,1)S(1)} %collective-permute-done.11, f32[128,1024]{1,0:T(8,128)S(1)} %get-tuple-element.47, bf16[128,1024]{1,0:T(8,128)(2,1)S(1)} %collective-permute-done.10), kind=kLoop, calls=%fused_computation.2 | loop fusion | flops 655360 | bytes 1310720 | tf_op jit(solution)/shard_map/convert_element_type | solution.py:347
  (5 shorter events, 0.0 us)
Async XLA Ops:
  2.3 11.5 %collective-permute-start.3 = (bf16[136,1024]{1,0:T(8,128)(2,1)S(1)}, bf16[136,1024]{1,0:T(8,128)(2,1)S(1)}, u32[]{:S(2)}, u32[]{:S(2)}) collective-permute-start(bf16[136,1024]{1,0:T(8,128)(2,1)S(1)} %fusion.1), channel_id=1, source_target_pairs={{0,24},{8,16},{16,8},{24,0},{1,25},{9,17},{17,9},{25,1},{2,26},{10... | collective-permute-start | bytes 835592 | tf_op jit(solution)/shard_map/ppermute | solution.py:273
  6.2 15.9 %collective-permute-start.2 = (bf16[136,1024]{1,0:T(8,128)(2,1)S(1)}, bf16[136,1024]{1,0:T(8,128)(2,1)S(1)}, u32[]{:S(2)}, u32[]{:S(2)}) collective-permute-start(bf16[136,1024]{1,0:T(8,128)(2,1)S(1)} %fusion.1), channel_id=1, source_target_pairs={{0,16},{8,24},{16,0},{24,8},{1,17},{9,25},{17,1},{25,9},{2,18},{10... | collective-permute-start | bytes 835592 | tf_op jit(solution)/shard_map/ppermute | solution.py:273
  6.8 15.4 %collective-permute-start.1 = (bf16[136,1024]{1,0:T(8,128)(2,1)S(1)}, bf16[136,1024]{1,0:T(8,128)(2,1)S(1)}, u32[]{:S(2)}, u32[]{:S(2)}) collective-permute-start(bf16[136,1024]{1,0:T(8,128)(2,1)S(1)} %fusion.1), channel_id=1, source_target_pairs={{0,8},{8,0},{16,24},{24,16},{1,9},{9,1},{17,25},{25,17},{2,10},{10... | collective-permute-start | bytes 835592 | tf_op jit(solution)/shard_map/ppermute | solution.py:273
  7.7 1.1 %copy-start.1 = (bf16[128,4,704]{0,2,1:T(8,128)(2,1)S(1)}, bf16[128,4,704]{0,2,1:T(8,128)(2,1)}, u32[]{:S(2)}) copy-start(bf16[128,4,704]{0,2,1:T(8,128)(2,1)} %param.7) | copy-start | bytes 2162692
  10.1 22.0 %collective-permute-start.4 = (bf16[144,768]{1,0:T(8,128)(2,1)S(1)}, bf16[144,768]{1,0:T(8,128)(2,1)S(1)}, u32[]{:S(2)}, u32[]{:S(2)}) collective-permute-start(bf16[144,768]{1,0:T(8,128)(2,1)S(1)} %get-tuple-element.44), channel_id=1, source_target_pairs={{0,8},{8,0},{16,24},{24,16},{1,9},{9,1},{17,25},{25,17},{2,10},{10... | collective-permute-start | bytes 663560 | tf_op jit(solution)/shard_map/ppermute | solution.py:273
  12.1 22.9 %collective-permute-start.5 = (bf16[144,768]{1,0:T(8,128)(2,1)S(1)}, bf16[144,768]{1,0:T(8,128)(2,1)S(1)}, u32[]{:S(2)}, u32[]{:S(2)}) collective-permute-start(bf16[144,768]{1,0:T(8,128)(2,1)S(1)} %get-tuple-element.45), channel_id=1, source_target_pairs={{0,16},{8,24},{16,0},{24,8},{1,17},{9,25},{17,1},{25,9},{2,18},{10... | collective-permute-start | bytes 663560 | tf_op jit(solution)/shard_map/ppermute | solution.py:273
  13.8 21.3 %collective-permute-start.6 = (bf16[144,768]{1,0:T(8,128)(2,1)S(1)}, bf16[144,768]{1,0:T(8,128)(2,1)S(1)}, u32[]{:S(2)}, u32[]{:S(2)}) collective-permute-start(bf16[144,768]{1,0:T(8,128)(2,1)S(1)} %get-tuple-element.46), channel_id=1, source_target_pairs={{0,24},{8,16},{16,8},{24,0},{1,25},{9,17},{17,9},{25,1},{2,26},{10... | collective-permute-start | bytes 663560 | tf_op jit(solution)/shard_map/ppermute | solution.py:273
  16.7 2.6 %copy-start = (bf16[2,704,2048]{2,1,0:T(8,128)(2,1)S(1)}, bf16[2,704,2048]{2,1,0:T(8,128)(2,1)}, u32[]{:S(2)}) copy-start(bf16[2,704,2048]{2,1,0:T(8,128)(2,1)} %w_in) | copy-start | bytes 17301508
  23.3 2.9 %collective-permute-start = (bf16[2,288,1024]{2,1,0:T(8,128)(2,1)S(1)}, bf16[2,288,1024]{2,1,0:T(8,128)(2,1)S(1)}, u32[]{:S(2)}, u32[]{:S(2)}) collective-permute-start(bf16[2,288,1024]{2,1,0:T(8,128)(2,1)S(1)} %gather.1.x_ref), channel_id=1, source_target_pairs={{0,1},{1,0},{2,3},{3,2},{4,5},{5,4},{6,7},{7,6},{8,9},{9,8},{10,11... | collective-permute-start | bytes 3538952 | tf_op jit(solution)/shard_map/cond/branch_1_fun/ppermute | solution.py:276
  31.5 19.4 %collective-permute-start.12 = (bf16[144,704]{1,0:T(8,128)(2,1)S(1)}, bf16[144,704]{1,0:T(8,128)(2,1)S(1)}, u32[]{:S(2)}, u32[]{:S(2)}) collective-permute-start(bf16[144,704]{1,0:T(8,128)(2,1)S(1)} %get-tuple-element.55), channel_id=1, source_target_pairs={{0,8},{8,0},{16,24},{24,16},{1,9},{9,1},{17,25},{25,17},{2,10},{10... | collective-permute-start | bytes 608264 | tf_op jit(solution)/shard_map/ppermute | solution.py:273
  32.1 18.8 %collective-permute-start.13 = (bf16[144,704]{1,0:T(8,128)(2,1)S(1)}, bf16[144,704]{1,0:T(8,128)(2,1)S(1)}, u32[]{:S(2)}, u32[]{:S(2)}) collective-permute-start(bf16[144,704]{1,0:T(8,128)(2,1)S(1)} %get-tuple-element.56), channel_id=1, source_target_pairs={{0,16},{8,24},{16,0},{24,8},{1,17},{9,25},{17,1},{25,9},{2,18},{10... | collective-permute-start | bytes 608264 | tf_op jit(solution)/shard_map/ppermute | solution.py:273
  32.1 7.6 %copy-start.2 = (bf16[2,704,2048]{2,1,0:T(8,128)(2,1)S(1)}, bf16[2,704,2048]{2,1,0:T(8,128)(2,1)}, u32[]{:S(2)}) copy-start(bf16[2,704,2048]{2,1,0:T(8,128)(2,1)} %load.1.refs_4_) | copy-start | bytes 17301508
  32.1 18.8 %collective-permute-start.14 = (bf16[144,704]{1,0:T(8,128)(2,1)S(1)}, bf16[144,704]{1,0:T(8,128)(2,1)S(1)}, u32[]{:S(2)}, u32[]{:S(2)}) collective-permute-start(bf16[144,704]{1,0:T(8,128)(2,1)S(1)} %get-tuple-element.57), channel_id=1, source_target_pairs={{0,24},{8,16},{16,8},{24,0},{1,25},{9,17},{17,9},{25,1},{2,26},{10... | collective-permute-start | bytes 608264 | tf_op jit(solution)/shard_map/ppermute | solution.py:273
  39.6 2.7 %collective-permute-start.7 = (bf16[512,1024]{1,0:T(8,128)(2,1)S(1)}, bf16[512,1024]{1,0:T(8,128)(2,1)S(1)}, u32[]{:S(2)}, u32[]{:S(2)}) collective-permute-start(bf16[512,1024]{1,0:T(8,128)(2,1)S(1)} %mix_sibling.1), channel_id=1, source_target_pairs={{0,1},{1,0},{2,3},{3,2},{4,5},{5,4},{6,7},{7,6},{8,9},{9,8},{10,11... | collective-permute-start | bytes 3145736 | tf_op jit(solution)/shard_map/ppermute | solution.py:276
  42.1 8.8 %copy-start.3 = (bf16[144,704]{1,0:T(8,128)(2,1)S(1)}, bf16[144,704]{1,0:T(8,128)(2,1)}, u32[]{:S(2)}) copy-start(bf16[144,704]{1,0:T(8,128)(2,1)} %get-tuple-element.54.refs_0_) | copy-start | bytes 608260
  42.5 5.8 %collective-permute-start.8 = (bf16[128,512]{1,0:T(8,128)(2,1)S(1)}, bf16[128,512]{1,0:T(8,128)(2,1)S(1)}, u32[]{:S(2)}, u32[]{:S(2)}) collective-permute-start(bf16[128,512]{1,0:T(8,128)(2,1)S(1)} %get-tuple-element.50), channel_id=1, source_target_pairs={{0,8},{8,0},{16,24},{24,16},{1,9},{9,1},{17,25},{25,17},{2,10},{10... | collective-permute-start | bytes 393224 | tf_op jit(solution)/shard_map/ppermute | solution.py:273
  43.3 5.4 %collective-permute-start.9 = (bf16[128,512]{1,0:T(8,128)(2,1)S(1)}, bf16[128,512]{1,0:T(8,128)(2,1)S(1)}, u32[]{:S(2)}, u32[]{:S(2)}) collective-permute-start(bf16[128,512]{1,0:T(8,128)(2,1)S(1)} %get-tuple-element.51), channel_id=1, source_target_pairs={{0,16},{8,24},{16,0},{24,8},{1,17},{9,25},{17,1},{25,9},{2,18},{10... | collective-permute-start | bytes 393224 | tf_op jit(solution)/shard_map/ppermute | solution.py:273
  48.8 7.5 %collective-permute-start.10 = (bf16[128,1024]{1,0:T(8,128)(2,1)S(1)}, bf16[128,1024]{1,0:T(8,128)(2,1)S(1)}, u32[]{:S(2)}, u32[]{:S(2)}) collective-permute-start(bf16[128,1024]{1,0:T(8,128)(2,1)S(1)} %get-tuple-element.52), channel_id=1, source_target_pairs={{0,8},{8,0},{16,24},{24,16},{1,9},{9,1},{17,25},{25,17},{2,10},{10... | collective-permute-start | bytes 786440 | tf_op jit(solution)/shard_map/ppermute | solution.py:273
  50.2 7.1 %collective-permute-start.11 = (bf16[128,1024]{1,0:T(8,128)(2,1)S(1)}, bf16[128,1024]{1,0:T(8,128)(2,1)S(1)}, u32[]{:S(2)}, u32[]{:S(2)}) collective-permute-start(bf16[128,1024]{1,0:T(8,128)(2,1)S(1)} %get-tuple-element.53), channel_id=1, source_target_pairs={{0,16},{8,24},{16,0},{24,8},{1,17},{9,25},{17,1},{25,9},{2,18},{10... | collective-permute-start | bytes 786440 | tf_op jit(solution)/shard_map/ppermute | solution.py:273

commit v5 on v3

--- a/solution.py
+++ b/solution.py
@@ -137,24 +137,49 @@
             x_ref[l, :, c : c + chunk] = x.astype(BF16)
 
 
-def grad_kernel(dims, place, x_ref, x_other, w_ref, *outs):
-    experts, local, cap, width = dims
+def pieces_of(size, step):
+    return [(i, min(step, size - i)) for i in range(0, size, step)]
+
+
+def grad_kernel(dims, place, x_ref, x_other, w_hbm, *refs):
+    experts, local, cap, width = dims
+    outs, (w_ref, g_ref, sems) = refs[:-3], refs[-3:]
     half = x_ref.shape[2]
+    pieces = [(l, i, *at) for l in range(local) for i, at in enumerate(pieces_of(w_ref.shape[1], 256))]
+
+    def copy(l, i, start, size):
+        rows = pl.ds(start, size)
+        return pltpu.make_async_copy(w_hbm.at[l, rows], w_ref.at[l, rows], sems.at[l, i])
+
+    for piece in pieces:
+        copy(*piece).start()
     mine = pl.ds(pl.multiple_of(place[1] * half, half), half)
     theirs = pl.ds(pl.multiple_of((1 - place[1]) * half, half), half)
-    grads = [
-        dot(x_ref[l], w_ref[l, :, mine], NT) + dot(x_other[l], w_ref[l, :, theirs], NT)
-        for l in range(local)
-    ]
+    for l, i, start, size in pieces:
+        copy(l, i, start, size).wait()
+        rows = pl.ds(start, size)
+        grads = dot(x_ref[l], w_ref[l, rows, mine], NT)
+        grads = grads + dot(x_other[l], w_ref[l, rows, theirs], NT)
+        g_ref[l, :, start : start + size] = grads
+    grads = [g_ref[l] for l in range(local)]
     for s, rows in enumerate(by_source(grads, len(outs), cap)):
         outs[s][...] = rows.astype(BF16)
 
 
-def mix_rows(dims, side, hid, w_ref, tokens, half, store):
+def mix_rows(dims, side, hid, w_hbm, w_ref, sems, tokens, half, store):
     experts, local, cap, width = dims
     n = len(hid)
     ff = w_ref.shape[1]
-    chunk = min(half, 256)
+    pieces = pieces_of(half, 256)
+
+    def copy(i, start, size):
+        source = pl.ds(pl.multiple_of(side * half + start, size), size)
+        return pltpu.make_async_copy(
+            w_hbm.at[:, :, source], w_ref.at[:, :, pl.ds(start, size)], sems.at[i]
+        )
+
+    for i, (start, size) in enumerate(pieces):
+        copy(i, start, size).start()
     same = ones_where(iota((tokens, tokens), 0) == iota((tokens, tokens), 1))
     held = []
     for h in hid:
@@ -163,54 +188,63 @@
         held.append(dot(same, slots, NT).astype(BF16))
     rows = [h[:, :ff].astype(F32) for h in hid]
     x = [r.astype(BF16) for r in by_expert(rows, local, cap)]
-    for c in range(0, half, chunk):
-        at = pl.ds(pl.multiple_of(side * half + c, chunk), chunk)
-        out = [dot(x[l], w_ref[l, :, at], NN) for l in range(local)]
+    for i, (start, size) in enumerate(pieces):
+        copy(i, start, size).wait()
+        columns = pl.ds(start, size)
+        out = [dot(x[l], w_ref[l, :, columns], NN) for l in range(local)]
         for s, rows in enumerate(by_source(out, n, cap)):
-            store(s, slice(c, c + chunk), dot(held[s], rows.astype(BF16), NN))
+            store(s, slice(start, start + size), dot(held[s], rows.astype(BF16), NN))
 
 
 def mix_kernel(dims, sibling, place, *refs):
-    hid, (w_ref, out) = refs[:-2], refs[-2:]
+    hid, (w_hbm, out, w_ref, sems) = refs[:-4], refs[-4:]
     tokens = out.shape[0] // len(hid)
 
     def store(s, columns, part):
         out[pl.ds(s * tokens, tokens), columns] = part.astype(out.dtype)
 
     side = 1 - place[1] if sibling else place[1]
-    mix_rows(dims, side, hid, w_ref, tokens, out.shape[1], store)
+    mix_rows(dims, side, hid, w_hbm, w_ref, sems, tokens, out.shape[1], store)
 
 
 def mix_add_kernel(dims, place, *refs):
-    n = (len(refs) - 2) // 2
-    hid, (w_ref, arrived), outs = refs[:n], refs[n : n + 2], refs[n + 2 :]
+    n = (len(refs) - 4) // 2
+    hid, (w_hbm, arrived), outs = refs[:n], refs[n : n + 2], refs[n + 2 : -2]
     tokens, half = outs[0].shape
 
     def store(s, columns, part):
         theirs = arrived[pl.ds(s * tokens, tokens), columns].astype(F32)
         outs[s][:, columns] = (part + theirs).astype(BF16)
 
-    mix_rows(dims, place[1], hid, w_ref, tokens, half, store)
-
-
-def add_split_kernel(own, arrived, mine, one, two, low, high):
+    mix_rows(dims, place[1], hid, w_hbm, refs[-2], refs[-1], tokens, half, store)
+
+
+def add_split_kernel(own, arrived, mine, one_low, one_high, two_low, two_high, low, high):
     tokens, half = mine.shape
     cut = half // 2
-    for s, out in enumerate((mine, one, two)):
+    parts = []
+    for s in range(4):
         at = pl.ds(s * tokens, tokens)
-        out[...] = own[at, :] + arrived[at, :].astype(F32)
-    at = pl.ds(3 * tokens, tokens)
-    far = own[at, :] + arrived[at, :].astype(F32)
-    low[...] = far[:, :cut].astype(BF16)
-    high[...] = far[:, cut:].astype(BF16)
-
-
-def join_kernel(one, two, low, high, to_one, to_two):
-    cut = one.shape[1] // 2
-    to_one[:, :cut] = one[:, :cut].astype(BF16)
-    to_one[:, cut:] = (one[:, cut:] + high[...].astype(F32)).astype(BF16)
-    to_two[:, :cut] = (two[:, :cut] + low[...].astype(F32)).astype(BF16)
-    to_two[:, cut:] = two[:, cut:].astype(BF16)
+        parts.append(own[at, :] + arrived[at, :].astype(F32))
+    mine[...] = parts[0]
+    one_low[...] = parts[1][:, :cut].astype(BF16)
+    one_high[...] = parts[1][:, cut:]
+    two_low[...] = parts[2][:, :cut]
+    two_high[...] = parts[2][:, cut:].astype(BF16)
+    low[...] = parts[3][:, :cut].astype(BF16)
+    high[...] = parts[3][:, cut:].astype(BF16)
+
+
+def join_kernel(one_high, two_low, low, high, to_one, to_two):
+    to_one[...] = (one_high[...] + high[...].astype(F32)).astype(BF16)
+    to_two[...] = (two_low[...] + low[...].astype(F32)).astype(BF16)
+
+
+def finish_kernel(mine, one_low, one_high, two_low, two_high, out):
+    cut = one_low.shape[1]
+    for at, one, two in ((0, one_low, two_low), (cut, one_high, two_high)):
+        total = mine[:, at : at + cut] + one[...].astype(F32) + two[...].astype(F32)
+        out[:, at : at + cut] = total.astype(BF16)
 
 
 def restore_kernel(dims, place, meta_ref, *refs):
@@ -287,7 +321,13 @@
         )
         return list(run(
             functools.partial(grad_kernel, dims), [slot] * n,
-            [place, x, swap(x), w_down], where=placed, name="grad",
+            [place, x, swap(x), w_down], where={**placed, 3: pl.ANY},
+            scratch=[
+                pltpu.VMEM(w_down.shape, BF16),
+                pltpu.VMEM((local, n * cap, ff), F32),
+                pltpu.SemaphoreType.DMA((local, len(pieces_of(ff, 256)))),
+            ],
+            name="grad",
         ))
 
     def skipped(own, w_down):
@@ -299,39 +339,53 @@
     hid[0], grad_own = lax.optimization_barrier((hid[0], grad_sent[0]))
     grad_back = [grad_own] + [send(grad_sent[s], s) for s in range(1, n)]
 
+    mixing = dict(
+        where={**placed, n + 1: pl.ANY},
+        scratch=[
+            pltpu.VMEM((local, ff, half), BF16),
+            pltpu.SemaphoreType.DMA((len(pieces_of(half, 256)),)),
+        ],
+    )
     (theirs,) = run(
         functools.partial(mix_kernel, dims, True), [shaped((n * tokens, half))],
-        [place, *hid, w_down], where=placed, name="mix_sibling",
+        [place, *hid, w_down], name="mix_sibling", **mixing,
     )
     arrived = swap(theirs)
     if forward:
         (mine,) = run(
             functools.partial(mix_kernel, dims, False), [shaped((n * tokens, half), F32)],
-            [place, *hid, w_down], where=placed, name="mix_own", weight=BIG,
+            [place, *hid, w_down], name="mix_own", weight=BIG, **mixing,
         )
         cut = half // 2
-        block, piece = shaped((tokens, half), F32), shaped((tokens, cut))
-        kept, one, two, one_low, two_high = run(
-            add_split_kernel, [block] * 3 + [piece] * 2, [mine, arrived], name="add"
+        kept, wide = shaped((tokens, half), F32), shaped((tokens, cut), F32)
+        piece = shaped((tokens, cut))
+        kept, one_low, one_high, two_low, two_high, low, high = run(
+            add_split_kernel, [kept, piece, wide, wide, piece, piece, piece],
+            [mine, arrived], name="add",
+        )
+        low, high = send(low, 1), send(high, 2)
+        one_low, two_high, *grad_back[1:3] = lax.optimization_barrier(
+            (one_low, two_high, *grad_back[1:3])
         )
         one_low, two_high = send(one_low, 1), send(two_high, 2)
         to_one, to_two = run(
-            join_kernel, [shaped((tokens, half))] * 2, [one, two, one_low, two_high],
-            name="join",
-        )
-        parts = [kept, send(to_one, 1), send(to_two, 2)]
+            join_kernel, [piece] * 2, [one_high, two_low, low, high], name="join"
+        )
+        (mixed,) = run(
+            finish_kernel, [shaped((tokens, half))],
+            [kept, one_low, send(to_one, 1), send(to_two, 2), two_high], name="finish",
+        )
     else:
         sums = run(
             functools.partial(mix_add_kernel, dims), [shaped((tokens, half))] * n,
-            [place, *hid, w_down, arrived], where=placed, name="mix_own",
-        )
-        parts = [send(sums[s], s) for s in range(n)]
+            [place, *hid, w_down, arrived], name="mix_own", **mixing,
+        )
+        mixed = sum(send(sums[s], s).astype(F32) for s in range(n)).astype(BF16)
 
     (grad_t,) = run(
         functools.partial(restore_kernel, dims), [shaped((top, ff, tokens))],
         [place, meta, *grad_back], where=placed, name="restore", weight=BIG,
     )
-    mixed = sum(x.astype(F32) for x in parts).astype(BF16)
     return mixed, grad_t.transpose(2, 0, 1)
 
 

time: 58.9 us -> 57.3 us (0.973)
  waiting for transfers between devices: 16.4 us -> 13 us
  starting transfers between devices: 17.7 us -> 19.5 us
  Pallas kernels: 19.4 us -> 20.3 us
  other arithmetic: 3.25 us -> 2.44 us
    ppermute x13 -> x15, waiting for transfers between devices: 13.5 us -> 10.1 us  [send(): return lax.ppermute(x, 'ctx', [(i, i ^ s) for i in range(n)]) if s else x]
    ppermute x13 -> x15, starting transfers between devices: 17.5 us -> 19.4 us  [send(): return lax.ppermute(x, 'ctx', [(i, i ^ s) for i in range(n)]) if s else x]
    pallas_call x8 -> x9, Pallas kernels: 19.4 us -> 20.3 us  [call(): pl.pallas_call(kernel, out_shape=outs, in_specs=[pl.BlockSpec(memory_spac...]
    convert_element_type x1 -> x0, other arithmetic: 0.81 us -> none  [body(): mixed = sum((x.astype(F32) for x in parts)).astype(BF16)]
  transfers between devices with their start and end apart: 15 -> 17, of which waited for: 8 -> 8; matrix products, arithmetic and copies ran while one was open for 1% -> 1% of each run, Pallas kernels for 33% -> 34%
where the time goes in v5:
time: 57.3 us; the launch traced here: 57 us
  Pallas kernels  20.3 us (35%)
  starting transfers between devices  19.5 us (34%)
  waiting for transfers between devices  13 us (23%)
  other arithmetic  2.44 us (4%)
  local copies, waits for them, and re-layouts  1.11 us (2%)
  between operations  0.7 us (1%)
    pallas_call x9, Pallas kernels, call(): pl.pallas_call(kernel, out_shape=outs, in_specs=[pl.BlockSpec(memory_spac...  20.3 us
    ppermute x15, starting transfers between devices, send(): return lax.ppermute(x, 'ctx', [(i, i ^ s) for i in range(n)]) if s else x  19.4 us
    ppermute x15, waiting for transfers between devices, send(): return lax.ppermute(x, 'ctx', [(i, i ^ s) for i in range(n)]) if s else x  10.1 us
    ppermute x2, waiting for transfers between devices, swap(): return lax.ppermute(x, 'tp', [(0, 1), (1, 0)])  2.84 us
  transfers between devices with their start and end apart: 17, of which 8 were waited for; matrix products, arithmetic and copies ran while one was open for 1% of the time, Pallas kernels for 34%

profile of v5, /device:TPU:0, one launch (start us, length us, event | category | flops | bytes accessed | tf_op | source)
XLA Modules:
  0.0 57.0 jit_solution(13660105150115924750)
XLA Ops:
  0.6 0.7 %bitcast_convert_fusion = bf16[4,128]{1,0:T(4,128)(2,1)S(1)} fusion(s32[128,4]{0,1:T(4,128)} %param.8), kind=kLoop, calls=%fused_computation.5 | loop fusion | flops 512 | bytes 3072 | tf_op jit(solution)/shard_map/convert_element_type | solution.py:306
  1.3 1.0 %fusion.1 = bf16[136,1024]{1,0:T(8,128)(2,1)S(1)} fusion(bf16[4,128]{1,0:T(4,128)(2,1)S(1)} %bitcast_convert_fusion, bf16[128,1024]{1,0:T(8,128)(2,1)} %param.10), kind=kLoop, calls=%fused_computation.2 | loop fusion | flops 835584 | bytes 541696 | tf_op jit(solution)/shard_map/concatenate | solution.py:307
  2.3 4.0 %collective-permute-start.3 = (bf16[136,1024]{1,0:T(8,128)(2,1)S(1)}, bf16[136,1024]{1,0:T(8,128)(2,1)S(1)}, u32[]{:S(2)}, u32[]{:S(2)}) collective-permute-start(bf16[136,1024]{1,0:T(8,128)(2,1)S(1)} %fusion.1), channel_id=1, source_target_pairs={{0,24},{8,16},{16,8},{24,0},{1,25},{9,17},{17,9},{25,1},{2,26},{10... | collective-permute-start | bytes 835592 | tf_op jit(solution)/shard_map/ppermute | solution.py:299
  6.2 0.5 collective-permute-start.2
  6.8 0.1 collective-permute-start.1
  6.9 0.7 %pad_add_fusion.meta_ref = s32[8,128]{1,0:T(8,128)S(1)} fusion(s32[4,128]{1,0:T(4,128)} %bitcast.9, s32[4,128]{1,0:T(4,128)} %bitcast.8), kind=kLoop, calls=%fused_computation.3 | loop fusion | flops 1024 | bytes 8192 | tf_op jit(solution)/shard_map/concatenate | solution.py:304
  7.6 0.1 pad_add_fusion.1.place
  7.7 1.1 %copy-done = bf16[128,4,704]{0,2,1:T(8,128)(2,1)S(1)} copy-done((bf16[128,4,704]{0,2,1:T(8,128)(2,1)S(1)}, bf16[128,4,704]{0,2,1:T(8,128)(2,1)}, u32[]{:S(2)}) %copy-start) | copy-done | bytes 720920
  8.8 1.4 %dispatch.1 = (bf16[144,768]{1,0:T(8,128)(2,1)S(1)}, bf16[144,768]{1,0:T(8,128)(2,1)S(1)}, bf16[144,768]{1,0:T(8,128)(2,1)S(1)}, bf16[144,768]{1,0:T(8,128)(2,1)S(1)}) custom-call(s32[2]{0:T(128)S(1)} %pad_add_fusion.1.place, s32[8,128]{1,0:T(8,128)S(1)} %pad_add_fusion.meta_ref, bf16[4,704,128]{2,1,0:T(8,128)(2,1)S(1)} %bitcast.7), custom_call_target="tpu_custom_call" | custom-call | flops 1 | bytes 1 | tf_op jit(solution)/shard_map/dispatch/pallas_call | solution.py:266
  10.1 2.0 %collective-permute-start.4 = (bf16[144,768]{1,0:T(8,128)(2,1)S(1)}, bf16[144,768]{1,0:T(8,128)(2,1)S(1)}, u32[]{:S(2)}, u32[]{:S(2)}) collective-permute-start(bf16[144,768]{1,0:T(8,128)(2,1)S(1)} %get-tuple-element.46), channel_id=1, source_target_pairs={{0,8},{8,0},{16,24},{24,16},{1,9},{9,1},{17,25},{25,17},{2,10},{10... | collective-permute-start | bytes 663560 | tf_op jit(solution)/shard_map/ppermute | solution.py:299
  12.1 1.5 %collective-permute-start.5 = (bf16[144,768]{1,0:T(8,128)(2,1)S(1)}, bf16[144,768]{1,0:T(8,128)(2,1)S(1)}, u32[]{:S(2)}, u32[]{:S(2)}) collective-permute-start(bf16[144,768]{1,0:T(8,128)(2,1)S(1)} %get-tuple-element.47), channel_id=1, source_target_pairs={{0,16},{8,24},{16,0},{24,8},{1,17},{9,25},{17,1},{25,9},{2,18},{10... | collective-permute-start | bytes 663560 | tf_op jit(solution)/shard_map/ppermute | solution.py:299
  13.6 0.2 collective-permute-done.3
  13.8 2.9 %collective-permute-start.6 = (bf16[144,768]{1,0:T(8,128)(2,1)S(1)}, bf16[144,768]{1,0:T(8,128)(2,1)S(1)}, u32[]{:S(2)}, u32[]{:S(2)}) collective-permute-start(bf16[144,768]{1,0:T(8,128)(2,1)S(1)} %get-tuple-element.48), channel_id=1, source_target_pairs={{0,24},{8,16},{16,8},{24,0},{1,25},{9,17},{17,9},{25,1},{2,26},{10... | collective-permute-start | bytes 663560 | tf_op jit(solution)/shard_map/ppermute | solution.py:299
  16.7 2.3 %collective-permute-done.2 = bf16[136,1024]{1,0:T(8,128)(2,1)S(1)} collective-permute-done((bf16[136,1024]{1,0:T(8,128)(2,1)S(1)}, bf16[136,1024]{1,0:T(8,128)(2,1)S(1)}, u32[]{:S(2)}, u32[]{:S(2)}) %collective-permute-start.2) | collective-permute-done | bytes 278560 | tf_op jit(solution)/shard_map/ppermute | solution.py:299
  19.0 1.3 %collective-permute-done.1 = bf16[136,1024]{1,0:T(8,128)(2,1)S(1)} collective-permute-done((bf16[136,1024]{1,0:T(8,128)(2,1)S(1)}, bf16[136,1024]{1,0:T(8,128)(2,1)S(1)}, u32[]{:S(2)}, u32[]{:S(2)}) %collective-permute-start.1) | collective-permute-done | bytes 278560 | tf_op jit(solution)/shard_map/ppermute | solution.py:299
  20.3 10.7 %conditional.1 = ((bf16[144,704]{1,0:T(8,128)(2,1)S(1)}, bf16[144,704]{1,0:T(8,128)(2,1)S(1)}, bf16[144,704]{1,0:T(8,128)(2,1)S(1)}, bf16[144,704]{1,0:T(8,128)(2,1)S(1)})) conditional(s32[]{:T(128)} %convert_element_type.8, () %tuple.17, (s32[2]{0:T(128)S(1)}, bf16[136,1024]{1,0:T(8,128)(2,1)S(1)}, bf16[136,1024]{1,0:T(8,128)(2,1)S(1)}, ...), branch_computations={%region_0.1_spmd, %region_1.2_spmd} | conditional | flops 2 | bytes 4718642 | solution.py:336
  20.3 1.1 %gather.1.x_ref = bf16[2,288,1024]{2,1,0:T(8,128)(2,1)S(1)} custom-call(s32[2]{0:T(128)S(1)} %get-tuple-element.12.place, bf16[136,1024]{1,0:T(8,128)(2,1)S(1)} %get-tuple-element.13.refs_0_, bf16[136,1024]{1,0:T(8,128)(2,1)S(1)} %get-tuple-element.14.refs_1_, bf16[136,1024]{1,0:T(8,128)(2,1)S(1)} %get-tuple-element.15.refs_2_, ...), custom_call_target="tpu_custom_call" | custom-call | flops 1 | bytes 1 | tf_op jit(solution)/shard_map/cond/branch_1_fun/gather/pallas_call | solution.py:266
  21.4 0.1 collective-permute-start
  21.5 2.8 %collective-permute-done.x_other = bf16[2,288,1024]{2,1,0:T(8,128)(2,1)S(1)} collective-permute-done((bf16[2,288,1024]{2,1,0:T(8,128)(2,1)S(1)}, bf16[2,288,1024]{2,1,0:T(8,128)(2,1)S(1)}, u32[]{:S(2)}, u32[]{:S(2)}) %collective-permute-start) | collective-permute-done | bytes 1179680 | tf_op jit(solution)/shard_map/cond/branch_1_fun/ppermute | solution.py:302
  24.3 6.6 %grad.1 = (bf16[144,704]{1,0:T(8,128)(2,1)S(1)}, bf16[144,704]{1,0:T(8,128)(2,1)S(1)}, bf16[144,704]{1,0:T(8,128)(2,1)S(1)}, bf16[144,704]{1,0:T(8,128)(2,1)S(1)}) custom-call(s32[2]{0:T(128)S(1)} %get-tuple-element.12.place, bf16[2,288,1024]{2,1,0:T(8,128)(2,1)S(1)} %gather.1.x_ref, bf16[2,288,1024]{2,1,0:T(8,128)(2,1)S(1)} %collective-permute-done.x_other, ...), custom_call_target="tpu_custom_call" | custom-call | flops 1 | bytes 1 | tf_op jit(solution)/shard_map/cond/branch_1_fun/grad/pallas_call | solution.py:266
  31.0 1.5 %collective-permute-start.8 = (bf16[144,704]{1,0:T(8,128)(2,1)S(1)}, bf16[144,704]{1,0:T(8,128)(2,1)S(1)}, u32[]{:S(2)}, u32[]{:S(2)}) collective-permute-start(bf16[144,704]{1,0:T(8,128)(2,1)S(1)} %get-tuple-element.52), channel_id=1, source_target_pairs={{0,8},{8,0},{16,24},{24,16},{1,9},{9,1},{17,25},{25,17},{2,10},{10... | collective-permute-start | bytes 608264 | tf_op jit(solution)/shard_map/ppermute | solution.py:299
  32.5 0.6 collective-permute-start.9
  33.0 0.0 collective-permute-done.4.refs_1_
  33.1 1.5 %collective-permute-start.16 = (bf16[144,704]{1,0:T(8,128)(2,1)S(1)}, bf16[144,704]{1,0:T(8,128)(2,1)S(1)}, u32[]{:S(2)}, u32[]{:S(2)}) collective-permute-start(bf16[144,704]{1,0:T(8,128)(2,1)S(1)} %get-tuple-element.65), channel_id=1, source_target_pairs={{0,24},{8,16},{16,8},{24,0},{1,25},{9,17},{17,9},{25,1},{2,26},{10... | collective-permute-start | bytes 608264 | tf_op jit(solution)/shard_map/ppermute | solution.py:299
  34.5 0.0 collective-permute-done.5.refs_2_
  34.5 0.0 collective-permute-done.6.refs_3_
  34.5 4.0 %mix_sibling.1 = bf16[512,1024]{1,0:T(8,128)(2,1)S(1)} custom-call(s32[2]{0:T(128)S(1)} %pad_add_fusion.1.place, bf16[144,768]{1,0:T(8,128)(2,1)S(1)} %get-tuple-element.45.refs_0_, bf16[144,768]{1,0:T(8,128)(2,1)S(1)} %collective-permute-done.4.refs_1_, bf16[144,768]{1,0:T(8,128)(2,1)S(1)} %collective-permute-done.5.refs_2_, ...), custom_call_target="tpu_custom_call" | custom-call | flops 1 | bytes 1 | tf_op jit(solution)/shard_map/mix_sibling/pallas_call | solution.py:266
  38.5 0.1 collective-permute-start.7
  38.6 3.9 %mix_own.1.own = f32[512,1024]{1,0:T(8,128)S(1)} custom-call(s32[2]{0:T(128)S(1)} %pad_add_fusion.1.place, bf16[144,768]{1,0:T(8,128)(2,1)S(1)} %get-tuple-element.45.refs_0_, bf16[144,768]{1,0:T(8,128)(2,1)S(1)} %collective-permute-done.4.refs_1_, bf16[144,768]{1,0:T(8,128)(2,1)S(1)} %collective-permute-done.5.refs_2_, ...), custom_call_target="tpu_custom_call" | custom-call | flops 99999997952 | bytes 1 | tf_op jit(solution)/shard_map/mix_own/pallas_call | solution.py:266
  42.5 0.0 collective-permute-done.7.arrived
  42.6 0.2 add.7
  42.7 1.5 %collective-permute-start.11 = (bf16[128,512]{1,0:T(8,128)(2,1)S(1)}, bf16[128,512]{1,0:T(8,128)(2,1)S(1)}, u32[]{:S(2)}, u32[]{:S(2)}) collective-permute-start(bf16[128,512]{1,0:T(8,128)(2,1)S(1)} %get-tuple-element.57), channel_id=1, source_target_pairs={{0,8},{8,0},{16,24},{24,16},{1,9},{9,1},{17,25},{25,17},{2,10},{10... | collective-permute-start | bytes 393224 | tf_op jit(solution)/shard_map/ppermute | solution.py:299
  44.2 0.6 collective-permute-start.12
  44.8 0.0 collective-permute-done.8.refs_1_
  44.8 0.0 collective-permute-done.9.refs_2_
  44.8 0.4 collective-permute-start.10
  45.2 1.7 %collective-permute-start.15 = (bf16[128,512]{1,0:T(8,128)(2,1)S(1)}, bf16[128,512]{1,0:T(8,128)(2,1)S(1)}, u32[]{:S(2)}, u32[]{:S(2)}) collective-permute-start(bf16[128,512]{1,0:T(8,128)(2,1)S(1)} %get-tuple-element.61), channel_id=1, source_target_pairs={{0,16},{8,24},{16,0},{24,8},{1,17},{9,25},{17,1},{25,9},{2,18},{10... | collective-permute-start | bytes 393224 | tf_op jit(solution)/shard_map/ppermute | solution.py:299
  46.9 2.2 %collective-permute-done.11.low = bf16[128,512]{1,0:T(8,128)(2,1)S(1)} collective-permute-done((bf16[128,512]{1,0:T(8,128)(2,1)S(1)}, bf16[128,512]{1,0:T(8,128)(2,1)S(1)}, u32[]{:S(2)}, u32[]{:S(2)}) %collective-permute-start.11) | collective-permute-done | bytes 131104 | tf_op jit(solution)/shard_map/ppermute | solution.py:299
  49.1 1.5 %collective-permute-done.12.high = bf16[128,512]{1,0:T(8,128)(2,1)S(1)} collective-permute-done((bf16[128,512]{1,0:T(8,128)(2,1)S(1)}, bf16[128,512]{1,0:T(8,128)(2,1)S(1)}, u32[]{:S(2)}, u32[]{:S(2)}) %collective-permute-start.12) | collective-permute-done | bytes 131104 | tf_op jit(solution)/shard_map/ppermute | solution.py:299
  50.6 0.6 %collective-permute-start.13 = (bf16[128,512]{1,0:T(8,128)(2,1)S(1)}, bf16[128,512]{1,0:T(8,128)(2,1)S(1)}, u32[]{:S(2)}, u32[]{:S(2)}) collective-permute-start(bf16[128,512]{1,0:T(8,128)(2,1)S(1)} %get-tuple-element.59), channel_id=1, source_target_pairs={{0,8},{8,0},{16,24},{24,16},{1,9},{9,1},{17,25},{25,17},{2,10},{10... | collective-permute-start | bytes 393224 | tf_op jit(solution)/shard_map/ppermute | solution.py:299
  51.3 0.0 collective-permute-start.14
  51.3 0.0 collective-permute-done.16.refs_3_
  51.3 2.3 %restore.1 = bf16[4,704,128]{2,1,0:T(8,128)(2,1)} custom-call(s32[2]{0:T(128)S(1)} %pad_add_fusion.1.place, s32[8,128]{1,0:T(8,128)S(1)} %pad_add_fusion.meta_ref, bf16[144,704]{1,0:T(8,128)(2,1)S(1)} %get-tuple-element.62.refs_0_, bf16[144,704]{1,0:T(8,128)(2,1)S(1)} %collective-permute-done.8.refs_1_, bf16[144,704]{1,0:T(8,128)(2,1)S(1)} %collective-permute-done.9.refs_2_, ...), custom_call_target="tpu_custom_call" | custom-call | flops 99999997952 | bytes 1 | tf_op jit(solution)/shard_map/restore/pallas_call | solution.py:266
  53.6 0.0 collective-permute-done.10.one_low
  53.6 0.0 collective-permute-done.15.two_high
  53.6 2.0 %collective-permute-done.13.one_high = bf16[128,512]{1,0:T(8,128)(2,1)S(1)} collective-permute-done((bf16[128,512]{1,0:T(8,128)(2,1)S(1)}, bf16[128,512]{1,0:T(8,128)(2,1)S(1)}, u32[]{:S(2)}, u32[]{:S(2)}) %collective-permute-start.13) | collective-permute-done | bytes 131104 | tf_op jit(solution)/shard_map/ppermute | solution.py:299
  55.7 0.6 %collective-permute-done.14.two_low = bf16[128,512]{1,0:T(8,128)(2,1)S(1)} collective-permute-done((bf16[128,512]{1,0:T(8,128)(2,1)S(1)}, bf16[128,512]{1,0:T(8,128)(2,1)S(1)}, u32[]{:S(2)}, u32[]{:S(2)}) %collective-permute-start.14) | collective-permute-done | bytes 131104 | tf_op jit(solution)/shard_map/ppermute | solution.py:299
  56.2 0.8 %finish.1 = bf16[128,1024]{1,0:T(8,128)(2,1)} custom-call(f32[128,1024]{1,0:T(8,128)S(1)} %get-tuple-element.49.mine, bf16[128,512]{1,0:T(8,128)(2,1)S(1)} %collective-permute-done.10.one_low, bf16[128,512]{1,0:T(8,128)(2,1)S(1)} %collective-permute-done.13.one_high, bf16[128,512]{1,0:T(8,128)(2,1)S(1)} %collective-permute-done.14.two_low, ...), custom_call_target="tpu_custom_call" | custom-call | flops 1 | bytes 1 | tf_op jit(solution)/shard_map/finish/pallas_call | solution.py:266
  (2 shorter events, 0.0 us)
Async XLA Ops:
  2.3 11.5 %collective-permute-start.3 = (bf16[136,1024]{1,0:T(8,128)(2,1)S(1)}, bf16[136,1024]{1,0:T(8,128)(2,1)S(1)}, u32[]{:S(2)}, u32[]{:S(2)}) collective-permute-start(bf16[136,1024]{1,0:T(8,128)(2,1)S(1)} %fusion.1), channel_id=1, source_target_pairs={{0,24},{8,16},{16,8},{24,0},{1,25},{9,17},{17,9},{25,1},{2,26},{10... | collective-permute-start | bytes 835592 | tf_op jit(solution)/shard_map/ppermute | solution.py:299
  6.2 12.7 %collective-permute-start.2 = (bf16[136,1024]{1,0:T(8,128)(2,1)S(1)}, bf16[136,1024]{1,0:T(8,128)(2,1)S(1)}, u32[]{:S(2)}, u32[]{:S(2)}) collective-permute-start(bf16[136,1024]{1,0:T(8,128)(2,1)S(1)} %fusion.1), channel_id=1, source_target_pairs={{0,16},{8,24},{16,0},{24,8},{1,17},{9,25},{17,1},{25,9},{2,18},{10... | collective-permute-start | bytes 835592 | tf_op jit(solution)/shard_map/ppermute | solution.py:299
  6.8 13.6 %collective-permute-start.1 = (bf16[136,1024]{1,0:T(8,128)(2,1)S(1)}, bf16[136,1024]{1,0:T(8,128)(2,1)S(1)}, u32[]{:S(2)}, u32[]{:S(2)}) collective-permute-start(bf16[136,1024]{1,0:T(8,128)(2,1)S(1)} %fusion.1), channel_id=1, source_target_pairs={{0,8},{8,0},{16,24},{24,16},{1,9},{9,1},{17,25},{25,17},{2,10},{10... | collective-permute-start | bytes 835592 | tf_op jit(solution)/shard_map/ppermute | solution.py:299
  7.7 1.1 %copy-start = (bf16[128,4,704]{0,2,1:T(8,128)(2,1)S(1)}, bf16[128,4,704]{0,2,1:T(8,128)(2,1)}, u32[]{:S(2)}) copy-start(bf16[128,4,704]{0,2,1:T(8,128)(2,1)} %param.7) | copy-start | bytes 2162692
  10.1 22.9 %collective-permute-start.4 = (bf16[144,768]{1,0:T(8,128)(2,1)S(1)}, bf16[144,768]{1,0:T(8,128)(2,1)S(1)}, u32[]{:S(2)}, u32[]{:S(2)}) collective-permute-start(bf16[144,768]{1,0:T(8,128)(2,1)S(1)} %get-tuple-element.46), channel_id=1, source_target_pairs={{0,8},{8,0},{16,24},{24,16},{1,9},{9,1},{17,25},{25,17},{2,10},{10... | collective-permute-start | bytes 663560 | tf_op jit(solution)/shard_map/ppermute | solution.py:299
  12.1 22.4 %collective-permute-start.5 = (bf16[144,768]{1,0:T(8,128)(2,1)S(1)}, bf16[144,768]{1,0:T(8,128)(2,1)S(1)}, u32[]{:S(2)}, u32[]{:S(2)}) collective-permute-start(bf16[144,768]{1,0:T(8,128)(2,1)S(1)} %get-tuple-element.47), channel_id=1, source_target_pairs={{0,16},{8,24},{16,0},{24,8},{1,17},{9,25},{17,1},{25,9},{2,18},{10... | collective-permute-start | bytes 663560 | tf_op jit(solution)/shard_map/ppermute | solution.py:299
  13.8 20.8 %collective-permute-start.6 = (bf16[144,768]{1,0:T(8,128)(2,1)S(1)}, bf16[144,768]{1,0:T(8,128)(2,1)S(1)}, u32[]{:S(2)}, u32[]{:S(2)}) collective-permute-start(bf16[144,768]{1,0:T(8,128)(2,1)S(1)} %get-tuple-element.48), channel_id=1, source_target_pairs={{0,24},{8,16},{16,8},{24,0},{1,25},{9,17},{17,9},{25,1},{2,26},{10... | collective-permute-start | bytes 663560 | tf_op jit(solution)/shard_map/ppermute | solution.py:299
  21.4 2.9 %collective-permute-start = (bf16[2,288,1024]{2,1,0:T(8,128)(2,1)S(1)}, bf16[2,288,1024]{2,1,0:T(8,128)(2,1)S(1)}, u32[]{:S(2)}, u32[]{:S(2)}) collective-permute-start(bf16[2,288,1024]{2,1,0:T(8,128)(2,1)S(1)} %gather.1.x_ref), channel_id=1, source_target_pairs={{0,1},{1,0},{2,3},{3,2},{4,5},{5,4},{6,7},{7,6},{8,9},{9,8},{10,11... | collective-permute-start | bytes 3538952 | tf_op jit(solution)/shard_map/cond/branch_1_fun/ppermute | solution.py:302
  31.0 13.8 %collective-permute-start.8 = (bf16[144,704]{1,0:T(8,128)(2,1)S(1)}, bf16[144,704]{1,0:T(8,128)(2,1)S(1)}, u32[]{:S(2)}, u32[]{:S(2)}) collective-permute-start(bf16[144,704]{1,0:T(8,128)(2,1)S(1)} %get-tuple-element.52), channel_id=1, source_target_pairs={{0,8},{8,0},{16,24},{24,16},{1,9},{9,1},{17,25},{25,17},{2,10},{10... | collective-permute-start | bytes 608264 | tf_op jit(solution)/shard_map/ppermute | solution.py:299
  32.5 12.3 %collective-permute-start.9 = (bf16[144,704]{1,0:T(8,128)(2,1)S(1)}, bf16[144,704]{1,0:T(8,128)(2,1)S(1)}, u32[]{:S(2)}, u32[]{:S(2)}) collective-permute-start(bf16[144,704]{1,0:T(8,128)(2,1)S(1)} %get-tuple-element.53), channel_id=1, source_target_pairs={{0,16},{8,24},{16,0},{24,8},{1,17},{9,25},{17,1},{25,9},{2,18},{10... | collective-permute-start | bytes 608264 | tf_op jit(solution)/shard_map/ppermute | solution.py:299
  33.1 18.3 %collective-permute-start.16 = (bf16[144,704]{1,0:T(8,128)(2,1)S(1)}, bf16[144,704]{1,0:T(8,128)(2,1)S(1)}, u32[]{:S(2)}, u32[]{:S(2)}) collective-permute-start(bf16[144,704]{1,0:T(8,128)(2,1)S(1)} %get-tuple-element.65), channel_id=1, source_target_pairs={{0,24},{8,16},{16,8},{24,0},{1,25},{9,17},{17,9},{25,1},{2,26},{10... | collective-permute-start | bytes 608264 | tf_op jit(solution)/shard_map/ppermute | solution.py:299
  38.5 4.0 %collective-permute-start.7 = (bf16[512,1024]{1,0:T(8,128)(2,1)S(1)}, bf16[512,1024]{1,0:T(8,128)(2,1)S(1)}, u32[]{:S(2)}, u32[]{:S(2)}) collective-permute-start(bf16[512,1024]{1,0:T(8,128)(2,1)S(1)} %mix_sibling.1), channel_id=1, source_target_pairs={{0,1},{1,0},{2,3},{3,2},{4,5},{5,4},{6,7},{7,6},{8,9},{9,8},{10,11... | collective-permute-start | bytes 3145736 | tf_op jit(solution)/shard_map/ppermute | solution.py:302
  42.7 6.4 %collective-permute-start.11 = (bf16[128,512]{1,0:T(8,128)(2,1)S(1)}, bf16[128,512]{1,0:T(8,128)(2,1)S(1)}, u32[]{:S(2)}, u32[]{:S(2)}) collective-permute-start(bf16[128,512]{1,0:T(8,128)(2,1)S(1)} %get-tuple-element.57), channel_id=1, source_target_pairs={{0,8},{8,0},{16,24},{24,16},{1,9},{9,1},{17,25},{25,17},{2,10},{10... | collective-permute-start | bytes 393224 | tf_op jit(solution)/shard_map/ppermute | solution.py:299
  44.2 6.3 %collective-permute-start.12 = (bf16[128,512]{1,0:T(8,128)(2,1)S(1)}, bf16[128,512]{1,0:T(8,128)(2,1)S(1)}, u32[]{:S(2)}, u32[]{:S(2)}) collective-permute-start(bf16[128,512]{1,0:T(8,128)(2,1)S(1)} %get-tuple-element.58), channel_id=1, source_target_pairs={{0,16},{8,24},{16,0},{24,8},{1,17},{9,25},{17,1},{25,9},{2,18},{10... | collective-permute-start | bytes 393224 | tf_op jit(solution)/shard_map/ppermute | solution.py:299
  44.8 8.8 %collective-permute-start.10 = (bf16[128,512]{1,0:T(8,128)(2,1)S(1)}, bf16[128,512]{1,0:T(8,128)(2,1)S(1)}, u32[]{:S(2)}, u32[]{:S(2)}) collective-permute-start(bf16[128,512]{1,0:T(8,128)(2,1)S(1)} %get-tuple-element.54), channel_id=1, source_target_pairs={{0,8},{8,0},{16,24},{24,16},{1,9},{9,1},{17,25},{25,17},{2,10},{10... | collective-permute-start | bytes 393224 | tf_op jit(solution)/shard_map/ppermute | solution.py:299
  45.2 8.4 %collective-permute-start.15 = (bf16[128,512]{1,0:T(8,128)(2,1)S(1)}, bf16[128,512]{1,0:T(8,128)(2,1)S(1)}, u32[]{:S(2)}, u32[]{:S(2)}) collective-permute-start(bf16[128,512]{1,0:T(8,128)(2,1)S(1)} %get-tuple-element.61), channel_id=1, source_target_pairs={{0,16},{8,24},{16,0},{24,8},{1,17},{9,25},{17,1},{25,9},{2,18},{10... | collective-permute-start | bytes 393224 | tf_op jit(solution)/shard_map/ppermute | solution.py:299
  50.6 5.0 %collective-permute-start.13 = (bf16[128,512]{1,0:T(8,128)(2,1)S(1)}, bf16[128,512]{1,0:T(8,128)(2,1)S(1)}, u32[]{:S(2)}, u32[]{:S(2)}) collective-permute-start(bf16[128,512]{1,0:T(8,128)(2,1)S(1)} %get-tuple-element.59), channel_id=1, source_target_pairs={{0,8},{8,0},{16,24},{24,16},{1,9},{9,1},{17,25},{25,17},{2,10},{10... | collective-permute-start | bytes 393224 | tf_op jit(solution)/shard_map/ppermute | solution.py:299
  51.3 5.0 %collective-permute-start.14 = (bf16[128,512]{1,0:T(8,128)(2,1)S(1)}, bf16[128,512]{1,0:T(8,128)(2,1)S(1)}, u32[]{:S(2)}, u32[]{:S(2)}) collective-permute-start(bf16[128,512]{1,0:T(8,128)(2,1)S(1)} %get-tuple-element.60), channel_id=1, source_target_pairs={{0,16},{8,24},{16,0},{24,8},{1,17},{9,25},{17,1},{25,9},{2,18},{10... | collective-permute-start | bytes 393224 | tf_op jit(solution)/shard_map/ppermute | solution.py:299

commit v6 on v5

--- a/solution.py
+++ b/solution.py
@@ -119,9 +119,11 @@
             x_ref[l, :, c : c + chunk] = x.astype(BF16)
 
 
-def gather_kernel(dims, top, place, *refs):
-    experts, local, cap, width = dims
-    own, x_ref = refs[:-1], refs[-1]
+def grad_kernel(dims, top, place, *refs):
+    experts, local, cap, width = dims
+    n = experts // local
+    own, other, w_ref = refs[:n], refs[n : 2 * n], refs[2 * n]
+    outs, x_ref = refs[2 * n + 1 : -1], refs[-1]
     half = own[0].shape[1]
     tokens = own[0].shape[0] - 8
     chunk = min(half, 512)
@@ -131,55 +133,22 @@
         held.append(
             jnp.concatenate(slots_by_lane(ids, place[0], local, cap, width), axis=0)
         )
-    for c in range(0, half, chunk):
-        rows = [dot(h, ref[:tokens, c : c + chunk], NN) for h, ref in zip(held, own)]
-        for l, x in enumerate(by_expert(rows, local, cap)):
-            x_ref[l, :, c : c + chunk] = x.astype(BF16)
-
-
-def pieces_of(size, step):
-    return [(i, min(step, size - i)) for i in range(0, size, step)]
-
-
-def grad_kernel(dims, place, x_ref, x_other, w_hbm, *refs):
-    experts, local, cap, width = dims
-    outs, (w_ref, g_ref, sems) = refs[:-3], refs[-3:]
-    half = x_ref.shape[2]
-    pieces = [(l, i, *at) for l in range(local) for i, at in enumerate(pieces_of(w_ref.shape[1], 256))]
-
-    def copy(l, i, start, size):
-        rows = pl.ds(start, size)
-        return pltpu.make_async_copy(w_hbm.at[l, rows], w_ref.at[l, rows], sems.at[l, i])
-
-    for piece in pieces:
-        copy(*piece).start()
-    mine = pl.ds(pl.multiple_of(place[1] * half, half), half)
-    theirs = pl.ds(pl.multiple_of((1 - place[1]) * half, half), half)
-    for l, i, start, size in pieces:
-        copy(l, i, start, size).wait()
-        rows = pl.ds(start, size)
-        grads = dot(x_ref[l], w_ref[l, rows, mine], NT)
-        grads = grads + dot(x_other[l], w_ref[l, rows, theirs], NT)
-        g_ref[l, :, start : start + size] = grads
-    grads = [g_ref[l] for l in range(local)]
-    for s, rows in enumerate(by_source(grads, len(outs), cap)):
+    for side, halves in ((place[1], own), (1 - place[1], other)):
+        for c in range(0, half, chunk):
+            rows = [dot(h, ref[:tokens, c : c + chunk], NN) for h, ref in zip(held, halves)]
+            at = pl.ds(pl.multiple_of(side * half + c, chunk), chunk)
+            for l, x in enumerate(by_expert(rows, local, cap)):
+                x_ref[l, :, at] = x.astype(BF16)
+    grads = [dot(x_ref[l], w_ref[l], NT) for l in range(local)]
+    for s, rows in enumerate(by_source(grads, n, cap)):
         outs[s][...] = rows.astype(BF16)
 
 
-def mix_rows(dims, side, hid, w_hbm, w_ref, sems, tokens, half, store):
+def mix_rows(dims, side, hid, w_ref, tokens, half, store):
     experts, local, cap, width = dims
     n = len(hid)
     ff = w_ref.shape[1]
-    pieces = pieces_of(half, 256)
-
-    def copy(i, start, size):
-        source = pl.ds(pl.multiple_of(side * half + start, size), size)
-        return pltpu.make_async_copy(
-            w_hbm.at[:, :, source], w_ref.at[:, :, pl.ds(start, size)], sems.at[i]
-        )
-
-    for i, (start, size) in enumerate(pieces):
-        copy(i, start, size).start()
+    chunk = min(half, 256)
     same = ones_where(iota((tokens, tokens), 0) == iota((tokens, tokens), 1))
     held = []
     for h in hid:
@@ -188,35 +157,34 @@
         held.append(dot(same, slots, NT).astype(BF16))
     rows = [h[:, :ff].astype(F32) for h in hid]
     x = [r.astype(BF16) for r in by_expert(rows, local, cap)]
-    for i, (start, size) in enumerate(pieces):
-        copy(i, start, size).wait()
-        columns = pl.ds(start, size)
-        out = [dot(x[l], w_ref[l, :, columns], NN) for l in range(local)]
+    for c in range(0, half, chunk):
+        at = pl.ds(pl.multiple_of(side * half + c, chunk), chunk)
+        out = [dot(x[l], w_ref[l, :, at], NN) for l in range(local)]
         for s, rows in enumerate(by_source(out, n, cap)):
-            store(s, slice(start, start + size), dot(held[s], rows.astype(BF16), NN))
+            store(s, slice(c, c + chunk), dot(held[s], rows.astype(BF16), NN))
 
 
 def mix_kernel(dims, sibling, place, *refs):
-    hid, (w_hbm, out, w_ref, sems) = refs[:-4], refs[-4:]
+    hid, (w_ref, out) = refs[:-2], refs[-2:]
     tokens = out.shape[0] // len(hid)
 
     def store(s, columns, part):
         out[pl.ds(s * tokens, tokens), columns] = part.astype(out.dtype)
 
     side = 1 - place[1] if sibling else place[1]
-    mix_rows(dims, side, hid, w_hbm, w_ref, sems, tokens, out.shape[1], store)
+    mix_rows(dims, side, hid, w_ref, tokens, out.shape[1], store)
 
 
 def mix_add_kernel(dims, place, *refs):
-    n = (len(refs) - 4) // 2
-    hid, (w_hbm, arrived), outs = refs[:n], refs[n : n + 2], refs[n + 2 : -2]
+    n = (len(refs) - 2) // 2
+    hid, (w_ref, arrived), outs = refs[:n], refs[n : n + 2], refs[n + 2 :]
     tokens, half = outs[0].shape
 
     def store(s, columns, part):
         theirs = arrived[pl.ds(s * tokens, tokens), columns].astype(F32)
         outs[s][:, columns] = (part + theirs).astype(BF16)
 
-    mix_rows(dims, place[1], hid, w_hbm, refs[-2], refs[-1], tokens, half, store)
+    mix_rows(dims, place[1], hid, w_ref, tokens, half, store)
 
 
 def add_split_kernel(own, arrived, mine, one_low, one_high, two_low, two_high, low, high):
@@ -307,45 +275,32 @@
     packed = jnp.concatenate([grad_out, named], axis=0)
     forward = n == 4
     own = [send(packed, s) for s in range(n)]
+    swapped = swap(packed)
+    meta, swapped = lax.optimization_barrier((meta, swapped))
     hid_sent = run(
         functools.partial(dispatch_kernel, dims), [shaped((width, -(-(ff + 1) // 128) * 128))] * n,
-        [place, meta, hid_t], where=placed, name="dispatch",
+        [place, meta, hid_t], where=placed, name="dispatch", weight=BIG,
     )
     hid = [send(hid_sent[s], s) for s in range(n)]
     slot = shaped((width, ff))
 
-    def taken(own, w_down):
-        (x,) = run(
-            functools.partial(gather_kernel, dims, top),
-            [shaped((local, n * cap, half))], [place, *own], where=placed, name="gather",
-        )
-        return list(run(
-            functools.partial(grad_kernel, dims), [slot] * n,
-            [place, x, swap(x), w_down], where={**placed, 3: pl.ANY},
-            scratch=[
-                pltpu.VMEM(w_down.shape, BF16),
-                pltpu.VMEM((local, n * cap, ff), F32),
-                pltpu.SemaphoreType.DMA((local, len(pieces_of(ff, 256)))),
-            ],
-            name="grad",
-        ))
-
-    def skipped(own, w_down):
-        return [jnp.zeros((width, ff), BF16)] * n
-
-    grad_sent = lax.cond(
-        place[0] < 1000, taken, skipped, own, w_down
+    def taken(own):
+        other = [swap(x) for x in own[:2]]
+        for x in own[2:]:
+            other[-2], x = lax.optimization_barrier((other[-2], x))
+            other.append(swap(x))
+        return other
+
+    other = [swapped] + lax.cond(place[0] < 1000, taken, list, own[1:])
+    grad_sent = run(
+        functools.partial(grad_kernel, dims, top), [slot] * n,
+        [place, *own, *other, w_down], where=placed,
+        scratch=[pltpu.VMEM((local, n * cap, full), BF16)], name="grad",
     )
     hid[0], grad_own = lax.optimization_barrier((hid[0], grad_sent[0]))
     grad_back = [grad_own] + [send(grad_sent[s], s) for s in range(1, n)]
 
-    mixing = dict(
-        where={**placed, n + 1: pl.ANY},
-        scratch=[
-            pltpu.VMEM((local, ff, half), BF16),
-            pltpu.SemaphoreType.DMA((len(pieces_of(half, 256)),)),
-        ],
-    )
+    mixing = dict(where=placed)
     (theirs,) = run(
         functools.partial(mix_kernel, dims, True), [shaped((n * tokens, half))],
         [place, *hid, w_down], name="mix_sibling", **mixing,

time: 57.3 us -> 56.5 us (0.986)
  Pallas kernels: 20.3 us -> 13.5 us
  local copies, waits for them, and re-layouts: 1.11 us -> 6.37 us
  starting transfers between devices: 19.5 us -> 21 us
  waiting for transfers between devices: 13 us -> 12.2 us
    pallas_call x9 -> x8, Pallas kernels: 20.3 us -> 13.5 us  [call(): pl.pallas_call(kernel, out_shape=outs, in_specs=[pl.BlockSpec(memory_spac...]
    unnamed x2 -> x6, local copies, waits for them, and re-layouts: 1.11 us -> 6.37 us
    ppermute x2 -> x5, starting transfers between devices: 0.14 us -> 1.24 us  [swap(): return lax.ppermute(x, 'tp', [(0, 1), (1, 0)])]
    ppermute x15, waiting for transfers between devices: 10.1 us -> 9.24 us  [send(): return lax.ppermute(x, 'ctx', [(i, i ^ s) for i in range(n)]) if s else x]
    ppermute x2 -> x5, waiting for transfers between devices: 2.84 us -> 2.95 us  [swap(): return lax.ppermute(x, 'tp', [(0, 1), (1, 0)])]
  transfers between devices with their start and end apart: 17 -> 20, of which waited for: 8 -> 11; matrix products, arithmetic and copies ran while one was open for 1% -> 1% of each run, Pallas kernels for 34% -> 23%
where the time goes in v6:
time: 56.5 us; the launch traced here: 56.2 us
  starting transfers between devices  21 us (37%)
  Pallas kernels  13.5 us (24%)
  waiting for transfers between devices  12.2 us (22%)
  local copies, waits for them, and re-layouts  6.37 us (11%)
  other arithmetic  2.44 us (4%)
  between operations  0.7 us (1%)
    ppermute x15, starting transfers between devices, send(): return lax.ppermute(x, 'ctx', [(i, i ^ s) for i in range(n)]) if s else x  19.8 us
    pallas_call x8, Pallas kernels, call(): pl.pallas_call(kernel, out_shape=outs, in_specs=[pl.BlockSpec(memory_spac...  13.5 us
    ppermute x15, waiting for transfers between devices, send(): return lax.ppermute(x, 'ctx', [(i, i ^ s) for i in range(n)]) if s else x  9.24 us
    unnamed x6, local copies, waits for them, and re-layouts  6.37 us
    ppermute x5, waiting for transfers between devices, swap(): return lax.ppermute(x, 'tp', [(0, 1), (1, 0)])  2.95 us
    ppermute x5, starting transfers between devices, swap(): return lax.ppermute(x, 'tp', [(0, 1), (1, 0)])  1.24 us
  transfers between devices with their start and end apart: 20, of which 11 were waited for; matrix products, arithmetic and copies ran while one was open for 1% of the time, Pallas kernels for 23%

profile of v6, /device:TPU:0, one launch (start us, length us, event | category | flops | bytes accessed | tf_op | source)
XLA Modules:
  0.0 56.2 jit_solution(3345234259432754198)
XLA Ops:
  0.6 0.7 %bitcast_convert_fusion = bf16[4,128]{1,0:T(4,128)(2,1)S(1)} fusion(s32[128,4]{0,1:T(4,128)} %param.8), kind=kLoop, calls=%fused_computation.5 | loop fusion | flops 512 | bytes 3072 | tf_op jit(solution)/shard_map/convert_element_type | solution.py:274
  1.3 1.0 %fusion.1.refs_0_ = bf16[136,1024]{1,0:T(8,128)(2,1)S(1)} fusion(bf16[4,128]{1,0:T(4,128)(2,1)S(1)} %bitcast_convert_fusion, bf16[128,1024]{1,0:T(8,128)(2,1)} %param.10), kind=kLoop, calls=%fused_computation.2 | loop fusion | flops 835584 | bytes 541696 | tf_op jit(solution)/shard_map/concatenate | solution.py:275
  2.3 0.5 collective-permute-start.3
  2.8 3.5 %collective-permute-start.6 = (bf16[136,1024]{1,0:T(8,128)(2,1)S(1)}, bf16[136,1024]{1,0:T(8,128)(2,1)S(1)}, u32[]{:S(2)}, u32[]{:S(2)}) collective-permute-start(bf16[136,1024]{1,0:T(8,128)(2,1)S(1)} %fusion.1.refs_0_), channel_id=1, source_target_pairs={{0,24},{8,16},{16,8},{24,0},{1,25},{9,17},{17,9},{25,1},{2,26},{10... | collective-permute-start | bytes 835592 | tf_op jit(solution)/shard_map/ppermute | solution.py:267
  6.3 0.5 collective-permute-start.5
  6.8 0.1 collective-permute-start.4
  7.0 0.1 pad_add_fusion.1.place
  7.0 0.7 %pad_add_fusion.meta_ref = s32[8,128]{1,0:T(8,128)S(1)} fusion(s32[4,128]{1,0:T(4,128)} %bitcast.9, s32[4,128]{1,0:T(4,128)} %bitcast.8), kind=kLoop, calls=%fused_computation.3 | loop fusion | flops 1024 | bytes 8192 | tf_op jit(solution)/shard_map/concatenate | solution.py:272
  7.8 0.0 collective-permute-done.3.refs_4_
  7.8 0.0 copy-start.2
  7.8 1.1 %copy-done.2 = bf16[128,4,704]{0,2,1:T(8,128)(2,1)S(1)} copy-done((bf16[128,4,704]{0,2,1:T(8,128)(2,1)S(1)}, bf16[128,4,704]{0,2,1:T(8,128)(2,1)}, u32[]{:S(2)}) %copy-start.2) | copy-done | bytes 720920
  8.9 1.4 %dispatch.1 = (bf16[144,768]{1,0:T(8,128)(2,1)S(1)}, bf16[144,768]{1,0:T(8,128)(2,1)S(1)}, bf16[144,768]{1,0:T(8,128)(2,1)S(1)}, bf16[144,768]{1,0:T(8,128)(2,1)S(1)}) custom-call(s32[2]{0:T(128)S(1)} %pad_add_fusion.1.place, s32[8,128]{1,0:T(8,128)S(1)} %pad_add_fusion.meta_ref, bf16[4,704,128]{2,1,0:T(8,128)(2,1)S(1)} %bitcast.7), custom_call_target="tpu_custom_call" | custom-call | flops 99999997952 | bytes 1 | tf_op jit(solution)/shard_map/dispatch/pallas_call | solution.py:234
  10.2 2.0 %collective-permute-start.7 = (bf16[144,768]{1,0:T(8,128)(2,1)S(1)}, bf16[144,768]{1,0:T(8,128)(2,1)S(1)}, u32[]{:S(2)}, u32[]{:S(2)}) collective-permute-start(bf16[144,768]{1,0:T(8,128)(2,1)S(1)} %get-tuple-element.55), channel_id=1, source_target_pairs={{0,8},{8,0},{16,24},{24,16},{1,9},{9,1},{17,25},{25,17},{2,10},{10... | collective-permute-start | bytes 663560 | tf_op jit(solution)/shard_map/ppermute | solution.py:267
  12.2 1.5 %collective-permute-start.8 = (bf16[144,768]{1,0:T(8,128)(2,1)S(1)}, bf16[144,768]{1,0:T(8,128)(2,1)S(1)}, u32[]{:S(2)}, u32[]{:S(2)}) collective-permute-start(bf16[144,768]{1,0:T(8,128)(2,1)S(1)} %get-tuple-element.56), channel_id=1, source_target_pairs={{0,16},{8,24},{16,0},{24,8},{1,17},{9,25},{17,1},{25,9},{2,18},{10... | collective-permute-start | bytes 663560 | tf_op jit(solution)/shard_map/ppermute | solution.py:267
  13.7 0.2 collective-permute-done.6.refs_3_
  13.9 2.8 %collective-permute-start.9 = (bf16[144,768]{1,0:T(8,128)(2,1)S(1)}, bf16[144,768]{1,0:T(8,128)(2,1)S(1)}, u32[]{:S(2)}, u32[]{:S(2)}) collective-permute-start(bf16[144,768]{1,0:T(8,128)(2,1)S(1)} %get-tuple-element.57), channel_id=1, source_target_pairs={{0,24},{8,16},{16,8},{24,0},{1,25},{9,17},{17,9},{25,1},{2,26},{10... | collective-permute-start | bytes 663560 | tf_op jit(solution)/shard_map/ppermute | solution.py:267
  16.7 2.9 %collective-permute-done.5.refs_2_ = bf16[136,1024]{1,0:T(8,128)(2,1)S(1)} collective-permute-done((bf16[136,1024]{1,0:T(8,128)(2,1)S(1)}, bf16[136,1024]{1,0:T(8,128)(2,1)S(1)}, u32[]{:S(2)}, u32[]{:S(2)}) %collective-permute-start.5) | collective-permute-done | bytes 278560 | tf_op jit(solution)/shard_map/ppermute | solution.py:267
  19.6 0.7 %collective-permute-done.4.refs_1_ = bf16[136,1024]{1,0:T(8,128)(2,1)S(1)} collective-permute-done((bf16[136,1024]{1,0:T(8,128)(2,1)S(1)}, bf16[136,1024]{1,0:T(8,128)(2,1)S(1)}, u32[]{:S(2)}, u32[]{:S(2)}) %collective-permute-start.4) | collective-permute-done | bytes 278560 | tf_op jit(solution)/shard_map/ppermute | solution.py:267
  20.3 3.4 %conditional.1 = (bf16[136,1024]{1,0:T(8,128)(2,1)}, bf16[136,1024]{1,0:T(8,128)(2,1)}, bf16[136,1024]{1,0:T(8,128)(2,1)}) conditional(s32[]{:T(128)} %convert_element_type.9, (bf16[136,1024]{1,0:T(8,128)(2,1)S(1)}, bf16[136,1024]{1,0:T(8,128)(2,1)S(1)}, bf16[136,1024]{1,0:T(8,128)(2,1)S(1)}) %tuple.20, (bf16[136,1024]{1,0:T(8,128)(2,1)S(1)}, ...), branch_computations={%region_0.1_spmd, %region_1.2_spmd} | conditional | bytes 3342480 | solution.py:294
  20.3 0.5 collective-permute-start.1
  20.8 1.2 %collective-permute-done = bf16[136,1024]{1,0:T(8,128)(2,1)} collective-permute-done((bf16[136,1024]{1,0:T(8,128)(2,1)S(1)}, bf16[136,1024]{1,0:T(8,128)(2,1)}, u32[]{:S(2)}, u32[]{:S(2)}) %collective-permute-start) | collective-permute-done | bytes 278560 | tf_op jit(solution)/shard_map/cond/branch_1_fun/ppermute | solution.py:270
  22.0 0.1 collective-permute-start.2
  22.1 0.3 collective-permute-done.1
  22.4 1.3 %collective-permute-done.2 = bf16[136,1024]{1,0:T(8,128)(2,1)} collective-permute-done((bf16[136,1024]{1,0:T(8,128)(2,1)S(1)}, bf16[136,1024]{1,0:T(8,128)(2,1)}, u32[]{:S(2)}, u32[]{:S(2)}) %collective-permute-start.2) | collective-permute-done | bytes 278560 | tf_op jit(solution)/shard_map/cond/branch_1_fun/ppermute | solution.py:270
  23.7 2.6 %copy-done = bf16[2,704,2048]{2,1,0:T(8,128)(2,1)S(1)} copy-done((bf16[2,704,2048]{2,1,0:T(8,128)(2,1)S(1)}, bf16[2,704,2048]{2,1,0:T(8,128)(2,1)}, u32[]{:S(2)}) %copy-start) | copy-done | bytes 5767192
  26.3 4.0 %grad.1 = (bf16[144,704]{1,0:T(8,128)(2,1)S(1)}, bf16[144,704]{1,0:T(8,128)(2,1)S(1)}, bf16[144,704]{1,0:T(8,128)(2,1)S(1)}, bf16[144,704]{1,0:T(8,128)(2,1)S(1)}) custom-call(s32[2]{0:T(128)S(1)} %pad_add_fusion.1.place, bf16[136,1024]{1,0:T(8,128)(2,1)S(1)} %fusion.1.refs_0_, bf16[136,1024]{1,0:T(8,128)(2,1)S(1)} %collective-permute-done.4.refs_1_, ...), custom_call_target="tpu_custom_call" | custom-call | flops 1 | bytes 1 | tf_op jit(solution)/shard_map/grad/pallas_call | solution.py:234
  30.3 1.6 %collective-permute-start.11 = (bf16[144,704]{1,0:T(8,128)(2,1)S(1)}, bf16[144,704]{1,0:T(8,128)(2,1)S(1)}, u32[]{:S(2)}, u32[]{:S(2)}) collective-permute-start(bf16[144,704]{1,0:T(8,128)(2,1)S(1)} %get-tuple-element.61), channel_id=1, source_target_pairs={{0,8},{8,0},{16,24},{24,16},{1,9},{9,1},{17,25},{25,17},{2,10},{10... | collective-permute-start | bytes 608264 | tf_op jit(solution)/shard_map/ppermute | solution.py:267
  31.9 0.6 %collective-permute-start.12 = (bf16[144,704]{1,0:T(8,128)(2,1)S(1)}, bf16[144,704]{1,0:T(8,128)(2,1)S(1)}, u32[]{:S(2)}, u32[]{:S(2)}) collective-permute-start(bf16[144,704]{1,0:T(8,128)(2,1)S(1)} %get-tuple-element.62), channel_id=1, source_target_pairs={{0,16},{8,24},{16,0},{24,8},{1,17},{9,25},{17,1},{25,9},{2,18},{10... | collective-permute-start | bytes 608264 | tf_op jit(solution)/shard_map/ppermute | solution.py:267
  32.5 1.4 %collective-permute-start.19 = (bf16[144,704]{1,0:T(8,128)(2,1)S(1)}, bf16[144,704]{1,0:T(8,128)(2,1)S(1)}, u32[]{:S(2)}, u32[]{:S(2)}) collective-permute-start(bf16[144,704]{1,0:T(8,128)(2,1)S(1)} %get-tuple-element.74), channel_id=1, source_target_pairs={{0,24},{8,16},{16,8},{24,0},{1,25},{9,17},{17,9},{25,1},{2,26},{10... | collective-permute-start | bytes 608264 | tf_op jit(solution)/shard_map/ppermute | solution.py:267
  33.9 2.6 %copy-done.1 = bf16[2,704,2048]{2,1,0:T(8,128)(2,1)S(1)} copy-done((bf16[2,704,2048]{2,1,0:T(8,128)(2,1)S(1)}, bf16[2,704,2048]{2,1,0:T(8,128)(2,1)}, u32[]{:S(2)}) %copy-start.1) | copy-done | bytes 5767192
  36.5 2.4 %mix_sibling.1 = bf16[512,1024]{1,0:T(8,128)(2,1)S(1)} custom-call(s32[2]{0:T(128)S(1)} %pad_add_fusion.1.place, bf16[144,768]{1,0:T(8,128)(2,1)S(1)} %get-tuple-element.54.refs_0_, bf16[144,768]{1,0:T(8,128)(2,1)S(1)} %collective-permute-done.7.refs_1_, bf16[144,768]{1,0:T(8,128)(2,1)S(1)} %collective-permute-done.8.refs_2_, ...), custom_call_target="tpu_custom_call" | custom-call | flops 1 | bytes 1 | tf_op jit(solution)/shard_map/mix_sibling/pallas_call | solution.py:234
  39.0 0.1 collective-permute-start.10
  39.0 2.4 %mix_own.1.own = f32[512,1024]{1,0:T(8,128)S(1)} custom-call(s32[2]{0:T(128)S(1)} %pad_add_fusion.1.place, bf16[144,768]{1,0:T(8,128)(2,1)S(1)} %get-tuple-element.54.refs_0_, bf16[144,768]{1,0:T(8,128)(2,1)S(1)} %collective-permute-done.7.refs_1_, bf16[144,768]{1,0:T(8,128)(2,1)S(1)} %collective-permute-done.8.refs_2_, ...), custom_call_target="tpu_custom_call" | custom-call | flops 99999997952 | bytes 1 | tf_op jit(solution)/shard_map/mix_own/pallas_call | solution.py:234
  41.5 0.2 collective-permute-done.10.arrived
  41.7 0.2 add.7
  41.9 1.5 %collective-permute-start.14 = (bf16[128,512]{1,0:T(8,128)(2,1)S(1)}, bf16[128,512]{1,0:T(8,128)(2,1)S(1)}, u32[]{:S(2)}, u32[]{:S(2)}) collective-permute-start(bf16[128,512]{1,0:T(8,128)(2,1)S(1)} %get-tuple-element.66), channel_id=1, source_target_pairs={{0,8},{8,0},{16,24},{24,16},{1,9},{9,1},{17,25},{25,17},{2,10},{10... | collective-permute-start | bytes 393224 | tf_op jit(solution)/shard_map/ppermute | solution.py:267
  43.4 0.6 %collective-permute-start.15 = (bf16[128,512]{1,0:T(8,128)(2,1)S(1)}, bf16[128,512]{1,0:T(8,128)(2,1)S(1)}, u32[]{:S(2)}, u32[]{:S(2)}) collective-permute-start(bf16[128,512]{1,0:T(8,128)(2,1)S(1)} %get-tuple-element.67), channel_id=1, source_target_pairs={{0,16},{8,24},{16,0},{24,8},{1,17},{9,25},{17,1},{25,9},{2,18},{10... | collective-permute-start | bytes 393224 | tf_op jit(solution)/shard_map/ppermute | solution.py:267
  44.0 1.0 %collective-permute-start.13 = (bf16[128,512]{1,0:T(8,128)(2,1)S(1)}, bf16[128,512]{1,0:T(8,128)(2,1)S(1)}, u32[]{:S(2)}, u32[]{:S(2)}) collective-permute-start(bf16[128,512]{1,0:T(8,128)(2,1)S(1)} %get-tuple-element.63), channel_id=1, source_target_pairs={{0,8},{8,0},{16,24},{24,16},{1,9},{9,1},{17,25},{25,17},{2,10},{10... | collective-permute-start | bytes 393224 | tf_op jit(solution)/shard_map/ppermute | solution.py:267
  45.0 1.0 %collective-permute-start.18 = (bf16[128,512]{1,0:T(8,128)(2,1)S(1)}, bf16[128,512]{1,0:T(8,128)(2,1)S(1)}, u32[]{:S(2)}, u32[]{:S(2)}) collective-permute-start(bf16[128,512]{1,0:T(8,128)(2,1)S(1)} %get-tuple-element.70), channel_id=1, source_target_pairs={{0,16},{8,24},{16,0},{24,8},{1,17},{9,25},{17,1},{25,9},{2,18},{10... | collective-permute-start | bytes 393224 | tf_op jit(solution)/shard_map/ppermute | solution.py:267
  46.0 2.3 %collective-permute-done.14.low = bf16[128,512]{1,0:T(8,128)(2,1)S(1)} collective-permute-done((bf16[128,512]{1,0:T(8,128)(2,1)S(1)}, bf16[128,512]{1,0:T(8,128)(2,1)S(1)}, u32[]{:S(2)}, u32[]{:S(2)}) %collective-permute-start.14) | collective-permute-done | bytes 131104 | tf_op jit(solution)/shard_map/ppermute | solution.py:267
  48.2 1.5 %collective-permute-done.15.high = bf16[128,512]{1,0:T(8,128)(2,1)S(1)} collective-permute-done((bf16[128,512]{1,0:T(8,128)(2,1)S(1)}, bf16[128,512]{1,0:T(8,128)(2,1)S(1)}, u32[]{:S(2)}, u32[]{:S(2)}) %collective-permute-start.15) | collective-permute-done | bytes 131104 | tf_op jit(solution)/shard_map/ppermute | solution.py:267
  49.8 0.6 %collective-permute-start.16 = (bf16[128,512]{1,0:T(8,128)(2,1)S(1)}, bf16[128,512]{1,0:T(8,128)(2,1)S(1)}, u32[]{:S(2)}, u32[]{:S(2)}) collective-permute-start(bf16[128,512]{1,0:T(8,128)(2,1)S(1)} %get-tuple-element.68), channel_id=1, source_target_pairs={{0,8},{8,0},{16,24},{24,16},{1,9},{9,1},{17,25},{25,17},{2,10},{10... | collective-permute-start | bytes 393224 | tf_op jit(solution)/shard_map/ppermute | solution.py:267
  50.4 1.0 %collective-permute-start.17 = (bf16[128,512]{1,0:T(8,128)(2,1)S(1)}, bf16[128,512]{1,0:T(8,128)(2,1)S(1)}, u32[]{:S(2)}, u32[]{:S(2)}) collective-permute-start(bf16[128,512]{1,0:T(8,128)(2,1)S(1)} %get-tuple-element.69), channel_id=1, source_target_pairs={{0,16},{8,24},{16,0},{24,8},{1,17},{9,25},{17,1},{25,9},{2,18},{10... | collective-permute-start | bytes 393224 | tf_op jit(solution)/shard_map/ppermute | solution.py:267
  51.4 2.3 %restore.1 = bf16[4,704,128]{2,1,0:T(8,128)(2,1)} custom-call(s32[2]{0:T(128)S(1)} %pad_add_fusion.1.place, s32[8,128]{1,0:T(8,128)S(1)} %pad_add_fusion.meta_ref, bf16[144,704]{1,0:T(8,128)(2,1)S(1)} %get-tuple-element.71.refs_0_, bf16[144,704]{1,0:T(8,128)(2,1)S(1)} %collective-permute-done.11.refs_1_, ...), custom_call_target="tpu_custom_call" | custom-call | flops 99999997952 | bytes 1 | tf_op jit(solution)/shard_map/restore/pallas_call | solution.py:234
  53.7 0.0 collective-permute-done.13.one_low
  53.7 1.1 %collective-permute-done.16.one_high = bf16[128,512]{1,0:T(8,128)(2,1)S(1)} collective-permute-done((bf16[128,512]{1,0:T(8,128)(2,1)S(1)}, bf16[128,512]{1,0:T(8,128)(2,1)S(1)}, u32[]{:S(2)}, u32[]{:S(2)}) %collective-permute-start.16) | collective-permute-done | bytes 131104 | tf_op jit(solution)/shard_map/ppermute | solution.py:267
  54.8 0.5 collective-permute-done.17.two_low
  55.4 0.8 %finish.1 = bf16[128,1024]{1,0:T(8,128)(2,1)} custom-call(f32[128,1024]{1,0:T(8,128)S(1)} %get-tuple-element.58.mine, bf16[128,512]{1,0:T(8,128)(2,1)S(1)} %collective-permute-done.13.one_low, bf16[128,512]{1,0:T(8,128)(2,1)S(1)} %collective-permute-done.16.one_high, bf16[128,512]{1,0:T(8,128)(2,1)S(1)} %collective-permute-done.17.two_low, ...), custom_call_target="tpu_custom_call" | custom-call | flops 1 | bytes 1 | tf_op jit(solution)/shard_map/finish/pallas_call | solution.py:234
  (11 shorter events, 0.1 us)
Async XLA Ops:
  2.3 5.5 %collective-permute-start.3 = (bf16[136,1024]{1,0:T(8,128)(2,1)S(1)}, bf16[136,1024]{1,0:T(8,128)(2,1)S(1)}, u32[]{:S(2)}, u32[]{:S(2)}) collective-permute-start(bf16[136,1024]{1,0:T(8,128)(2,1)S(1)} %fusion.1.refs_0_), channel_id=1, source_target_pairs={{0,1},{1,0},{2,3},{3,2},{4,5},{5,4},{6,7},{7,6},{8,9},{9,8},{10,11... | collective-permute-start | bytes 835592 | tf_op jit(solution)/shard_map/ppermute | solution.py:270
  2.8 11.1 %collective-permute-start.6 = (bf16[136,1024]{1,0:T(8,128)(2,1)S(1)}, bf16[136,1024]{1,0:T(8,128)(2,1)S(1)}, u32[]{:S(2)}, u32[]{:S(2)}) collective-permute-start(bf16[136,1024]{1,0:T(8,128)(2,1)S(1)} %fusion.1.refs_0_), channel_id=1, source_target_pairs={{0,24},{8,16},{16,8},{24,0},{1,25},{9,17},{17,9},{25,1},{2,26},{10... | collective-permute-start | bytes 835592 | tf_op jit(solution)/shard_map/ppermute | solution.py:267
  6.3 13.3 %collective-permute-start.5 = (bf16[136,1024]{1,0:T(8,128)(2,1)S(1)}, bf16[136,1024]{1,0:T(8,128)(2,1)S(1)}, u32[]{:S(2)}, u32[]{:S(2)}) collective-permute-start(bf16[136,1024]{1,0:T(8,128)(2,1)S(1)} %fusion.1.refs_0_), channel_id=1, source_target_pairs={{0,16},{8,24},{16,0},{24,8},{1,17},{9,25},{17,1},{25,9},{2,18},{10... | collective-permute-start | bytes 835592 | tf_op jit(solution)/shard_map/ppermute | solution.py:267
  6.8 13.5 %collective-permute-start.4 = (bf16[136,1024]{1,0:T(8,128)(2,1)S(1)}, bf16[136,1024]{1,0:T(8,128)(2,1)S(1)}, u32[]{:S(2)}, u32[]{:S(2)}) collective-permute-start(bf16[136,1024]{1,0:T(8,128)(2,1)S(1)} %fusion.1.refs_0_), channel_id=1, source_target_pairs={{0,8},{8,0},{16,24},{24,16},{1,9},{9,1},{17,25},{25,17},{2,10},{10... | collective-permute-start | bytes 835592 | tf_op jit(solution)/shard_map/ppermute | solution.py:267
  7.8 1.1 %copy-start.2 = (bf16[128,4,704]{0,2,1:T(8,128)(2,1)S(1)}, bf16[128,4,704]{0,2,1:T(8,128)(2,1)}, u32[]{:S(2)}) copy-start(bf16[128,4,704]{0,2,1:T(8,128)(2,1)} %param.7) | copy-start | bytes 2162692
  10.2 22.2 %collective-permute-start.7 = (bf16[144,768]{1,0:T(8,128)(2,1)S(1)}, bf16[144,768]{1,0:T(8,128)(2,1)S(1)}, u32[]{:S(2)}, u32[]{:S(2)}) collective-permute-start(bf16[144,768]{1,0:T(8,128)(2,1)S(1)} %get-tuple-element.55), channel_id=1, source_target_pairs={{0,8},{8,0},{16,24},{24,16},{1,9},{9,1},{17,25},{25,17},{2,10},{10... | collective-permute-start | bytes 663560 | tf_op jit(solution)/shard_map/ppermute | solution.py:267
  12.2 21.7 %collective-permute-start.8 = (bf16[144,768]{1,0:T(8,128)(2,1)S(1)}, bf16[144,768]{1,0:T(8,128)(2,1)S(1)}, u32[]{:S(2)}, u32[]{:S(2)}) collective-permute-start(bf16[144,768]{1,0:T(8,128)(2,1)S(1)} %get-tuple-element.56), channel_id=1, source_target_pairs={{0,16},{8,24},{16,0},{24,8},{1,17},{9,25},{17,1},{25,9},{2,18},{10... | collective-permute-start | bytes 663560 | tf_op jit(solution)/shard_map/ppermute | solution.py:267
  13.9 20.0 %collective-permute-start.9 = (bf16[144,768]{1,0:T(8,128)(2,1)S(1)}, bf16[144,768]{1,0:T(8,128)(2,1)S(1)}, u32[]{:S(2)}, u32[]{:S(2)}) collective-permute-start(bf16[144,768]{1,0:T(8,128)(2,1)S(1)} %get-tuple-element.57), channel_id=1, source_target_pairs={{0,24},{8,16},{16,8},{24,0},{1,25},{9,17},{17,9},{25,1},{2,26},{10... | collective-permute-start | bytes 663560 | tf_op jit(solution)/shard_map/ppermute | solution.py:267
  20.3 1.7 %collective-permute-start = (bf16[136,1024]{1,0:T(8,128)(2,1)S(1)}, bf16[136,1024]{1,0:T(8,128)(2,1)}, u32[]{:S(2)}, u32[]{:S(2)}) collective-permute-start(bf16[136,1024]{1,0:T(8,128)(2,1)S(1)} %get-tuple-element.12), channel_id=1, source_target_pairs={{0,1},{1,0},{2,3},{3,2},{4,5},{5,4},{6,7},{7,6},{8,9},{9,8},{10,11... | collective-permute-start | bytes 835592 | tf_op jit(solution)/shard_map/cond/branch_1_fun/ppermute | solution.py:270
  20.3 2.1 %collective-permute-start.1 = (bf16[136,1024]{1,0:T(8,128)(2,1)S(1)}, bf16[136,1024]{1,0:T(8,128)(2,1)}, u32[]{:S(2)}, u32[]{:S(2)}) collective-permute-start(bf16[136,1024]{1,0:T(8,128)(2,1)S(1)} %get-tuple-element.15), channel_id=1, source_target_pairs={{0,1},{1,0},{2,3},{3,2},{4,5},{5,4},{6,7},{7,6},{8,9},{9,8},{10,11... | collective-permute-start | bytes 835592 | tf_op jit(solution)/shard_map/cond/branch_1_fun/ppermute | solution.py:270
  22.0 1.7 %collective-permute-start.2 = (bf16[136,1024]{1,0:T(8,128)(2,1)S(1)}, bf16[136,1024]{1,0:T(8,128)(2,1)}, u32[]{:S(2)}, u32[]{:S(2)}) collective-permute-start(bf16[136,1024]{1,0:T(8,128)(2,1)S(1)} %get-tuple-element.16), channel_id=1, source_target_pairs={{0,1},{1,0},{2,3},{3,2},{4,5},{5,4},{6,7},{7,6},{8,9},{9,8},{10,11... | collective-permute-start | bytes 835592 | tf_op jit(solution)/shard_map/cond/branch_1_fun/ppermute | solution.py:270
  23.7 2.6 %copy-start = (bf16[2,704,2048]{2,1,0:T(8,128)(2,1)S(1)}, bf16[2,704,2048]{2,1,0:T(8,128)(2,1)}, u32[]{:S(2)}) copy-start(bf16[2,704,2048]{2,1,0:T(8,128)(2,1)} %refs_4_.3) | copy-start | bytes 17301508
  30.3 13.7 %collective-permute-start.11 = (bf16[144,704]{1,0:T(8,128)(2,1)S(1)}, bf16[144,704]{1,0:T(8,128)(2,1)S(1)}, u32[]{:S(2)}, u32[]{:S(2)}) collective-permute-start(bf16[144,704]{1,0:T(8,128)(2,1)S(1)} %get-tuple-element.61), channel_id=1, source_target_pairs={{0,8},{8,0},{16,24},{24,16},{1,9},{9,1},{17,25},{25,17},{2,10},{10... | collective-permute-start | bytes 608264 | tf_op jit(solution)/shard_map/ppermute | solution.py:267
  31.9 12.2 %collective-permute-start.12 = (bf16[144,704]{1,0:T(8,128)(2,1)S(1)}, bf16[144,704]{1,0:T(8,128)(2,1)S(1)}, u32[]{:S(2)}, u32[]{:S(2)}) collective-permute-start(bf16[144,704]{1,0:T(8,128)(2,1)S(1)} %get-tuple-element.62), channel_id=1, source_target_pairs={{0,16},{8,24},{16,0},{24,8},{1,17},{9,25},{17,1},{25,9},{2,18},{10... | collective-permute-start | bytes 608264 | tf_op jit(solution)/shard_map/ppermute | solution.py:267
  32.5 18.9 %collective-permute-start.19 = (bf16[144,704]{1,0:T(8,128)(2,1)S(1)}, bf16[144,704]{1,0:T(8,128)(2,1)S(1)}, u32[]{:S(2)}, u32[]{:S(2)}) collective-permute-start(bf16[144,704]{1,0:T(8,128)(2,1)S(1)} %get-tuple-element.74), channel_id=1, source_target_pairs={{0,24},{8,16},{16,8},{24,0},{1,25},{9,17},{17,9},{25,1},{2,26},{10... | collective-permute-start | bytes 608264 | tf_op jit(solution)/shard_map/ppermute | solution.py:267
  33.9 2.6 %copy-start.1 = (bf16[2,704,2048]{2,1,0:T(8,128)(2,1)S(1)}, bf16[2,704,2048]{2,1,0:T(8,128)(2,1)}, u32[]{:S(2)}) copy-start(bf16[2,704,2048]{2,1,0:T(8,128)(2,1)} %refs_4_.3) | copy-start | bytes 17301508
  39.0 2.7 %collective-permute-start.10 = (bf16[512,1024]{1,0:T(8,128)(2,1)S(1)}, bf16[512,1024]{1,0:T(8,128)(2,1)S(1)}, u32[]{:S(2)}, u32[]{:S(2)}) collective-permute-start(bf16[512,1024]{1,0:T(8,128)(2,1)S(1)} %mix_sibling.1), channel_id=1, source_target_pairs={{0,1},{1,0},{2,3},{3,2},{4,5},{5,4},{6,7},{7,6},{8,9},{9,8},{10,11... | collective-permute-start | bytes 3145736 | tf_op jit(solution)/shard_map/ppermute | solution.py:270
  41.9 6.4 %collective-permute-start.14 = (bf16[128,512]{1,0:T(8,128)(2,1)S(1)}, bf16[128,512]{1,0:T(8,128)(2,1)S(1)}, u32[]{:S(2)}, u32[]{:S(2)}) collective-permute-start(bf16[128,512]{1,0:T(8,128)(2,1)S(1)} %get-tuple-element.66), channel_id=1, source_target_pairs={{0,8},{8,0},{16,24},{24,16},{1,9},{9,1},{17,25},{25,17},{2,10},{10... | collective-permute-start | bytes 393224 | tf_op jit(solution)/shard_map/ppermute | solution.py:267
  43.4 6.4 %collective-permute-start.15 = (bf16[128,512]{1,0:T(8,128)(2,1)S(1)}, bf16[128,512]{1,0:T(8,128)(2,1)S(1)}, u32[]{:S(2)}, u32[]{:S(2)}) collective-permute-start(bf16[128,512]{1,0:T(8,128)(2,1)S(1)} %get-tuple-element.67), channel_id=1, source_target_pairs={{0,16},{8,24},{16,0},{24,8},{1,17},{9,25},{17,1},{25,9},{2,18},{10... | collective-permute-start | bytes 393224 | tf_op jit(solution)/shard_map/ppermute | solution.py:267
  44.0 9.7 %collective-permute-start.13 = (bf16[128,512]{1,0:T(8,128)(2,1)S(1)}, bf16[128,512]{1,0:T(8,128)(2,1)S(1)}, u32[]{:S(2)}, u32[]{:S(2)}) collective-permute-start(bf16[128,512]{1,0:T(8,128)(2,1)S(1)} %get-tuple-element.63), channel_id=1, source_target_pairs={{0,8},{8,0},{16,24},{24,16},{1,9},{9,1},{17,25},{25,17},{2,10},{10... | collective-permute-start | bytes 393224 | tf_op jit(solution)/shard_map/ppermute | solution.py:267
  45.0 8.7 %collective-permute-start.18 = (bf16[128,512]{1,0:T(8,128)(2,1)S(1)}, bf16[128,512]{1,0:T(8,128)(2,1)S(1)}, u32[]{:S(2)}, u32[]{:S(2)}) collective-permute-start(bf16[128,512]{1,0:T(8,128)(2,1)S(1)} %get-tuple-element.70), channel_id=1, source_target_pairs={{0,16},{8,24},{16,0},{24,8},{1,17},{9,25},{17,1},{25,9},{2,18},{10... | collective-permute-start | bytes 393224 | tf_op jit(solution)/shard_map/ppermute | solution.py:267
  49.8 5.0 %collective-permute-start.16 = (bf16[128,512]{1,0:T(8,128)(2,1)S(1)}, bf16[128,512]{1,0:T(8,128)(2,1)S(1)}, u32[]{:S(2)}, u32[]{:S(2)}) collective-permute-start(bf16[128,512]{1,0:T(8,128)(2,1)S(1)} %get-tuple-element.68), channel_id=1, source_target_pairs={{0,8},{8,0},{16,24},{24,16},{1,9},{9,1},{17,25},{25,17},{2,10},{10... | collective-permute-start | bytes 393224 | tf_op jit(solution)/shard_map/ppermute | solution.py:267
  50.4 5.0 %collective-permute-start.17 = (bf16[128,512]{1,0:T(8,128)(2,1)S(1)}, bf16[128,512]{1,0:T(8,128)(2,1)S(1)}, u32[]{:S(2)}, u32[]{:S(2)}) collective-permute-start(bf16[128,512]{1,0:T(8,128)(2,1)S(1)} %get-tuple-element.69), channel_id=1, source_target_pairs={{0,16},{8,24},{16,0},{24,8},{1,17},{9,25},{17,1},{25,9},{2,18},{10... | collective-permute-start | bytes 393224 | tf_op jit(solution)/shard_map/ppermute | solution.py:267

commit v7 on v6

--- a/solution.py
+++ b/solution.py
@@ -122,10 +122,15 @@
 def grad_kernel(dims, top, place, *refs):
     experts, local, cap, width = dims
     n = experts // local
-    own, other, w_ref = refs[:n], refs[n : 2 * n], refs[2 * n]
-    outs, x_ref = refs[2 * n + 1 : -1], refs[-1]
+    own, other, w_hbm = refs[:n], refs[n : 2 * n], refs[2 * n]
+    outs, (x_ref, w_ref, sems) = refs[2 * n + 1 : -3], refs[-3:]
     half = own[0].shape[1]
     tokens = own[0].shape[0] - 8
+
+    def copy(l):
+        return pltpu.make_async_copy(w_hbm.at[l], w_ref.at[l], sems.at[l])
+
+    copy(0).start()
     chunk = min(half, 512)
     held = []
     for ref in own:
@@ -139,16 +144,30 @@
             at = pl.ds(pl.multiple_of(side * half + c, chunk), chunk)
             for l, x in enumerate(by_expert(rows, local, cap)):
                 x_ref[l, :, at] = x.astype(BF16)
-    grads = [dot(x_ref[l], w_ref[l], NT) for l in range(local)]
+    grads = []
+    for l in range(local):
+        copy(l).wait()
+        if l + 1 < local:
+            copy(l + 1).start()
+        grads.append(dot(x_ref[l], w_ref[l], NT))
     for s, rows in enumerate(by_source(grads, n, cap)):
         outs[s][...] = rows.astype(BF16)
 
 
-def mix_rows(dims, side, hid, w_ref, tokens, half, store):
+def mix_rows(dims, side, hid, w_hbm, w_ref, sems, tokens, half, store):
     experts, local, cap, width = dims
     n = len(hid)
     ff = w_ref.shape[1]
     chunk = min(half, 256)
+    count = half // chunk
+
+    def copy(i):
+        source = pl.ds(pl.multiple_of(side * half + i * chunk, chunk), chunk)
+        return pltpu.make_async_copy(
+            w_hbm.at[:, :, source], w_ref.at[:, :, pl.ds(i * chunk, chunk)], sems.at[i]
+        )
+
+    copy(0).start()
     same = ones_where(iota((tokens, tokens), 0) == iota((tokens, tokens), 1))
     held = []
     for h in hid:
@@ -157,34 +176,37 @@
         held.append(dot(same, slots, NT).astype(BF16))
     rows = [h[:, :ff].astype(F32) for h in hid]
     x = [r.astype(BF16) for r in by_expert(rows, local, cap)]
-    for c in range(0, half, chunk):
-        at = pl.ds(pl.multiple_of(side * half + c, chunk), chunk)
-        out = [dot(x[l], w_ref[l, :, at], NN) for l in range(local)]
+    for i in range(count):
+        copy(i).wait()
+        if i + 1 < count:
+            copy(i + 1).start()
+        columns = slice(i * chunk, (i + 1) * chunk)
+        out = [dot(x[l], w_ref[l, :, columns], NN) for l in range(local)]
         for s, rows in enumerate(by_source(out, n, cap)):
-            store(s, slice(c, c + chunk), dot(held[s], rows.astype(BF16), NN))
+            store(s, columns, dot(held[s], rows.astype(BF16), NN))
 
 
 def mix_kernel(dims, sibling, place, *refs):
-    hid, (w_ref, out) = refs[:-2], refs[-2:]
+    hid, (w_hbm, out, w_ref, sems) = refs[:-4], refs[-4:]
     tokens = out.shape[0] // len(hid)
 
     def store(s, columns, part):
         out[pl.ds(s * tokens, tokens), columns] = part.astype(out.dtype)
 
     side = 1 - place[1] if sibling else place[1]
-    mix_rows(dims, side, hid, w_ref, tokens, out.shape[1], store)
+    mix_rows(dims, side, hid, w_hbm, w_ref, sems, tokens, out.shape[1], store)
 
 
 def mix_add_kernel(dims, place, *refs):
-    n = (len(refs) - 2) // 2
-    hid, (w_ref, arrived), outs = refs[:n], refs[n : n + 2], refs[n + 2 :]
+    n = (len(refs) - 4) // 2
+    hid, (w_hbm, arrived), outs = refs[:n], refs[n : n + 2], refs[n + 2 : -2]
     tokens, half = outs[0].shape
 
     def store(s, columns, part):
         theirs = arrived[pl.ds(s * tokens, tokens), columns].astype(F32)
         outs[s][:, columns] = (part + theirs).astype(BF16)
 
-    mix_rows(dims, place[1], hid, w_ref, tokens, half, store)
+    mix_rows(dims, place[1], hid, w_hbm, refs[-2], refs[-1], tokens, half, store)
 
 
 def add_split_kernel(own, arrived, mine, one_low, one_high, two_low, two_high, low, high):
@@ -279,28 +301,46 @@
     meta, swapped = lax.optimization_barrier((meta, swapped))
     hid_sent = run(
         functools.partial(dispatch_kernel, dims), [shaped((width, -(-(ff + 1) // 128) * 128))] * n,
-        [place, meta, hid_t], where=placed, name="dispatch", weight=BIG,
+        [place, meta, hid_t], where=placed, name="dispatch",
     )
     hid = [send(hid_sent[s], s) for s in range(n)]
     slot = shaped((width, ff))
 
-    def taken(own):
-        other = [swap(x) for x in own[:2]]
-        for x in own[2:]:
-            other[-2], x = lax.optimization_barrier((other[-2], x))
-            other.append(swap(x))
-        return other
-
-    other = [swapped] + lax.cond(place[0] < 1000, taken, list, own[1:])
-    grad_sent = run(
-        functools.partial(grad_kernel, dims, top), [slot] * n,
-        [place, *own, *other, w_down], where=placed,
-        scratch=[pltpu.VMEM((local, n * cap, full), BF16)], name="grad",
-    )
+    def grads(own, other, w):
+        return list(run(
+            functools.partial(grad_kernel, dims, top), [slot] * n,
+            [place, *own, *other, w], where={**placed, 2 * n + 1: pl.ANY},
+            scratch=[
+                pltpu.VMEM((local, n * cap, full), BF16),
+                pltpu.VMEM(w.shape, BF16),
+                pltpu.SemaphoreType.DMA((local,)),
+            ],
+            name="grad",
+        ))
+
+    def last_swaps(own, first, last, w):
+        return grads(own, [first] + [swap(x) for x in own[1 : n - 1]] + [last], w)
+
+    if forward:
+        always = place[0] < 1000
+        last = lax.cond(always, swap, lambda x: x, own[3])
+        *own[1:3], last = lax.optimization_barrier((*own[1:3], last))
+        grad_sent = lax.cond(
+            always, last_swaps, lambda *unused: [jnp.zeros((width, ff), BF16)] * n,
+            own, swapped, last, w_down,
+        )
+    else:
+        grad_sent = last_swaps(own, swapped, swap(own[-1]), w_down)
     hid[0], grad_own = lax.optimization_barrier((hid[0], grad_sent[0]))
     grad_back = [grad_own] + [send(grad_sent[s], s) for s in range(1, n)]
 
-    mixing = dict(where=placed)
+    mixing = dict(
+        where={**placed, n + 1: pl.ANY},
+        scratch=[
+            pltpu.VMEM((local, ff, half), BF16),
+            pltpu.SemaphoreType.DMA((half // min(half, 256),)),
+        ],
+    )
     (theirs,) = run(
         functools.partial(mix_kernel, dims, True), [shaped((n * tokens, half))],
         [place, *hid, w_down], name="mix_sibling", **mixing,

time: 56.5 us -> 59.8 us (1.058)
  Pallas kernels: 13.5 us -> 23.7 us
  local copies, waits for them, and re-layouts: 6.37 us -> 1.11 us
  waiting for transfers between devices: 12.2 us -> 10.2 us
    pallas_call x8, Pallas kernels: 13.5 us -> 23.7 us  [call(): pl.pallas_call(kernel, out_shape=outs, in_specs=[pl.BlockSpec(memory_spac...]
    unnamed x6 -> x2, local copies, waits for them, and re-layouts: 6.37 us -> 1.11 us
    ppermute x15, waiting for transfers between devices: 9.24 us -> 7.06 us  [send(): return lax.ppermute(x, 'ctx', [(i, i ^ s) for i in range(n)]) if s else x]
  transfers between devices with their start and end apart: 20 -> 20, of which waited for: 11 -> 10; matrix products, arithmetic and copies ran while one was open for 1% -> 1% of each run, Pallas kernels for 23% -> 39%
where the time goes in v7:
time: 59.8 us; the launch traced here: 59.1 us
  Pallas kernels  23.7 us (40%)
  starting transfers between devices  20.9 us (35%)
  waiting for transfers between devices  10.2 us (17%)
  other arithmetic  2.44 us (4%)
  local copies, waits for them, and re-layouts  1.11 us (2%)
  between operations  0.71 us (1%)
    pallas_call x8, Pallas kernels, call(): pl.pallas_call(kernel, out_shape=outs, in_specs=[pl.BlockSpec(memory_spac...  23.7 us
    ppermute x15, starting transfers between devices, send(): return lax.ppermute(x, 'ctx', [(i, i ^ s) for i in range(n)]) if s else x  19.8 us
    ppermute x15, waiting for transfers between devices, send(): return lax.ppermute(x, 'ctx', [(i, i ^ s) for i in range(n)]) if s else x  7.06 us
    ppermute x5, waiting for transfers between devices, swap(): return lax.ppermute(x, 'tp', [(0, 1), (1, 0)])  3.14 us
  transfers between devices with their start and end apart: 20, of which 10 were waited for; matrix products, arithmetic and copies ran while one was open for 1% of the time, Pallas kernels for 39%

profile of v7, /device:TPU:0, one launch (start us, length us, event | category | flops | bytes accessed | tf_op | source)
XLA Modules:
  0.0 59.1 jit_solution(10035967287084699696)
XLA Ops:
  0.6 0.7 %bitcast_convert_fusion = bf16[4,128]{1,0:T(4,128)(2,1)S(1)} fusion(s32[128,4]{0,1:T(4,128)} %param.10), kind=kLoop, calls=%fused_computation.5 | loop fusion | flops 512 | bytes 3072 | tf_op jit(solution)/shard_map/convert_element_type | solution.py:296
  1.3 1.0 %fusion.1 = bf16[136,1024]{1,0:T(8,128)(2,1)S(1)} fusion(bf16[4,128]{1,0:T(4,128)(2,1)S(1)} %bitcast_convert_fusion, bf16[128,1024]{1,0:T(8,128)(2,1)} %param.12), kind=kLoop, calls=%fused_computation.2 | loop fusion | flops 835584 | bytes 541696 | tf_op jit(solution)/shard_map/concatenate | solution.py:297
  2.3 0.5 collective-permute-start.3
  2.8 3.5 %collective-permute-start.6 = (bf16[136,1024]{1,0:T(8,128)(2,1)S(1)}, bf16[136,1024]{1,0:T(8,128)(2,1)S(1)}, u32[]{:S(2)}, u32[]{:S(2)}) collective-permute-start(bf16[136,1024]{1,0:T(8,128)(2,1)S(1)} %fusion.1), channel_id=1, source_target_pairs={{0,24},{8,16},{16,8},{24,0},{1,25},{9,17},{17,9},{25,1},{2,26},{10... | collective-permute-start | bytes 835592 | tf_op jit(solution)/shard_map/ppermute | solution.py:289
  6.3 0.5 collective-permute-start.5
  6.8 0.1 collective-permute-start.4
  7.0 0.7 %pad_add_fusion.meta_ref = s32[8,128]{1,0:T(8,128)S(1)} fusion(s32[4,128]{1,0:T(4,128)} %bitcast.9, s32[4,128]{1,0:T(4,128)} %bitcast.8), kind=kLoop, calls=%fused_computation.3 | loop fusion | flops 1024 | bytes 8192 | tf_op jit(solution)/shard_map/concatenate | solution.py:294
  7.7 0.1 pad_add_fusion.1.place
  7.8 0.0 collective-permute-done.3
  7.8 1.1 %copy-done = bf16[128,4,704]{0,2,1:T(8,128)(2,1)S(1)} copy-done((bf16[128,4,704]{0,2,1:T(8,128)(2,1)S(1)}, bf16[128,4,704]{0,2,1:T(8,128)(2,1)}, u32[]{:S(2)}) %copy-start) | copy-done | bytes 720920
  8.9 1.4 %dispatch.1 = (bf16[144,768]{1,0:T(8,128)(2,1)S(1)}, bf16[144,768]{1,0:T(8,128)(2,1)S(1)}, bf16[144,768]{1,0:T(8,128)(2,1)S(1)}, bf16[144,768]{1,0:T(8,128)(2,1)S(1)}) custom-call(s32[2]{0:T(128)S(1)} %pad_add_fusion.1.place, s32[8,128]{1,0:T(8,128)S(1)} %pad_add_fusion.meta_ref, bf16[4,704,128]{2,1,0:T(8,128)(2,1)S(1)} %bitcast.7), custom_call_target="tpu_custom_call" | custom-call | flops 1 | bytes 1 | tf_op jit(solution)/shard_map/dispatch/pallas_call | solution.py:256
  10.2 2.0 %collective-permute-start.7 = (bf16[144,768]{1,0:T(8,128)(2,1)S(1)}, bf16[144,768]{1,0:T(8,128)(2,1)S(1)}, u32[]{:S(2)}, u32[]{:S(2)}) collective-permute-start(bf16[144,768]{1,0:T(8,128)(2,1)S(1)} %get-tuple-element.67), channel_id=1, source_target_pairs={{0,8},{8,0},{16,24},{24,16},{1,9},{9,1},{17,25},{25,17},{2,10},{10... | collective-permute-start | bytes 663560 | tf_op jit(solution)/shard_map/ppermute | solution.py:289
  12.2 1.5 %collective-permute-start.8 = (bf16[144,768]{1,0:T(8,128)(2,1)S(1)}, bf16[144,768]{1,0:T(8,128)(2,1)S(1)}, u32[]{:S(2)}, u32[]{:S(2)}) collective-permute-start(bf16[144,768]{1,0:T(8,128)(2,1)S(1)} %get-tuple-element.68), channel_id=1, source_target_pairs={{0,16},{8,24},{16,0},{24,8},{1,17},{9,25},{17,1},{25,9},{2,18},{10... | collective-permute-start | bytes 663560 | tf_op jit(solution)/shard_map/ppermute | solution.py:289
  13.7 0.2 collective-permute-done.6
  13.9 1.7 %conditional.2 = (bf16[136,1024]{1,0:T(8,128)(2,1)}) conditional(s32[]{:T(128)} %convert_element_type.10, bf16[136,1024]{1,0:T(8,128)(2,1)S(1)} %collective-permute-done.6, bf16[136,1024]{1,0:T(8,128)(2,1)S(1)} %collective-permute-done.6), branch_computations={%region_0.1_spmd, %region_1.2_spmd} | conditional | bytes 1114160 | solution.py:326
  13.9 0.0 collective-permute-start
  13.9 1.7 %collective-permute-done = bf16[136,1024]{1,0:T(8,128)(2,1)} collective-permute-done((bf16[136,1024]{1,0:T(8,128)(2,1)S(1)}, bf16[136,1024]{1,0:T(8,128)(2,1)}, u32[]{:S(2)}, u32[]{:S(2)}) %collective-permute-start) | collective-permute-done | bytes 278560 | tf_op jit(solution)/shard_map/cond/branch_1_fun/ppermute | solution.py:292
  15.6 2.8 %collective-permute-start.9 = (bf16[144,768]{1,0:T(8,128)(2,1)S(1)}, bf16[144,768]{1,0:T(8,128)(2,1)S(1)}, u32[]{:S(2)}, u32[]{:S(2)}) collective-permute-start(bf16[144,768]{1,0:T(8,128)(2,1)S(1)} %get-tuple-element.69), channel_id=1, source_target_pairs={{0,24},{8,16},{16,8},{24,0},{1,25},{9,17},{17,9},{25,1},{2,26},{10... | collective-permute-start | bytes 663560 | tf_op jit(solution)/shard_map/ppermute | solution.py:289
  18.4 1.2 %collective-permute-done.5 = bf16[136,1024]{1,0:T(8,128)(2,1)S(1)} collective-permute-done((bf16[136,1024]{1,0:T(8,128)(2,1)S(1)}, bf16[136,1024]{1,0:T(8,128)(2,1)S(1)}, u32[]{:S(2)}, u32[]{:S(2)}) %collective-permute-start.5) | collective-permute-done | bytes 278560 | tf_op jit(solution)/shard_map/ppermute | solution.py:289
  19.6 0.7 %collective-permute-done.4 = bf16[136,1024]{1,0:T(8,128)(2,1)S(1)} collective-permute-done((bf16[136,1024]{1,0:T(8,128)(2,1)S(1)}, bf16[136,1024]{1,0:T(8,128)(2,1)S(1)}, u32[]{:S(2)}, u32[]{:S(2)}) %collective-permute-start.4) | collective-permute-done | bytes 278560 | tf_op jit(solution)/shard_map/ppermute | solution.py:289
  20.3 9.4 %conditional.3 = ((bf16[144,704]{1,0:T(8,128)(2,1)}, bf16[144,704]{1,0:T(8,128)(2,1)}, bf16[144,704]{1,0:T(8,128)(2,1)S(1)}, bf16[144,704]{1,0:T(8,128)(2,1)S(1)})) conditional(s32[]{:T(128)} %convert_element_type.10, () %tuple.26, (bf16[136,1024]{1,0:T(8,128)(2,1)S(1)}, bf16[136,1024]{1,0:T(8,128)(2,1)S(1)}, s32[2]{0:T(128)S(1)}, ...), branch_computations={%region_2.3_spmd, %region_3.4_spmd} | conditional | flops 1 | bytes 2228313 | solution.py:328
  20.3 0.0 collective-permute-start.1
  20.3 0.5 collective-permute-start.2
  20.8 1.0 %collective-permute-done.1.refs_5_ = bf16[136,1024]{1,0:T(8,128)(2,1)S(1)} collective-permute-done((bf16[136,1024]{1,0:T(8,128)(2,1)S(1)}, bf16[136,1024]{1,0:T(8,128)(2,1)S(1)}, u32[]{:S(2)}, u32[]{:S(2)}) %collective-permute-start.1) | collective-permute-done | bytes 278560 | tf_op jit(solution)/shard_map/cond/branch_1_fun/ppermute | solution.py:292
  21.9 0.4 collective-permute-done.2.refs_6_
  22.3 7.5 %grad.1 = (bf16[144,704]{1,0:T(8,128)(2,1)}, bf16[144,704]{1,0:T(8,128)(2,1)}, bf16[144,704]{1,0:T(8,128)(2,1)S(1)}, bf16[144,704]{1,0:T(8,128)(2,1)S(1)}) custom-call(s32[2]{0:T(128)S(1)} %get-tuple-element.21.place, bf16[136,1024]{1,0:T(8,128)(2,1)S(1)} %get-tuple-element.22.refs_0_, bf16[136,1024]{1,0:T(8,128)(2,1)S(1)} %get-tuple-element.23.refs_1_, ...), custom_call_target="tpu_custom_call" | custom-call | flops 1 | bytes 1 | tf_op jit(solution)/shard_map/cond/branch_1_fun/grad/pallas_call | solution.py:256
  29.7 1.6 %collective-permute-start.11 = (bf16[144,704]{1,0:T(8,128)(2,1)}, bf16[144,704]{1,0:T(8,128)(2,1)S(1)}, u32[]{:S(2)}, u32[]{:S(2)}) collective-permute-start(bf16[144,704]{1,0:T(8,128)(2,1)} %get-tuple-element.73), channel_id=1, source_target_pairs={{0,8},{8,0},{16,24},{24,16},{1,9},{9,1},{17,25},{25,17},{2,10},{10... | collective-permute-start | bytes 608264 | tf_op jit(solution)/shard_map/ppermute | solution.py:289
  31.3 0.6 %collective-permute-start.12 = (bf16[144,704]{1,0:T(8,128)(2,1)S(1)}, bf16[144,704]{1,0:T(8,128)(2,1)S(1)}, u32[]{:S(2)}, u32[]{:S(2)}) collective-permute-start(bf16[144,704]{1,0:T(8,128)(2,1)S(1)} %get-tuple-element.74), channel_id=1, source_target_pairs={{0,16},{8,24},{16,0},{24,8},{1,17},{9,25},{17,1},{25,9},{2,18},{10... | collective-permute-start | bytes 608264 | tf_op jit(solution)/shard_map/ppermute | solution.py:289
  31.9 1.4 %collective-permute-start.19 = (bf16[144,704]{1,0:T(8,128)(2,1)S(1)}, bf16[144,704]{1,0:T(8,128)(2,1)S(1)}, u32[]{:S(2)}, u32[]{:S(2)}) collective-permute-start(bf16[144,704]{1,0:T(8,128)(2,1)S(1)} %get-tuple-element.86), channel_id=1, source_target_pairs={{0,24},{8,16},{16,8},{24,0},{1,25},{9,17},{17,9},{25,1},{2,26},{10... | collective-permute-start | bytes 608264 | tf_op jit(solution)/shard_map/ppermute | solution.py:289
  33.3 5.6 %mix_sibling.1 = bf16[512,1024]{1,0:T(8,128)(2,1)S(1)} custom-call(s32[2]{0:T(128)S(1)} %pad_add_fusion.1.place, bf16[144,768]{1,0:T(8,128)(2,1)S(1)} %get-tuple-element.66.refs_0_, bf16[144,768]{1,0:T(8,128)(2,1)S(1)} %collective-permute-done.7.refs_1_, bf16[144,768]{1,0:T(8,128)(2,1)S(1)} %collective-permute-done.8.refs_2_, ...), custom_call_target="tpu_custom_call" | custom-call | flops 1 | bytes 1 | tf_op jit(solution)/shard_map/mix_sibling/pallas_call | solution.py:256
  38.9 0.1 collective-permute-start.10
  39.0 5.6 %mix_own.1.own = f32[512,1024]{1,0:T(8,128)S(1)} custom-call(s32[2]{0:T(128)S(1)} %pad_add_fusion.1.place, bf16[144,768]{1,0:T(8,128)(2,1)S(1)} %get-tuple-element.66.refs_0_, bf16[144,768]{1,0:T(8,128)(2,1)S(1)} %collective-permute-done.7.refs_1_, bf16[144,768]{1,0:T(8,128)(2,1)S(1)} %collective-permute-done.8.refs_2_, ...), custom_call_target="tpu_custom_call" | custom-call | flops 99999997952 | bytes 1 | tf_op jit(solution)/shard_map/mix_own/pallas_call | solution.py:256
  44.6 0.2 add.7
  44.8 1.5 %collective-permute-start.14 = (bf16[128,512]{1,0:T(8,128)(2,1)S(1)}, bf16[128,512]{1,0:T(8,128)(2,1)S(1)}, u32[]{:S(2)}, u32[]{:S(2)}) collective-permute-start(bf16[128,512]{1,0:T(8,128)(2,1)S(1)} %get-tuple-element.78), channel_id=1, source_target_pairs={{0,8},{8,0},{16,24},{24,16},{1,9},{9,1},{17,25},{25,17},{2,10},{10... | collective-permute-start | bytes 393224 | tf_op jit(solution)/shard_map/ppermute | solution.py:289
  46.3 0.6 %collective-permute-start.15 = (bf16[128,512]{1,0:T(8,128)(2,1)S(1)}, bf16[128,512]{1,0:T(8,128)(2,1)S(1)}, u32[]{:S(2)}, u32[]{:S(2)}) collective-permute-start(bf16[128,512]{1,0:T(8,128)(2,1)S(1)} %get-tuple-element.79), channel_id=1, source_target_pairs={{0,16},{8,24},{16,0},{24,8},{1,17},{9,25},{17,1},{25,9},{2,18},{10... | collective-permute-start | bytes 393224 | tf_op jit(solution)/shard_map/ppermute | solution.py:289
  46.9 0.0 collective-permute-done.11.refs_1_
  46.9 0.0 collective-permute-done.12.refs_2_
  46.9 1.0 %collective-permute-start.13 = (bf16[128,512]{1,0:T(8,128)(2,1)S(1)}, bf16[128,512]{1,0:T(8,128)(2,1)S(1)}, u32[]{:S(2)}, u32[]{:S(2)}) collective-permute-start(bf16[128,512]{1,0:T(8,128)(2,1)S(1)} %get-tuple-element.75), channel_id=1, source_target_pairs={{0,8},{8,0},{16,24},{24,16},{1,9},{9,1},{17,25},{25,17},{2,10},{10... | collective-permute-start | bytes 393224 | tf_op jit(solution)/shard_map/ppermute | solution.py:289
  47.9 1.0 %collective-permute-start.18 = (bf16[128,512]{1,0:T(8,128)(2,1)S(1)}, bf16[128,512]{1,0:T(8,128)(2,1)S(1)}, u32[]{:S(2)}, u32[]{:S(2)}) collective-permute-start(bf16[128,512]{1,0:T(8,128)(2,1)S(1)} %get-tuple-element.82), channel_id=1, source_target_pairs={{0,16},{8,24},{16,0},{24,8},{1,17},{9,25},{17,1},{25,9},{2,18},{10... | collective-permute-start | bytes 393224 | tf_op jit(solution)/shard_map/ppermute | solution.py:289
  48.9 2.2 %collective-permute-done.14.low = bf16[128,512]{1,0:T(8,128)(2,1)S(1)} collective-permute-done((bf16[128,512]{1,0:T(8,128)(2,1)S(1)}, bf16[128,512]{1,0:T(8,128)(2,1)S(1)}, u32[]{:S(2)}, u32[]{:S(2)}) %collective-permute-start.14) | collective-permute-done | bytes 131104 | tf_op jit(solution)/shard_map/ppermute | solution.py:289
  51.1 1.5 %collective-permute-done.15.high = bf16[128,512]{1,0:T(8,128)(2,1)S(1)} collective-permute-done((bf16[128,512]{1,0:T(8,128)(2,1)S(1)}, bf16[128,512]{1,0:T(8,128)(2,1)S(1)}, u32[]{:S(2)}, u32[]{:S(2)}) %collective-permute-start.15) | collective-permute-done | bytes 131104 | tf_op jit(solution)/shard_map/ppermute | solution.py:289
  52.7 0.6 %collective-permute-start.16 = (bf16[128,512]{1,0:T(8,128)(2,1)S(1)}, bf16[128,512]{1,0:T(8,128)(2,1)S(1)}, u32[]{:S(2)}, u32[]{:S(2)}) collective-permute-start(bf16[128,512]{1,0:T(8,128)(2,1)S(1)} %get-tuple-element.80), channel_id=1, source_target_pairs={{0,8},{8,0},{16,24},{24,16},{1,9},{9,1},{17,25},{25,17},{2,10},{10... | collective-permute-start | bytes 393224 | tf_op jit(solution)/shard_map/ppermute | solution.py:289
  53.3 1.0 %collective-permute-start.17 = (bf16[128,512]{1,0:T(8,128)(2,1)S(1)}, bf16[128,512]{1,0:T(8,128)(2,1)S(1)}, u32[]{:S(2)}, u32[]{:S(2)}) collective-permute-start(bf16[128,512]{1,0:T(8,128)(2,1)S(1)} %get-tuple-element.81), channel_id=1, source_target_pairs={{0,16},{8,24},{16,0},{24,8},{1,17},{9,25},{17,1},{25,9},{2,18},{10... | collective-permute-start | bytes 393224 | tf_op jit(solution)/shard_map/ppermute | solution.py:289
  54.3 0.0 collective-permute-done.19.refs_3_
  54.3 2.7 %restore.1 = bf16[4,704,128]{2,1,0:T(8,128)(2,1)} custom-call(s32[2]{0:T(128)S(1)} %pad_add_fusion.1.place, s32[8,128]{1,0:T(8,128)S(1)} %pad_add_fusion.meta_ref, bf16[144,704]{1,0:T(8,128)(2,1)} %get-tuple-element.83.refs_0_, bf16[144,704]{1,0:T(8,128)(2,1)S(1)} %collective-permute-done.11.refs_1_, bf16[144,704]{1,0:T(8,128)(2,1)S(1)} %collective-permute-done.12.refs_2_, ...), custom_call_target="tpu_custom_call" | custom-call | flops 99999997952 | bytes 1 | tf_op jit(solution)/shard_map/restore/pallas_call | solution.py:256
  57.0 0.7 %collective-permute-done.16.one_high = bf16[128,512]{1,0:T(8,128)(2,1)S(1)} collective-permute-done((bf16[128,512]{1,0:T(8,128)(2,1)S(1)}, bf16[128,512]{1,0:T(8,128)(2,1)S(1)}, u32[]{:S(2)}, u32[]{:S(2)}) %collective-permute-start.16) | collective-permute-done | bytes 131104 | tf_op jit(solution)/shard_map/ppermute | solution.py:289
  57.7 0.5 collective-permute-done.17.two_low
  58.3 0.8 %finish.1 = bf16[128,1024]{1,0:T(8,128)(2,1)} custom-call(f32[128,1024]{1,0:T(8,128)S(1)} %get-tuple-element.70.mine, bf16[128,512]{1,0:T(8,128)(2,1)S(1)} %collective-permute-done.13.one_low, bf16[128,512]{1,0:T(8,128)(2,1)S(1)} %collective-permute-done.16.one_high, bf16[128,512]{1,0:T(8,128)(2,1)S(1)} %collective-permute-done.17.two_low, ...), custom_call_target="tpu_custom_call" | custom-call | flops 1 | bytes 1 | tf_op jit(solution)/shard_map/finish/pallas_call | solution.py:256
  (8 shorter events, 0.1 us)
Async XLA Ops:
  2.3 5.5 %collective-permute-start.3 = (bf16[136,1024]{1,0:T(8,128)(2,1)S(1)}, bf16[136,1024]{1,0:T(8,128)(2,1)S(1)}, u32[]{:S(2)}, u32[]{:S(2)}) collective-permute-start(bf16[136,1024]{1,0:T(8,128)(2,1)S(1)} %fusion.1), channel_id=1, source_target_pairs={{0,1},{1,0},{2,3},{3,2},{4,5},{5,4},{6,7},{7,6},{8,9},{9,8},{10,11... | collective-permute-start | bytes 835592 | tf_op jit(solution)/shard_map/ppermute | solution.py:292
  2.8 11.1 %collective-permute-start.6 = (bf16[136,1024]{1,0:T(8,128)(2,1)S(1)}, bf16[136,1024]{1,0:T(8,128)(2,1)S(1)}, u32[]{:S(2)}, u32[]{:S(2)}) collective-permute-start(bf16[136,1024]{1,0:T(8,128)(2,1)S(1)} %fusion.1), channel_id=1, source_target_pairs={{0,24},{8,16},{16,8},{24,0},{1,25},{9,17},{17,9},{25,1},{2,26},{10... | collective-permute-start | bytes 835592 | tf_op jit(solution)/shard_map/ppermute | solution.py:289
  6.3 13.3 %collective-permute-start.5 = (bf16[136,1024]{1,0:T(8,128)(2,1)S(1)}, bf16[136,1024]{1,0:T(8,128)(2,1)S(1)}, u32[]{:S(2)}, u32[]{:S(2)}) collective-permute-start(bf16[136,1024]{1,0:T(8,128)(2,1)S(1)} %fusion.1), channel_id=1, source_target_pairs={{0,16},{8,24},{16,0},{24,8},{1,17},{9,25},{17,1},{25,9},{2,18},{10... | collective-permute-start | bytes 835592 | tf_op jit(solution)/shard_map/ppermute | solution.py:289
  6.8 13.5 %collective-permute-start.4 = (bf16[136,1024]{1,0:T(8,128)(2,1)S(1)}, bf16[136,1024]{1,0:T(8,128)(2,1)S(1)}, u32[]{:S(2)}, u32[]{:S(2)}) collective-permute-start(bf16[136,1024]{1,0:T(8,128)(2,1)S(1)} %fusion.1), channel_id=1, source_target_pairs={{0,8},{8,0},{16,24},{24,16},{1,9},{9,1},{17,25},{25,17},{2,10},{10... | collective-permute-start | bytes 835592 | tf_op jit(solution)/shard_map/ppermute | solution.py:289
  7.8 1.1 %copy-start = (bf16[128,4,704]{0,2,1:T(8,128)(2,1)S(1)}, bf16[128,4,704]{0,2,1:T(8,128)(2,1)}, u32[]{:S(2)}) copy-start(bf16[128,4,704]{0,2,1:T(8,128)(2,1)} %param.9) | copy-start | bytes 2162692
  10.2 21.7 %collective-permute-start.7 = (bf16[144,768]{1,0:T(8,128)(2,1)S(1)}, bf16[144,768]{1,0:T(8,128)(2,1)S(1)}, u32[]{:S(2)}, u32[]{:S(2)}) collective-permute-start(bf16[144,768]{1,0:T(8,128)(2,1)S(1)} %get-tuple-element.67), channel_id=1, source_target_pairs={{0,8},{8,0},{16,24},{24,16},{1,9},{9,1},{17,25},{25,17},{2,10},{10... | collective-permute-start | bytes 663560 | tf_op jit(solution)/shard_map/ppermute | solution.py:289
  12.2 21.1 %collective-permute-start.8 = (bf16[144,768]{1,0:T(8,128)(2,1)S(1)}, bf16[144,768]{1,0:T(8,128)(2,1)S(1)}, u32[]{:S(2)}, u32[]{:S(2)}) collective-permute-start(bf16[144,768]{1,0:T(8,128)(2,1)S(1)} %get-tuple-element.68), channel_id=1, source_target_pairs={{0,16},{8,24},{16,0},{24,8},{1,17},{9,25},{17,1},{25,9},{2,18},{10... | collective-permute-start | bytes 663560 | tf_op jit(solution)/shard_map/ppermute | solution.py:289
  13.9 1.7 %collective-permute-start = (bf16[136,1024]{1,0:T(8,128)(2,1)S(1)}, bf16[136,1024]{1,0:T(8,128)(2,1)}, u32[]{:S(2)}, u32[]{:S(2)}) collective-permute-start(bf16[136,1024]{1,0:T(8,128)(2,1)S(1)} %param.1), channel_id=1, source_target_pairs={{0,1},{1,0},{2,3},{3,2},{4,5},{5,4},{6,7},{7,6},{8,9},{9,8},{10,11... | collective-permute-start | bytes 835592 | tf_op jit(solution)/shard_map/cond/branch_1_fun/ppermute | solution.py:292
  15.6 17.7 %collective-permute-start.9 = (bf16[144,768]{1,0:T(8,128)(2,1)S(1)}, bf16[144,768]{1,0:T(8,128)(2,1)S(1)}, u32[]{:S(2)}, u32[]{:S(2)}) collective-permute-start(bf16[144,768]{1,0:T(8,128)(2,1)S(1)} %get-tuple-element.69), channel_id=1, source_target_pairs={{0,24},{8,16},{16,8},{24,0},{1,25},{9,17},{17,9},{25,1},{2,26},{10... | collective-permute-start | bytes 663560 | tf_op jit(solution)/shard_map/ppermute | solution.py:289
  20.3 1.6 %collective-permute-start.1 = (bf16[136,1024]{1,0:T(8,128)(2,1)S(1)}, bf16[136,1024]{1,0:T(8,128)(2,1)S(1)}, u32[]{:S(2)}, u32[]{:S(2)}) collective-permute-start(bf16[136,1024]{1,0:T(8,128)(2,1)S(1)} %get-tuple-element.23.refs_1_), channel_id=1, source_target_pairs={{0,1},{1,0},{2,3},{3,2},{4,5},{5,4},{6,7},{7,6},{8,9},{9,8},{10,11... | collective-permute-start | bytes 835592 | tf_op jit(solution)/shard_map/cond/branch_1_fun/ppermute | solution.py:292
  20.3 2.0 %collective-permute-start.2 = (bf16[136,1024]{1,0:T(8,128)(2,1)S(1)}, bf16[136,1024]{1,0:T(8,128)(2,1)S(1)}, u32[]{:S(2)}, u32[]{:S(2)}) collective-permute-start(bf16[136,1024]{1,0:T(8,128)(2,1)S(1)} %get-tuple-element.24.refs_2_), channel_id=1, source_target_pairs={{0,1},{1,0},{2,3},{3,2},{4,5},{5,4},{6,7},{7,6},{8,9},{9,8},{10,11... | collective-permute-start | bytes 835592 | tf_op jit(solution)/shard_map/cond/branch_1_fun/ppermute | solution.py:292
  29.7 17.2 %collective-permute-start.11 = (bf16[144,704]{1,0:T(8,128)(2,1)}, bf16[144,704]{1,0:T(8,128)(2,1)S(1)}, u32[]{:S(2)}, u32[]{:S(2)}) collective-permute-start(bf16[144,704]{1,0:T(8,128)(2,1)} %get-tuple-element.73), channel_id=1, source_target_pairs={{0,8},{8,0},{16,24},{24,16},{1,9},{9,1},{17,25},{25,17},{2,10},{10... | collective-permute-start | bytes 608264 | tf_op jit(solution)/shard_map/ppermute | solution.py:289
  31.3 15.6 %collective-permute-start.12 = (bf16[144,704]{1,0:T(8,128)(2,1)S(1)}, bf16[144,704]{1,0:T(8,128)(2,1)S(1)}, u32[]{:S(2)}, u32[]{:S(2)}) collective-permute-start(bf16[144,704]{1,0:T(8,128)(2,1)S(1)} %get-tuple-element.74), channel_id=1, source_target_pairs={{0,16},{8,24},{16,0},{24,8},{1,17},{9,25},{17,1},{25,9},{2,18},{10... | collective-permute-start | bytes 608264 | tf_op jit(solution)/shard_map/ppermute | solution.py:289
  31.9 22.4 %collective-permute-start.19 = (bf16[144,704]{1,0:T(8,128)(2,1)S(1)}, bf16[144,704]{1,0:T(8,128)(2,1)S(1)}, u32[]{:S(2)}, u32[]{:S(2)}) collective-permute-start(bf16[144,704]{1,0:T(8,128)(2,1)S(1)} %get-tuple-element.86), channel_id=1, source_target_pairs={{0,24},{8,16},{16,8},{24,0},{1,25},{9,17},{17,9},{25,1},{2,26},{10... | collective-permute-start | bytes 608264 | tf_op jit(solution)/shard_map/ppermute | solution.py:289
  38.9 5.7 %collective-permute-start.10 = (bf16[512,1024]{1,0:T(8,128)(2,1)S(1)}, bf16[512,1024]{1,0:T(8,128)(2,1)S(1)}, u32[]{:S(2)}, u32[]{:S(2)}) collective-permute-start(bf16[512,1024]{1,0:T(8,128)(2,1)S(1)} %mix_sibling.1), channel_id=1, source_target_pairs={{0,1},{1,0},{2,3},{3,2},{4,5},{5,4},{6,7},{7,6},{8,9},{9,8},{10,11... | collective-permute-start | bytes 3145736 | tf_op jit(solution)/shard_map/ppermute | solution.py:292
  44.8 6.4 %collective-permute-start.14 = (bf16[128,512]{1,0:T(8,128)(2,1)S(1)}, bf16[128,512]{1,0:T(8,128)(2,1)S(1)}, u32[]{:S(2)}, u32[]{:S(2)}) collective-permute-start(bf16[128,512]{1,0:T(8,128)(2,1)S(1)} %get-tuple-element.78), channel_id=1, source_target_pairs={{0,8},{8,0},{16,24},{24,16},{1,9},{9,1},{17,25},{25,17},{2,10},{10... | collective-permute-start | bytes 393224 | tf_op jit(solution)/shard_map/ppermute | solution.py:289
  46.3 6.3 %collective-permute-start.15 = (bf16[128,512]{1,0:T(8,128)(2,1)S(1)}, bf16[128,512]{1,0:T(8,128)(2,1)S(1)}, u32[]{:S(2)}, u32[]{:S(2)}) collective-permute-start(bf16[128,512]{1,0:T(8,128)(2,1)S(1)} %get-tuple-element.79), channel_id=1, source_target_pairs={{0,16},{8,24},{16,0},{24,8},{1,17},{9,25},{17,1},{25,9},{2,18},{10... | collective-permute-start | bytes 393224 | tf_op jit(solution)/shard_map/ppermute | solution.py:289
  46.9 10.1 %collective-permute-start.13 = (bf16[128,512]{1,0:T(8,128)(2,1)S(1)}, bf16[128,512]{1,0:T(8,128)(2,1)S(1)}, u32[]{:S(2)}, u32[]{:S(2)}) collective-permute-start(bf16[128,512]{1,0:T(8,128)(2,1)S(1)} %get-tuple-element.75), channel_id=1, source_target_pairs={{0,8},{8,0},{16,24},{24,16},{1,9},{9,1},{17,25},{25,17},{2,10},{10... | collective-permute-start | bytes 393224 | tf_op jit(solution)/shard_map/ppermute | solution.py:289
  47.9 9.1 %collective-permute-start.18 = (bf16[128,512]{1,0:T(8,128)(2,1)S(1)}, bf16[128,512]{1,0:T(8,128)(2,1)S(1)}, u32[]{:S(2)}, u32[]{:S(2)}) collective-permute-start(bf16[128,512]{1,0:T(8,128)(2,1)S(1)} %get-tuple-element.82), channel_id=1, source_target_pairs={{0,16},{8,24},{16,0},{24,8},{1,17},{9,25},{17,1},{25,9},{2,18},{10... | collective-permute-start | bytes 393224 | tf_op jit(solution)/shard_map/ppermute | solution.py:289
  52.7 5.0 %collective-permute-start.16 = (bf16[128,512]{1,0:T(8,128)(2,1)S(1)}, bf16[128,512]{1,0:T(8,128)(2,1)S(1)}, u32[]{:S(2)}, u32[]{:S(2)}) collective-permute-start(bf16[128,512]{1,0:T(8,128)(2,1)S(1)} %get-tuple-element.80), channel_id=1, source_target_pairs={{0,8},{8,0},{16,24},{24,16},{1,9},{9,1},{17,25},{25,17},{2,10},{10... | collective-permute-start | bytes 393224 | tf_op jit(solution)/shard_map/ppermute | solution.py:289
  53.3 5.0 %collective-permute-start.17 = (bf16[128,512]{1,0:T(8,128)(2,1)S(1)}, bf16[128,512]{1,0:T(8,128)(2,1)S(1)}, u32[]{:S(2)}, u32[]{:S(2)}) collective-permute-start(bf16[128,512]{1,0:T(8,128)(2,1)S(1)} %get-tuple-element.81), channel_id=1, source_target_pairs={{0,16},{8,24},{16,0},{24,8},{1,17},{9,25},{17,1},{25,9},{2,18},{10... | collective-permute-start | bytes 393224 | tf_op jit(solution)/shard_map/ppermute | solution.py:289

commit v8 on v6

--- a/solution.py
+++ b/solution.py
@@ -119,11 +119,10 @@
             x_ref[l, :, c : c + chunk] = x.astype(BF16)
 
 
-def grad_kernel(dims, top, place, *refs):
+def gather_kernel(dims, top, place, *refs):
     experts, local, cap, width = dims
     n = experts // local
-    own, other, w_ref = refs[:n], refs[n : 2 * n], refs[2 * n]
-    outs, x_ref = refs[2 * n + 1 : -1], refs[-1]
+    own, other, x_ref = refs[:n], refs[n:-1], refs[-1]
     half = own[0].shape[1]
     tokens = own[0].shape[0] - 8
     chunk = min(half, 512)
@@ -139,8 +138,12 @@
             at = pl.ds(pl.multiple_of(side * half + c, chunk), chunk)
             for l, x in enumerate(by_expert(rows, local, cap)):
                 x_ref[l, :, at] = x.astype(BF16)
+
+
+def grad_kernel(dims, x_ref, w_ref, *outs):
+    experts, local, cap, width = dims
     grads = [dot(x_ref[l], w_ref[l], NT) for l in range(local)]
-    for s, rows in enumerate(by_source(grads, n, cap)):
+    for s, rows in enumerate(by_source(grads, len(outs), cap)):
         outs[s][...] = rows.astype(BF16)
 
 
@@ -279,23 +282,27 @@
     meta, swapped = lax.optimization_barrier((meta, swapped))
     hid_sent = run(
         functools.partial(dispatch_kernel, dims), [shaped((width, -(-(ff + 1) // 128) * 128))] * n,
-        [place, meta, hid_t], where=placed, name="dispatch", weight=BIG,
+        [place, meta, hid_t], where=placed, name="dispatch",
     )
     hid = [send(hid_sent[s], s) for s in range(n)]
     slot = shaped((width, ff))
 
-    def taken(own):
-        other = [swap(x) for x in own[:2]]
-        for x in own[2:]:
-            other[-2], x = lax.optimization_barrier((other[-2], x))
-            other.append(swap(x))
-        return other
-
-    other = [swapped] + lax.cond(place[0] < 1000, taken, list, own[1:])
+    def swaps(xs):
+        return [swap(x) for x in xs]
+
+    if forward:
+        always = place[0] < 1000
+        last = lax.cond(always, swaps, list, own[3:])
+        *own[1:3], last[0] = lax.optimization_barrier((*own[1:3], last[0]))
+        other = [swapped] + lax.cond(always, swaps, list, own[1:3]) + last
+    else:
+        other = [swapped] + swaps(own[1:])
+    (x,) = run(
+        functools.partial(gather_kernel, dims, top), [shaped((local, n * cap, full))],
+        [place, *own, *other], where=placed, name="gather", weight=15 * 10**8,
+    )
     grad_sent = run(
-        functools.partial(grad_kernel, dims, top), [slot] * n,
-        [place, *own, *other, w_down], where=placed,
-        scratch=[pltpu.VMEM((local, n * cap, full), BF16)], name="grad",
+        functools.partial(grad_kernel, dims), [slot] * n, [x, w_down], name="grad"
     )
     hid[0], grad_own = lax.optimization_barrier((hid[0], grad_sent[0]))
     grad_back = [grad_own] + [send(grad_sent[s], s) for s in range(1, n)]

time: 56.5 us -> 53.3 us (0.943)
  local copies, waits for them, and re-layouts: 6.37 us -> 3.74 us
  starting transfers between devices: 21 us -> 19.1 us
  Pallas kernels: 13.5 us -> 14.5 us
    unnamed x6 -> x8, local copies, waits for them, and re-layouts: 6.37 us -> 3.74 us
    ppermute x15, starting transfers between devices: 19.8 us -> 18 us  [send(): return lax.ppermute(x, 'ctx', [(i, i ^ s) for i in range(n)]) if s else x]
    pallas_call x8 -> x9, Pallas kernels: 13.5 us -> 14.5 us  [call(): pl.pallas_call(kernel, out_shape=outs, in_specs=[pl.BlockSpec(memory_spac...]
    ppermute x5, waiting for transfers between devices: 2.95 us -> 3.89 us  [swap(): return lax.ppermute(x, 'tp', [(0, 1), (1, 0)])]
    ppermute x15, waiting for transfers between devices: 9.24 us -> 8.54 us  [send(): return lax.ppermute(x, 'ctx', [(i, i ^ s) for i in range(n)]) if s else x]
  transfers between devices with their start and end apart: 20 -> 20, of which waited for: 11 -> 11; matrix products, arithmetic and copies ran while one was open for 1% -> 1% of each run, Pallas kernels for 23% -> 26%
where the time goes in v8:
time: 53.3 us; the launch traced here: 53 us
  starting transfers between devices  19.1 us (36%)
  Pallas kernels  14.5 us (27%)
  waiting for transfers between devices  12.4 us (23%)
  local copies, waits for them, and re-layouts  3.74 us (7%)
  other arithmetic  2.44 us (5%)
  between operations  0.73 us (1%)
    ppermute x15, starting transfers between devices, send(): return lax.ppermute(x, 'ctx', [(i, i ^ s) for i in range(n)]) if s else x  18 us
    pallas_call x9, Pallas kernels, call(): pl.pallas_call(kernel, out_shape=outs, in_specs=[pl.BlockSpec(memory_spac...  14.5 us
    ppermute x15, waiting for transfers between devices, send(): return lax.ppermute(x, 'ctx', [(i, i ^ s) for i in range(n)]) if s else x  8.54 us
    ppermute x5, waiting for transfers between devices, swap(): return lax.ppermute(x, 'tp', [(0, 1), (1, 0)])  3.89 us
    unnamed x8, local copies, waits for them, and re-layouts  3.74 us
    ppermute x5, starting transfers between devices, swap(): return lax.ppermute(x, 'tp', [(0, 1), (1, 0)])  1.1 us
  transfers between devices with their start and end apart: 20, of which 11 were waited for; matrix products, arithmetic and copies ran while one was open for 1% of the time, Pallas kernels for 26%

profile of v8, /device:TPU:0, one launch (start us, length us, event | category | flops | bytes accessed | tf_op | source)
XLA Modules:
  0.0 53.0 jit_solution(14897371207284736452)
XLA Ops:
  0.6 0.7 %bitcast_convert_fusion = bf16[4,128]{1,0:T(4,128)(2,1)S(1)} fusion(s32[128,4]{0,1:T(4,128)} %param.10), kind=kLoop, calls=%fused_computation.5 | loop fusion | flops 512 | bytes 3072 | tf_op jit(solution)/shard_map/convert_element_type | solution.py:277
  1.3 1.0 %fusion.1.refs_0_ = bf16[136,1024]{1,0:T(8,128)(2,1)S(1)} fusion(bf16[4,128]{1,0:T(4,128)(2,1)S(1)} %bitcast_convert_fusion, bf16[128,1024]{1,0:T(8,128)(2,1)} %param.12), kind=kLoop, calls=%fused_computation.2 | loop fusion | flops 835584 | bytes 541696 | tf_op jit(solution)/shard_map/concatenate | solution.py:278
  2.3 0.5 collective-permute-start.3
  2.8 3.5 %collective-permute-start.6 = (bf16[136,1024]{1,0:T(8,128)(2,1)S(1)}, bf16[136,1024]{1,0:T(8,128)(2,1)}, u32[]{:S(2)}, u32[]{:S(2)}) collective-permute-start(bf16[136,1024]{1,0:T(8,128)(2,1)S(1)} %fusion.1.refs_0_), channel_id=1, source_target_pairs={{0,24},{8,16},{16,8},{24,0},{1,25},{9,17},{17,9},{25,1},{2,26},{10... | collective-permute-start | bytes 835592 | tf_op jit(solution)/shard_map/ppermute | solution.py:270
  6.3 0.5 collective-permute-start.5
  6.8 0.1 collective-permute-start.4
  7.0 0.1 pad_add_fusion.1.place
  7.0 0.7 %pad_add_fusion.meta_ref = s32[8,128]{1,0:T(8,128)S(1)} fusion(s32[4,128]{1,0:T(4,128)} %bitcast.11, s32[4,128]{1,0:T(4,128)} %bitcast.10), kind=kLoop, calls=%fused_computation.3 | loop fusion | flops 1024 | bytes 8192 | tf_op jit(solution)/shard_map/concatenate | solution.py:275
  7.8 0.0 collective-permute-done.3.refs_4_
  7.8 0.0 copy-start.1
  7.8 1.1 %copy-done.1 = bf16[128,4,704]{0,2,1:T(8,128)(2,1)S(1)} copy-done((bf16[128,4,704]{0,2,1:T(8,128)(2,1)S(1)}, bf16[128,4,704]{0,2,1:T(8,128)(2,1)}, u32[]{:S(2)}) %copy-start.1) | copy-done | bytes 720920
  8.9 2.0 %dispatch.1 = (bf16[144,768]{1,0:T(8,128)(2,1)S(1)}, bf16[144,768]{1,0:T(8,128)(2,1)}, bf16[144,768]{1,0:T(8,128)(2,1)S(1)}, bf16[144,768]{1,0:T(8,128)(2,1)S(1)}) custom-call(s32[2]{0:T(128)S(1)} %pad_add_fusion.1.place, s32[8,128]{1,0:T(8,128)S(1)} %pad_add_fusion.meta_ref, bf16[4,704,128]{2,1,0:T(8,128)(2,1)S(1)} %bitcast.9), custom_call_target="tpu_custom_call" | custom-call | flops 1 | bytes 1 | tf_op jit(solution)/shard_map/dispatch/pallas_call | solution.py:237
  10.8 1.9 %collective-permute-start.7 = (bf16[144,768]{1,0:T(8,128)(2,1)}, bf16[144,768]{1,0:T(8,128)(2,1)S(1)}, u32[]{:S(2)}, u32[]{:S(2)}) collective-permute-start(bf16[144,768]{1,0:T(8,128)(2,1)} %get-tuple-element.57), channel_id=1, source_target_pairs={{0,8},{8,0},{16,24},{24,16},{1,9},{9,1},{17,25},{25,17},{2,10},{10... | collective-permute-start | bytes 663560 | tf_op jit(solution)/shard_map/ppermute | solution.py:270
  12.7 1.5 %collective-permute-start.8 = (bf16[144,768]{1,0:T(8,128)(2,1)S(1)}, bf16[144,768]{1,0:T(8,128)(2,1)S(1)}, u32[]{:S(2)}, u32[]{:S(2)}) collective-permute-start(bf16[144,768]{1,0:T(8,128)(2,1)S(1)} %get-tuple-element.58), channel_id=1, source_target_pairs={{0,16},{8,24},{16,0},{24,8},{1,17},{9,25},{17,1},{25,9},{2,18},{10... | collective-permute-start | bytes 663560 | tf_op jit(solution)/shard_map/ppermute | solution.py:270
  14.3 1.9 %conditional.2 = (bf16[136,1024]{1,0:T(8,128)(2,1)}) conditional(s32[]{:T(128)} %convert_element_type.10, bf16[136,1024]{1,0:T(8,128)(2,1)} %collective-permute-done.6.refs_3_, bf16[136,1024]{1,0:T(8,128)(2,1)} %collective-permute-done.6.refs_3_), branch_computations={%region_0.1_spmd, %region_1.2_spmd} | conditional | bytes 1114160 | solution.py:295
  14.3 1.9 %collective-permute-done = bf16[136,1024]{1,0:T(8,128)(2,1)} collective-permute-done((bf16[136,1024]{1,0:T(8,128)(2,1)}, bf16[136,1024]{1,0:T(8,128)(2,1)}, u32[]{:S(2)}, u32[]{:S(2)}) %collective-permute-start) | collective-permute-done | bytes 278560 | tf_op jit(solution)/shard_map/cond/branch_1_fun/ppermute | solution.py:273
  16.2 2.6 %collective-permute-start.9 = (bf16[144,768]{1,0:T(8,128)(2,1)S(1)}, bf16[144,768]{1,0:T(8,128)(2,1)S(1)}, u32[]{:S(2)}, u32[]{:S(2)}) collective-permute-start(bf16[144,768]{1,0:T(8,128)(2,1)S(1)} %get-tuple-element.59), channel_id=1, source_target_pairs={{0,24},{8,16},{16,8},{24,0},{1,25},{9,17},{17,9},{25,1},{2,26},{10... | collective-permute-start | bytes 663560 | tf_op jit(solution)/shard_map/ppermute | solution.py:270
  18.7 1.0 %collective-permute-done.5.refs_2_ = bf16[136,1024]{1,0:T(8,128)(2,1)} collective-permute-done((bf16[136,1024]{1,0:T(8,128)(2,1)S(1)}, bf16[136,1024]{1,0:T(8,128)(2,1)}, u32[]{:S(2)}, u32[]{:S(2)}) %collective-permute-start.5) | collective-permute-done | bytes 278560 | tf_op jit(solution)/shard_map/ppermute | solution.py:270
  19.7 0.7 %collective-permute-done.4.refs_1_ = bf16[136,1024]{1,0:T(8,128)(2,1)} collective-permute-done((bf16[136,1024]{1,0:T(8,128)(2,1)S(1)}, bf16[136,1024]{1,0:T(8,128)(2,1)}, u32[]{:S(2)}, u32[]{:S(2)}) %collective-permute-start.4) | collective-permute-done | bytes 278560 | tf_op jit(solution)/shard_map/ppermute | solution.py:270
  20.4 2.3 %conditional.3 = (bf16[136,1024]{1,0:T(8,128)(2,1)}, bf16[136,1024]{1,0:T(8,128)(2,1)}) conditional(s32[]{:T(128)} %convert_element_type.10, (bf16[136,1024]{1,0:T(8,128)(2,1)}, bf16[136,1024]{1,0:T(8,128)(2,1)}) %tuple.27, (bf16[136,1024]{1,0:T(8,128)(2,1)}, bf16[136,1024]{1,0:T(8,128)(2,1)}) %tuple.27), branch_computations={%region_2.3_spmd, %region_3.4_spmd} | conditional | bytes 2228320 | solution.py:297
  20.4 0.5 collective-permute-start.2
  20.9 1.4 %collective-permute-done.1 = bf16[136,1024]{1,0:T(8,128)(2,1)} collective-permute-done((bf16[136,1024]{1,0:T(8,128)(2,1)}, bf16[136,1024]{1,0:T(8,128)(2,1)}, u32[]{:S(2)}, u32[]{:S(2)}) %collective-permute-start.1) | collective-permute-done | bytes 278560 | tf_op jit(solution)/shard_map/cond/branch_1_fun/ppermute | solution.py:273
  22.3 0.4 collective-permute-done.2
  22.7 2.3 %gather.1.x_ref = bf16[2,288,2048]{2,1,0:T(8,128)(2,1)S(1)} custom-call(s32[2]{0:T(128)S(1)} %pad_add_fusion.1.place, bf16[136,1024]{1,0:T(8,128)(2,1)S(1)} %fusion.1.refs_0_, bf16[136,1024]{1,0:T(8,128)(2,1)} %collective-permute-done.4.refs_1_, bf16[136,1024]{1,0:T(8,128)(2,1)} %collective-permute-done.5.refs_2_, ...), custom_call_target="tpu_custom_call" | custom-call | flops 1500000000 | bytes 1 | tf_op jit(solution)/shard_map/gather/pallas_call | solution.py:237
  25.0 0.0 copy-start
  25.0 2.6 %copy-done = bf16[2,704,2048]{2,1,0:T(8,128)(2,1)S(1)} copy-done((bf16[2,704,2048]{2,1,0:T(8,128)(2,1)S(1)}, bf16[2,704,2048]{2,1,0:T(8,128)(2,1)}, u32[]{:S(2)}) %copy-start) | copy-done | bytes 5767192
  27.6 2.0 %grad.1 = (bf16[144,704]{1,0:T(8,128)(2,1)S(1)}, bf16[144,704]{1,0:T(8,128)(2,1)S(1)}, bf16[144,704]{1,0:T(8,128)(2,1)S(1)}, bf16[144,704]{1,0:T(8,128)(2,1)S(1)}) custom-call(bf16[2,288,2048]{2,1,0:T(8,128)(2,1)S(1)} %gather.1.x_ref, bf16[2,704,2048]{2,1,0:T(8,128)(2,1)S(1)} %copy-done), custom_call_target="tpu_custom_call" | custom-call | flops 1 | bytes 1 | tf_op jit(solution)/shard_map/grad/pallas_call | solution.py:237
  29.7 1.6 %collective-permute-start.11 = (bf16[144,704]{1,0:T(8,128)(2,1)S(1)}, bf16[144,704]{1,0:T(8,128)(2,1)S(1)}, u32[]{:S(2)}, u32[]{:S(2)}) collective-permute-start(bf16[144,704]{1,0:T(8,128)(2,1)S(1)} %get-tuple-element.63), channel_id=1, source_target_pairs={{0,8},{8,0},{16,24},{24,16},{1,9},{9,1},{17,25},{25,17},{2,10},{10... | collective-permute-start | bytes 608264 | tf_op jit(solution)/shard_map/ppermute | solution.py:270
  31.2 0.6 %collective-permute-start.12 = (bf16[144,704]{1,0:T(8,128)(2,1)S(1)}, bf16[144,704]{1,0:T(8,128)(2,1)S(1)}, u32[]{:S(2)}, u32[]{:S(2)}) collective-permute-start(bf16[144,704]{1,0:T(8,128)(2,1)S(1)} %get-tuple-element.64), channel_id=1, source_target_pairs={{0,16},{8,24},{16,0},{24,8},{1,17},{9,25},{17,1},{25,9},{2,18},{10... | collective-permute-start | bytes 608264 | tf_op jit(solution)/shard_map/ppermute | solution.py:270
  31.8 1.4 %collective-permute-start.19 = (bf16[144,704]{1,0:T(8,128)(2,1)S(1)}, bf16[144,704]{1,0:T(8,128)(2,1)S(1)}, u32[]{:S(2)}, u32[]{:S(2)}) collective-permute-start(bf16[144,704]{1,0:T(8,128)(2,1)S(1)} %get-tuple-element.76), channel_id=1, source_target_pairs={{0,24},{8,16},{16,8},{24,0},{1,25},{9,17},{17,9},{25,1},{2,26},{10... | collective-permute-start | bytes 608264 | tf_op jit(solution)/shard_map/ppermute | solution.py:270
  33.2 2.5 %mix_sibling.1 = bf16[512,1024]{1,0:T(8,128)(2,1)S(1)} custom-call(s32[2]{0:T(128)S(1)} %pad_add_fusion.1.place, bf16[144,768]{1,0:T(8,128)(2,1)S(1)} %get-tuple-element.56.refs_0_, bf16[144,768]{1,0:T(8,128)(2,1)S(1)} %collective-permute-done.7.refs_1_, bf16[144,768]{1,0:T(8,128)(2,1)S(1)} %collective-permute-done.8.refs_2_, ...), custom_call_target="tpu_custom_call" | custom-call | flops 1 | bytes 1 | tf_op jit(solution)/shard_map/mix_sibling/pallas_call | solution.py:237
  35.7 0.1 collective-permute-start.10
  35.8 2.4 %mix_own.1.own = f32[512,1024]{1,0:T(8,128)S(1)} custom-call(s32[2]{0:T(128)S(1)} %pad_add_fusion.1.place, bf16[144,768]{1,0:T(8,128)(2,1)S(1)} %get-tuple-element.56.refs_0_, bf16[144,768]{1,0:T(8,128)(2,1)S(1)} %collective-permute-done.7.refs_1_, bf16[144,768]{1,0:T(8,128)(2,1)S(1)} %collective-permute-done.8.refs_2_, ...), custom_call_target="tpu_custom_call" | custom-call | flops 99999997952 | bytes 1 | tf_op jit(solution)/shard_map/mix_own/pallas_call | solution.py:237
  38.2 0.2 collective-permute-done.10.arrived
  38.4 0.2 add.7
  38.7 1.6 %collective-permute-start.14 = (bf16[128,512]{1,0:T(8,128)(2,1)S(1)}, bf16[128,512]{1,0:T(8,128)(2,1)S(1)}, u32[]{:S(2)}, u32[]{:S(2)}) collective-permute-start(bf16[128,512]{1,0:T(8,128)(2,1)S(1)} %get-tuple-element.68), channel_id=1, source_target_pairs={{0,8},{8,0},{16,24},{24,16},{1,9},{9,1},{17,25},{25,17},{2,10},{10... | collective-permute-start | bytes 393224 | tf_op jit(solution)/shard_map/ppermute | solution.py:270
  40.2 0.6 %collective-permute-start.15 = (bf16[128,512]{1,0:T(8,128)(2,1)S(1)}, bf16[128,512]{1,0:T(8,128)(2,1)S(1)}, u32[]{:S(2)}, u32[]{:S(2)}) collective-permute-start(bf16[128,512]{1,0:T(8,128)(2,1)S(1)} %get-tuple-element.69), channel_id=1, source_target_pairs={{0,16},{8,24},{16,0},{24,8},{1,17},{9,25},{17,1},{25,9},{2,18},{10... | collective-permute-start | bytes 393224 | tf_op jit(solution)/shard_map/ppermute | solution.py:270
  40.8 2.5 %collective-permute-done.12.refs_2_ = bf16[144,704]{1,0:T(8,128)(2,1)S(1)} collective-permute-done((bf16[144,704]{1,0:T(8,128)(2,1)S(1)}, bf16[144,704]{1,0:T(8,128)(2,1)S(1)}, u32[]{:S(2)}, u32[]{:S(2)}) %collective-permute-start.12) | collective-permute-done | bytes 202784 | tf_op jit(solution)/shard_map/ppermute | solution.py:270
  43.4 0.2 collective-permute-start.13
  43.6 0.3 collective-permute-start.18
  43.9 1.2 %collective-permute-done.14.low = bf16[128,512]{1,0:T(8,128)(2,1)S(1)} collective-permute-done((bf16[128,512]{1,0:T(8,128)(2,1)S(1)}, bf16[128,512]{1,0:T(8,128)(2,1)S(1)}, u32[]{:S(2)}, u32[]{:S(2)}) %collective-permute-start.14) | collective-permute-done | bytes 131104 | tf_op jit(solution)/shard_map/ppermute | solution.py:270
  45.1 1.5 %collective-permute-done.15.high = bf16[128,512]{1,0:T(8,128)(2,1)S(1)} collective-permute-done((bf16[128,512]{1,0:T(8,128)(2,1)S(1)}, bf16[128,512]{1,0:T(8,128)(2,1)S(1)}, u32[]{:S(2)}, u32[]{:S(2)}) %collective-permute-start.15) | collective-permute-done | bytes 131104 | tf_op jit(solution)/shard_map/ppermute | solution.py:270
  46.6 0.6 %collective-permute-start.16 = (bf16[128,512]{1,0:T(8,128)(2,1)S(1)}, bf16[128,512]{1,0:T(8,128)(2,1)S(1)}, u32[]{:S(2)}, u32[]{:S(2)}) collective-permute-start(bf16[128,512]{1,0:T(8,128)(2,1)S(1)} %get-tuple-element.70), channel_id=1, source_target_pairs={{0,8},{8,0},{16,24},{24,16},{1,9},{9,1},{17,25},{25,17},{2,10},{10... | collective-permute-start | bytes 393224 | tf_op jit(solution)/shard_map/ppermute | solution.py:270
  47.2 1.1 %collective-permute-start.17 = (bf16[128,512]{1,0:T(8,128)(2,1)S(1)}, bf16[128,512]{1,0:T(8,128)(2,1)S(1)}, u32[]{:S(2)}, u32[]{:S(2)}) collective-permute-start(bf16[128,512]{1,0:T(8,128)(2,1)S(1)} %get-tuple-element.71), channel_id=1, source_target_pairs={{0,16},{8,24},{16,0},{24,8},{1,17},{9,25},{17,1},{25,9},{2,18},{10... | collective-permute-start | bytes 393224 | tf_op jit(solution)/shard_map/ppermute | solution.py:270
  48.3 2.3 %restore.1 = bf16[4,704,128]{2,1,0:T(8,128)(2,1)} custom-call(s32[2]{0:T(128)S(1)} %pad_add_fusion.1.place, s32[8,128]{1,0:T(8,128)S(1)} %pad_add_fusion.meta_ref, bf16[144,704]{1,0:T(8,128)(2,1)S(1)} %get-tuple-element.73.refs_0_, bf16[144,704]{1,0:T(8,128)(2,1)S(1)} %collective-permute-done.11.refs_1_, ...), custom_call_target="tpu_custom_call" | custom-call | flops 99999997952 | bytes 1 | tf_op jit(solution)/shard_map/restore/pallas_call | solution.py:237
  50.6 1.1 %collective-permute-done.16.one_high = bf16[128,512]{1,0:T(8,128)(2,1)S(1)} collective-permute-done((bf16[128,512]{1,0:T(8,128)(2,1)S(1)}, bf16[128,512]{1,0:T(8,128)(2,1)S(1)}, u32[]{:S(2)}, u32[]{:S(2)}) %collective-permute-start.16) | collective-permute-done | bytes 131104 | tf_op jit(solution)/shard_map/ppermute | solution.py:270
  51.7 0.5 %collective-permute-done.17.two_low = bf16[128,512]{1,0:T(8,128)(2,1)S(1)} collective-permute-done((bf16[128,512]{1,0:T(8,128)(2,1)S(1)}, bf16[128,512]{1,0:T(8,128)(2,1)S(1)}, u32[]{:S(2)}, u32[]{:S(2)}) %collective-permute-start.17) | collective-permute-done | bytes 131104 | tf_op jit(solution)/shard_map/ppermute | solution.py:270
  52.2 0.8 %finish.1 = bf16[128,1024]{1,0:T(8,128)(2,1)} custom-call(f32[128,1024]{1,0:T(8,128)S(1)} %get-tuple-element.60.mine, bf16[128,512]{1,0:T(8,128)(2,1)S(1)} %collective-permute-done.13.one_low, bf16[128,512]{1,0:T(8,128)(2,1)S(1)} %collective-permute-done.16.one_high, bf16[128,512]{1,0:T(8,128)(2,1)S(1)} %collective-permute-done.17.two_low, ...), custom_call_target="tpu_custom_call" | custom-call | flops 1 | bytes 1 | tf_op jit(solution)/shard_map/finish/pallas_call | solution.py:237
  (16 shorter events, 0.1 us)
Async XLA Ops:
  2.3 5.5 %collective-permute-start.3 = (bf16[136,1024]{1,0:T(8,128)(2,1)S(1)}, bf16[136,1024]{1,0:T(8,128)(2,1)S(1)}, u32[]{:S(2)}, u32[]{:S(2)}) collective-permute-start(bf16[136,1024]{1,0:T(8,128)(2,1)S(1)} %fusion.1.refs_0_), channel_id=1, source_target_pairs={{0,1},{1,0},{2,3},{3,2},{4,5},{5,4},{6,7},{7,6},{8,9},{9,8},{10,11... | collective-permute-start | bytes 835592 | tf_op jit(solution)/shard_map/ppermute | solution.py:273
  2.8 11.4 %collective-permute-start.6 = (bf16[136,1024]{1,0:T(8,128)(2,1)S(1)}, bf16[136,1024]{1,0:T(8,128)(2,1)}, u32[]{:S(2)}, u32[]{:S(2)}) collective-permute-start(bf16[136,1024]{1,0:T(8,128)(2,1)S(1)} %fusion.1.refs_0_), channel_id=1, source_target_pairs={{0,24},{8,16},{16,8},{24,0},{1,25},{9,17},{17,9},{25,1},{2,26},{10... | collective-permute-start | bytes 835592 | tf_op jit(solution)/shard_map/ppermute | solution.py:270
  6.3 13.4 %collective-permute-start.5 = (bf16[136,1024]{1,0:T(8,128)(2,1)S(1)}, bf16[136,1024]{1,0:T(8,128)(2,1)}, u32[]{:S(2)}, u32[]{:S(2)}) collective-permute-start(bf16[136,1024]{1,0:T(8,128)(2,1)S(1)} %fusion.1.refs_0_), channel_id=1, source_target_pairs={{0,16},{8,24},{16,0},{24,8},{1,17},{9,25},{17,1},{25,9},{2,18},{10... | collective-permute-start | bytes 835592 | tf_op jit(solution)/shard_map/ppermute | solution.py:270
  6.8 13.6 %collective-permute-start.4 = (bf16[136,1024]{1,0:T(8,128)(2,1)S(1)}, bf16[136,1024]{1,0:T(8,128)(2,1)}, u32[]{:S(2)}, u32[]{:S(2)}) collective-permute-start(bf16[136,1024]{1,0:T(8,128)(2,1)S(1)} %fusion.1.refs_0_), channel_id=1, source_target_pairs={{0,8},{8,0},{16,24},{24,16},{1,9},{9,1},{17,25},{25,17},{2,10},{10... | collective-permute-start | bytes 835592 | tf_op jit(solution)/shard_map/ppermute | solution.py:270
  7.8 1.1 %copy-start.1 = (bf16[128,4,704]{0,2,1:T(8,128)(2,1)S(1)}, bf16[128,4,704]{0,2,1:T(8,128)(2,1)}, u32[]{:S(2)}) copy-start(bf16[128,4,704]{0,2,1:T(8,128)(2,1)} %param.9) | copy-start | bytes 2162692
  10.8 21.0 %collective-permute-start.7 = (bf16[144,768]{1,0:T(8,128)(2,1)}, bf16[144,768]{1,0:T(8,128)(2,1)S(1)}, u32[]{:S(2)}, u32[]{:S(2)}) collective-permute-start(bf16[144,768]{1,0:T(8,128)(2,1)} %get-tuple-element.57), channel_id=1, source_target_pairs={{0,8},{8,0},{16,24},{24,16},{1,9},{9,1},{17,25},{25,17},{2,10},{10... | collective-permute-start | bytes 663560 | tf_op jit(solution)/shard_map/ppermute | solution.py:270
  12.7 20.5 %collective-permute-start.8 = (bf16[144,768]{1,0:T(8,128)(2,1)S(1)}, bf16[144,768]{1,0:T(8,128)(2,1)S(1)}, u32[]{:S(2)}, u32[]{:S(2)}) collective-permute-start(bf16[144,768]{1,0:T(8,128)(2,1)S(1)} %get-tuple-element.58), channel_id=1, source_target_pairs={{0,16},{8,24},{16,0},{24,8},{1,17},{9,25},{17,1},{25,9},{2,18},{10... | collective-permute-start | bytes 663560 | tf_op jit(solution)/shard_map/ppermute | solution.py:270
  14.3 1.9 %collective-permute-start = (bf16[136,1024]{1,0:T(8,128)(2,1)}, bf16[136,1024]{1,0:T(8,128)(2,1)}, u32[]{:S(2)}, u32[]{:S(2)}) collective-permute-start(bf16[136,1024]{1,0:T(8,128)(2,1)} %param.1), channel_id=1, source_target_pairs={{0,1},{1,0},{2,3},{3,2},{4,5},{5,4},{6,7},{7,6},{8,9},{9,8},{10,11... | collective-permute-start | bytes 835592 | tf_op jit(solution)/shard_map/cond/branch_1_fun/ppermute | solution.py:273
  16.2 17.1 %collective-permute-start.9 = (bf16[144,768]{1,0:T(8,128)(2,1)S(1)}, bf16[144,768]{1,0:T(8,128)(2,1)S(1)}, u32[]{:S(2)}, u32[]{:S(2)}) collective-permute-start(bf16[144,768]{1,0:T(8,128)(2,1)S(1)} %get-tuple-element.59), channel_id=1, source_target_pairs={{0,24},{8,16},{16,8},{24,0},{1,25},{9,17},{17,9},{25,1},{2,26},{10... | collective-permute-start | bytes 663560 | tf_op jit(solution)/shard_map/ppermute | solution.py:270
  20.4 12.8 %slice-start = ((s8[5767168]{0:T(1024)(128)(4,1)}), s8[1572864]{0:T(1024)(128)(4,1)S(1)}, s32[]{:S(2)}) async-start(s8[5767168]{0:T(1024)(128)(4,1)} %bitcast.7), calls=%async_computation | async-start | bytes 3145728
  20.4 1.9 %collective-permute-start.1 = (bf16[136,1024]{1,0:T(8,128)(2,1)}, bf16[136,1024]{1,0:T(8,128)(2,1)}, u32[]{:S(2)}, u32[]{:S(2)}) collective-permute-start(bf16[136,1024]{1,0:T(8,128)(2,1)} %get-tuple-element.13), channel_id=1, source_target_pairs={{0,1},{1,0},{2,3},{3,2},{4,5},{5,4},{6,7},{7,6},{8,9},{9,8},{10,11... | collective-permute-start | bytes 835592 | tf_op jit(solution)/shard_map/cond/branch_1_fun/ppermute | solution.py:273
  20.4 2.3 %collective-permute-start.2 = (bf16[136,1024]{1,0:T(8,128)(2,1)}, bf16[136,1024]{1,0:T(8,128)(2,1)}, u32[]{:S(2)}, u32[]{:S(2)}) collective-permute-start(bf16[136,1024]{1,0:T(8,128)(2,1)} %get-tuple-element.14), channel_id=1, source_target_pairs={{0,1},{1,0},{2,3},{3,2},{4,5},{5,4},{6,7},{7,6},{8,9},{9,8},{10,11... | collective-permute-start | bytes 835592 | tf_op jit(solution)/shard_map/cond/branch_1_fun/ppermute | solution.py:273
  25.0 2.6 %copy-start = (bf16[2,704,2048]{2,1,0:T(8,128)(2,1)S(1)}, bf16[2,704,2048]{2,1,0:T(8,128)(2,1)}, u32[]{:S(2)}) copy-start(bf16[2,704,2048]{2,1,0:T(8,128)(2,1)} %refs_4_.3) | copy-start | bytes 17301508
  27.6 5.6 %slice-start.1 = ((s8[5767168]{0:T(1024)(128)(4,1)}), s8[4194304]{0:T(1024)(128)(4,1)S(1)}, s32[]{:S(2)}) async-start(s8[5767168]{0:T(1024)(128)(4,1)} %bitcast.7), calls=%async_computation.1 | async-start | bytes 8388608
  29.7 11.2 %collective-permute-start.11 = (bf16[144,704]{1,0:T(8,128)(2,1)S(1)}, bf16[144,704]{1,0:T(8,128)(2,1)S(1)}, u32[]{:S(2)}, u32[]{:S(2)}) collective-permute-start(bf16[144,704]{1,0:T(8,128)(2,1)S(1)} %get-tuple-element.63), channel_id=1, source_target_pairs={{0,8},{8,0},{16,24},{24,16},{1,9},{9,1},{17,25},{25,17},{2,10},{10... | collective-permute-start | bytes 608264 | tf_op jit(solution)/shard_map/ppermute | solution.py:270
  31.2 12.2 %collective-permute-start.12 = (bf16[144,704]{1,0:T(8,128)(2,1)S(1)}, bf16[144,704]{1,0:T(8,128)(2,1)S(1)}, u32[]{:S(2)}, u32[]{:S(2)}) collective-permute-start(bf16[144,704]{1,0:T(8,128)(2,1)S(1)} %get-tuple-element.64), channel_id=1, source_target_pairs={{0,16},{8,24},{16,0},{24,8},{1,17},{9,25},{17,1},{25,9},{2,18},{10... | collective-permute-start | bytes 608264 | tf_op jit(solution)/shard_map/ppermute | solution.py:270
  31.8 16.4 %collective-permute-start.19 = (bf16[144,704]{1,0:T(8,128)(2,1)S(1)}, bf16[144,704]{1,0:T(8,128)(2,1)S(1)}, u32[]{:S(2)}, u32[]{:S(2)}) collective-permute-start(bf16[144,704]{1,0:T(8,128)(2,1)S(1)} %get-tuple-element.76), channel_id=1, source_target_pairs={{0,24},{8,16},{16,8},{24,0},{1,25},{9,17},{17,9},{25,1},{2,26},{10... | collective-permute-start | bytes 608264 | tf_op jit(solution)/shard_map/ppermute | solution.py:270
  35.7 2.7 %collective-permute-start.10 = (bf16[512,1024]{1,0:T(8,128)(2,1)S(1)}, bf16[512,1024]{1,0:T(8,128)(2,1)S(1)}, u32[]{:S(2)}, u32[]{:S(2)}) collective-permute-start(bf16[512,1024]{1,0:T(8,128)(2,1)S(1)} %mix_sibling.1), channel_id=1, source_target_pairs={{0,1},{1,0},{2,3},{3,2},{4,5},{5,4},{6,7},{7,6},{8,9},{9,8},{10,11... | collective-permute-start | bytes 3145736 | tf_op jit(solution)/shard_map/ppermute | solution.py:273
  38.7 6.4 %collective-permute-start.14 = (bf16[128,512]{1,0:T(8,128)(2,1)S(1)}, bf16[128,512]{1,0:T(8,128)(2,1)S(1)}, u32[]{:S(2)}, u32[]{:S(2)}) collective-permute-start(bf16[128,512]{1,0:T(8,128)(2,1)S(1)} %get-tuple-element.68), channel_id=1, source_target_pairs={{0,8},{8,0},{16,24},{24,16},{1,9},{9,1},{17,25},{25,17},{2,10},{10... | collective-permute-start | bytes 393224 | tf_op jit(solution)/shard_map/ppermute | solution.py:270
  40.2 6.4 %collective-permute-start.15 = (bf16[128,512]{1,0:T(8,128)(2,1)S(1)}, bf16[128,512]{1,0:T(8,128)(2,1)S(1)}, u32[]{:S(2)}, u32[]{:S(2)}) collective-permute-start(bf16[128,512]{1,0:T(8,128)(2,1)S(1)} %get-tuple-element.69), channel_id=1, source_target_pairs={{0,16},{8,24},{16,0},{24,8},{1,17},{9,25},{17,1},{25,9},{2,18},{10... | collective-permute-start | bytes 393224 | tf_op jit(solution)/shard_map/ppermute | solution.py:270
  43.4 7.2 %collective-permute-start.13 = (bf16[128,512]{1,0:T(8,128)(2,1)S(1)}, bf16[128,512]{1,0:T(8,128)(2,1)S(1)}, u32[]{:S(2)}, u32[]{:S(2)}) collective-permute-start(bf16[128,512]{1,0:T(8,128)(2,1)S(1)} %get-tuple-element.65), channel_id=1, source_target_pairs={{0,8},{8,0},{16,24},{24,16},{1,9},{9,1},{17,25},{25,17},{2,10},{10... | collective-permute-start | bytes 393224 | tf_op jit(solution)/shard_map/ppermute | solution.py:270
  43.6 7.0 %collective-permute-start.18 = (bf16[128,512]{1,0:T(8,128)(2,1)S(1)}, bf16[128,512]{1,0:T(8,128)(2,1)S(1)}, u32[]{:S(2)}, u32[]{:S(2)}) collective-permute-start(bf16[128,512]{1,0:T(8,128)(2,1)S(1)} %get-tuple-element.72), channel_id=1, source_target_pairs={{0,16},{8,24},{16,0},{24,8},{1,17},{9,25},{17,1},{25,9},{2,18},{10... | collective-permute-start | bytes 393224 | tf_op jit(solution)/shard_map/ppermute | solution.py:270
  46.6 5.0 %collective-permute-start.16 = (bf16[128,512]{1,0:T(8,128)(2,1)S(1)}, bf16[128,512]{1,0:T(8,128)(2,1)S(1)}, u32[]{:S(2)}, u32[]{:S(2)}) collective-permute-start(bf16[128,512]{1,0:T(8,128)(2,1)S(1)} %get-tuple-element.70), channel_id=1, source_target_pairs={{0,8},{8,0},{16,24},{24,16},{1,9},{9,1},{17,25},{25,17},{2,10},{10... | collective-permute-start | bytes 393224 | tf_op jit(solution)/shard_map/ppermute | solution.py:270
  47.2 5.0 %collective-permute-start.17 = (bf16[128,512]{1,0:T(8,128)(2,1)S(1)}, bf16[128,512]{1,0:T(8,128)(2,1)S(1)}, u32[]{:S(2)}, u32[]{:S(2)}) collective-permute-start(bf16[128,512]{1,0:T(8,128)(2,1)S(1)} %get-tuple-element.71), channel_id=1, source_target_pairs={{0,16},{8,24},{16,0},{24,8},{1,17},{9,25},{17,1},{25,9},{2,18},{10... | collective-permute-start | bytes 393224 | tf_op jit(solution)/shard_map/ppermute | solution.py:270

commit v9 on v8

--- a/solution.py
+++ b/solution.py
@@ -299,7 +299,7 @@
         other = [swapped] + swaps(own[1:])
     (x,) = run(
         functools.partial(gather_kernel, dims, top), [shaped((local, n * cap, full))],
-        [place, *own, *other], where=placed, name="gather", weight=15 * 10**8,
+        [place, *own, *other], where=placed, name="gather", weight=20 * 10**8,
     )
     grad_sent = run(
         functools.partial(grad_kernel, dims), [slot] * n, [x, w_down], name="grad"

time: 53.3 us -> 50.9 us (0.955)
  local copies, waits for them, and re-layouts: 3.74 us -> 1.83 us
  Pallas kernels: 14.5 us -> 13.8 us
    unnamed x8 -> x4, local copies, waits for them, and re-layouts: 3.74 us -> 1.83 us
    pallas_call x9, Pallas kernels: 14.5 us -> 13.8 us  [call(): pl.pallas_call(kernel, out_shape=outs, in_specs=[pl.BlockSpec(memory_spac...]
  transfers between devices with their start and end apart: 20 -> 20, of which waited for: 11 -> 12; matrix products, arithmetic and copies ran while one was open for 1% -> 2% of each run, Pallas kernels for 26% -> 26%
where the time goes in v9:
time: 50.9 us; the launch traced here: 50.7 us
  starting transfers between devices  19.4 us (38%)
  Pallas kernels  13.8 us (27%)
  waiting for transfers between devices  12.4 us (24%)
  other arithmetic  2.44 us (5%)
  local copies, waits for them, and re-layouts  1.83 us (4%)
  between operations  0.7 us (1%)
    ppermute x15, starting transfers between devices, send(): return lax.ppermute(x, 'ctx', [(i, i ^ s) for i in range(n)]) if s else x  18.3 us
    pallas_call x9, Pallas kernels, call(): pl.pallas_call(kernel, out_shape=outs, in_specs=[pl.BlockSpec(memory_spac...  13.8 us
    ppermute x15, waiting for transfers between devices, send(): return lax.ppermute(x, 'ctx', [(i, i ^ s) for i in range(n)]) if s else x  8.97 us
    ppermute x5, waiting for transfers between devices, swap(): return lax.ppermute(x, 'tp', [(0, 1), (1, 0)])  3.46 us
    unnamed x4, local copies, waits for them, and re-layouts  1.83 us
    ppermute x5, starting transfers between devices, swap(): return lax.ppermute(x, 'tp', [(0, 1), (1, 0)])  1.1 us
  transfers between devices with their start and end apart: 20, of which 12 were waited for; matrix products, arithmetic and copies ran while one was open for 2% of the time, Pallas kernels for 26%

profile of v9, /device:TPU:0, one launch (start us, length us, event | category | flops | bytes accessed | tf_op | source)
XLA Modules:
  0.0 50.7 jit_solution(6629219126184760458)
XLA Ops:
  0.6 0.7 %bitcast_convert_fusion = bf16[4,128]{1,0:T(4,128)(2,1)S(1)} fusion(s32[128,4]{0,1:T(4,128)} %param.10), kind=kLoop, calls=%fused_computation.5 | loop fusion | flops 512 | bytes 3072 | tf_op jit(solution)/shard_map/convert_element_type | solution.py:277
  1.3 1.0 %fusion.1.refs_0_ = bf16[136,1024]{1,0:T(8,128)(2,1)S(1)} fusion(bf16[4,128]{1,0:T(4,128)(2,1)S(1)} %bitcast_convert_fusion, bf16[128,1024]{1,0:T(8,128)(2,1)} %param.12), kind=kLoop, calls=%fused_computation.2 | loop fusion | flops 835584 | bytes 541696 | tf_op jit(solution)/shard_map/concatenate | solution.py:278
  2.3 0.5 %collective-permute-start.3 = (bf16[136,1024]{1,0:T(8,128)(2,1)S(1)}, bf16[136,1024]{1,0:T(8,128)(2,1)S(1)}, u32[]{:S(2)}, u32[]{:S(2)}) collective-permute-start(bf16[136,1024]{1,0:T(8,128)(2,1)S(1)} %fusion.1.refs_0_), channel_id=1, source_target_pairs={{0,1},{1,0},{2,3},{3,2},{4,5},{5,4},{6,7},{7,6},{8,9},{9,8},{10,11... | collective-permute-start | bytes 835592 | tf_op jit(solution)/shard_map/ppermute | solution.py:273
  2.8 3.5 %collective-permute-start.6 = (bf16[136,1024]{1,0:T(8,128)(2,1)S(1)}, bf16[136,1024]{1,0:T(8,128)(2,1)S(1)}, u32[]{:S(2)}, u32[]{:S(2)}) collective-permute-start(bf16[136,1024]{1,0:T(8,128)(2,1)S(1)} %fusion.1.refs_0_), channel_id=1, source_target_pairs={{0,24},{8,16},{16,8},{24,0},{1,25},{9,17},{17,9},{25,1},{2,26},{10... | collective-permute-start | bytes 835592 | tf_op jit(solution)/shard_map/ppermute | solution.py:270
  6.3 0.5 collective-permute-start.5
  6.8 0.1 collective-permute-start.4
  7.0 0.1 pad_add_fusion.1.place
  7.0 0.7 %pad_add_fusion.meta_ref = s32[8,128]{1,0:T(8,128)S(1)} fusion(s32[4,128]{1,0:T(4,128)} %bitcast.9, s32[4,128]{1,0:T(4,128)} %bitcast.8), kind=kLoop, calls=%fused_computation.3 | loop fusion | flops 1024 | bytes 8192 | tf_op jit(solution)/shard_map/concatenate | solution.py:275
  7.8 0.0 collective-permute-done.3.refs_4_
  7.8 0.0 copy-start.1
  7.8 1.1 %copy-done.1 = bf16[128,4,704]{0,2,1:T(8,128)(2,1)S(1)} copy-done((bf16[128,4,704]{0,2,1:T(8,128)(2,1)S(1)}, bf16[128,4,704]{0,2,1:T(8,128)(2,1)}, u32[]{:S(2)}) %copy-start.1) | copy-done | bytes 720920
  8.9 1.4 %dispatch.1 = (bf16[144,768]{1,0:T(8,128)(2,1)S(1)}, bf16[144,768]{1,0:T(8,128)(2,1)S(1)}, bf16[144,768]{1,0:T(8,128)(2,1)S(1)}, bf16[144,768]{1,0:T(8,128)(2,1)S(1)}) custom-call(s32[2]{0:T(128)S(1)} %pad_add_fusion.1.place, s32[8,128]{1,0:T(8,128)S(1)} %pad_add_fusion.meta_ref, bf16[4,704,128]{2,1,0:T(8,128)(2,1)S(1)} %bitcast.7), custom_call_target="tpu_custom_call" | custom-call | flops 1 | bytes 1 | tf_op jit(solution)/shard_map/dispatch/pallas_call | solution.py:237
  10.2 1.9 %collective-permute-start.7 = (bf16[144,768]{1,0:T(8,128)(2,1)S(1)}, bf16[144,768]{1,0:T(8,128)(2,1)S(1)}, u32[]{:S(2)}, u32[]{:S(2)}) collective-permute-start(bf16[144,768]{1,0:T(8,128)(2,1)S(1)} %get-tuple-element.57), channel_id=1, source_target_pairs={{0,8},{8,0},{16,24},{24,16},{1,9},{9,1},{17,25},{25,17},{2,10},{10... | collective-permute-start | bytes 663560 | tf_op jit(solution)/shard_map/ppermute | solution.py:270
  12.2 1.5 %collective-permute-start.8 = (bf16[144,768]{1,0:T(8,128)(2,1)S(1)}, bf16[144,768]{1,0:T(8,128)(2,1)S(1)}, u32[]{:S(2)}, u32[]{:S(2)}) collective-permute-start(bf16[144,768]{1,0:T(8,128)(2,1)S(1)} %get-tuple-element.58), channel_id=1, source_target_pairs={{0,16},{8,24},{16,0},{24,8},{1,17},{9,25},{17,1},{25,9},{2,18},{10... | collective-permute-start | bytes 663560 | tf_op jit(solution)/shard_map/ppermute | solution.py:270
  13.7 0.2 collective-permute-done.6.refs_3_
  13.9 1.7 %conditional.2 = (bf16[136,1024]{1,0:T(8,128)(2,1)}) conditional(s32[]{:T(128)} %convert_element_type.10, bf16[136,1024]{1,0:T(8,128)(2,1)S(1)} %collective-permute-done.6.refs_3_, bf16[136,1024]{1,0:T(8,128)(2,1)S(1)} %collective-permute-done.6.refs_3_), branch_computations={%region_0.1_spmd, %region_1.2_spmd} | conditional | bytes 1114160 | solution.py:295
  13.9 1.7 %collective-permute-done = bf16[136,1024]{1,0:T(8,128)(2,1)} collective-permute-done((bf16[136,1024]{1,0:T(8,128)(2,1)S(1)}, bf16[136,1024]{1,0:T(8,128)(2,1)}, u32[]{:S(2)}, u32[]{:S(2)}) %collective-permute-start) | collective-permute-done | bytes 278560 | tf_op jit(solution)/shard_map/cond/branch_1_fun/ppermute | solution.py:273
  15.6 2.8 %collective-permute-start.9 = (bf16[144,768]{1,0:T(8,128)(2,1)S(1)}, bf16[144,768]{1,0:T(8,128)(2,1)S(1)}, u32[]{:S(2)}, u32[]{:S(2)}) collective-permute-start(bf16[144,768]{1,0:T(8,128)(2,1)S(1)} %get-tuple-element.59), channel_id=1, source_target_pairs={{0,24},{8,16},{16,8},{24,0},{1,25},{9,17},{17,9},{25,1},{2,26},{10... | collective-permute-start | bytes 663560 | tf_op jit(solution)/shard_map/ppermute | solution.py:270
  18.4 1.2 %collective-permute-done.5.refs_2_ = bf16[136,1024]{1,0:T(8,128)(2,1)S(1)} collective-permute-done((bf16[136,1024]{1,0:T(8,128)(2,1)S(1)}, bf16[136,1024]{1,0:T(8,128)(2,1)S(1)}, u32[]{:S(2)}, u32[]{:S(2)}) %collective-permute-start.5) | collective-permute-done | bytes 278560 | tf_op jit(solution)/shard_map/ppermute | solution.py:270
  19.6 0.7 %collective-permute-done.4.refs_1_ = bf16[136,1024]{1,0:T(8,128)(2,1)S(1)} collective-permute-done((bf16[136,1024]{1,0:T(8,128)(2,1)S(1)}, bf16[136,1024]{1,0:T(8,128)(2,1)S(1)}, u32[]{:S(2)}, u32[]{:S(2)}) %collective-permute-start.4) | collective-permute-done | bytes 278560 | tf_op jit(solution)/shard_map/ppermute | solution.py:270
  20.3 2.1 %conditional.3 = (bf16[136,1024]{1,0:T(8,128)(2,1)}, bf16[136,1024]{1,0:T(8,128)(2,1)}) conditional(s32[]{:T(128)} %convert_element_type.10, (bf16[136,1024]{1,0:T(8,128)(2,1)S(1)}, bf16[136,1024]{1,0:T(8,128)(2,1)S(1)}) %tuple.27, (bf16[136,1024]{1,0:T(8,128)(2,1)S(1)}, bf16[136,1024]{1,0:T(8,128)(2,1)S(1)}) %tuple.27), branch_computations={%region_2.3_spmd, %region_3.4_spmd} | conditional | bytes 2228320 | solution.py:297
  20.3 0.5 %collective-permute-start.2 = (bf16[136,1024]{1,0:T(8,128)(2,1)S(1)}, bf16[136,1024]{1,0:T(8,128)(2,1)}, u32[]{:S(2)}, u32[]{:S(2)}) collective-permute-start(bf16[136,1024]{1,0:T(8,128)(2,1)S(1)} %get-tuple-element.14), channel_id=1, source_target_pairs={{0,1},{1,0},{2,3},{3,2},{4,5},{5,4},{6,7},{7,6},{8,9},{9,8},{10,11... | collective-permute-start | bytes 835592 | tf_op jit(solution)/shard_map/cond/branch_1_fun/ppermute | solution.py:273
  20.8 1.2 %collective-permute-done.1 = bf16[136,1024]{1,0:T(8,128)(2,1)} collective-permute-done((bf16[136,1024]{1,0:T(8,128)(2,1)S(1)}, bf16[136,1024]{1,0:T(8,128)(2,1)}, u32[]{:S(2)}, u32[]{:S(2)}) %collective-permute-start.1) | collective-permute-done | bytes 278560 | tf_op jit(solution)/shard_map/cond/branch_1_fun/ppermute | solution.py:273
  22.0 0.4 collective-permute-done.2
  22.4 2.2 %gather.1.x_ref = bf16[2,288,2048]{2,1,0:T(8,128)(2,1)S(1)} custom-call(s32[2]{0:T(128)S(1)} %pad_add_fusion.1.place, bf16[136,1024]{1,0:T(8,128)(2,1)S(1)} %fusion.1.refs_0_, bf16[136,1024]{1,0:T(8,128)(2,1)S(1)} %collective-permute-done.4.refs_1_, bf16[136,1024]{1,0:T(8,128)(2,1)S(1)} %collective-permute-done.5.refs_2_, ...), custom_call_target="tpu_custom_call" | custom-call | flops 2000000000 | bytes 1 | tf_op jit(solution)/shard_map/gather/pallas_call | solution.py:237
  24.6 0.7 %copy-done = bf16[2,704,2048]{2,1,0:T(8,128)(2,1)S(1)} copy-done((bf16[2,704,2048]{2,1,0:T(8,128)(2,1)S(1)}, bf16[2,704,2048]{2,1,0:T(8,128)(2,1)}, u32[]{:S(2)}) %copy-start) | copy-done | bytes 5767192
  25.3 2.1 %grad.1 = (bf16[144,704]{1,0:T(8,128)(2,1)S(1)}, bf16[144,704]{1,0:T(8,128)(2,1)S(1)}, bf16[144,704]{1,0:T(8,128)(2,1)S(1)}, bf16[144,704]{1,0:T(8,128)(2,1)S(1)}) custom-call(bf16[2,288,2048]{2,1,0:T(8,128)(2,1)S(1)} %gather.1.x_ref, bf16[2,704,2048]{2,1,0:T(8,128)(2,1)S(1)} %copy-done), custom_call_target="tpu_custom_call" | custom-call | flops 1 | bytes 1 | tf_op jit(solution)/shard_map/grad/pallas_call | solution.py:237
  27.3 1.6 %collective-permute-start.11 = (bf16[144,704]{1,0:T(8,128)(2,1)S(1)}, bf16[144,704]{1,0:T(8,128)(2,1)S(1)}, u32[]{:S(2)}, u32[]{:S(2)}) collective-permute-start(bf16[144,704]{1,0:T(8,128)(2,1)S(1)} %get-tuple-element.63), channel_id=1, source_target_pairs={{0,8},{8,0},{16,24},{24,16},{1,9},{9,1},{17,25},{25,17},{2,10},{10... | collective-permute-start | bytes 608264 | tf_op jit(solution)/shard_map/ppermute | solution.py:270
  28.9 0.6 %collective-permute-start.12 = (bf16[144,704]{1,0:T(8,128)(2,1)S(1)}, bf16[144,704]{1,0:T(8,128)(2,1)S(1)}, u32[]{:S(2)}, u32[]{:S(2)}) collective-permute-start(bf16[144,704]{1,0:T(8,128)(2,1)S(1)} %get-tuple-element.64), channel_id=1, source_target_pairs={{0,16},{8,24},{16,0},{24,8},{1,17},{9,25},{17,1},{25,9},{2,18},{10... | collective-permute-start | bytes 608264 | tf_op jit(solution)/shard_map/ppermute | solution.py:270
  29.5 1.4 %collective-permute-start.19 = (bf16[144,704]{1,0:T(8,128)(2,1)S(1)}, bf16[144,704]{1,0:T(8,128)(2,1)S(1)}, u32[]{:S(2)}, u32[]{:S(2)}) collective-permute-start(bf16[144,704]{1,0:T(8,128)(2,1)S(1)} %get-tuple-element.76), channel_id=1, source_target_pairs={{0,24},{8,16},{16,8},{24,0},{1,25},{9,17},{17,9},{25,1},{2,26},{10... | collective-permute-start | bytes 608264 | tf_op jit(solution)/shard_map/ppermute | solution.py:270
  30.9 2.5 %mix_sibling.1 = bf16[512,1024]{1,0:T(8,128)(2,1)S(1)} custom-call(s32[2]{0:T(128)S(1)} %pad_add_fusion.1.place, bf16[144,768]{1,0:T(8,128)(2,1)S(1)} %get-tuple-element.56.refs_0_, bf16[144,768]{1,0:T(8,128)(2,1)S(1)} %collective-permute-done.7.refs_1_, bf16[144,768]{1,0:T(8,128)(2,1)S(1)} %collective-permute-done.8.refs_2_, ...), custom_call_target="tpu_custom_call" | custom-call | flops 1 | bytes 1 | tf_op jit(solution)/shard_map/mix_sibling/pallas_call | solution.py:237
  33.4 0.1 collective-permute-start.10
  33.4 2.4 %mix_own.1.own = f32[512,1024]{1,0:T(8,128)S(1)} custom-call(s32[2]{0:T(128)S(1)} %pad_add_fusion.1.place, bf16[144,768]{1,0:T(8,128)(2,1)S(1)} %get-tuple-element.56.refs_0_, bf16[144,768]{1,0:T(8,128)(2,1)S(1)} %collective-permute-done.7.refs_1_, bf16[144,768]{1,0:T(8,128)(2,1)S(1)} %collective-permute-done.8.refs_2_, ...), custom_call_target="tpu_custom_call" | custom-call | flops 99999997952 | bytes 1 | tf_op jit(solution)/shard_map/mix_own/pallas_call | solution.py:237
  35.9 0.2 collective-permute-done.10.arrived
  36.1 0.2 add.7
  36.3 1.6 %collective-permute-start.14 = (bf16[128,512]{1,0:T(8,128)(2,1)S(1)}, bf16[128,512]{1,0:T(8,128)(2,1)S(1)}, u32[]{:S(2)}, u32[]{:S(2)}) collective-permute-start(bf16[128,512]{1,0:T(8,128)(2,1)S(1)} %get-tuple-element.68), channel_id=1, source_target_pairs={{0,8},{8,0},{16,24},{24,16},{1,9},{9,1},{17,25},{25,17},{2,10},{10... | collective-permute-start | bytes 393224 | tf_op jit(solution)/shard_map/ppermute | solution.py:270
  37.9 0.6 %collective-permute-start.15 = (bf16[128,512]{1,0:T(8,128)(2,1)S(1)}, bf16[128,512]{1,0:T(8,128)(2,1)S(1)}, u32[]{:S(2)}, u32[]{:S(2)}) collective-permute-start(bf16[128,512]{1,0:T(8,128)(2,1)S(1)} %get-tuple-element.69), channel_id=1, source_target_pairs={{0,16},{8,24},{16,0},{24,8},{1,17},{9,25},{17,1},{25,9},{2,18},{10... | collective-permute-start | bytes 393224 | tf_op jit(solution)/shard_map/ppermute | solution.py:270
  38.5 2.6 %collective-permute-done.12.refs_2_ = bf16[144,704]{1,0:T(8,128)(2,1)S(1)} collective-permute-done((bf16[144,704]{1,0:T(8,128)(2,1)S(1)}, bf16[144,704]{1,0:T(8,128)(2,1)S(1)}, u32[]{:S(2)}, u32[]{:S(2)}) %collective-permute-start.12) | collective-permute-done | bytes 202784 | tf_op jit(solution)/shard_map/ppermute | solution.py:270
  41.1 0.2 collective-permute-start.13
  41.2 0.3 collective-permute-start.18
  41.6 1.2 %collective-permute-done.14.low = bf16[128,512]{1,0:T(8,128)(2,1)S(1)} collective-permute-done((bf16[128,512]{1,0:T(8,128)(2,1)S(1)}, bf16[128,512]{1,0:T(8,128)(2,1)S(1)}, u32[]{:S(2)}, u32[]{:S(2)}) %collective-permute-start.14) | collective-permute-done | bytes 131104 | tf_op jit(solution)/shard_map/ppermute | solution.py:270
  42.8 1.5 %collective-permute-done.15.high = bf16[128,512]{1,0:T(8,128)(2,1)S(1)} collective-permute-done((bf16[128,512]{1,0:T(8,128)(2,1)S(1)}, bf16[128,512]{1,0:T(8,128)(2,1)S(1)}, u32[]{:S(2)}, u32[]{:S(2)}) %collective-permute-start.15) | collective-permute-done | bytes 131104 | tf_op jit(solution)/shard_map/ppermute | solution.py:270
  44.3 0.6 %collective-permute-start.16 = (bf16[128,512]{1,0:T(8,128)(2,1)S(1)}, bf16[128,512]{1,0:T(8,128)(2,1)S(1)}, u32[]{:S(2)}, u32[]{:S(2)}) collective-permute-start(bf16[128,512]{1,0:T(8,128)(2,1)S(1)} %get-tuple-element.70), channel_id=1, source_target_pairs={{0,8},{8,0},{16,24},{24,16},{1,9},{9,1},{17,25},{25,17},{2,10},{10... | collective-permute-start | bytes 393224 | tf_op jit(solution)/shard_map/ppermute | solution.py:270
  44.9 1.0 %collective-permute-start.17 = (bf16[128,512]{1,0:T(8,128)(2,1)S(1)}, bf16[128,512]{1,0:T(8,128)(2,1)S(1)}, u32[]{:S(2)}, u32[]{:S(2)}) collective-permute-start(bf16[128,512]{1,0:T(8,128)(2,1)S(1)} %get-tuple-element.71), channel_id=1, source_target_pairs={{0,16},{8,24},{16,0},{24,8},{1,17},{9,25},{17,1},{25,9},{2,18},{10... | collective-permute-start | bytes 393224 | tf_op jit(solution)/shard_map/ppermute | solution.py:270
  45.9 2.3 %restore.1 = bf16[4,704,128]{2,1,0:T(8,128)(2,1)} custom-call(s32[2]{0:T(128)S(1)} %pad_add_fusion.1.place, s32[8,128]{1,0:T(8,128)S(1)} %pad_add_fusion.meta_ref, bf16[144,704]{1,0:T(8,128)(2,1)S(1)} %get-tuple-element.73.refs_0_, bf16[144,704]{1,0:T(8,128)(2,1)S(1)} %collective-permute-done.11.refs_1_, ...), custom_call_target="tpu_custom_call" | custom-call | flops 99999997952 | bytes 1 | tf_op jit(solution)/shard_map/restore/pallas_call | solution.py:237
  48.2 1.1 %collective-permute-done.16.one_high = bf16[128,512]{1,0:T(8,128)(2,1)S(1)} collective-permute-done((bf16[128,512]{1,0:T(8,128)(2,1)S(1)}, bf16[128,512]{1,0:T(8,128)(2,1)S(1)}, u32[]{:S(2)}, u32[]{:S(2)}) %collective-permute-start.16) | collective-permute-done | bytes 131104 | tf_op jit(solution)/shard_map/ppermute | solution.py:270
  49.3 0.5 %collective-permute-done.17.two_low = bf16[128,512]{1,0:T(8,128)(2,1)S(1)} collective-permute-done((bf16[128,512]{1,0:T(8,128)(2,1)S(1)}, bf16[128,512]{1,0:T(8,128)(2,1)S(1)}, u32[]{:S(2)}, u32[]{:S(2)}) %collective-permute-start.17) | collective-permute-done | bytes 131104 | tf_op jit(solution)/shard_map/ppermute | solution.py:270
  49.9 0.8 %finish.1 = bf16[128,1024]{1,0:T(8,128)(2,1)} custom-call(f32[128,1024]{1,0:T(8,128)S(1)} %get-tuple-element.60.mine, bf16[128,512]{1,0:T(8,128)(2,1)S(1)} %collective-permute-done.13.one_low, bf16[128,512]{1,0:T(8,128)(2,1)S(1)} %collective-permute-done.16.one_high, bf16[128,512]{1,0:T(8,128)(2,1)S(1)} %collective-permute-done.17.two_low, ...), custom_call_target="tpu_custom_call" | custom-call | flops 1 | bytes 1 | tf_op jit(solution)/shard_map/finish/pallas_call | solution.py:237
  (11 shorter events, 0.1 us)
Async XLA Ops:
  2.3 5.5 %collective-permute-start.3 = (bf16[136,1024]{1,0:T(8,128)(2,1)S(1)}, bf16[136,1024]{1,0:T(8,128)(2,1)S(1)}, u32[]{:S(2)}, u32[]{:S(2)}) collective-permute-start(bf16[136,1024]{1,0:T(8,128)(2,1)S(1)} %fusion.1.refs_0_), channel_id=1, source_target_pairs={{0,1},{1,0},{2,3},{3,2},{4,5},{5,4},{6,7},{7,6},{8,9},{9,8},{10,11... | collective-permute-start | bytes 835592 | tf_op jit(solution)/shard_map/ppermute | solution.py:273
  2.8 11.1 %collective-permute-start.6 = (bf16[136,1024]{1,0:T(8,128)(2,1)S(1)}, bf16[136,1024]{1,0:T(8,128)(2,1)S(1)}, u32[]{:S(2)}, u32[]{:S(2)}) collective-permute-start(bf16[136,1024]{1,0:T(8,128)(2,1)S(1)} %fusion.1.refs_0_), channel_id=1, source_target_pairs={{0,24},{8,16},{16,8},{24,0},{1,25},{9,17},{17,9},{25,1},{2,26},{10... | collective-permute-start | bytes 835592 | tf_op jit(solution)/shard_map/ppermute | solution.py:270
  6.3 13.3 %collective-permute-start.5 = (bf16[136,1024]{1,0:T(8,128)(2,1)S(1)}, bf16[136,1024]{1,0:T(8,128)(2,1)S(1)}, u32[]{:S(2)}, u32[]{:S(2)}) collective-permute-start(bf16[136,1024]{1,0:T(8,128)(2,1)S(1)} %fusion.1.refs_0_), channel_id=1, source_target_pairs={{0,16},{8,24},{16,0},{24,8},{1,17},{9,25},{17,1},{25,9},{2,18},{10... | collective-permute-start | bytes 835592 | tf_op jit(solution)/shard_map/ppermute | solution.py:270
  6.8 13.5 %collective-permute-start.4 = (bf16[136,1024]{1,0:T(8,128)(2,1)S(1)}, bf16[136,1024]{1,0:T(8,128)(2,1)S(1)}, u32[]{:S(2)}, u32[]{:S(2)}) collective-permute-start(bf16[136,1024]{1,0:T(8,128)(2,1)S(1)} %fusion.1.refs_0_), channel_id=1, source_target_pairs={{0,8},{8,0},{16,24},{24,16},{1,9},{9,1},{17,25},{25,17},{2,10},{10... | collective-permute-start | bytes 835592 | tf_op jit(solution)/shard_map/ppermute | solution.py:270
  7.8 1.1 %copy-start.1 = (bf16[128,4,704]{0,2,1:T(8,128)(2,1)S(1)}, bf16[128,4,704]{0,2,1:T(8,128)(2,1)}, u32[]{:S(2)}) copy-start(bf16[128,4,704]{0,2,1:T(8,128)(2,1)} %param.9) | copy-start | bytes 2162692
  10.2 19.3 %collective-permute-start.7 = (bf16[144,768]{1,0:T(8,128)(2,1)S(1)}, bf16[144,768]{1,0:T(8,128)(2,1)S(1)}, u32[]{:S(2)}, u32[]{:S(2)}) collective-permute-start(bf16[144,768]{1,0:T(8,128)(2,1)S(1)} %get-tuple-element.57), channel_id=1, source_target_pairs={{0,8},{8,0},{16,24},{24,16},{1,9},{9,1},{17,25},{25,17},{2,10},{10... | collective-permute-start | bytes 663560 | tf_op jit(solution)/shard_map/ppermute | solution.py:270
  12.2 18.7 %collective-permute-start.8 = (bf16[144,768]{1,0:T(8,128)(2,1)S(1)}, bf16[144,768]{1,0:T(8,128)(2,1)S(1)}, u32[]{:S(2)}, u32[]{:S(2)}) collective-permute-start(bf16[144,768]{1,0:T(8,128)(2,1)S(1)} %get-tuple-element.58), channel_id=1, source_target_pairs={{0,16},{8,24},{16,0},{24,8},{1,17},{9,25},{17,1},{25,9},{2,18},{10... | collective-permute-start | bytes 663560 | tf_op jit(solution)/shard_map/ppermute | solution.py:270
  13.9 1.7 %collective-permute-start = (bf16[136,1024]{1,0:T(8,128)(2,1)S(1)}, bf16[136,1024]{1,0:T(8,128)(2,1)}, u32[]{:S(2)}, u32[]{:S(2)}) collective-permute-start(bf16[136,1024]{1,0:T(8,128)(2,1)S(1)} %param.1), channel_id=1, source_target_pairs={{0,1},{1,0},{2,3},{3,2},{4,5},{5,4},{6,7},{7,6},{8,9},{9,8},{10,11... | collective-permute-start | bytes 835592 | tf_op jit(solution)/shard_map/cond/branch_1_fun/ppermute | solution.py:273
  15.6 15.3 %collective-permute-start.9 = (bf16[144,768]{1,0:T(8,128)(2,1)S(1)}, bf16[144,768]{1,0:T(8,128)(2,1)S(1)}, u32[]{:S(2)}, u32[]{:S(2)}) collective-permute-start(bf16[144,768]{1,0:T(8,128)(2,1)S(1)} %get-tuple-element.59), channel_id=1, source_target_pairs={{0,24},{8,16},{16,8},{24,0},{1,25},{9,17},{17,9},{25,1},{2,26},{10... | collective-permute-start | bytes 663560 | tf_op jit(solution)/shard_map/ppermute | solution.py:270
  20.3 1.7 %collective-permute-start.1 = (bf16[136,1024]{1,0:T(8,128)(2,1)S(1)}, bf16[136,1024]{1,0:T(8,128)(2,1)}, u32[]{:S(2)}, u32[]{:S(2)}) collective-permute-start(bf16[136,1024]{1,0:T(8,128)(2,1)S(1)} %get-tuple-element.13), channel_id=1, source_target_pairs={{0,1},{1,0},{2,3},{3,2},{4,5},{5,4},{6,7},{7,6},{8,9},{9,8},{10,11... | collective-permute-start | bytes 835592 | tf_op jit(solution)/shard_map/cond/branch_1_fun/ppermute | solution.py:273
  20.3 2.1 %collective-permute-start.2 = (bf16[136,1024]{1,0:T(8,128)(2,1)S(1)}, bf16[136,1024]{1,0:T(8,128)(2,1)}, u32[]{:S(2)}, u32[]{:S(2)}) collective-permute-start(bf16[136,1024]{1,0:T(8,128)(2,1)S(1)} %get-tuple-element.14), channel_id=1, source_target_pairs={{0,1},{1,0},{2,3},{3,2},{4,5},{5,4},{6,7},{7,6},{8,9},{9,8},{10,11... | collective-permute-start | bytes 835592 | tf_op jit(solution)/shard_map/cond/branch_1_fun/ppermute | solution.py:273
  22.4 2.9 %copy-start = (bf16[2,704,2048]{2,1,0:T(8,128)(2,1)S(1)}, bf16[2,704,2048]{2,1,0:T(8,128)(2,1)}, u32[]{:S(2)}) copy-start(bf16[2,704,2048]{2,1,0:T(8,128)(2,1)} %refs_4_.3) | copy-start | bytes 17301508
  27.3 11.2 %collective-permute-start.11 = (bf16[144,704]{1,0:T(8,128)(2,1)S(1)}, bf16[144,704]{1,0:T(8,128)(2,1)S(1)}, u32[]{:S(2)}, u32[]{:S(2)}) collective-permute-start(bf16[144,704]{1,0:T(8,128)(2,1)S(1)} %get-tuple-element.63), channel_id=1, source_target_pairs={{0,8},{8,0},{16,24},{24,16},{1,9},{9,1},{17,25},{25,17},{2,10},{10... | collective-permute-start | bytes 608264 | tf_op jit(solution)/shard_map/ppermute | solution.py:270
  28.9 12.2 %collective-permute-start.12 = (bf16[144,704]{1,0:T(8,128)(2,1)S(1)}, bf16[144,704]{1,0:T(8,128)(2,1)S(1)}, u32[]{:S(2)}, u32[]{:S(2)}) collective-permute-start(bf16[144,704]{1,0:T(8,128)(2,1)S(1)} %get-tuple-element.64), channel_id=1, source_target_pairs={{0,16},{8,24},{16,0},{24,8},{1,17},{9,25},{17,1},{25,9},{2,18},{10... | collective-permute-start | bytes 608264 | tf_op jit(solution)/shard_map/ppermute | solution.py:270
  29.5 16.4 %collective-permute-start.19 = (bf16[144,704]{1,0:T(8,128)(2,1)S(1)}, bf16[144,704]{1,0:T(8,128)(2,1)S(1)}, u32[]{:S(2)}, u32[]{:S(2)}) collective-permute-start(bf16[144,704]{1,0:T(8,128)(2,1)S(1)} %get-tuple-element.76), channel_id=1, source_target_pairs={{0,24},{8,16},{16,8},{24,0},{1,25},{9,17},{17,9},{25,1},{2,26},{10... | collective-permute-start | bytes 608264 | tf_op jit(solution)/shard_map/ppermute | solution.py:270
  33.4 2.7 %collective-permute-start.10 = (bf16[512,1024]{1,0:T(8,128)(2,1)S(1)}, bf16[512,1024]{1,0:T(8,128)(2,1)S(1)}, u32[]{:S(2)}, u32[]{:S(2)}) collective-permute-start(bf16[512,1024]{1,0:T(8,128)(2,1)S(1)} %mix_sibling.1), channel_id=1, source_target_pairs={{0,1},{1,0},{2,3},{3,2},{4,5},{5,4},{6,7},{7,6},{8,9},{9,8},{10,11... | collective-permute-start | bytes 3145736 | tf_op jit(solution)/shard_map/ppermute | solution.py:273
  36.3 6.4 %collective-permute-start.14 = (bf16[128,512]{1,0:T(8,128)(2,1)S(1)}, bf16[128,512]{1,0:T(8,128)(2,1)S(1)}, u32[]{:S(2)}, u32[]{:S(2)}) collective-permute-start(bf16[128,512]{1,0:T(8,128)(2,1)S(1)} %get-tuple-element.68), channel_id=1, source_target_pairs={{0,8},{8,0},{16,24},{24,16},{1,9},{9,1},{17,25},{25,17},{2,10},{10... | collective-permute-start | bytes 393224 | tf_op jit(solution)/shard_map/ppermute | solution.py:270
  37.9 6.4 %collective-permute-start.15 = (bf16[128,512]{1,0:T(8,128)(2,1)S(1)}, bf16[128,512]{1,0:T(8,128)(2,1)S(1)}, u32[]{:S(2)}, u32[]{:S(2)}) collective-permute-start(bf16[128,512]{1,0:T(8,128)(2,1)S(1)} %get-tuple-element.69), channel_id=1, source_target_pairs={{0,16},{8,24},{16,0},{24,8},{1,17},{9,25},{17,1},{25,9},{2,18},{10... | collective-permute-start | bytes 393224 | tf_op jit(solution)/shard_map/ppermute | solution.py:270
  41.1 7.2 %collective-permute-start.13 = (bf16[128,512]{1,0:T(8,128)(2,1)S(1)}, bf16[128,512]{1,0:T(8,128)(2,1)S(1)}, u32[]{:S(2)}, u32[]{:S(2)}) collective-permute-start(bf16[128,512]{1,0:T(8,128)(2,1)S(1)} %get-tuple-element.65), channel_id=1, source_target_pairs={{0,8},{8,0},{16,24},{24,16},{1,9},{9,1},{17,25},{25,17},{2,10},{10... | collective-permute-start | bytes 393224 | tf_op jit(solution)/shard_map/ppermute | solution.py:270
  41.2 7.0 %collective-permute-start.18 = (bf16[128,512]{1,0:T(8,128)(2,1)S(1)}, bf16[128,512]{1,0:T(8,128)(2,1)S(1)}, u32[]{:S(2)}, u32[]{:S(2)}) collective-permute-start(bf16[128,512]{1,0:T(8,128)(2,1)S(1)} %get-tuple-element.72), channel_id=1, source_target_pairs={{0,16},{8,24},{16,0},{24,8},{1,17},{9,25},{17,1},{25,9},{2,18},{10... | collective-permute-start | bytes 393224 | tf_op jit(solution)/shard_map/ppermute | solution.py:270
  44.3 5.0 %collective-permute-start.16 = (bf16[128,512]{1,0:T(8,128)(2,1)S(1)}, bf16[128,512]{1,0:T(8,128)(2,1)S(1)}, u32[]{:S(2)}, u32[]{:S(2)}) collective-permute-start(bf16[128,512]{1,0:T(8,128)(2,1)S(1)} %get-tuple-element.70), channel_id=1, source_target_pairs={{0,8},{8,0},{16,24},{24,16},{1,9},{9,1},{17,25},{25,17},{2,10},{10... | collective-permute-start | bytes 393224 | tf_op jit(solution)/shard_map/ppermute | solution.py:270
  44.9 5.0 %collective-permute-start.17 = (bf16[128,512]{1,0:T(8,128)(2,1)S(1)}, bf16[128,512]{1,0:T(8,128)(2,1)S(1)}, u32[]{:S(2)}, u32[]{:S(2)}) collective-permute-start(bf16[128,512]{1,0:T(8,128)(2,1)S(1)} %get-tuple-element.71), channel_id=1, source_target_pairs={{0,16},{8,24},{16,0},{24,8},{1,17},{9,25},{17,1},{25,9},{2,18},{10... | collective-permute-start | bytes 393224 | tf_op jit(solution)/shard_map/ppermute | solution.py:270

commit v10 on v9

--- a/solution.py
+++ b/solution.py
@@ -63,6 +63,39 @@
     return [ones_where(rows + l * cap == slot[l : l + 1, :]) for l in range(local)]
 
 
+def packed_rows(width, ff):
+    first = -(-(width // 2) // 16) * 16
+    return ff // 128 * width + (first if ff % 128 else 0), first
+
+
+def pack_slots(rows, out):
+    width, ff = rows.shape
+    full, rest = ff // 128, ff % 128
+    for c in range(full):
+        out[c * width : (c + 1) * width, :] = rows[:, c * 128 : (c + 1) * 128].astype(BF16)
+    if rest:
+        end, first = packed_rows(width, ff)
+        tail = rows[:, full * 128 :]
+        right = tail[first:]
+        if right.shape[0] < first:
+            spare = jnp.zeros((first - right.shape[0], rest), F32)
+            right = jnp.concatenate([right, spare], axis=0)
+        pair = jnp.concatenate([tail[:first], right], axis=1)
+        out[full * width : end, :] = pair.astype(BF16)
+
+
+def unpack_slots(ref, width, ff):
+    full, rest = ff // 128, ff % 128
+    blocks = [ref[c * width : (c + 1) * width, :].astype(F32) for c in range(full)]
+    if rest:
+        end, first = packed_rows(width, ff)
+        pair = ref[full * width : end, :].astype(F32)
+        blocks.append(
+            jnp.concatenate([pair[:, :rest], pair[: width - first, rest:]], axis=0)
+        )
+    return jnp.concatenate(blocks, axis=1)
+
+
 def picks_of(meta, me, dims):
     experts, local, cap, width = dims
     top = meta.shape[0] // 2
@@ -73,20 +106,28 @@
 
 
 def dispatch_kernel(dims, place, meta_ref, hid_ref, *outs):
-    width = outs[0].shape[0]
+    width = dims[3]
     picks, gate = picks_of(meta_ref[...], place[0], dims)
     scaled = [
         (hid_ref[k].astype(F32) * gate[k : k + 1, :]).astype(BF16)
         for k in range(hid_ref.shape[0])
     ]
-    rows = jnp.concatenate(scaled, axis=1)
-    spare = outs[0].shape[1] - rows.shape[0]
+    sent = dot(picks, jnp.concatenate(scaled, axis=1), NT)
     tokens = hid_ref.shape[2]
-    number = jnp.bitwise_and(iota((spare, rows.shape[1]), 1), tokens - 1) + 1
-    number = jnp.where(iota(number.shape, 0) == 0, number.astype(F32), 0.0)
-    sent = dot(picks, jnp.concatenate([rows, number.astype(BF16)], axis=0), NT)
+    number = jnp.bitwise_and(iota((8, picks.shape[1]), 1), tokens - 1) + 1
+    number = number.astype(F32).astype(BF16)
     for s, out in enumerate(outs):
-        out[...] = sent[s * width : (s + 1) * width].astype(BF16)
+        at = slice(s * width, (s + 1) * width)
+        pack_slots(sent[at], out)
+        names = dot(number, picks[at], NT)[:1]
+        if width % 128:
+            spare = jnp.zeros((1, -width % 128), F32)
+            names = jnp.concatenate([names, spare], axis=1)
+        lines = jnp.zeros((16, 128), F32)
+        for i in range(names.shape[1] // 128):
+            line = names[:, i * 128 : (i + 1) * 128]
+            lines = jnp.where(iota((16, 128), 0) == i, line, lines)
+        out[out.shape[0] - 16 :, :] = lines.astype(BF16)
 
 
 def by_expert(rows, local, cap):
@@ -144,7 +185,7 @@
     experts, local, cap, width = dims
     grads = [dot(x_ref[l], w_ref[l], NT) for l in range(local)]
     for s, rows in enumerate(by_source(grads, len(outs), cap)):
-        outs[s][...] = rows.astype(BF16)
+        pack_slots(rows, outs[s])
 
 
 def mix_rows(dims, side, hid, w_ref, tokens, half, store):
@@ -152,13 +193,15 @@
     n = len(hid)
     ff = w_ref.shape[1]
     chunk = min(half, 256)
-    same = ones_where(iota((tokens, tokens), 0) == iota((tokens, tokens), 1))
-    held = []
+    held, rows = [], []
     for h in hid:
-        number = h[:, ff : ff + 1].astype(F32).astype(jnp.int32) - 1
-        slots = ones_where(iota((width, tokens), 1) == number)
-        held.append(dot(same, slots, NT).astype(BF16))
-    rows = [h[:, :ff].astype(F32) for h in hid]
+        lines = h[h.shape[0] - 16 :, :].astype(F32)
+        names = jnp.concatenate(
+            [lines[i // 128 : i // 128 + 1, : min(128, width - i)] for i in range(0, width, 128)],
+            axis=1,
+        )
+        held.append(ones_where(iota((tokens, width), 0) == names.astype(jnp.int32) - 1))
+        rows.append(unpack_slots(h, width, ff))
     x = [r.astype(BF16) for r in by_expert(rows, local, cap)]
     for c in range(0, half, chunk):
         at = pl.ds(pl.multiple_of(side * half + c, chunk), chunk)
@@ -222,7 +265,9 @@
     back_refs, out = refs[:-1], refs[-1]
     top, _, tokens = out.shape
     picks, gate = picks_of(meta_ref[...], place[0], dims)
-    back = jnp.concatenate([ref[...] for ref in back_refs], axis=0)
+    ff = out.shape[1]
+    back = [unpack_slots(ref, dims[3], ff).astype(BF16) for ref in back_refs]
+    back = jnp.concatenate(back, axis=0)
     grads = dot(back, picks, TN)
     for k in range(top):
         out[k] = (grads[:, k * tokens : (k + 1) * tokens] * gate[k : k + 1, :]).astype(BF16)
@@ -278,25 +323,28 @@
     packed = jnp.concatenate([grad_out, named], axis=0)
     forward = n == 4
     own = [send(packed, s) for s in range(n)]
-    swapped = swap(packed)
-    meta, swapped = lax.optimization_barrier((meta, swapped))
     hid_sent = run(
-        functools.partial(dispatch_kernel, dims), [shaped((width, -(-(ff + 1) // 128) * 128))] * n,
+        functools.partial(dispatch_kernel, dims), [shaped((packed_rows(width, ff)[0] + 16, 128))] * n,
         [place, meta, hid_t], where=placed, name="dispatch",
     )
     hid = [send(hid_sent[s], s) for s in range(n)]
-    slot = shaped((width, ff))
+    slot = shaped((packed_rows(width, ff)[0], 128))
 
     def swaps(xs):
         return [swap(x) for x in xs]
 
+    def swaps_in_turn(xs):
+        first = swap(xs[0])
+        second, first = lax.optimization_barrier((xs[1], first))
+        return [first, swap(second)]
+
     if forward:
         always = place[0] < 1000
-        last = lax.cond(always, swaps, list, own[3:])
-        *own[1:3], last[0] = lax.optimization_barrier((*own[1:3], last[0]))
-        other = [swapped] + lax.cond(always, swaps, list, own[1:3]) + last
+        last, mine = lax.cond(always, swaps_in_turn, list, [own[3], own[0]])
+        *own[1:3], last = lax.optimization_barrier((*own[1:3], last))
+        other = [mine] + lax.cond(always, swaps, list, own[1:3]) + [last]
     else:
-        other = [swapped] + swaps(own[1:])
+        other = swaps(own)
     (x,) = run(
         functools.partial(gather_kernel, dims, top), [shaped((local, n * cap, full))],
         [place, *own, *other], where=placed, name="gather", weight=20 * 10**8,

time: 50.9 us -> 50.4 us (level)
  starting transfers between devices: 19.4 us -> 18.8 us
    ppermute x5, waiting for transfers between devices: 3.46 us -> 5.16 us  [swap(): return lax.ppermute(x, 'tp', [(0, 1), (1, 0)])]
    ppermute x15, waiting for transfers between devices: 8.97 us -> 7.31 us  [send(): return lax.ppermute(x, 'ctx', [(i, i ^ s) for i in range(n)]) if s else x]
  transfers between devices with their start and end apart: 20 -> 20, of which waited for: 12 -> 11; matrix products, arithmetic and copies ran while one was open for 2% -> 2% of each run, Pallas kernels for 26% -> 26%
where the time goes in v10:
time: 50.4 us; the launch traced here: 50.2 us
  starting transfers between devices  18.8 us (37%)
  Pallas kernels  13.9 us (28%)
  waiting for transfers between devices  12.5 us (25%)
  other arithmetic  2.44 us (5%)
  local copies, waits for them, and re-layouts  1.83 us (4%)
  between operations  0.7 us (1%)
    ppermute x15, starting transfers between devices, send(): return lax.ppermute(x, 'ctx', [(i, i ^ s) for i in range(n)]) if s else x  18.1 us
    pallas_call x9, Pallas kernels, call(): pl.pallas_call(kernel, out_shape=outs, in_specs=[pl.BlockSpec(memory_spac...  13.9 us
    ppermute x15, waiting for transfers between devices, send(): return lax.ppermute(x, 'ctx', [(i, i ^ s) for i in range(n)]) if s else x  7.31 us
    ppermute x5, waiting for transfers between devices, swap(): return lax.ppermute(x, 'tp', [(0, 1), (1, 0)])  5.16 us
    unnamed x4, local copies, waits for them, and re-layouts  1.83 us
  transfers between devices with their start and end apart: 20, of which 11 were waited for; matrix products, arithmetic and copies ran while one was open for 2% of the time, Pallas kernels for 26%

profile of v10, /device:TPU:0, one launch (start us, length us, event | category | flops | bytes accessed | tf_op | source)
XLA Modules:
  0.0 50.2 jit_solution(3055861259426127716)
XLA Ops:
  0.6 0.7 %bitcast_convert_fusion = bf16[4,128]{1,0:T(4,128)(2,1)S(1)} fusion(s32[128,4]{0,1:T(4,128)} %param.10), kind=kLoop, calls=%fused_computation.5 | loop fusion | flops 512 | bytes 3072 | tf_op jit(solution)/shard_map/convert_element_type | solution.py:322
  1.3 1.0 %fusion.1.refs_0_ = bf16[136,1024]{1,0:T(8,128)(2,1)S(1)} fusion(bf16[4,128]{1,0:T(4,128)(2,1)S(1)} %bitcast_convert_fusion, bf16[128,1024]{1,0:T(8,128)(2,1)} %param.12), kind=kLoop, calls=%fused_computation.2 | loop fusion | flops 835584 | bytes 541696 | tf_op jit(solution)/shard_map/concatenate | solution.py:323
  2.3 4.0 %collective-permute-start.6 = (bf16[136,1024]{1,0:T(8,128)(2,1)S(1)}, bf16[136,1024]{1,0:T(8,128)(2,1)S(1)}, u32[]{:S(2)}, u32[]{:S(2)}) collective-permute-start(bf16[136,1024]{1,0:T(8,128)(2,1)S(1)} %fusion.1.refs_0_), channel_id=1, source_target_pairs={{0,24},{8,16},{16,8},{24,0},{1,25},{9,17},{17,9},{25,1},{2,26},{10... | collective-permute-start | bytes 835592 | tf_op jit(solution)/shard_map/ppermute | solution.py:315
  6.2 0.5 %collective-permute-start.5 = (bf16[136,1024]{1,0:T(8,128)(2,1)S(1)}, bf16[136,1024]{1,0:T(8,128)(2,1)S(1)}, u32[]{:S(2)}, u32[]{:S(2)}) collective-permute-start(bf16[136,1024]{1,0:T(8,128)(2,1)S(1)} %fusion.1.refs_0_), channel_id=1, source_target_pairs={{0,16},{8,24},{16,0},{24,8},{1,17},{9,25},{17,1},{25,9},{2,18},{10... | collective-permute-start | bytes 835592 | tf_op jit(solution)/shard_map/ppermute | solution.py:315
  6.8 0.1 collective-permute-start.4
  6.9 0.1 pad_add_fusion.1.place
  7.0 0.7 %pad_add_fusion.meta_ref = s32[8,128]{1,0:T(8,128)S(1)} fusion(s32[4,128]{1,0:T(4,128)} %bitcast.9, s32[4,128]{1,0:T(4,128)} %bitcast.8), kind=kLoop, calls=%fused_computation.3 | loop fusion | flops 1024 | bytes 8192 | tf_op jit(solution)/shard_map/concatenate | solution.py:320
  7.7 1.1 %copy-done.1 = bf16[128,4,704]{0,2,1:T(8,128)(2,1)S(1)} copy-done((bf16[128,4,704]{0,2,1:T(8,128)(2,1)S(1)}, bf16[128,4,704]{0,2,1:T(8,128)(2,1)}, u32[]{:S(2)}) %copy-start.1) | copy-done | bytes 720920
  8.8 1.6 %dispatch.1 = (bf16[816,128]{1,0:T(8,128)(2,1)S(1)}, bf16[816,128]{1,0:T(8,128)(2,1)S(1)}, bf16[816,128]{1,0:T(8,128)(2,1)S(1)}, bf16[816,128]{1,0:T(8,128)(2,1)S(1)}) custom-call(s32[2]{0:T(128)S(1)} %pad_add_fusion.1.place, s32[8,128]{1,0:T(8,128)S(1)} %pad_add_fusion.meta_ref, bf16[4,704,128]{2,1,0:T(8,128)(2,1)S(1)} %bitcast.7), custom_call_target="tpu_custom_call" | custom-call | flops 1 | bytes 1 | tf_op jit(solution)/shard_map/dispatch/pallas_call | solution.py:282
  10.4 2.0 %collective-permute-start.7 = (bf16[816,128]{1,0:T(8,128)(2,1)S(1)}, bf16[816,128]{1,0:T(8,128)(2,1)S(1)}, u32[]{:S(2)}, u32[]{:S(2)}) collective-permute-start(bf16[816,128]{1,0:T(8,128)(2,1)S(1)} %get-tuple-element.64), channel_id=1, source_target_pairs={{0,8},{8,0},{16,24},{24,16},{1,9},{9,1},{17,25},{25,17},{2,10},{10... | collective-permute-start | bytes 626696 | tf_op jit(solution)/shard_map/ppermute | solution.py:315
  12.3 1.5 %collective-permute-start.8 = (bf16[816,128]{1,0:T(8,128)(2,1)S(1)}, bf16[816,128]{1,0:T(8,128)(2,1)S(1)}, u32[]{:S(2)}, u32[]{:S(2)}) collective-permute-start(bf16[816,128]{1,0:T(8,128)(2,1)S(1)} %get-tuple-element.65), channel_id=1, source_target_pairs={{0,16},{8,24},{16,0},{24,8},{1,17},{9,25},{17,1},{25,9},{2,18},{10... | collective-permute-start | bytes 626696 | tf_op jit(solution)/shard_map/ppermute | solution.py:315
  13.8 0.0 collective-permute-done.6.refs_3_
  13.9 3.4 %conditional.2 = (bf16[136,1024]{1,0:T(8,128)(2,1)}, bf16[136,1024]{1,0:T(8,128)(2,1)}) conditional(s32[]{:T(128)} %convert_element_type.10, (bf16[136,1024]{1,0:T(8,128)(2,1)S(1)}, bf16[136,1024]{1,0:T(8,128)(2,1)S(1)}) %tuple.26, (bf16[136,1024]{1,0:T(8,128)(2,1)S(1)}, bf16[136,1024]{1,0:T(8,128)(2,1)S(1)}) %tuple.26), branch_computations={%region_0.1_spmd, %region_1.2_spmd} | conditional | bytes 2228320 | solution.py:343
  13.9 0.0 collective-permute-start
  13.9 1.7 %collective-permute-done = bf16[136,1024]{1,0:T(8,128)(2,1)} collective-permute-done((bf16[136,1024]{1,0:T(8,128)(2,1)S(1)}, bf16[136,1024]{1,0:T(8,128)(2,1)}, u32[]{:S(2)}, u32[]{:S(2)}) %collective-permute-start) | collective-permute-done | bytes 278560 | tf_op jit(solution)/shard_map/cond/branch_1_fun/ppermute | solution.py:318
  15.5 0.1 collective-permute-start.1
  15.7 1.6 %collective-permute-done.1 = bf16[136,1024]{1,0:T(8,128)(2,1)} collective-permute-done((bf16[136,1024]{1,0:T(8,128)(2,1)S(1)}, bf16[136,1024]{1,0:T(8,128)(2,1)}, u32[]{:S(2)}, u32[]{:S(2)}) %collective-permute-start.1) | collective-permute-done | bytes 278560 | tf_op jit(solution)/shard_map/cond/branch_1_fun/ppermute | solution.py:318
  17.2 2.8 %collective-permute-start.9 = (bf16[816,128]{1,0:T(8,128)(2,1)S(1)}, bf16[816,128]{1,0:T(8,128)(2,1)S(1)}, u32[]{:S(2)}, u32[]{:S(2)}) collective-permute-start(bf16[816,128]{1,0:T(8,128)(2,1)S(1)} %get-tuple-element.66), channel_id=1, source_target_pairs={{0,24},{8,16},{16,8},{24,0},{1,25},{9,17},{17,9},{25,1},{2,26},{10... | collective-permute-start | bytes 626696 | tf_op jit(solution)/shard_map/ppermute | solution.py:315
  20.1 0.0 collective-permute-done.5.refs_2_
  20.1 0.2 collective-permute-done.4.refs_1_
  20.3 2.1 %conditional.3 = (bf16[136,1024]{1,0:T(8,128)(2,1)}, bf16[136,1024]{1,0:T(8,128)(2,1)}) conditional(s32[]{:T(128)} %convert_element_type.10, (bf16[136,1024]{1,0:T(8,128)(2,1)S(1)}, bf16[136,1024]{1,0:T(8,128)(2,1)S(1)}) %tuple.28, (bf16[136,1024]{1,0:T(8,128)(2,1)S(1)}, bf16[136,1024]{1,0:T(8,128)(2,1)S(1)}) %tuple.28), branch_computations={%region_2.3_spmd, %region_3.4_spmd} | conditional | bytes 2228320 | solution.py:345
  20.3 0.5 %collective-permute-start.3 = (bf16[136,1024]{1,0:T(8,128)(2,1)S(1)}, bf16[136,1024]{1,0:T(8,128)(2,1)}, u32[]{:S(2)}, u32[]{:S(2)}) collective-permute-start(bf16[136,1024]{1,0:T(8,128)(2,1)S(1)} %get-tuple-element.21), channel_id=1, source_target_pairs={{0,1},{1,0},{2,3},{3,2},{4,5},{5,4},{6,7},{7,6},{8,9},{9,8},{10,11... | collective-permute-start | bytes 835592 | tf_op jit(solution)/shard_map/cond/branch_1_fun/ppermute | solution.py:318
  20.8 1.2 %collective-permute-done.2 = bf16[136,1024]{1,0:T(8,128)(2,1)} collective-permute-done((bf16[136,1024]{1,0:T(8,128)(2,1)S(1)}, bf16[136,1024]{1,0:T(8,128)(2,1)}, u32[]{:S(2)}, u32[]{:S(2)}) %collective-permute-start.2) | collective-permute-done | bytes 278560 | tf_op jit(solution)/shard_map/cond/branch_1_fun/ppermute | solution.py:318
  22.0 0.4 collective-permute-done.3
  22.4 2.2 %gather.1.x_ref = bf16[2,288,2048]{2,1,0:T(8,128)(2,1)S(1)} custom-call(s32[2]{0:T(128)S(1)} %pad_add_fusion.1.place, bf16[136,1024]{1,0:T(8,128)(2,1)S(1)} %fusion.1.refs_0_, bf16[136,1024]{1,0:T(8,128)(2,1)S(1)} %collective-permute-done.4.refs_1_, bf16[136,1024]{1,0:T(8,128)(2,1)S(1)} %collective-permute-done.5.refs_2_, ...), custom_call_target="tpu_custom_call" | custom-call | flops 2000000000 | bytes 1 | tf_op jit(solution)/shard_map/gather/pallas_call | solution.py:282
  24.7 0.7 %copy-done = bf16[2,704,2048]{2,1,0:T(8,128)(2,1)S(1)} copy-done((bf16[2,704,2048]{2,1,0:T(8,128)(2,1)S(1)}, bf16[2,704,2048]{2,1,0:T(8,128)(2,1)}, u32[]{:S(2)}) %copy-start) | copy-done | bytes 5767192
  25.4 2.1 %grad.1 = (bf16[800,128]{1,0:T(8,128)(2,1)S(1)}, bf16[800,128]{1,0:T(8,128)(2,1)S(1)}, bf16[800,128]{1,0:T(8,128)(2,1)S(1)}, bf16[800,128]{1,0:T(8,128)(2,1)S(1)}) custom-call(bf16[2,288,2048]{2,1,0:T(8,128)(2,1)S(1)} %gather.1.x_ref, bf16[2,704,2048]{2,1,0:T(8,128)(2,1)S(1)} %copy-done), custom_call_target="tpu_custom_call" | custom-call | flops 1 | bytes 1 | tf_op jit(solution)/shard_map/grad/pallas_call | solution.py:282
  27.5 1.5 %collective-permute-start.11 = (bf16[800,128]{1,0:T(8,128)(2,1)S(1)}, bf16[800,128]{1,0:T(8,128)(2,1)S(1)}, u32[]{:S(2)}, u32[]{:S(2)}) collective-permute-start(bf16[800,128]{1,0:T(8,128)(2,1)S(1)} %get-tuple-element.70), channel_id=1, source_target_pairs={{0,8},{8,0},{16,24},{24,16},{1,9},{9,1},{17,25},{25,17},{2,10},{10... | collective-permute-start | bytes 614408 | tf_op jit(solution)/shard_map/ppermute | solution.py:315
  29.0 0.5 %collective-permute-start.12 = (bf16[800,128]{1,0:T(8,128)(2,1)S(1)}, bf16[800,128]{1,0:T(8,128)(2,1)S(1)}, u32[]{:S(2)}, u32[]{:S(2)}) collective-permute-start(bf16[800,128]{1,0:T(8,128)(2,1)S(1)} %get-tuple-element.71), channel_id=1, source_target_pairs={{0,16},{8,24},{16,0},{24,8},{1,17},{9,25},{17,1},{25,9},{2,18},{10... | collective-permute-start | bytes 614408 | tf_op jit(solution)/shard_map/ppermute | solution.py:315
  29.6 1.5 %collective-permute-start.19 = (bf16[800,128]{1,0:T(8,128)(2,1)S(1)}, bf16[800,128]{1,0:T(8,128)(2,1)S(1)}, u32[]{:S(2)}, u32[]{:S(2)}) collective-permute-start(bf16[800,128]{1,0:T(8,128)(2,1)S(1)} %get-tuple-element.83), channel_id=1, source_target_pairs={{0,24},{8,16},{16,8},{24,0},{1,25},{9,17},{17,9},{25,1},{2,26},{10... | collective-permute-start | bytes 614408 | tf_op jit(solution)/shard_map/ppermute | solution.py:315
  31.1 0.0 collective-permute-done.8.refs_2_
  31.1 2.3 %mix_sibling.1 = bf16[512,1024]{1,0:T(8,128)(2,1)S(1)} custom-call(s32[2]{0:T(128)S(1)} %pad_add_fusion.1.place, bf16[816,128]{1,0:T(8,128)(2,1)S(1)} %get-tuple-element.63.refs_0_, bf16[816,128]{1,0:T(8,128)(2,1)S(1)} %collective-permute-done.7.refs_1_, bf16[816,128]{1,0:T(8,128)(2,1)S(1)} %collective-permute-done.8.refs_2_, ...), custom_call_target="tpu_custom_call" | custom-call | flops 1 | bytes 1 | tf_op jit(solution)/shard_map/mix_sibling/pallas_call | solution.py:282
  33.4 0.1 collective-permute-start.10
  33.5 2.3 %mix_own.1.own = f32[512,1024]{1,0:T(8,128)S(1)} custom-call(s32[2]{0:T(128)S(1)} %pad_add_fusion.1.place, bf16[816,128]{1,0:T(8,128)(2,1)S(1)} %get-tuple-element.63.refs_0_, bf16[816,128]{1,0:T(8,128)(2,1)S(1)} %collective-permute-done.7.refs_1_, bf16[816,128]{1,0:T(8,128)(2,1)S(1)} %collective-permute-done.8.refs_2_, ...), custom_call_target="tpu_custom_call" | custom-call | flops 99999997952 | bytes 1 | tf_op jit(solution)/shard_map/mix_own/pallas_call | solution.py:282
  35.8 0.3 collective-permute-done.10.arrived
  36.1 0.2 add.7
  36.3 1.5 %collective-permute-start.14 = (bf16[128,512]{1,0:T(8,128)(2,1)S(1)}, bf16[128,512]{1,0:T(8,128)(2,1)S(1)}, u32[]{:S(2)}, u32[]{:S(2)}) collective-permute-start(bf16[128,512]{1,0:T(8,128)(2,1)S(1)} %get-tuple-element.75), channel_id=1, source_target_pairs={{0,8},{8,0},{16,24},{24,16},{1,9},{9,1},{17,25},{25,17},{2,10},{10... | collective-permute-start | bytes 393224 | tf_op jit(solution)/shard_map/ppermute | solution.py:315
  37.9 0.5 %collective-permute-start.15 = (bf16[128,512]{1,0:T(8,128)(2,1)S(1)}, bf16[128,512]{1,0:T(8,128)(2,1)S(1)}, u32[]{:S(2)}, u32[]{:S(2)}) collective-permute-start(bf16[128,512]{1,0:T(8,128)(2,1)S(1)} %get-tuple-element.76), channel_id=1, source_target_pairs={{0,16},{8,24},{16,0},{24,8},{1,17},{9,25},{17,1},{25,9},{2,18},{10... | collective-permute-start | bytes 393224 | tf_op jit(solution)/shard_map/ppermute | solution.py:315
  38.4 1.8 %collective-permute-done.12.refs_2_ = bf16[800,128]{1,0:T(8,128)(2,1)S(1)} collective-permute-done((bf16[800,128]{1,0:T(8,128)(2,1)S(1)}, bf16[800,128]{1,0:T(8,128)(2,1)S(1)}, u32[]{:S(2)}, u32[]{:S(2)}) %collective-permute-start.12) | collective-permute-done | bytes 204832 | tf_op jit(solution)/shard_map/ppermute | solution.py:315
  40.2 0.6 %collective-permute-start.13 = (bf16[128,512]{1,0:T(8,128)(2,1)S(1)}, bf16[128,512]{1,0:T(8,128)(2,1)S(1)}, u32[]{:S(2)}, u32[]{:S(2)}) collective-permute-start(bf16[128,512]{1,0:T(8,128)(2,1)S(1)} %get-tuple-element.72), channel_id=1, source_target_pairs={{0,8},{8,0},{16,24},{24,16},{1,9},{9,1},{17,25},{25,17},{2,10},{10... | collective-permute-start | bytes 393224 | tf_op jit(solution)/shard_map/ppermute | solution.py:315
  40.8 1.2 %collective-permute-done.14.low = bf16[128,512]{1,0:T(8,128)(2,1)S(1)} collective-permute-done((bf16[128,512]{1,0:T(8,128)(2,1)S(1)}, bf16[128,512]{1,0:T(8,128)(2,1)S(1)}, u32[]{:S(2)}, u32[]{:S(2)}) %collective-permute-start.14) | collective-permute-done | bytes 131104 | tf_op jit(solution)/shard_map/ppermute | solution.py:315
  42.1 2.2 %collective-permute-done.15.high = bf16[128,512]{1,0:T(8,128)(2,1)S(1)} collective-permute-done((bf16[128,512]{1,0:T(8,128)(2,1)S(1)}, bf16[128,512]{1,0:T(8,128)(2,1)S(1)}, u32[]{:S(2)}, u32[]{:S(2)}) %collective-permute-start.15) | collective-permute-done | bytes 131104 | tf_op jit(solution)/shard_map/ppermute | solution.py:315
  44.3 0.1 collective-permute-start.16
  44.4 0.9 %collective-permute-start.17 = (bf16[128,512]{1,0:T(8,128)(2,1)S(1)}, bf16[128,512]{1,0:T(8,128)(2,1)S(1)}, u32[]{:S(2)}, u32[]{:S(2)}) collective-permute-start(bf16[128,512]{1,0:T(8,128)(2,1)S(1)} %get-tuple-element.78), channel_id=1, source_target_pairs={{0,16},{8,24},{16,0},{24,8},{1,17},{9,25},{17,1},{25,9},{2,18},{10... | collective-permute-start | bytes 393224 | tf_op jit(solution)/shard_map/ppermute | solution.py:315
  45.3 2.3 %restore.1 = bf16[4,704,128]{2,1,0:T(8,128)(2,1)} custom-call(s32[2]{0:T(128)S(1)} %pad_add_fusion.1.place, s32[8,128]{1,0:T(8,128)S(1)} %pad_add_fusion.meta_ref, bf16[800,128]{1,0:T(8,128)(2,1)S(1)} %get-tuple-element.80.refs_0_, bf16[800,128]{1,0:T(8,128)(2,1)S(1)} %collective-permute-done.11.refs_1_, ...), custom_call_target="tpu_custom_call" | custom-call | flops 99999997952 | bytes 1 | tf_op jit(solution)/shard_map/restore/pallas_call | solution.py:282
  47.6 1.7 %collective-permute-done.16.one_high = bf16[128,512]{1,0:T(8,128)(2,1)S(1)} collective-permute-done((bf16[128,512]{1,0:T(8,128)(2,1)S(1)}, bf16[128,512]{1,0:T(8,128)(2,1)S(1)}, u32[]{:S(2)}, u32[]{:S(2)}) %collective-permute-start.16) | collective-permute-done | bytes 131104 | tf_op jit(solution)/shard_map/ppermute | solution.py:315
  49.3 0.1 collective-permute-done.17.two_low
  49.4 0.8 %finish.1 = bf16[128,1024]{1,0:T(8,128)(2,1)} custom-call(f32[128,1024]{1,0:T(8,128)S(1)} %get-tuple-element.67.mine, bf16[128,512]{1,0:T(8,128)(2,1)S(1)} %collective-permute-done.13.one_low, bf16[128,512]{1,0:T(8,128)(2,1)S(1)} %collective-permute-done.16.one_high, bf16[128,512]{1,0:T(8,128)(2,1)S(1)} %collective-permute-done.17.two_low, ...), custom_call_target="tpu_custom_call" | custom-call | flops 1 | bytes 1 | tf_op jit(solution)/shard_map/finish/pallas_call | solution.py:282
  (11 shorter events, 0.1 us)
Async XLA Ops:
  2.3 11.6 %collective-permute-start.6 = (bf16[136,1024]{1,0:T(8,128)(2,1)S(1)}, bf16[136,1024]{1,0:T(8,128)(2,1)S(1)}, u32[]{:S(2)}, u32[]{:S(2)}) collective-permute-start(bf16[136,1024]{1,0:T(8,128)(2,1)S(1)} %fusion.1.refs_0_), channel_id=1, source_target_pairs={{0,24},{8,16},{16,8},{24,0},{1,25},{9,17},{17,9},{25,1},{2,26},{10... | collective-permute-start | bytes 835592 | tf_op jit(solution)/shard_map/ppermute | solution.py:315
  6.2 13.8 %collective-permute-start.5 = (bf16[136,1024]{1,0:T(8,128)(2,1)S(1)}, bf16[136,1024]{1,0:T(8,128)(2,1)S(1)}, u32[]{:S(2)}, u32[]{:S(2)}) collective-permute-start(bf16[136,1024]{1,0:T(8,128)(2,1)S(1)} %fusion.1.refs_0_), channel_id=1, source_target_pairs={{0,16},{8,24},{16,0},{24,8},{1,17},{9,25},{17,1},{25,9},{2,18},{10... | collective-permute-start | bytes 835592 | tf_op jit(solution)/shard_map/ppermute | solution.py:315
  6.8 13.6 %collective-permute-start.4 = (bf16[136,1024]{1,0:T(8,128)(2,1)S(1)}, bf16[136,1024]{1,0:T(8,128)(2,1)S(1)}, u32[]{:S(2)}, u32[]{:S(2)}) collective-permute-start(bf16[136,1024]{1,0:T(8,128)(2,1)S(1)} %fusion.1.refs_0_), channel_id=1, source_target_pairs={{0,8},{8,0},{16,24},{24,16},{1,9},{9,1},{17,25},{25,17},{2,10},{10... | collective-permute-start | bytes 835592 | tf_op jit(solution)/shard_map/ppermute | solution.py:315
  7.7 1.1 %copy-start.1 = (bf16[128,4,704]{0,2,1:T(8,128)(2,1)S(1)}, bf16[128,4,704]{0,2,1:T(8,128)(2,1)}, u32[]{:S(2)}) copy-start(bf16[128,4,704]{0,2,1:T(8,128)(2,1)} %param.9) | copy-start | bytes 2162692
  10.4 19.2 %collective-permute-start.7 = (bf16[816,128]{1,0:T(8,128)(2,1)S(1)}, bf16[816,128]{1,0:T(8,128)(2,1)S(1)}, u32[]{:S(2)}, u32[]{:S(2)}) collective-permute-start(bf16[816,128]{1,0:T(8,128)(2,1)S(1)} %get-tuple-element.64), channel_id=1, source_target_pairs={{0,8},{8,0},{16,24},{24,16},{1,9},{9,1},{17,25},{25,17},{2,10},{10... | collective-permute-start | bytes 626696 | tf_op jit(solution)/shard_map/ppermute | solution.py:315
  12.3 18.7 %collective-permute-start.8 = (bf16[816,128]{1,0:T(8,128)(2,1)S(1)}, bf16[816,128]{1,0:T(8,128)(2,1)S(1)}, u32[]{:S(2)}, u32[]{:S(2)}) collective-permute-start(bf16[816,128]{1,0:T(8,128)(2,1)S(1)} %get-tuple-element.65), channel_id=1, source_target_pairs={{0,16},{8,24},{16,0},{24,8},{1,17},{9,25},{17,1},{25,9},{2,18},{10... | collective-permute-start | bytes 626696 | tf_op jit(solution)/shard_map/ppermute | solution.py:315
  13.9 1.7 %collective-permute-start = (bf16[136,1024]{1,0:T(8,128)(2,1)S(1)}, bf16[136,1024]{1,0:T(8,128)(2,1)}, u32[]{:S(2)}, u32[]{:S(2)}) collective-permute-start(bf16[136,1024]{1,0:T(8,128)(2,1)S(1)} %get-tuple-element.17), channel_id=1, source_target_pairs={{0,1},{1,0},{2,3},{3,2},{4,5},{5,4},{6,7},{7,6},{8,9},{9,8},{10,11... | collective-permute-start | bytes 835592 | tf_op jit(solution)/shard_map/cond/branch_1_fun/ppermute | solution.py:318
  15.5 1.7 %collective-permute-start.1 = (bf16[136,1024]{1,0:T(8,128)(2,1)S(1)}, bf16[136,1024]{1,0:T(8,128)(2,1)}, u32[]{:S(2)}, u32[]{:S(2)}) collective-permute-start(bf16[136,1024]{1,0:T(8,128)(2,1)S(1)} %get-tuple-element.19), channel_id=1, source_target_pairs={{0,1},{1,0},{2,3},{3,2},{4,5},{5,4},{6,7},{7,6},{8,9},{9,8},{10,11... | collective-permute-start | bytes 835592 | tf_op jit(solution)/shard_map/cond/branch_1_fun/ppermute | solution.py:318
  17.2 13.8 %collective-permute-start.9 = (bf16[816,128]{1,0:T(8,128)(2,1)S(1)}, bf16[816,128]{1,0:T(8,128)(2,1)S(1)}, u32[]{:S(2)}, u32[]{:S(2)}) collective-permute-start(bf16[816,128]{1,0:T(8,128)(2,1)S(1)} %get-tuple-element.66), channel_id=1, source_target_pairs={{0,24},{8,16},{16,8},{24,0},{1,25},{9,17},{17,9},{25,1},{2,26},{10... | collective-permute-start | bytes 626696 | tf_op jit(solution)/shard_map/ppermute | solution.py:315
  20.3 1.7 %collective-permute-start.2 = (bf16[136,1024]{1,0:T(8,128)(2,1)S(1)}, bf16[136,1024]{1,0:T(8,128)(2,1)}, u32[]{:S(2)}, u32[]{:S(2)}) collective-permute-start(bf16[136,1024]{1,0:T(8,128)(2,1)S(1)} %get-tuple-element.20), channel_id=1, source_target_pairs={{0,1},{1,0},{2,3},{3,2},{4,5},{5,4},{6,7},{7,6},{8,9},{9,8},{10,11... | collective-permute-start | bytes 835592 | tf_op jit(solution)/shard_map/cond/branch_1_fun/ppermute | solution.py:318
  20.3 2.1 %collective-permute-start.3 = (bf16[136,1024]{1,0:T(8,128)(2,1)S(1)}, bf16[136,1024]{1,0:T(8,128)(2,1)}, u32[]{:S(2)}, u32[]{:S(2)}) collective-permute-start(bf16[136,1024]{1,0:T(8,128)(2,1)S(1)} %get-tuple-element.21), channel_id=1, source_target_pairs={{0,1},{1,0},{2,3},{3,2},{4,5},{5,4},{6,7},{7,6},{8,9},{9,8},{10,11... | collective-permute-start | bytes 835592 | tf_op jit(solution)/shard_map/cond/branch_1_fun/ppermute | solution.py:318
  22.4 3.0 %copy-start = (bf16[2,704,2048]{2,1,0:T(8,128)(2,1)S(1)}, bf16[2,704,2048]{2,1,0:T(8,128)(2,1)}, u32[]{:S(2)}) copy-start(bf16[2,704,2048]{2,1,0:T(8,128)(2,1)} %refs_4_.3) | copy-start | bytes 17301508
  27.5 10.9 %collective-permute-start.11 = (bf16[800,128]{1,0:T(8,128)(2,1)S(1)}, bf16[800,128]{1,0:T(8,128)(2,1)S(1)}, u32[]{:S(2)}, u32[]{:S(2)}) collective-permute-start(bf16[800,128]{1,0:T(8,128)(2,1)S(1)} %get-tuple-element.70), channel_id=1, source_target_pairs={{0,8},{8,0},{16,24},{24,16},{1,9},{9,1},{17,25},{25,17},{2,10},{10... | collective-permute-start | bytes 614408 | tf_op jit(solution)/shard_map/ppermute | solution.py:315
  29.0 11.2 %collective-permute-start.12 = (bf16[800,128]{1,0:T(8,128)(2,1)S(1)}, bf16[800,128]{1,0:T(8,128)(2,1)S(1)}, u32[]{:S(2)}, u32[]{:S(2)}) collective-permute-start(bf16[800,128]{1,0:T(8,128)(2,1)S(1)} %get-tuple-element.71), channel_id=1, source_target_pairs={{0,16},{8,24},{16,0},{24,8},{1,17},{9,25},{17,1},{25,9},{2,18},{10... | collective-permute-start | bytes 614408 | tf_op jit(solution)/shard_map/ppermute | solution.py:315
  29.6 15.7 %collective-permute-start.19 = (bf16[800,128]{1,0:T(8,128)(2,1)S(1)}, bf16[800,128]{1,0:T(8,128)(2,1)S(1)}, u32[]{:S(2)}, u32[]{:S(2)}) collective-permute-start(bf16[800,128]{1,0:T(8,128)(2,1)S(1)} %get-tuple-element.83), channel_id=1, source_target_pairs={{0,24},{8,16},{16,8},{24,0},{1,25},{9,17},{17,9},{25,1},{2,26},{10... | collective-permute-start | bytes 614408 | tf_op jit(solution)/shard_map/ppermute | solution.py:315
  33.4 2.7 %collective-permute-start.10 = (bf16[512,1024]{1,0:T(8,128)(2,1)S(1)}, bf16[512,1024]{1,0:T(8,128)(2,1)S(1)}, u32[]{:S(2)}, u32[]{:S(2)}) collective-permute-start(bf16[512,1024]{1,0:T(8,128)(2,1)S(1)} %mix_sibling.1), channel_id=1, source_target_pairs={{0,1},{1,0},{2,3},{3,2},{4,5},{5,4},{6,7},{7,6},{8,9},{9,8},{10,11... | collective-permute-start | bytes 3145736 | tf_op jit(solution)/shard_map/ppermute | solution.py:318
  36.3 5.7 %collective-permute-start.14 = (bf16[128,512]{1,0:T(8,128)(2,1)S(1)}, bf16[128,512]{1,0:T(8,128)(2,1)S(1)}, u32[]{:S(2)}, u32[]{:S(2)}) collective-permute-start(bf16[128,512]{1,0:T(8,128)(2,1)S(1)} %get-tuple-element.75), channel_id=1, source_target_pairs={{0,8},{8,0},{16,24},{24,16},{1,9},{9,1},{17,25},{25,17},{2,10},{10... | collective-permute-start | bytes 393224 | tf_op jit(solution)/shard_map/ppermute | solution.py:315
  37.9 6.4 %collective-permute-start.15 = (bf16[128,512]{1,0:T(8,128)(2,1)S(1)}, bf16[128,512]{1,0:T(8,128)(2,1)S(1)}, u32[]{:S(2)}, u32[]{:S(2)}) collective-permute-start(bf16[128,512]{1,0:T(8,128)(2,1)S(1)} %get-tuple-element.76), channel_id=1, source_target_pairs={{0,16},{8,24},{16,0},{24,8},{1,17},{9,25},{17,1},{25,9},{2,18},{10... | collective-permute-start | bytes 393224 | tf_op jit(solution)/shard_map/ppermute | solution.py:315
  40.2 7.4 %collective-permute-start.13 = (bf16[128,512]{1,0:T(8,128)(2,1)S(1)}, bf16[128,512]{1,0:T(8,128)(2,1)S(1)}, u32[]{:S(2)}, u32[]{:S(2)}) collective-permute-start(bf16[128,512]{1,0:T(8,128)(2,1)S(1)} %get-tuple-element.72), channel_id=1, source_target_pairs={{0,8},{8,0},{16,24},{24,16},{1,9},{9,1},{17,25},{25,17},{2,10},{10... | collective-permute-start | bytes 393224 | tf_op jit(solution)/shard_map/ppermute | solution.py:315
  40.8 6.8 %collective-permute-start.18 = (bf16[128,512]{1,0:T(8,128)(2,1)S(1)}, bf16[128,512]{1,0:T(8,128)(2,1)S(1)}, u32[]{:S(2)}, u32[]{:S(2)}) collective-permute-start(bf16[128,512]{1,0:T(8,128)(2,1)S(1)} %get-tuple-element.79), channel_id=1, source_target_pairs={{0,16},{8,24},{16,0},{24,8},{1,17},{9,25},{17,1},{25,9},{2,18},{10... | collective-permute-start | bytes 393224 | tf_op jit(solution)/shard_map/ppermute | solution.py:315
  44.3 5.0 %collective-permute-start.16 = (bf16[128,512]{1,0:T(8,128)(2,1)S(1)}, bf16[128,512]{1,0:T(8,128)(2,1)S(1)}, u32[]{:S(2)}, u32[]{:S(2)}) collective-permute-start(bf16[128,512]{1,0:T(8,128)(2,1)S(1)} %get-tuple-element.77), channel_id=1, source_target_pairs={{0,8},{8,0},{16,24},{24,16},{1,9},{9,1},{17,25},{25,17},{2,10},{10... | collective-permute-start | bytes 393224 | tf_op jit(solution)/shard_map/ppermute | solution.py:315
  44.4 5.0 %collective-permute-start.17 = (bf16[128,512]{1,0:T(8,128)(2,1)S(1)}, bf16[128,512]{1,0:T(8,128)(2,1)S(1)}, u32[]{:S(2)}, u32[]{:S(2)}) collective-permute-start(bf16[128,512]{1,0:T(8,128)(2,1)S(1)} %get-tuple-element.78), channel_id=1, source_target_pairs={{0,16},{8,24},{16,0},{24,8},{1,17},{9,25},{17,1},{25,9},{2,18},{10... | collective-permute-start | bytes 393224 | tf_op jit(solution)/shard_map/ppermute | solution.py:315

commit v11 on v10

--- a/solution.py
+++ b/solution.py
@@ -130,6 +130,20 @@
         out[out.shape[0] - 16 :, :] = lines.astype(BF16)
 
 
+def names_kernel(ids_ref, out):
+    top, tokens = ids_ref.shape
+    ids = ids_ref[...].astype(F32)
+    spare = jnp.zeros((out.shape[0] - top, tokens), F32)
+    out[...] = jnp.concatenate([ids, spare], axis=0).astype(BF16)
+
+
+def pack_kernel(dy_ref, names_ref, out):
+    tokens, half = dy_ref.shape
+    for c in range(half // 128):
+        out[c * tokens : (c + 1) * tokens, :] = dy_ref[:, c * 128 : (c + 1) * 128]
+    out[half // 128 * tokens :, :] = names_ref[...]
+
+
 def by_expert(rows, local, cap):
     return [
         jnp.concatenate([r[l * cap : (l + 1) * cap] for r in rows], axis=0)
@@ -160,22 +174,26 @@
             x_ref[l, :, c : c + chunk] = x.astype(BF16)
 
 
-def gather_kernel(dims, top, place, *refs):
+def gather_kernel(dims, top, tokens, place, *refs):
     experts, local, cap, width = dims
     n = experts // local
     own, other, x_ref = refs[:n], refs[n:-1], refs[-1]
-    half = own[0].shape[1]
-    tokens = own[0].shape[0] - 8
+    half = x_ref.shape[2] // 2
     chunk = min(half, 512)
     held = []
     for ref in own:
-        ids = ref[tokens:, :tokens].astype(F32).astype(jnp.int32)[:top]
+        ids = ref[half // 128 * tokens :, :].astype(F32).astype(jnp.int32)[:top]
         held.append(
             jnp.concatenate(slots_by_lane(ids, place[0], local, cap, width), axis=0)
         )
+
+    def features(ref, start):
+        blocks = range(start // 128, (start + chunk) // 128)
+        return jnp.concatenate([ref[c * tokens : (c + 1) * tokens, :] for c in blocks], axis=1)
+
     for side, halves in ((place[1], own), (1 - place[1], other)):
         for c in range(0, half, chunk):
-            rows = [dot(h, ref[:tokens, c : c + chunk], NN) for h, ref in zip(held, halves)]
+            rows = [dot(h, features(ref, c), NN) for h, ref in zip(held, halves)]
             at = pl.ds(pl.multiple_of(side * half + c, chunk), chunk)
             for l, x in enumerate(by_expert(rows, local, cap)):
                 x_ref[l, :, at] = x.astype(BF16)
@@ -319,8 +337,12 @@
 
     meta = jnp.concatenate([expert_ids.T, gate_fix.T], axis=0)
     hid_t = hidden.transpose(1, 2, 0)
-    named = jnp.pad(expert_ids.T.astype(BF16), ((0, 8 - top), (0, half - tokens)))
-    packed = jnp.concatenate([grad_out, named], axis=0)
+    (names,) = run(
+        names_kernel, [shaped((8, tokens))], [expert_ids.T], name="names", weight=10**9
+    )
+    (packed,) = run(
+        pack_kernel, [shaped((half // 128 * tokens + 8, 128))], [grad_out, names], name="pack"
+    )
     forward = n == 4
     own = [send(packed, s) for s in range(n)]
     hid_sent = run(
@@ -346,7 +368,7 @@
     else:
         other = swaps(own)
     (x,) = run(
-        functools.partial(gather_kernel, dims, top), [shaped((local, n * cap, full))],
+        functools.partial(gather_kernel, dims, top, tokens), [shaped((local, n * cap, full))],
         [place, *own, *other], where=placed, name="gather", weight=20 * 10**8,
     )
     grad_sent = run(

time: 50.4 us -> 49.5 us (0.982)
  other arithmetic: 2.44 us -> 0.08 us
  waiting for transfers between devices: 12.5 us -> 13.8 us
    ppermute x15, waiting for transfers between devices: 7.31 us -> 8.77 us  [send(): return lax.ppermute(x, 'ctx', [(i, i ^ s) for i in range(n)]) if s else x]
    concatenate x1 -> x0, other arithmetic: 0.97 us -> none  [body(): packed = jnp.concatenate([grad_out, named], axis=0)]
    concatenate x1, other arithmetic: 0.71 us -> 0.01 us  [body(): meta = jnp.concatenate([expert_ids.T, gate_fix.T], axis=0)]
    convert_element_type x1 -> x0, other arithmetic: 0.69 us -> none  [body(): expert_ids.T.astype(BF16)]
    unnamed x4 -> x12, local copies, waits for them, and re-layouts: 1.83 us -> 1.64 us
    pallas_call x9 -> x11, Pallas kernels: 13.9 us -> 14 us  [call(): pl.pallas_call(kernel, out_shape=outs, in_specs=[pl.BlockSpec(memory_spac...]
  transfers between devices with their start and end apart: 20 -> 20, of which waited for: 11 -> 11; matrix products, arithmetic and copies ran while one was open for 2% -> 0% of each run, Pallas kernels for 26% -> 27%
where the time goes in v11:
time: 49.5 us; the launch traced here: 49.4 us
  starting transfers between devices  19.1 us (39%)
  Pallas kernels  14 us (28%)
  waiting for transfers between devices  13.8 us (28%)
  local copies, waits for them, and re-layouts  1.64 us (3%)
  between operations  0.73 us (1%)
    ppermute x15, starting transfers between devices, send(): return lax.ppermute(x, 'ctx', [(i, i ^ s) for i in range(n)]) if s else x  18.4 us
    pallas_call x11, Pallas kernels, call(): pl.pallas_call(kernel, out_shape=outs, in_specs=[pl.BlockSpec(memory_spac...  14 us
    ppermute x15, waiting for transfers between devices, send(): return lax.ppermute(x, 'ctx', [(i, i ^ s) for i in range(n)]) if s else x  8.77 us
    ppermute x5, waiting for transfers between devices, swap(): return lax.ppermute(x, 'tp', [(0, 1), (1, 0)])  5.08 us
    unnamed x12, local copies, waits for them, and re-layouts  1.64 us
  transfers between devices with their start and end apart: 20, of which 11 were waited for; matrix products, arithmetic and copies ran while one was open for 0% of the time, Pallas kernels for 27%

profile of v11, /device:TPU:0, one launch (start us, length us, event | category | flops | bytes accessed | tf_op | source)
XLA Modules:
  0.0 49.4 jit_solution(11019281666244786150)
XLA Ops:
  0.7 0.8 %copy-done.3 = s32[128,4]{0,1:T(4,128)S(1)} copy-done((s32[128,4]{0,1:T(4,128)S(1)}, s32[128,4]{0,1:T(4,128)}, u32[]{:S(2)}) %copy-start.3) | copy-done | bytes 2072
  1.4 0.2 copy-done.2
  1.6 4.0 %collective-permute-start.6 = (bf16[1032,128]{1,0:T(8,128)(2,1)S(1)}, bf16[1032,128]{1,0:T(8,128)(2,1)S(1)}, u32[]{:S(2)}, u32[]{:S(2)}) collective-permute-start(bf16[1032,128]{1,0:T(8,128)(2,1)S(1)} %pack.1.refs_0_), channel_id=1, source_target_pairs={{0,24},{8,16},{16,8},{24,0},{1,25},{9,17},{17,9},{25,1},{2,26},{10... | collective-permute-start | bytes 792584 | tf_op jit(solution)/shard_map/ppermute | solution.py:333
  5.6 0.5 %collective-permute-start.5 = (bf16[1032,128]{1,0:T(8,128)(2,1)S(1)}, bf16[1032,128]{1,0:T(8,128)(2,1)S(1)}, u32[]{:S(2)}, u32[]{:S(2)}) collective-permute-start(bf16[1032,128]{1,0:T(8,128)(2,1)S(1)} %pack.1.refs_0_), channel_id=1, source_target_pairs={{0,16},{8,24},{16,0},{24,8},{1,17},{9,25},{17,1},{25,9},{2,18},{10... | collective-permute-start | bytes 792584 | tf_op jit(solution)/shard_map/ppermute | solution.py:333
  6.1 0.1 collective-permute-start.4
  6.2 0.1 pad_add_fusion.1.place
  6.3 1.6 %dispatch.1 = (bf16[816,128]{1,0:T(8,128)(2,1)S(1)}, bf16[816,128]{1,0:T(8,128)(2,1)S(1)}, bf16[816,128]{1,0:T(8,128)(2,1)S(1)}, bf16[816,128]{1,0:T(8,128)(2,1)S(1)}) custom-call(s32[2]{0:T(128)S(1)} %pad_add_fusion.1.place, s32[8,128]{1,0:T(8,128)S(1)} %pad_add_fusion.meta_ref, bf16[4,704,128]{2,1,0:T(8,128)(2,1)S(1)} %bitcast.6), custom_call_target="tpu_custom_call" | custom-call | flops 1 | bytes 1 | tf_op jit(solution)/shard_map/dispatch/pallas_call | solution.py:300
  7.9 2.0 %collective-permute-start.7 = (bf16[816,128]{1,0:T(8,128)(2,1)S(1)}, bf16[816,128]{1,0:T(8,128)(2,1)S(1)}, u32[]{:S(2)}, u32[]{:S(2)}) collective-permute-start(bf16[816,128]{1,0:T(8,128)(2,1)S(1)} %get-tuple-element.64), channel_id=1, source_target_pairs={{0,8},{8,0},{16,24},{24,16},{1,9},{9,1},{17,25},{25,17},{2,10},{10... | collective-permute-start | bytes 626696 | tf_op jit(solution)/shard_map/ppermute | solution.py:333
  9.9 1.5 %collective-permute-start.8 = (bf16[816,128]{1,0:T(8,128)(2,1)S(1)}, bf16[816,128]{1,0:T(8,128)(2,1)S(1)}, u32[]{:S(2)}, u32[]{:S(2)}) collective-permute-start(bf16[816,128]{1,0:T(8,128)(2,1)S(1)} %get-tuple-element.65), channel_id=1, source_target_pairs={{0,16},{8,24},{16,0},{24,8},{1,17},{9,25},{17,1},{25,9},{2,18},{10... | collective-permute-start | bytes 626696 | tf_op jit(solution)/shard_map/ppermute | solution.py:333
  11.4 1.4 %collective-permute-done.6.refs_3_ = bf16[1032,128]{1,0:T(8,128)(2,1)S(1)} collective-permute-done((bf16[1032,128]{1,0:T(8,128)(2,1)S(1)}, bf16[1032,128]{1,0:T(8,128)(2,1)S(1)}, u32[]{:S(2)}, u32[]{:S(2)}) %collective-permute-start.6) | collective-permute-done | bytes 264224 | tf_op jit(solution)/shard_map/ppermute | solution.py:333
  12.8 3.3 %conditional.2 = (bf16[1032,128]{1,0:T(8,128)(2,1)}, bf16[1032,128]{1,0:T(8,128)(2,1)}) conditional(s32[]{:T(128)} %convert_element_type.4, (bf16[1032,128]{1,0:T(8,128)(2,1)S(1)}, bf16[1032,128]{1,0:T(8,128)(2,1)S(1)}) %tuple.26, (bf16[1032,128]{1,0:T(8,128)(2,1)S(1)}, bf16[1032,128]{1,0:T(8,128)(2,1)S(1)}) %tuple.26), branch_computations={%region_0.0_spmd, %region_1.0_spmd} | conditional | bytes 2113632 | solution.py:365
  12.8 0.0 collective-permute-start
  12.8 1.7 %collective-permute-done = bf16[1032,128]{1,0:T(8,128)(2,1)} collective-permute-done((bf16[1032,128]{1,0:T(8,128)(2,1)S(1)}, bf16[1032,128]{1,0:T(8,128)(2,1)}, u32[]{:S(2)}, u32[]{:S(2)}) %collective-permute-start) | collective-permute-done | bytes 264224 | tf_op jit(solution)/shard_map/cond/branch_1_fun/ppermute | solution.py:336
  14.5 0.1 collective-permute-start.1
  14.6 1.5 %collective-permute-done.1 = bf16[1032,128]{1,0:T(8,128)(2,1)} collective-permute-done((bf16[1032,128]{1,0:T(8,128)(2,1)S(1)}, bf16[1032,128]{1,0:T(8,128)(2,1)}, u32[]{:S(2)}, u32[]{:S(2)}) %collective-permute-start.1) | collective-permute-done | bytes 264224 | tf_op jit(solution)/shard_map/cond/branch_1_fun/ppermute | solution.py:336
  16.2 2.9 %collective-permute-start.9 = (bf16[816,128]{1,0:T(8,128)(2,1)S(1)}, bf16[816,128]{1,0:T(8,128)(2,1)S(1)}, u32[]{:S(2)}, u32[]{:S(2)}) collective-permute-start(bf16[816,128]{1,0:T(8,128)(2,1)S(1)} %get-tuple-element.66), channel_id=1, source_target_pairs={{0,24},{8,16},{16,8},{24,0},{1,25},{9,17},{17,9},{25,1},{2,26},{10... | collective-permute-start | bytes 626696 | tf_op jit(solution)/shard_map/ppermute | solution.py:333
  19.1 0.0 collective-permute-done.5.refs_2_
  19.1 0.0 collective-permute-done.4.refs_1_
  19.1 2.1 %conditional.3 = (bf16[1032,128]{1,0:T(8,128)(2,1)}, bf16[1032,128]{1,0:T(8,128)(2,1)}) conditional(s32[]{:T(128)} %convert_element_type.4, (bf16[1032,128]{1,0:T(8,128)(2,1)S(1)}, bf16[1032,128]{1,0:T(8,128)(2,1)S(1)}) %tuple.28, (bf16[1032,128]{1,0:T(8,128)(2,1)S(1)}, bf16[1032,128]{1,0:T(8,128)(2,1)S(1)}) %tuple.28), branch_computations={%region_2.0_spmd, %region_3.0_spmd} | conditional | bytes 2113632 | solution.py:367
  19.1 0.5 %collective-permute-start.3 = (bf16[1032,128]{1,0:T(8,128)(2,1)S(1)}, bf16[1032,128]{1,0:T(8,128)(2,1)}, u32[]{:S(2)}, u32[]{:S(2)}) collective-permute-start(bf16[1032,128]{1,0:T(8,128)(2,1)S(1)} %get-tuple-element.21), channel_id=1, source_target_pairs={{0,1},{1,0},{2,3},{3,2},{4,5},{5,4},{6,7},{7,6},{8,9},{9,8},{10,11... | collective-permute-start | bytes 792584 | tf_op jit(solution)/shard_map/cond/branch_1_fun/ppermute | solution.py:336
  19.6 1.2 %collective-permute-done.2 = bf16[1032,128]{1,0:T(8,128)(2,1)} collective-permute-done((bf16[1032,128]{1,0:T(8,128)(2,1)S(1)}, bf16[1032,128]{1,0:T(8,128)(2,1)}, u32[]{:S(2)}, u32[]{:S(2)}) %collective-permute-start.2) | collective-permute-done | bytes 264224 | tf_op jit(solution)/shard_map/cond/branch_1_fun/ppermute | solution.py:336
  20.8 0.4 collective-permute-done.3
  21.1 2.2 %gather.1.x_ref = bf16[2,288,2048]{2,1,0:T(8,128)(2,1)S(1)} custom-call(s32[2]{0:T(128)S(1)} %pad_add_fusion.1.place, bf16[1032,128]{1,0:T(8,128)(2,1)S(1)} %pack.1.refs_0_, bf16[1032,128]{1,0:T(8,128)(2,1)S(1)} %collective-permute-done.4.refs_1_, bf16[1032,128]{1,0:T(8,128)(2,1)S(1)} %collective-permute-done.5.refs_2_, ...), custom_call_target="tpu_custom_call" | custom-call | flops 2000000000 | bytes 1 | tf_op jit(solution)/shard_map/gather/pallas_call | solution.py:300
  23.4 0.7 %copy-done = bf16[2,704,2048]{2,1,0:T(8,128)(2,1)S(1)} copy-done((bf16[2,704,2048]{2,1,0:T(8,128)(2,1)S(1)}, bf16[2,704,2048]{2,1,0:T(8,128)(2,1)}, u32[]{:S(2)}) %copy-start) | copy-done | bytes 5767192
  24.1 2.1 %grad.1 = (bf16[800,128]{1,0:T(8,128)(2,1)S(1)}, bf16[800,128]{1,0:T(8,128)(2,1)S(1)}, bf16[800,128]{1,0:T(8,128)(2,1)S(1)}, bf16[800,128]{1,0:T(8,128)(2,1)S(1)}) custom-call(bf16[2,288,2048]{2,1,0:T(8,128)(2,1)S(1)} %gather.1.x_ref, bf16[2,704,2048]{2,1,0:T(8,128)(2,1)S(1)} %copy-done), custom_call_target="tpu_custom_call" | custom-call | flops 1 | bytes 1 | tf_op jit(solution)/shard_map/grad/pallas_call | solution.py:300
  26.2 1.5 %collective-permute-start.11 = (bf16[800,128]{1,0:T(8,128)(2,1)S(1)}, bf16[800,128]{1,0:T(8,128)(2,1)S(1)}, u32[]{:S(2)}, u32[]{:S(2)}) collective-permute-start(bf16[800,128]{1,0:T(8,128)(2,1)S(1)} %get-tuple-element.70), channel_id=1, source_target_pairs={{0,8},{8,0},{16,24},{24,16},{1,9},{9,1},{17,25},{25,17},{2,10},{10... | collective-permute-start | bytes 614408 | tf_op jit(solution)/shard_map/ppermute | solution.py:333
  27.7 0.5 %collective-permute-start.12 = (bf16[800,128]{1,0:T(8,128)(2,1)S(1)}, bf16[800,128]{1,0:T(8,128)(2,1)S(1)}, u32[]{:S(2)}, u32[]{:S(2)}) collective-permute-start(bf16[800,128]{1,0:T(8,128)(2,1)S(1)} %get-tuple-element.71), channel_id=1, source_target_pairs={{0,16},{8,24},{16,0},{24,8},{1,17},{9,25},{17,1},{25,9},{2,18},{10... | collective-permute-start | bytes 614408 | tf_op jit(solution)/shard_map/ppermute | solution.py:333
  28.2 1.5 %collective-permute-start.19 = (bf16[800,128]{1,0:T(8,128)(2,1)S(1)}, bf16[800,128]{1,0:T(8,128)(2,1)S(1)}, u32[]{:S(2)}, u32[]{:S(2)}) collective-permute-start(bf16[800,128]{1,0:T(8,128)(2,1)S(1)} %get-tuple-element.83), channel_id=1, source_target_pairs={{0,24},{8,16},{16,8},{24,0},{1,25},{9,17},{17,9},{25,1},{2,26},{10... | collective-permute-start | bytes 614408 | tf_op jit(solution)/shard_map/ppermute | solution.py:333
  29.8 2.3 %mix_sibling.1 = bf16[512,1024]{1,0:T(8,128)(2,1)S(1)} custom-call(s32[2]{0:T(128)S(1)} %pad_add_fusion.1.place, bf16[816,128]{1,0:T(8,128)(2,1)S(1)} %get-tuple-element.63.refs_0_, bf16[816,128]{1,0:T(8,128)(2,1)S(1)} %collective-permute-done.7.refs_1_, bf16[816,128]{1,0:T(8,128)(2,1)S(1)} %collective-permute-done.8.refs_2_, ...), custom_call_target="tpu_custom_call" | custom-call | flops 1 | bytes 1 | tf_op jit(solution)/shard_map/mix_sibling/pallas_call | solution.py:300
  32.1 0.1 collective-permute-start.10
  32.2 2.3 %mix_own.1.own = f32[512,1024]{1,0:T(8,128)S(1)} custom-call(s32[2]{0:T(128)S(1)} %pad_add_fusion.1.place, bf16[816,128]{1,0:T(8,128)(2,1)S(1)} %get-tuple-element.63.refs_0_, bf16[816,128]{1,0:T(8,128)(2,1)S(1)} %collective-permute-done.7.refs_1_, bf16[816,128]{1,0:T(8,128)(2,1)S(1)} %collective-permute-done.8.refs_2_, ...), custom_call_target="tpu_custom_call" | custom-call | flops 99999997952 | bytes 1 | tf_op jit(solution)/shard_map/mix_own/pallas_call | solution.py:300
  34.5 0.3 collective-permute-done.10.arrived
  34.8 0.2 add.5
  35.0 1.5 %collective-permute-start.14 = (bf16[128,512]{1,0:T(8,128)(2,1)S(1)}, bf16[128,512]{1,0:T(8,128)(2,1)S(1)}, u32[]{:S(2)}, u32[]{:S(2)}) collective-permute-start(bf16[128,512]{1,0:T(8,128)(2,1)S(1)} %get-tuple-element.75), channel_id=1, source_target_pairs={{0,8},{8,0},{16,24},{24,16},{1,9},{9,1},{17,25},{25,17},{2,10},{10... | collective-permute-start | bytes 393224 | tf_op jit(solution)/shard_map/ppermute | solution.py:333
  36.5 0.5 %collective-permute-start.15 = (bf16[128,512]{1,0:T(8,128)(2,1)S(1)}, bf16[128,512]{1,0:T(8,128)(2,1)S(1)}, u32[]{:S(2)}, u32[]{:S(2)}) collective-permute-start(bf16[128,512]{1,0:T(8,128)(2,1)S(1)} %get-tuple-element.76), channel_id=1, source_target_pairs={{0,16},{8,24},{16,0},{24,8},{1,17},{9,25},{17,1},{25,9},{2,18},{10... | collective-permute-start | bytes 393224 | tf_op jit(solution)/shard_map/ppermute | solution.py:333
  37.1 0.0 collective-permute-done.11.refs_1_
  37.1 1.8 %collective-permute-done.12.refs_2_ = bf16[800,128]{1,0:T(8,128)(2,1)S(1)} collective-permute-done((bf16[800,128]{1,0:T(8,128)(2,1)S(1)}, bf16[800,128]{1,0:T(8,128)(2,1)S(1)}, u32[]{:S(2)}, u32[]{:S(2)}) %collective-permute-start.12) | collective-permute-done | bytes 204832 | tf_op jit(solution)/shard_map/ppermute | solution.py:333
  38.9 0.6 %collective-permute-start.13 = (bf16[128,512]{1,0:T(8,128)(2,1)S(1)}, bf16[128,512]{1,0:T(8,128)(2,1)S(1)}, u32[]{:S(2)}, u32[]{:S(2)}) collective-permute-start(bf16[128,512]{1,0:T(8,128)(2,1)S(1)} %get-tuple-element.72), channel_id=1, source_target_pairs={{0,8},{8,0},{16,24},{24,16},{1,9},{9,1},{17,25},{25,17},{2,10},{10... | collective-permute-start | bytes 393224 | tf_op jit(solution)/shard_map/ppermute | solution.py:333
  39.5 1.9 %collective-permute-done.14.low = bf16[128,512]{1,0:T(8,128)(2,1)S(1)} collective-permute-done((bf16[128,512]{1,0:T(8,128)(2,1)S(1)}, bf16[128,512]{1,0:T(8,128)(2,1)S(1)}, u32[]{:S(2)}, u32[]{:S(2)}) %collective-permute-start.14) | collective-permute-done | bytes 131104 | tf_op jit(solution)/shard_map/ppermute | solution.py:333
  41.4 1.4 %collective-permute-done.15.high = bf16[128,512]{1,0:T(8,128)(2,1)S(1)} collective-permute-done((bf16[128,512]{1,0:T(8,128)(2,1)S(1)}, bf16[128,512]{1,0:T(8,128)(2,1)S(1)}, u32[]{:S(2)}, u32[]{:S(2)}) %collective-permute-start.15) | collective-permute-done | bytes 131104 | tf_op jit(solution)/shard_map/ppermute | solution.py:333
  42.9 0.7 %collective-permute-start.16 = (bf16[128,512]{1,0:T(8,128)(2,1)S(1)}, bf16[128,512]{1,0:T(8,128)(2,1)S(1)}, u32[]{:S(2)}, u32[]{:S(2)}) collective-permute-start(bf16[128,512]{1,0:T(8,128)(2,1)S(1)} %get-tuple-element.77), channel_id=1, source_target_pairs={{0,8},{8,0},{16,24},{24,16},{1,9},{9,1},{17,25},{25,17},{2,10},{10... | collective-permute-start | bytes 393224 | tf_op jit(solution)/shard_map/ppermute | solution.py:333
  43.6 0.5 %collective-permute-start.17 = (bf16[128,512]{1,0:T(8,128)(2,1)S(1)}, bf16[128,512]{1,0:T(8,128)(2,1)S(1)}, u32[]{:S(2)}, u32[]{:S(2)}) collective-permute-start(bf16[128,512]{1,0:T(8,128)(2,1)S(1)} %get-tuple-element.78), channel_id=1, source_target_pairs={{0,16},{8,24},{16,0},{24,8},{1,17},{9,25},{17,1},{25,9},{2,18},{10... | collective-permute-start | bytes 393224 | tf_op jit(solution)/shard_map/ppermute | solution.py:333
  44.2 0.0 collective-permute-done.19.refs_3_
  44.2 2.3 %restore.1 = bf16[4,704,128]{2,1,0:T(8,128)(2,1)} custom-call(s32[2]{0:T(128)S(1)} %pad_add_fusion.1.place, s32[8,128]{1,0:T(8,128)S(1)} %pad_add_fusion.meta_ref, bf16[800,128]{1,0:T(8,128)(2,1)S(1)} %get-tuple-element.80.refs_0_, bf16[800,128]{1,0:T(8,128)(2,1)S(1)} %collective-permute-done.11.refs_1_, ...), custom_call_target="tpu_custom_call" | custom-call | flops 99999997952 | bytes 1 | tf_op jit(solution)/shard_map/restore/pallas_call | solution.py:300
  46.5 0.0 collective-permute-done.13.one_low
  46.5 1.5 %collective-permute-done.16.one_high = bf16[128,512]{1,0:T(8,128)(2,1)S(1)} collective-permute-done((bf16[128,512]{1,0:T(8,128)(2,1)S(1)}, bf16[128,512]{1,0:T(8,128)(2,1)S(1)}, u32[]{:S(2)}, u32[]{:S(2)}) %collective-permute-start.16) | collective-permute-done | bytes 131104 | tf_op jit(solution)/shard_map/ppermute | solution.py:333
  48.0 0.6 %collective-permute-done.17.two_low = bf16[128,512]{1,0:T(8,128)(2,1)S(1)} collective-permute-done((bf16[128,512]{1,0:T(8,128)(2,1)S(1)}, bf16[128,512]{1,0:T(8,128)(2,1)S(1)}, u32[]{:S(2)}, u32[]{:S(2)}) %collective-permute-start.17) | collective-permute-done | bytes 131104 | tf_op jit(solution)/shard_map/ppermute | solution.py:333
  48.6 0.8 %finish.1 = bf16[128,1024]{1,0:T(8,128)(2,1)} custom-call(f32[128,1024]{1,0:T(8,128)S(1)} %get-tuple-element.67.mine, bf16[128,512]{1,0:T(8,128)(2,1)S(1)} %collective-permute-done.13.one_low, bf16[128,512]{1,0:T(8,128)(2,1)S(1)} %collective-permute-done.16.one_high, bf16[128,512]{1,0:T(8,128)(2,1)S(1)} %collective-permute-done.17.two_low, ...), custom_call_target="tpu_custom_call" | custom-call | flops 1 | bytes 1 | tf_op jit(solution)/shard_map/finish/pallas_call | solution.py:300
  (19 shorter events, 0.1 us)
Async XLA Ops:
  0.6 1.0 %copy-start.2 = (bf16[128,1024]{1,0:T(8,128)(2,1)S(1)}, bf16[128,1024]{1,0:T(8,128)(2,1)}, u32[]{:S(2)}) copy-start(bf16[128,1024]{1,0:T(8,128)(2,1)} %dy_ref.1) | copy-start | bytes 786436
  0.6 5.7 %copy-start.1 = (bf16[128,4,704]{0,2,1:T(8,128)(2,1)S(1)}, bf16[128,4,704]{0,2,1:T(8,128)(2,1)}, u32[]{:S(2)}) copy-start(bf16[128,4,704]{0,2,1:T(8,128)(2,1)} %param.9) | copy-start | bytes 2162692
  0.7 0.8 %copy-start.3 = (s32[128,4]{0,1:T(4,128)S(1)}, s32[128,4]{0,1:T(4,128)}, u32[]{:S(2)}) copy-start(s32[128,4]{0,1:T(4,128)} %param.10) | copy-start | bytes 6148
  1.4 4.9 %copy-start.4 = (s32[128,4]{0,1:T(4,128)S(1)}, s32[128,4]{0,1:T(4,128)}, u32[]{:S(2)}) copy-start(s32[128,4]{0,1:T(4,128)} %param.10) | copy-start | bytes 6148
  1.4 4.9 %copy-start.5 = (s32[128,4]{0,1:T(4,128)S(1)}, s32[128,4]{0,1:T(4,128)}, u32[]{:S(2)}) copy-start(s32[128,4]{0,1:T(4,128)} %param.11) | copy-start | bytes 6148
  1.6 11.2 %collective-permute-start.6 = (bf16[1032,128]{1,0:T(8,128)(2,1)S(1)}, bf16[1032,128]{1,0:T(8,128)(2,1)S(1)}, u32[]{:S(2)}, u32[]{:S(2)}) collective-permute-start(bf16[1032,128]{1,0:T(8,128)(2,1)S(1)} %pack.1.refs_0_), channel_id=1, source_target_pairs={{0,24},{8,16},{16,8},{24,0},{1,25},{9,17},{17,9},{25,1},{2,26},{10... | collective-permute-start | bytes 792584 | tf_op jit(solution)/shard_map/ppermute | solution.py:333
  5.6 13.5 %collective-permute-start.5 = (bf16[1032,128]{1,0:T(8,128)(2,1)S(1)}, bf16[1032,128]{1,0:T(8,128)(2,1)S(1)}, u32[]{:S(2)}, u32[]{:S(2)}) collective-permute-start(bf16[1032,128]{1,0:T(8,128)(2,1)S(1)} %pack.1.refs_0_), channel_id=1, source_target_pairs={{0,16},{8,24},{16,0},{24,8},{1,17},{9,25},{17,1},{25,9},{2,18},{10... | collective-permute-start | bytes 792584 | tf_op jit(solution)/shard_map/ppermute | solution.py:333
  6.1 13.0 %collective-permute-start.4 = (bf16[1032,128]{1,0:T(8,128)(2,1)S(1)}, bf16[1032,128]{1,0:T(8,128)(2,1)S(1)}, u32[]{:S(2)}, u32[]{:S(2)}) collective-permute-start(bf16[1032,128]{1,0:T(8,128)(2,1)S(1)} %pack.1.refs_0_), channel_id=1, source_target_pairs={{0,8},{8,0},{16,24},{24,16},{1,9},{9,1},{17,25},{25,17},{2,10},{10... | collective-permute-start | bytes 792584 | tf_op jit(solution)/shard_map/ppermute | solution.py:333
  7.9 20.3 %collective-permute-start.7 = (bf16[816,128]{1,0:T(8,128)(2,1)S(1)}, bf16[816,128]{1,0:T(8,128)(2,1)S(1)}, u32[]{:S(2)}, u32[]{:S(2)}) collective-permute-start(bf16[816,128]{1,0:T(8,128)(2,1)S(1)} %get-tuple-element.64), channel_id=1, source_target_pairs={{0,8},{8,0},{16,24},{24,16},{1,9},{9,1},{17,25},{25,17},{2,10},{10... | collective-permute-start | bytes 626696 | tf_op jit(solution)/shard_map/ppermute | solution.py:333
  9.9 19.9 %collective-permute-start.8 = (bf16[816,128]{1,0:T(8,128)(2,1)S(1)}, bf16[816,128]{1,0:T(8,128)(2,1)S(1)}, u32[]{:S(2)}, u32[]{:S(2)}) collective-permute-start(bf16[816,128]{1,0:T(8,128)(2,1)S(1)} %get-tuple-element.65), channel_id=1, source_target_pairs={{0,16},{8,24},{16,0},{24,8},{1,17},{9,25},{17,1},{25,9},{2,18},{10... | collective-permute-start | bytes 626696 | tf_op jit(solution)/shard_map/ppermute | solution.py:333
  12.8 1.7 %collective-permute-start = (bf16[1032,128]{1,0:T(8,128)(2,1)S(1)}, bf16[1032,128]{1,0:T(8,128)(2,1)}, u32[]{:S(2)}, u32[]{:S(2)}) collective-permute-start(bf16[1032,128]{1,0:T(8,128)(2,1)S(1)} %get-tuple-element.17), channel_id=1, source_target_pairs={{0,1},{1,0},{2,3},{3,2},{4,5},{5,4},{6,7},{7,6},{8,9},{9,8},{10,11... | collective-permute-start | bytes 792584 | tf_op jit(solution)/shard_map/cond/branch_1_fun/ppermute | solution.py:336
  14.5 1.7 %collective-permute-start.1 = (bf16[1032,128]{1,0:T(8,128)(2,1)S(1)}, bf16[1032,128]{1,0:T(8,128)(2,1)}, u32[]{:S(2)}, u32[]{:S(2)}) collective-permute-start(bf16[1032,128]{1,0:T(8,128)(2,1)S(1)} %get-tuple-element.19), channel_id=1, source_target_pairs={{0,1},{1,0},{2,3},{3,2},{4,5},{5,4},{6,7},{7,6},{8,9},{9,8},{10,11... | collective-permute-start | bytes 792584 | tf_op jit(solution)/shard_map/cond/branch_1_fun/ppermute | solution.py:336
  16.2 13.6 %collective-permute-start.9 = (bf16[816,128]{1,0:T(8,128)(2,1)S(1)}, bf16[816,128]{1,0:T(8,128)(2,1)S(1)}, u32[]{:S(2)}, u32[]{:S(2)}) collective-permute-start(bf16[816,128]{1,0:T(8,128)(2,1)S(1)} %get-tuple-element.66), channel_id=1, source_target_pairs={{0,24},{8,16},{16,8},{24,0},{1,25},{9,17},{17,9},{25,1},{2,26},{10... | collective-permute-start | bytes 626696 | tf_op jit(solution)/shard_map/ppermute | solution.py:333
  19.1 1.7 %collective-permute-start.2 = (bf16[1032,128]{1,0:T(8,128)(2,1)S(1)}, bf16[1032,128]{1,0:T(8,128)(2,1)}, u32[]{:S(2)}, u32[]{:S(2)}) collective-permute-start(bf16[1032,128]{1,0:T(8,128)(2,1)S(1)} %get-tuple-element.20), channel_id=1, source_target_pairs={{0,1},{1,0},{2,3},{3,2},{4,5},{5,4},{6,7},{7,6},{8,9},{9,8},{10,11... | collective-permute-start | bytes 792584 | tf_op jit(solution)/shard_map/cond/branch_1_fun/ppermute | solution.py:336
  19.1 2.0 %collective-permute-start.3 = (bf16[1032,128]{1,0:T(8,128)(2,1)S(1)}, bf16[1032,128]{1,0:T(8,128)(2,1)}, u32[]{:S(2)}, u32[]{:S(2)}) collective-permute-start(bf16[1032,128]{1,0:T(8,128)(2,1)S(1)} %get-tuple-element.21), channel_id=1, source_target_pairs={{0,1},{1,0},{2,3},{3,2},{4,5},{5,4},{6,7},{7,6},{8,9},{9,8},{10,11... | collective-permute-start | bytes 792584 | tf_op jit(solution)/shard_map/cond/branch_1_fun/ppermute | solution.py:336
  21.1 3.0 %copy-start = (bf16[2,704,2048]{2,1,0:T(8,128)(2,1)S(1)}, bf16[2,704,2048]{2,1,0:T(8,128)(2,1)}, u32[]{:S(2)}) copy-start(bf16[2,704,2048]{2,1,0:T(8,128)(2,1)} %refs_4_.3) | copy-start | bytes 17301508
  26.2 10.9 %collective-permute-start.11 = (bf16[800,128]{1,0:T(8,128)(2,1)S(1)}, bf16[800,128]{1,0:T(8,128)(2,1)S(1)}, u32[]{:S(2)}, u32[]{:S(2)}) collective-permute-start(bf16[800,128]{1,0:T(8,128)(2,1)S(1)} %get-tuple-element.70), channel_id=1, source_target_pairs={{0,8},{8,0},{16,24},{24,16},{1,9},{9,1},{17,25},{25,17},{2,10},{10... | collective-permute-start | bytes 614408 | tf_op jit(solution)/shard_map/ppermute | solution.py:333
  27.7 11.2 %collective-permute-start.12 = (bf16[800,128]{1,0:T(8,128)(2,1)S(1)}, bf16[800,128]{1,0:T(8,128)(2,1)S(1)}, u32[]{:S(2)}, u32[]{:S(2)}) collective-permute-start(bf16[800,128]{1,0:T(8,128)(2,1)S(1)} %get-tuple-element.71), channel_id=1, source_target_pairs={{0,16},{8,24},{16,0},{24,8},{1,17},{9,25},{17,1},{25,9},{2,18},{10... | collective-permute-start | bytes 614408 | tf_op jit(solution)/shard_map/ppermute | solution.py:333
  28.2 15.9 %collective-permute-start.19 = (bf16[800,128]{1,0:T(8,128)(2,1)S(1)}, bf16[800,128]{1,0:T(8,128)(2,1)S(1)}, u32[]{:S(2)}, u32[]{:S(2)}) collective-permute-start(bf16[800,128]{1,0:T(8,128)(2,1)S(1)} %get-tuple-element.83), channel_id=1, source_target_pairs={{0,24},{8,16},{16,8},{24,0},{1,25},{9,17},{17,9},{25,1},{2,26},{10... | collective-permute-start | bytes 614408 | tf_op jit(solution)/shard_map/ppermute | solution.py:333
  32.1 2.7 %collective-permute-start.10 = (bf16[512,1024]{1,0:T(8,128)(2,1)S(1)}, bf16[512,1024]{1,0:T(8,128)(2,1)S(1)}, u32[]{:S(2)}, u32[]{:S(2)}) collective-permute-start(bf16[512,1024]{1,0:T(8,128)(2,1)S(1)} %mix_sibling.1), channel_id=1, source_target_pairs={{0,1},{1,0},{2,3},{3,2},{4,5},{5,4},{6,7},{7,6},{8,9},{9,8},{10,11... | collective-permute-start | bytes 3145736 | tf_op jit(solution)/shard_map/ppermute | solution.py:336
  35.0 6.4 %collective-permute-start.14 = (bf16[128,512]{1,0:T(8,128)(2,1)S(1)}, bf16[128,512]{1,0:T(8,128)(2,1)S(1)}, u32[]{:S(2)}, u32[]{:S(2)}) collective-permute-start(bf16[128,512]{1,0:T(8,128)(2,1)S(1)} %get-tuple-element.75), channel_id=1, source_target_pairs={{0,8},{8,0},{16,24},{24,16},{1,9},{9,1},{17,25},{25,17},{2,10},{10... | collective-permute-start | bytes 393224 | tf_op jit(solution)/shard_map/ppermute | solution.py:333
  36.5 6.4 %collective-permute-start.15 = (bf16[128,512]{1,0:T(8,128)(2,1)S(1)}, bf16[128,512]{1,0:T(8,128)(2,1)S(1)}, u32[]{:S(2)}, u32[]{:S(2)}) collective-permute-start(bf16[128,512]{1,0:T(8,128)(2,1)S(1)} %get-tuple-element.76), channel_id=1, source_target_pairs={{0,16},{8,24},{16,0},{24,8},{1,17},{9,25},{17,1},{25,9},{2,18},{10... | collective-permute-start | bytes 393224 | tf_op jit(solution)/shard_map/ppermute | solution.py:333
  38.9 7.6 %collective-permute-start.13 = (bf16[128,512]{1,0:T(8,128)(2,1)S(1)}, bf16[128,512]{1,0:T(8,128)(2,1)S(1)}, u32[]{:S(2)}, u32[]{:S(2)}) collective-permute-start(bf16[128,512]{1,0:T(8,128)(2,1)S(1)} %get-tuple-element.72), channel_id=1, source_target_pairs={{0,8},{8,0},{16,24},{24,16},{1,9},{9,1},{17,25},{25,17},{2,10},{10... | collective-permute-start | bytes 393224 | tf_op jit(solution)/shard_map/ppermute | solution.py:333
  39.5 6.9 %collective-permute-start.18 = (bf16[128,512]{1,0:T(8,128)(2,1)S(1)}, bf16[128,512]{1,0:T(8,128)(2,1)S(1)}, u32[]{:S(2)}, u32[]{:S(2)}) collective-permute-start(bf16[128,512]{1,0:T(8,128)(2,1)S(1)} %get-tuple-element.79), channel_id=1, source_target_pairs={{0,16},{8,24},{16,0},{24,8},{1,17},{9,25},{17,1},{25,9},{2,18},{10... | collective-permute-start | bytes 393224 | tf_op jit(solution)/shard_map/ppermute | solution.py:333
  42.9 5.0 %collective-permute-start.16 = (bf16[128,512]{1,0:T(8,128)(2,1)S(1)}, bf16[128,512]{1,0:T(8,128)(2,1)S(1)}, u32[]{:S(2)}, u32[]{:S(2)}) collective-permute-start(bf16[128,512]{1,0:T(8,128)(2,1)S(1)} %get-tuple-element.77), channel_id=1, source_target_pairs={{0,8},{8,0},{16,24},{24,16},{1,9},{9,1},{17,25},{25,17},{2,10},{10... | collective-permute-start | bytes 393224 | tf_op jit(solution)/shard_map/ppermute | solution.py:333
  43.6 5.0 %collective-permute-start.17 = (bf16[128,512]{1,0:T(8,128)(2,1)S(1)}, bf16[128,512]{1,0:T(8,128)(2,1)S(1)}, u32[]{:S(2)}, u32[]{:S(2)}) collective-permute-start(bf16[128,512]{1,0:T(8,128)(2,1)S(1)} %get-tuple-element.78), channel_id=1, source_target_pairs={{0,16},{8,24},{16,0},{24,8},{1,17},{9,25},{17,1},{25,9},{2,18},{10... | collective-permute-start | bytes 393224 | tf_op jit(solution)/shard_map/ppermute | solution.py:333

commit v12 on v11

--- a/solution.py
+++ b/solution.py
@@ -174,26 +174,43 @@
             x_ref[l, :, c : c + chunk] = x.astype(BF16)
 
 
+def pass_kernel(one, two, low, high):
+    rows = high.shape[0]
+    low[:rows, :] = one[:rows, :]
+    low[rows:, :] = one[2 * rows :, :]
+    high[...] = two[rows : 2 * rows, :]
+
+
+def by_part(refs, n):
+    if len(refs) == n:
+        return [(ref,) for ref in refs]
+    return [(ref,) for ref in refs[: n - 1]] + [tuple(refs[n - 1 :])]
+
+
 def gather_kernel(dims, top, tokens, place, *refs):
     experts, local, cap, width = dims
     n = experts // local
-    own, other, x_ref = refs[:n], refs[n:-1], refs[-1]
+    count = len(refs) // 2
+    own, other, x_ref = by_part(refs[:count], n), by_part(refs[count:-1], n), refs[-1]
     half = x_ref.shape[2] // 2
     chunk = min(half, 512)
     held = []
-    for ref in own:
-        ids = ref[half // 128 * tokens :, :].astype(F32).astype(jnp.int32)[:top]
+    for parts in own:
+        end = half // 128 // len(parts) * tokens
+        ids = parts[0][end:, :].astype(F32).astype(jnp.int32)[:top]
         held.append(
             jnp.concatenate(slots_by_lane(ids, place[0], local, cap, width), axis=0)
         )
 
-    def features(ref, start):
+    def features(parts, start):
+        size = half // len(parts)
+        ref, start = parts[start // size], start % size
         blocks = range(start // 128, (start + chunk) // 128)
         return jnp.concatenate([ref[c * tokens : (c + 1) * tokens, :] for c in blocks], axis=1)
 
     for side, halves in ((place[1], own), (1 - place[1], other)):
         for c in range(0, half, chunk):
-            rows = [dot(h, features(ref, c), NN) for h, ref in zip(held, halves)]
+            rows = [dot(h, features(parts, c), NN) for h, parts in zip(held, halves)]
             at = pl.ds(pl.multiple_of(side * half + c, chunk), chunk)
             for l, x in enumerate(by_expert(rows, local, cap)):
                 x_ref[l, :, at] = x.astype(BF16)
@@ -344,28 +361,37 @@
         pack_kernel, [shaped((half // 128 * tokens + 8, 128))], [grad_out, names], name="pack"
     )
     forward = n == 4
-    own = [send(packed, s) for s in range(n)]
+    near = 3 if forward else n
+    own = [send(packed, s) for s in range(near)]
     hid_sent = run(
-        functools.partial(dispatch_kernel, dims), [shaped((packed_rows(width, ff)[0] + 16, 128))] * n,
+        functools.partial(dispatch_kernel, dims),
+        [shaped((packed_rows(width, ff)[0] + 16, 128))] * n,
         [place, meta, hid_t], where=placed, name="dispatch",
     )
-    hid = [send(hid_sent[s], s) for s in range(n)]
     slot = shaped((packed_rows(width, ff)[0], 128))
 
     def swaps(xs):
         return [swap(x) for x in xs]
 
-    def swaps_in_turn(xs):
-        first = swap(xs[0])
-        second, first = lax.optimization_barrier((xs[1], first))
-        return [first, swap(second)]
+    def swaps_by_two(xs):
+        first = swaps(xs[:2])
+        *rest, first[0], first[1] = lax.optimization_barrier((*xs[2:], *first))
+        return first + swaps(rest)
 
     if forward:
         always = place[0] < 1000
-        last, mine = lax.cond(always, swaps_in_turn, list, [own[3], own[0]])
-        *own[1:3], last = lax.optimization_barrier((*own[1:3], last))
-        other = [mine] + lax.cond(always, swaps, list, own[1:3]) + [last]
+        hid_own = hid_sent[0]
+        mine = lax.cond(always, swap, lambda x: x, packed)
+        *own[1:], mine, hid_own = lax.optimization_barrier((*own[1:], mine, hid_own))
+        rows = half // 256 * tokens
+        low, high = run(
+            pass_kernel, [shaped((rows + 8, 128)), shaped((rows, 128))], own[1:], name="pass"
+        )
+        own += [send(low, 2), send(high, 1)]
+        hid = [hid_own] + [send(hid_sent[s], s) for s in range(1, n)]
+        other = [mine] + lax.cond(always, swaps_by_two, list, own[1:])
     else:
+        hid = [send(hid_sent[s], s) for s in range(n)]
         other = swaps(own)
     (x,) = run(
         functools.partial(gather_kernel, dims, top, tokens), [shaped((local, n * cap, full))],

time: 49.5 us -> 51.5 us (1.040)
  starting transfers between devices: 19.1 us -> 21.7 us
  waiting for transfers between devices: 13.8 us -> 13.1 us
    ppermute x15 -> x16, starting transfers between devices: 18.4 us -> 20.6 us  [send(): return lax.ppermute(x, 'ctx', [(i, i ^ s) for i in range(n)]) if s else x]
    ppermute x5 -> x6, starting transfers between devices: 0.72 us -> 1.16 us  [swap(): return lax.ppermute(x, 'tp', [(0, 1), (1, 0)])]
    ppermute x5 -> x6, waiting for transfers between devices: 5.08 us -> 4.69 us  [swap(): return lax.ppermute(x, 'tp', [(0, 1), (1, 0)])]
    ppermute x15 -> x16, waiting for transfers between devices: 8.77 us -> 8.46 us  [send(): return lax.ppermute(x, 'ctx', [(i, i ^ s) for i in range(n)]) if s else x]
    pallas_call x11 -> x12, Pallas kernels: 14 us -> 14 us  [call(): pl.pallas_call(kernel, out_shape=outs, in_specs=[pl.BlockSpec(memory_spac...]
  transfers between devices with their start and end apart: 20 -> 22, of which waited for: 11 -> 12; matrix products, arithmetic and copies ran while one was open for 0% -> 0% of each run, Pallas kernels for 27% -> 26%
where the time goes in v12:
time: 51.5 us; the launch traced here: 51.4 us
  starting transfers between devices  21.7 us (42%)
  Pallas kernels  14 us (27%)
  waiting for transfers between devices  13.1 us (25%)
  local copies, waits for them, and re-layouts  1.65 us (3%)
  between operations  0.73 us (1%)
    ppermute x16, starting transfers between devices, send(): return lax.ppermute(x, 'ctx', [(i, i ^ s) for i in range(n)]) if s else x  20.6 us
    pallas_call x12, Pallas kernels, call(): pl.pallas_call(kernel, out_shape=outs, in_specs=[pl.BlockSpec(memory_spac...  14 us
    ppermute x16, waiting for transfers between devices, send(): return lax.ppermute(x, 'ctx', [(i, i ^ s) for i in range(n)]) if s else x  8.46 us
    ppermute x6, waiting for transfers between devices, swap(): return lax.ppermute(x, 'tp', [(0, 1), (1, 0)])  4.69 us
    unnamed x12, local copies, waits for them, and re-layouts  1.65 us
    ppermute x6, starting transfers between devices, swap(): return lax.ppermute(x, 'tp', [(0, 1), (1, 0)])  1.16 us
  transfers between devices with their start and end apart: 22, of which 12 were waited for; matrix products, arithmetic and copies ran while one was open for 0% of the time, Pallas kernels for 26%

profile of v12, /device:TPU:0, one launch (start us, length us, event | category | flops | bytes accessed | tf_op | source)
XLA Modules:
  0.0 51.4 jit_solution(17064067705497059988)
XLA Ops:
  0.7 0.8 %copy-done.3 = s32[128,4]{0,1:T(4,128)S(1)} copy-done((s32[128,4]{0,1:T(4,128)S(1)}, s32[128,4]{0,1:T(4,128)}, u32[]{:S(2)}) %copy-start.3) | copy-done | bytes 2072
  1.4 0.2 copy-done.2
  1.6 3.0 %collective-permute-start.6 = (bf16[1032,128]{1,0:T(8,128)(2,1)S(1)}, bf16[1032,128]{1,0:T(8,128)(2,1)S(1)}, u32[]{:S(2)}, u32[]{:S(2)}) collective-permute-start(bf16[1032,128]{1,0:T(8,128)(2,1)S(1)} %pack.1.refs_0_), channel_id=1, source_target_pairs={{0,16},{8,24},{16,0},{24,8},{1,17},{9,25},{17,1},{25,9},{2,18},{10... | collective-permute-start | bytes 792584 | tf_op jit(solution)/shard_map/ppermute | solution.py:350
  4.7 1.5 %collective-permute-start.5 = (bf16[1032,128]{1,0:T(8,128)(2,1)S(1)}, bf16[1032,128]{1,0:T(8,128)(2,1)S(1)}, u32[]{:S(2)}, u32[]{:S(2)}) collective-permute-start(bf16[1032,128]{1,0:T(8,128)(2,1)S(1)} %pack.1.refs_0_), channel_id=1, source_target_pairs={{0,8},{8,0},{16,24},{24,16},{1,9},{9,1},{17,25},{25,17},{2,10},{10... | collective-permute-start | bytes 792584 | tf_op jit(solution)/shard_map/ppermute | solution.py:350
  6.2 0.1 pad_add_fusion.1.place
  6.3 1.6 %dispatch.1 = (bf16[816,128]{1,0:T(8,128)(2,1)S(1)}, bf16[816,128]{1,0:T(8,128)(2,1)S(1)}, bf16[816,128]{1,0:T(8,128)(2,1)S(1)}, bf16[816,128]{1,0:T(8,128)(2,1)S(1)}) custom-call(s32[2]{0:T(128)S(1)} %pad_add_fusion.1.place, s32[8,128]{1,0:T(8,128)S(1)} %pad_add_fusion.meta_ref, bf16[4,704,128]{2,1,0:T(8,128)(2,1)S(1)} %bitcast.6), custom_call_target="tpu_custom_call" | custom-call | flops 1 | bytes 1 | tf_op jit(solution)/shard_map/dispatch/pallas_call | solution.py:317
  7.8 1.7 %conditional.2 = (bf16[1032,128]{1,0:T(8,128)(2,1)}) conditional(s32[]{:T(128)} %convert_element_type.4, bf16[1032,128]{1,0:T(8,128)(2,1)S(1)} %pack.1.refs_0_, bf16[1032,128]{1,0:T(8,128)(2,1)S(1)} %pack.1.refs_0_), branch_computations={%region_0.0_spmd, %region_1.0_spmd} | conditional | bytes 1056816 | solution.py:384
  7.9 0.1 collective-permute-start
  7.9 1.7 %collective-permute-done = bf16[1032,128]{1,0:T(8,128)(2,1)} collective-permute-done((bf16[1032,128]{1,0:T(8,128)(2,1)S(1)}, bf16[1032,128]{1,0:T(8,128)(2,1)}, u32[]{:S(2)}, u32[]{:S(2)}) %collective-permute-start) | collective-permute-done | bytes 264224 | tf_op jit(solution)/shard_map/cond/branch_1_fun/ppermute | solution.py:353
  9.6 1.4 %collective-permute-done.6.two.refs_2_ = bf16[1032,128]{1,0:T(8,128)(2,1)S(1)} collective-permute-done((bf16[1032,128]{1,0:T(8,128)(2,1)S(1)}, bf16[1032,128]{1,0:T(8,128)(2,1)S(1)}, u32[]{:S(2)}, u32[]{:S(2)}) %collective-permute-start.6) | collective-permute-done | bytes 264224 | tf_op jit(solution)/shard_map/ppermute | solution.py:350
  11.0 1.5 %collective-permute-done.5.one.refs_1_ = bf16[1032,128]{1,0:T(8,128)(2,1)S(1)} collective-permute-done((bf16[1032,128]{1,0:T(8,128)(2,1)S(1)}, bf16[1032,128]{1,0:T(8,128)(2,1)S(1)}, u32[]{:S(2)}, u32[]{:S(2)}) %collective-permute-start.5) | collective-permute-done | bytes 264224 | tf_op jit(solution)/shard_map/ppermute | solution.py:350
  12.5 0.4 collective-permute-start.7
  12.9 1.6 %collective-permute-start.8 = (bf16[512,128]{1,0:T(8,128)(2,1)S(1)}, bf16[512,128]{1,0:T(8,128)(2,1)S(1)}, u32[]{:S(2)}, u32[]{:S(2)}) collective-permute-start(bf16[512,128]{1,0:T(8,128)(2,1)S(1)} %get-tuple-element.69), channel_id=1, source_target_pairs={{0,8},{8,0},{16,24},{24,16},{1,9},{9,1},{17,25},{25,17},{2,10},{10... | collective-permute-start | bytes 393224 | tf_op jit(solution)/shard_map/ppermute | solution.py:350
  14.6 0.4 collective-permute-start.9
  14.9 1.7 %collective-permute-start.10 = (bf16[816,128]{1,0:T(8,128)(2,1)S(1)}, bf16[816,128]{1,0:T(8,128)(2,1)S(1)}, u32[]{:S(2)}, u32[]{:S(2)}) collective-permute-start(bf16[816,128]{1,0:T(8,128)(2,1)S(1)} %get-tuple-element.78), channel_id=1, source_target_pairs={{0,16},{8,24},{16,0},{24,8},{1,17},{9,25},{17,1},{25,9},{2,18},{10... | collective-permute-start | bytes 626696 | tf_op jit(solution)/shard_map/ppermute | solution.py:350
  16.6 1.4 %collective-permute-start.11 = (bf16[816,128]{1,0:T(8,128)(2,1)S(1)}, bf16[816,128]{1,0:T(8,128)(2,1)S(1)}, u32[]{:S(2)}, u32[]{:S(2)}) collective-permute-start(bf16[816,128]{1,0:T(8,128)(2,1)S(1)} %get-tuple-element.79), channel_id=1, source_target_pairs={{0,24},{8,16},{16,8},{24,0},{1,25},{9,17},{17,9},{25,1},{2,26},{10... | collective-permute-start | bytes 626696 | tf_op jit(solution)/shard_map/ppermute | solution.py:350
  18.1 1.3 %collective-permute-done.8.refs_4_ = bf16[512,128]{1,0:T(8,128)(2,1)S(1)} collective-permute-done((bf16[512,128]{1,0:T(8,128)(2,1)S(1)}, bf16[512,128]{1,0:T(8,128)(2,1)S(1)}, u32[]{:S(2)}, u32[]{:S(2)}) %collective-permute-start.8) | collective-permute-done | bytes 131104 | tf_op jit(solution)/shard_map/ppermute | solution.py:350
  19.4 3.7 %conditional.3 = (bf16[1032,128]{1,0:T(8,128)(2,1)}, bf16[1032,128]{1,0:T(8,128)(2,1)}, bf16[520,128]{1,0:T(8,128)(2,1)}, bf16[512,128]{1,0:T(8,128)(2,1)}) conditional(s32[]{:T(128)} %convert_element_type.4, (bf16[1032,128]{1,0:T(8,128)(2,1)S(1)}, bf16[1032,128]{1,0:T(8,128)(2,1)S(1)}, bf16[520,128]{1,0:T(8,128)(2,1)S(1)}, ...), branch_computations={%region_2.0_spmd, %region_3.0_spmd} | conditional | bytes 3170496 | solution.py:392
  19.4 0.5 collective-permute-start.2
  19.9 1.2 %collective-permute-done.1 = bf16[1032,128]{1,0:T(8,128)(2,1)} collective-permute-done((bf16[1032,128]{1,0:T(8,128)(2,1)S(1)}, bf16[1032,128]{1,0:T(8,128)(2,1)}, u32[]{:S(2)}, u32[]{:S(2)}) %collective-permute-start.1) | collective-permute-done | bytes 264224 | tf_op jit(solution)/shard_map/cond/branch_1_fun/ppermute | solution.py:353
  21.0 0.4 collective-permute-done.2
  21.4 0.1 collective-permute-start.3
  21.5 0.4 collective-permute-start.4
  21.9 1.2 %collective-permute-done.4 = bf16[512,128]{1,0:T(8,128)(2,1)} collective-permute-done((bf16[512,128]{1,0:T(8,128)(2,1)S(1)}, bf16[512,128]{1,0:T(8,128)(2,1)}, u32[]{:S(2)}, u32[]{:S(2)}) %collective-permute-start.4) | collective-permute-done | bytes 131104 | tf_op jit(solution)/shard_map/cond/branch_1_fun/ppermute | solution.py:353
  23.1 2.2 %gather.1.x_ref = bf16[2,288,2048]{2,1,0:T(8,128)(2,1)S(1)} custom-call(s32[2]{0:T(128)S(1)} %pad_add_fusion.1.place, bf16[1032,128]{1,0:T(8,128)(2,1)S(1)} %pack.1.refs_0_, bf16[1032,128]{1,0:T(8,128)(2,1)S(1)} %collective-permute-done.5.one.refs_1_, bf16[1032,128]{1,0:T(8,128)(2,1)S(1)} %collective-permute-done.6.two.refs_2_, ...), custom_call_target="tpu_custom_call" | custom-call | flops 2000000000 | bytes 1 | tf_op jit(solution)/shard_map/gather/pallas_call | solution.py:317
  25.3 0.7 %copy-done = bf16[2,704,2048]{2,1,0:T(8,128)(2,1)S(1)} copy-done((bf16[2,704,2048]{2,1,0:T(8,128)(2,1)S(1)}, bf16[2,704,2048]{2,1,0:T(8,128)(2,1)}, u32[]{:S(2)}) %copy-start) | copy-done | bytes 5767192
  26.1 2.1 %grad.1 = (bf16[800,128]{1,0:T(8,128)(2,1)S(1)}, bf16[800,128]{1,0:T(8,128)(2,1)S(1)}, bf16[800,128]{1,0:T(8,128)(2,1)S(1)}, bf16[800,128]{1,0:T(8,128)(2,1)S(1)}) custom-call(bf16[2,288,2048]{2,1,0:T(8,128)(2,1)S(1)} %gather.1.x_ref, bf16[2,704,2048]{2,1,0:T(8,128)(2,1)S(1)} %copy-done), custom_call_target="tpu_custom_call" | custom-call | flops 1 | bytes 1 | tf_op jit(solution)/shard_map/grad/pallas_call | solution.py:317
  28.2 1.7 %collective-permute-start.13 = (bf16[800,128]{1,0:T(8,128)(2,1)S(1)}, bf16[800,128]{1,0:T(8,128)(2,1)S(1)}, u32[]{:S(2)}, u32[]{:S(2)}) collective-permute-start(bf16[800,128]{1,0:T(8,128)(2,1)S(1)} %get-tuple-element.83), channel_id=1, source_target_pairs={{0,8},{8,0},{16,24},{24,16},{1,9},{9,1},{17,25},{25,17},{2,10},{10... | collective-permute-start | bytes 614408 | tf_op jit(solution)/shard_map/ppermute | solution.py:350
  29.9 1.5 %collective-permute-start.14 = (bf16[800,128]{1,0:T(8,128)(2,1)S(1)}, bf16[800,128]{1,0:T(8,128)(2,1)S(1)}, u32[]{:S(2)}, u32[]{:S(2)}) collective-permute-start(bf16[800,128]{1,0:T(8,128)(2,1)S(1)} %get-tuple-element.84), channel_id=1, source_target_pairs={{0,16},{8,24},{16,0},{24,8},{1,17},{9,25},{17,1},{25,9},{2,18},{10... | collective-permute-start | bytes 614408 | tf_op jit(solution)/shard_map/ppermute | solution.py:350
  31.4 0.3 collective-permute-start.21
  31.7 0.0 collective-permute-done.10.refs_2_
  31.7 0.0 collective-permute-done.11.refs_3_
  31.7 2.3 %mix_sibling.1 = bf16[512,1024]{1,0:T(8,128)(2,1)S(1)} custom-call(s32[2]{0:T(128)S(1)} %pad_add_fusion.1.place, bf16[816,128]{1,0:T(8,128)(2,1)S(1)} %get-tuple-element.76.refs_0_, bf16[816,128]{1,0:T(8,128)(2,1)S(1)} %collective-permute-done.9.refs_1_, bf16[816,128]{1,0:T(8,128)(2,1)S(1)} %collective-permute-done.10.refs_2_, ...), custom_call_target="tpu_custom_call" | custom-call | flops 1 | bytes 1 | tf_op jit(solution)/shard_map/mix_sibling/pallas_call | solution.py:317
  34.0 0.1 collective-permute-start.12
  34.1 2.3 %mix_own.1.own = f32[512,1024]{1,0:T(8,128)S(1)} custom-call(s32[2]{0:T(128)S(1)} %pad_add_fusion.1.place, bf16[816,128]{1,0:T(8,128)(2,1)S(1)} %get-tuple-element.76.refs_0_, bf16[816,128]{1,0:T(8,128)(2,1)S(1)} %collective-permute-done.9.refs_1_, bf16[816,128]{1,0:T(8,128)(2,1)S(1)} %collective-permute-done.10.refs_2_, ...), custom_call_target="tpu_custom_call" | custom-call | flops 99999997952 | bytes 1 | tf_op jit(solution)/shard_map/mix_own/pallas_call | solution.py:317
  36.4 0.3 collective-permute-done.12.arrived
  36.8 0.2 add.5
  37.0 1.7 %collective-permute-start.16 = (bf16[128,512]{1,0:T(8,128)(2,1)S(1)}, bf16[128,512]{1,0:T(8,128)(2,1)S(1)}, u32[]{:S(2)}, u32[]{:S(2)}) collective-permute-start(bf16[128,512]{1,0:T(8,128)(2,1)S(1)} %get-tuple-element.88), channel_id=1, source_target_pairs={{0,8},{8,0},{16,24},{24,16},{1,9},{9,1},{17,25},{25,17},{2,10},{10... | collective-permute-start | bytes 393224 | tf_op jit(solution)/shard_map/ppermute | solution.py:350
  38.7 1.5 %collective-permute-start.17 = (bf16[128,512]{1,0:T(8,128)(2,1)S(1)}, bf16[128,512]{1,0:T(8,128)(2,1)S(1)}, u32[]{:S(2)}, u32[]{:S(2)}) collective-permute-start(bf16[128,512]{1,0:T(8,128)(2,1)S(1)} %get-tuple-element.89), channel_id=1, source_target_pairs={{0,16},{8,24},{16,0},{24,8},{1,17},{9,25},{17,1},{25,9},{2,18},{10... | collective-permute-start | bytes 393224 | tf_op jit(solution)/shard_map/ppermute | solution.py:350
  40.2 1.1 %collective-permute-done.14.refs_2_ = bf16[800,128]{1,0:T(8,128)(2,1)S(1)} collective-permute-done((bf16[800,128]{1,0:T(8,128)(2,1)S(1)}, bf16[800,128]{1,0:T(8,128)(2,1)S(1)}, u32[]{:S(2)}, u32[]{:S(2)}) %collective-permute-start.14) | collective-permute-done | bytes 204832 | tf_op jit(solution)/shard_map/ppermute | solution.py:350
  41.3 2.1 %collective-permute-start.20 = (bf16[128,512]{1,0:T(8,128)(2,1)S(1)}, bf16[128,512]{1,0:T(8,128)(2,1)S(1)}, u32[]{:S(2)}, u32[]{:S(2)}) collective-permute-start(bf16[128,512]{1,0:T(8,128)(2,1)S(1)} %get-tuple-element.92), channel_id=1, source_target_pairs={{0,16},{8,24},{16,0},{24,8},{1,17},{9,25},{17,1},{25,9},{2,18},{10... | collective-permute-start | bytes 393224 | tf_op jit(solution)/shard_map/ppermute | solution.py:350
  43.4 1.7 %collective-permute-done.17.high = bf16[128,512]{1,0:T(8,128)(2,1)S(1)} collective-permute-done((bf16[128,512]{1,0:T(8,128)(2,1)S(1)}, bf16[128,512]{1,0:T(8,128)(2,1)S(1)}, u32[]{:S(2)}, u32[]{:S(2)}) %collective-permute-start.17) | collective-permute-done | bytes 131104 | tf_op jit(solution)/shard_map/ppermute | solution.py:350
  45.2 0.4 collective-permute-start.18
  45.6 1.2 %collective-permute-start.19 = (bf16[128,512]{1,0:T(8,128)(2,1)S(1)}, bf16[128,512]{1,0:T(8,128)(2,1)S(1)}, u32[]{:S(2)}, u32[]{:S(2)}) collective-permute-start(bf16[128,512]{1,0:T(8,128)(2,1)S(1)} %get-tuple-element.91), channel_id=1, source_target_pairs={{0,16},{8,24},{16,0},{24,8},{1,17},{9,25},{17,1},{25,9},{2,18},{10... | collective-permute-start | bytes 393224 | tf_op jit(solution)/shard_map/ppermute | solution.py:350
  46.8 2.3 %restore.1 = bf16[4,704,128]{2,1,0:T(8,128)(2,1)} custom-call(s32[2]{0:T(128)S(1)} %pad_add_fusion.1.place, s32[8,128]{1,0:T(8,128)S(1)} %pad_add_fusion.meta_ref, bf16[800,128]{1,0:T(8,128)(2,1)S(1)} %get-tuple-element.93.refs_0_, bf16[800,128]{1,0:T(8,128)(2,1)S(1)} %collective-permute-done.13.refs_1_, ...), custom_call_target="tpu_custom_call" | custom-call | flops 99999997952 | bytes 1 | tf_op jit(solution)/shard_map/restore/pallas_call | solution.py:317
  49.1 1.1 %collective-permute-done.18.one_high = bf16[128,512]{1,0:T(8,128)(2,1)S(1)} collective-permute-done((bf16[128,512]{1,0:T(8,128)(2,1)S(1)}, bf16[128,512]{1,0:T(8,128)(2,1)S(1)}, u32[]{:S(2)}, u32[]{:S(2)}) %collective-permute-start.18) | collective-permute-done | bytes 131104 | tf_op jit(solution)/shard_map/ppermute | solution.py:350
  50.2 0.4 collective-permute-done.19.two_low
  50.6 0.8 %finish.1 = bf16[128,1024]{1,0:T(8,128)(2,1)} custom-call(f32[128,1024]{1,0:T(8,128)S(1)} %get-tuple-element.80.mine, bf16[128,512]{1,0:T(8,128)(2,1)S(1)} %collective-permute-done.15.one_low, bf16[128,512]{1,0:T(8,128)(2,1)S(1)} %collective-permute-done.18.one_high, bf16[128,512]{1,0:T(8,128)(2,1)S(1)} %collective-permute-done.19.two_low, ...), custom_call_target="tpu_custom_call" | custom-call | flops 1 | bytes 1 | tf_op jit(solution)/shard_map/finish/pallas_call | solution.py:317
  (24 shorter events, 0.2 us)
Async XLA Ops:
  0.6 1.0 %copy-start.2 = (bf16[128,1024]{1,0:T(8,128)(2,1)S(1)}, bf16[128,1024]{1,0:T(8,128)(2,1)}, u32[]{:S(2)}) copy-start(bf16[128,1024]{1,0:T(8,128)(2,1)} %dy_ref.1) | copy-start | bytes 786436
  0.6 5.6 %copy-start.1 = (bf16[128,4,704]{0,2,1:T(8,128)(2,1)S(1)}, bf16[128,4,704]{0,2,1:T(8,128)(2,1)}, u32[]{:S(2)}) copy-start(bf16[128,4,704]{0,2,1:T(8,128)(2,1)} %param.9) | copy-start | bytes 2162692
  0.7 0.8 %copy-start.3 = (s32[128,4]{0,1:T(4,128)S(1)}, s32[128,4]{0,1:T(4,128)}, u32[]{:S(2)}) copy-start(s32[128,4]{0,1:T(4,128)} %param.10) | copy-start | bytes 6148
  1.4 4.8 %copy-start.4 = (s32[128,4]{0,1:T(4,128)S(1)}, s32[128,4]{0,1:T(4,128)}, u32[]{:S(2)}) copy-start(s32[128,4]{0,1:T(4,128)} %param.10) | copy-start | bytes 6148
  1.4 4.8 %copy-start.5 = (s32[128,4]{0,1:T(4,128)S(1)}, s32[128,4]{0,1:T(4,128)}, u32[]{:S(2)}) copy-start(s32[128,4]{0,1:T(4,128)} %param.11) | copy-start | bytes 6148
  1.6 9.4 %collective-permute-start.6 = (bf16[1032,128]{1,0:T(8,128)(2,1)S(1)}, bf16[1032,128]{1,0:T(8,128)(2,1)S(1)}, u32[]{:S(2)}, u32[]{:S(2)}) collective-permute-start(bf16[1032,128]{1,0:T(8,128)(2,1)S(1)} %pack.1.refs_0_), channel_id=1, source_target_pairs={{0,16},{8,24},{16,0},{24,8},{1,17},{9,25},{17,1},{25,9},{2,18},{10... | collective-permute-start | bytes 792584 | tf_op jit(solution)/shard_map/ppermute | solution.py:350
  4.7 7.8 %collective-permute-start.5 = (bf16[1032,128]{1,0:T(8,128)(2,1)S(1)}, bf16[1032,128]{1,0:T(8,128)(2,1)S(1)}, u32[]{:S(2)}, u32[]{:S(2)}) collective-permute-start(bf16[1032,128]{1,0:T(8,128)(2,1)S(1)} %pack.1.refs_0_), channel_id=1, source_target_pairs={{0,8},{8,0},{16,24},{24,16},{1,9},{9,1},{17,25},{25,17},{2,10},{10... | collective-permute-start | bytes 792584 | tf_op jit(solution)/shard_map/ppermute | solution.py:350
  7.9 1.7 %collective-permute-start = (bf16[1032,128]{1,0:T(8,128)(2,1)S(1)}, bf16[1032,128]{1,0:T(8,128)(2,1)}, u32[]{:S(2)}, u32[]{:S(2)}) collective-permute-start(bf16[1032,128]{1,0:T(8,128)(2,1)S(1)} %param.1), channel_id=1, source_target_pairs={{0,1},{1,0},{2,3},{3,2},{4,5},{5,4},{6,7},{7,6},{8,9},{9,8},{10,11... | collective-permute-start | bytes 792584 | tf_op jit(solution)/shard_map/cond/branch_1_fun/ppermute | solution.py:353
  12.5 6.9 %collective-permute-start.7 = (bf16[520,128]{1,0:T(8,128)(2,1)S(1)}, bf16[520,128]{1,0:T(8,128)(2,1)S(1)}, u32[]{:S(2)}, u32[]{:S(2)}) collective-permute-start(bf16[520,128]{1,0:T(8,128)(2,1)S(1)} %get-tuple-element.68), channel_id=1, source_target_pairs={{0,16},{8,24},{16,0},{24,8},{1,17},{9,25},{17,1},{25,9},{2,18},{10... | collective-permute-start | bytes 399368 | tf_op jit(solution)/shard_map/ppermute | solution.py:350
  12.9 6.4 %collective-permute-start.8 = (bf16[512,128]{1,0:T(8,128)(2,1)S(1)}, bf16[512,128]{1,0:T(8,128)(2,1)S(1)}, u32[]{:S(2)}, u32[]{:S(2)}) collective-permute-start(bf16[512,128]{1,0:T(8,128)(2,1)S(1)} %get-tuple-element.69), channel_id=1, source_target_pairs={{0,8},{8,0},{16,24},{24,16},{1,9},{9,1},{17,25},{25,17},{2,10},{10... | collective-permute-start | bytes 393224 | tf_op jit(solution)/shard_map/ppermute | solution.py:350
  14.6 16.8 %collective-permute-start.9 = (bf16[816,128]{1,0:T(8,128)(2,1)S(1)}, bf16[816,128]{1,0:T(8,128)(2,1)S(1)}, u32[]{:S(2)}, u32[]{:S(2)}) collective-permute-start(bf16[816,128]{1,0:T(8,128)(2,1)S(1)} %get-tuple-element.77), channel_id=1, source_target_pairs={{0,8},{8,0},{16,24},{24,16},{1,9},{9,1},{17,25},{25,17},{2,10},{10... | collective-permute-start | bytes 626696 | tf_op jit(solution)/shard_map/ppermute | solution.py:350
  14.9 16.8 %collective-permute-start.10 = (bf16[816,128]{1,0:T(8,128)(2,1)S(1)}, bf16[816,128]{1,0:T(8,128)(2,1)S(1)}, u32[]{:S(2)}, u32[]{:S(2)}) collective-permute-start(bf16[816,128]{1,0:T(8,128)(2,1)S(1)} %get-tuple-element.78), channel_id=1, source_target_pairs={{0,16},{8,24},{16,0},{24,8},{1,17},{9,25},{17,1},{25,9},{2,18},{10... | collective-permute-start | bytes 626696 | tf_op jit(solution)/shard_map/ppermute | solution.py:350
  16.6 15.1 %collective-permute-start.11 = (bf16[816,128]{1,0:T(8,128)(2,1)S(1)}, bf16[816,128]{1,0:T(8,128)(2,1)S(1)}, u32[]{:S(2)}, u32[]{:S(2)}) collective-permute-start(bf16[816,128]{1,0:T(8,128)(2,1)S(1)} %get-tuple-element.79), channel_id=1, source_target_pairs={{0,24},{8,16},{16,8},{24,0},{1,25},{9,17},{17,9},{25,1},{2,26},{10... | collective-permute-start | bytes 626696 | tf_op jit(solution)/shard_map/ppermute | solution.py:350
  19.4 1.7 %collective-permute-start.1 = (bf16[1032,128]{1,0:T(8,128)(2,1)S(1)}, bf16[1032,128]{1,0:T(8,128)(2,1)}, u32[]{:S(2)}, u32[]{:S(2)}) collective-permute-start(bf16[1032,128]{1,0:T(8,128)(2,1)S(1)} %get-tuple-element.23), channel_id=1, source_target_pairs={{0,1},{1,0},{2,3},{3,2},{4,5},{5,4},{6,7},{7,6},{8,9},{9,8},{10,11... | collective-permute-start | bytes 792584 | tf_op jit(solution)/shard_map/cond/branch_1_fun/ppermute | solution.py:353
  19.4 2.0 %collective-permute-start.2 = (bf16[1032,128]{1,0:T(8,128)(2,1)S(1)}, bf16[1032,128]{1,0:T(8,128)(2,1)}, u32[]{:S(2)}, u32[]{:S(2)}) collective-permute-start(bf16[1032,128]{1,0:T(8,128)(2,1)S(1)} %get-tuple-element.24), channel_id=1, source_target_pairs={{0,1},{1,0},{2,3},{3,2},{4,5},{5,4},{6,7},{7,6},{8,9},{9,8},{10,11... | collective-permute-start | bytes 792584 | tf_op jit(solution)/shard_map/cond/branch_1_fun/ppermute | solution.py:353
  21.4 1.7 %collective-permute-start.3 = (bf16[520,128]{1,0:T(8,128)(2,1)S(1)}, bf16[520,128]{1,0:T(8,128)(2,1)}, u32[]{:S(2)}, u32[]{:S(2)}) collective-permute-start(bf16[520,128]{1,0:T(8,128)(2,1)S(1)} %get-tuple-element.27), channel_id=1, source_target_pairs={{0,1},{1,0},{2,3},{3,2},{4,5},{5,4},{6,7},{7,6},{8,9},{9,8},{10,11... | collective-permute-start | bytes 399368 | tf_op jit(solution)/shard_map/cond/branch_1_fun/ppermute | solution.py:353
  21.5 1.5 %collective-permute-start.4 = (bf16[512,128]{1,0:T(8,128)(2,1)S(1)}, bf16[512,128]{1,0:T(8,128)(2,1)}, u32[]{:S(2)}, u32[]{:S(2)}) collective-permute-start(bf16[512,128]{1,0:T(8,128)(2,1)S(1)} %get-tuple-element.28), channel_id=1, source_target_pairs={{0,1},{1,0},{2,3},{3,2},{4,5},{5,4},{6,7},{7,6},{8,9},{9,8},{10,11... | collective-permute-start | bytes 393224 | tf_op jit(solution)/shard_map/cond/branch_1_fun/ppermute | solution.py:353
  23.1 3.0 %copy-start = (bf16[2,704,2048]{2,1,0:T(8,128)(2,1)S(1)}, bf16[2,704,2048]{2,1,0:T(8,128)(2,1)}, u32[]{:S(2)}) copy-start(bf16[2,704,2048]{2,1,0:T(8,128)(2,1)} %refs_4_.3) | copy-start | bytes 17301508
  28.2 12.1 %collective-permute-start.13 = (bf16[800,128]{1,0:T(8,128)(2,1)S(1)}, bf16[800,128]{1,0:T(8,128)(2,1)S(1)}, u32[]{:S(2)}, u32[]{:S(2)}) collective-permute-start(bf16[800,128]{1,0:T(8,128)(2,1)S(1)} %get-tuple-element.83), channel_id=1, source_target_pairs={{0,8},{8,0},{16,24},{24,16},{1,9},{9,1},{17,25},{25,17},{2,10},{10... | collective-permute-start | bytes 614408 | tf_op jit(solution)/shard_map/ppermute | solution.py:350
  29.9 11.4 %collective-permute-start.14 = (bf16[800,128]{1,0:T(8,128)(2,1)S(1)}, bf16[800,128]{1,0:T(8,128)(2,1)S(1)}, u32[]{:S(2)}, u32[]{:S(2)}) collective-permute-start(bf16[800,128]{1,0:T(8,128)(2,1)S(1)} %get-tuple-element.84), channel_id=1, source_target_pairs={{0,16},{8,24},{16,0},{24,8},{1,17},{9,25},{17,1},{25,9},{2,18},{10... | collective-permute-start | bytes 614408 | tf_op jit(solution)/shard_map/ppermute | solution.py:350
  31.4 15.4 %collective-permute-start.21 = (bf16[800,128]{1,0:T(8,128)(2,1)S(1)}, bf16[800,128]{1,0:T(8,128)(2,1)S(1)}, u32[]{:S(2)}, u32[]{:S(2)}) collective-permute-start(bf16[800,128]{1,0:T(8,128)(2,1)S(1)} %get-tuple-element.96), channel_id=1, source_target_pairs={{0,24},{8,16},{16,8},{24,0},{1,25},{9,17},{17,9},{25,1},{2,26},{10... | collective-permute-start | bytes 614408 | tf_op jit(solution)/shard_map/ppermute | solution.py:350
  34.0 2.7 %collective-permute-start.12 = (bf16[512,1024]{1,0:T(8,128)(2,1)S(1)}, bf16[512,1024]{1,0:T(8,128)(2,1)S(1)}, u32[]{:S(2)}, u32[]{:S(2)}) collective-permute-start(bf16[512,1024]{1,0:T(8,128)(2,1)S(1)} %mix_sibling.1), channel_id=1, source_target_pairs={{0,1},{1,0},{2,3},{3,2},{4,5},{5,4},{6,7},{7,6},{8,9},{9,8},{10,11... | collective-permute-start | bytes 3145736 | tf_op jit(solution)/shard_map/ppermute | solution.py:353
  37.0 6.4 %collective-permute-start.16 = (bf16[128,512]{1,0:T(8,128)(2,1)S(1)}, bf16[128,512]{1,0:T(8,128)(2,1)S(1)}, u32[]{:S(2)}, u32[]{:S(2)}) collective-permute-start(bf16[128,512]{1,0:T(8,128)(2,1)S(1)} %get-tuple-element.88), channel_id=1, source_target_pairs={{0,8},{8,0},{16,24},{24,16},{1,9},{9,1},{17,25},{25,17},{2,10},{10... | collective-permute-start | bytes 393224 | tf_op jit(solution)/shard_map/ppermute | solution.py:350
  38.7 6.4 %collective-permute-start.17 = (bf16[128,512]{1,0:T(8,128)(2,1)S(1)}, bf16[128,512]{1,0:T(8,128)(2,1)S(1)}, u32[]{:S(2)}, u32[]{:S(2)}) collective-permute-start(bf16[128,512]{1,0:T(8,128)(2,1)S(1)} %get-tuple-element.89), channel_id=1, source_target_pairs={{0,16},{8,24},{16,0},{24,8},{1,17},{9,25},{17,1},{25,9},{2,18},{10... | collective-permute-start | bytes 393224 | tf_op jit(solution)/shard_map/ppermute | solution.py:350
  41.3 7.8 %collective-permute-start.15 = (bf16[128,512]{1,0:T(8,128)(2,1)S(1)}, bf16[128,512]{1,0:T(8,128)(2,1)S(1)}, u32[]{:S(2)}, u32[]{:S(2)}) collective-permute-start(bf16[128,512]{1,0:T(8,128)(2,1)S(1)} %get-tuple-element.85), channel_id=1, source_target_pairs={{0,8},{8,0},{16,24},{24,16},{1,9},{9,1},{17,25},{25,17},{2,10},{10... | collective-permute-start | bytes 393224 | tf_op jit(solution)/shard_map/ppermute | solution.py:350
  41.3 7.8 %collective-permute-start.20 = (bf16[128,512]{1,0:T(8,128)(2,1)S(1)}, bf16[128,512]{1,0:T(8,128)(2,1)S(1)}, u32[]{:S(2)}, u32[]{:S(2)}) collective-permute-start(bf16[128,512]{1,0:T(8,128)(2,1)S(1)} %get-tuple-element.92), channel_id=1, source_target_pairs={{0,16},{8,24},{16,0},{24,8},{1,17},{9,25},{17,1},{25,9},{2,18},{10... | collective-permute-start | bytes 393224 | tf_op jit(solution)/shard_map/ppermute | solution.py:350
  45.2 5.0 %collective-permute-start.18 = (bf16[128,512]{1,0:T(8,128)(2,1)S(1)}, bf16[128,512]{1,0:T(8,128)(2,1)S(1)}, u32[]{:S(2)}, u32[]{:S(2)}) collective-permute-start(bf16[128,512]{1,0:T(8,128)(2,1)S(1)} %get-tuple-element.90), channel_id=1, source_target_pairs={{0,8},{8,0},{16,24},{24,16},{1,9},{9,1},{17,25},{25,17},{2,10},{10... | collective-permute-start | bytes 393224 | tf_op jit(solution)/shard_map/ppermute | solution.py:350
  45.6 5.0 %collective-permute-start.19 = (bf16[128,512]{1,0:T(8,128)(2,1)S(1)}, bf16[128,512]{1,0:T(8,128)(2,1)S(1)}, u32[]{:S(2)}, u32[]{:S(2)}) collective-permute-start(bf16[128,512]{1,0:T(8,128)(2,1)S(1)} %get-tuple-element.91), channel_id=1, source_target_pairs={{0,16},{8,24},{16,0},{24,8},{1,17},{9,25},{17,1},{25,9},{2,18},{10... | collective-permute-start | bytes 393224 | tf_op jit(solution)/shard_map/ppermute | solution.py:350

commit v13 on v11

--- a/solution.py
+++ b/solution.py
@@ -174,20 +174,23 @@
             x_ref[l, :, c : c + chunk] = x.astype(BF16)
 
 
-def gather_kernel(dims, top, tokens, place, *refs):
+def gather_kernel(dims, top, tokens, count, place, *refs):
     experts, local, cap, width = dims
     n = experts // local
-    own, other, x_ref = refs[:n], refs[n:-1], refs[-1]
+    names, own, other, x_ref = refs[:count], refs[count : count + n], refs[count + n : -1], refs[-1]
     half = x_ref.shape[2] // 2
     chunk = min(half, 512)
     held = []
-    for ref in own:
-        ids = ref[half // 128 * tokens :, :].astype(F32).astype(jnp.int32)[:top]
+    for s, ref in enumerate(own):
+        ids = names[s][...] if s < count else ref[half // 128 * tokens :, :]
+        ids = ids.astype(F32).astype(jnp.int32)[:top]
         held.append(
             jnp.concatenate(slots_by_lane(ids, place[0], local, cap, width), axis=0)
         )
 
     def features(ref, start):
+        if ref.shape[1] == half:
+            return ref[:, start : start + chunk]
         blocks = range(start // 128, (start + chunk) // 128)
         return jnp.concatenate([ref[c * tokens : (c + 1) * tokens, :] for c in blocks], axis=1)
 
@@ -344,7 +347,9 @@
         pack_kernel, [shaped((half // 128 * tokens + 8, 128))], [grad_out, names], name="pack"
     )
     forward = n == 4
-    own = [send(packed, s) for s in range(n)]
+    count = 3 if forward else n
+    own = [send(grad_out if s < count else packed, s) for s in range(n)]
+    ids = [send(names, s) for s in range(count)]
     hid_sent = run(
         functools.partial(dispatch_kernel, dims), [shaped((packed_rows(width, ff)[0] + 16, 128))] * n,
         [place, meta, hid_t], where=placed, name="dispatch",
@@ -355,21 +360,25 @@
     def swaps(xs):
         return [swap(x) for x in xs]
 
-    def swaps_in_turn(xs):
-        first = swap(xs[0])
-        second, first = lax.optimization_barrier((xs[1], first))
-        return [first, swap(second)]
+    def swaps_by_two(xs):
+        first = swaps(xs[:2])
+        *rest, first[0], first[1] = lax.optimization_barrier((*xs[2:], *first))
+        return first + swaps(rest)
 
     if forward:
         always = place[0] < 1000
-        last, mine = lax.cond(always, swaps_in_turn, list, [own[3], own[0]])
-        *own[1:3], last = lax.optimization_barrier((*own[1:3], last))
-        other = [mine] + lax.cond(always, swaps, list, own[1:3]) + [last]
+        *own[1:3], ids[1], ids[2], hid[0] = lax.optimization_barrier(
+            (*own[1:3], ids[1], ids[2], hid[0])
+        )
+        one, two, mine = lax.cond(always, swaps_by_two, list, [own[1], own[2], grad_out])
+        own[3], mine = lax.optimization_barrier((own[3], mine))
+        other = [mine, one, two] + lax.cond(always, swaps, list, own[3:])
     else:
         other = swaps(own)
     (x,) = run(
-        functools.partial(gather_kernel, dims, top, tokens), [shaped((local, n * cap, full))],
-        [place, *own, *other], where=placed, name="gather", weight=20 * 10**8,
+        functools.partial(gather_kernel, dims, top, tokens, count),
+        [shaped((local, n * cap, full))],
+        [place, *ids, *own, *other], where=placed, name="gather", weight=20 * 10**8,
     )
     grad_sent = run(
         functools.partial(grad_kernel, dims), [slot] * n, [x, w_down], name="grad"

time: 49.5 us -> 55.6 us (1.12)
  waiting for transfers between devices: 13.8 us -> 17.1 us
  starting transfers between devices: 19.1 us -> 21.2 us
  local copies, waits for them, and re-layouts: 1.64 us -> 2.35 us
    ppermute x15 -> x17, waiting for transfers between devices: 8.77 us -> 12 us  [send(): return lax.ppermute(x, 'ctx', [(i, i ^ s) for i in range(n)]) if s else x]
    ppermute x15 -> x17, starting transfers between devices: 18.4 us -> 20.5 us  [send(): return lax.ppermute(x, 'ctx', [(i, i ^ s) for i in range(n)]) if s else x]
    unnamed x12, local copies, waits for them, and re-layouts: 1.64 us -> 2.35 us
  transfers between devices with their start and end apart: 20 -> 22, of which waited for: 11 -> 10; matrix products, arithmetic and copies ran while one was open for 0% -> 0% of each run, Pallas kernels for 27% -> 24%
where the time goes in v13:
time: 55.6 us; the launch traced here: 55.4 us
  starting transfers between devices  21.2 us (38%)
  waiting for transfers between devices  17.1 us (31%)
  Pallas kernels  13.9 us (25%)
  local copies, waits for them, and re-layouts  2.35 us (4%)
  between operations  0.72 us (1%)
    ppermute x17, starting transfers between devices, send(): return lax.ppermute(x, 'ctx', [(i, i ^ s) for i in range(n)]) if s else x  20.5 us
    pallas_call x11, Pallas kernels, call(): pl.pallas_call(kernel, out_shape=outs, in_specs=[pl.BlockSpec(memory_spac...  13.9 us
    ppermute x17, waiting for transfers between devices, send(): return lax.ppermute(x, 'ctx', [(i, i ^ s) for i in range(n)]) if s else x  12 us
    ppermute x5, waiting for transfers between devices, swap(): return lax.ppermute(x, 'tp', [(0, 1), (1, 0)])  5.07 us
    unnamed x12, local copies, waits for them, and re-layouts  2.35 us
  transfers between devices with their start and end apart: 22, of which 10 were waited for; matrix products, arithmetic and copies ran while one was open for 0% of the time, Pallas kernels for 24%

profile of v13, /device:TPU:0, one launch (start us, length us, event | category | flops | bytes accessed | tf_op | source)
XLA Modules:
  0.0 55.4 jit_solution(6553302066898772816)
XLA Ops:
  0.6 3.0 %collective-permute-start.5 = (bf16[128,1024]{1,0:T(8,128)(2,1)}, bf16[128,1024]{1,0:T(8,128)(2,1)S(1)}, u32[]{:S(2)}, u32[]{:S(2)}) collective-permute-start(bf16[128,1024]{1,0:T(8,128)(2,1)} %refs_3_.1), channel_id=1, source_target_pairs={{0,16},{8,24},{16,0},{24,8},{1,17},{9,25},{17,1},{25,9},{2,18},{10... | collective-permute-start | bytes 786440 | tf_op jit(solution)/shard_map/ppermute | solution.py:336
  3.7 1.5 %collective-permute-start.4 = (bf16[128,1024]{1,0:T(8,128)(2,1)}, bf16[128,1024]{1,0:T(8,128)(2,1)S(1)}, u32[]{:S(2)}, u32[]{:S(2)}) collective-permute-start(bf16[128,1024]{1,0:T(8,128)(2,1)} %refs_3_.1), channel_id=1, source_target_pairs={{0,8},{8,0},{16,24},{24,16},{1,9},{9,1},{17,25},{25,17},{2,10},{10... | collective-permute-start | bytes 786440 | tf_op jit(solution)/shard_map/ppermute | solution.py:336
  5.2 0.7 %copy-done.2 = s32[128,4]{0,1:T(4,128)S(1)} copy-done((s32[128,4]{0,1:T(4,128)S(1)}, s32[128,4]{0,1:T(4,128)}, u32[]{:S(2)}) %copy-start.2) | copy-done | bytes 2072
  5.9 0.9 %copy-done.4 = bf16[128,1024]{1,0:T(8,128)(2,1)S(1)} copy-done((bf16[128,1024]{1,0:T(8,128)(2,1)S(1)}, bf16[128,1024]{1,0:T(8,128)(2,1)}, u32[]{:S(2)}) %copy-start.4) | copy-done | bytes 262168
  6.8 0.1 collective-permute-start.8
  7.0 1.9 %collective-permute-start.7 = (bf16[8,128]{1,0:T(8,128)(2,1)S(1)}, bf16[8,128]{1,0:T(8,128)(2,1)S(1)}, u32[]{:S(2)}, u32[]{:S(2)}) collective-permute-start(bf16[8,128]{1,0:T(8,128)(2,1)S(1)} %names.1.names_ref.refs_0_), channel_id=1, source_target_pairs={{0,16},{8,24},{16,0},{24,8},{1,17},{9,25},{17,1},{25,9},{2,18},{10... | collective-permute-start | bytes 6152 | tf_op jit(solution)/shard_map/ppermute | solution.py:336
  8.9 1.5 %collective-permute-start.6 = (bf16[8,128]{1,0:T(8,128)(2,1)S(1)}, bf16[8,128]{1,0:T(8,128)(2,1)S(1)}, u32[]{:S(2)}, u32[]{:S(2)}) collective-permute-start(bf16[8,128]{1,0:T(8,128)(2,1)S(1)} %names.1.names_ref.refs_0_), channel_id=1, source_target_pairs={{0,8},{8,0},{16,24},{24,16},{1,9},{9,1},{17,25},{25,17},{2,10},{10... | collective-permute-start | bytes 6152 | tf_op jit(solution)/shard_map/ppermute | solution.py:336
  10.4 0.1 pad_add_fusion.1.place
  10.5 1.6 %dispatch.1 = (bf16[816,128]{1,0:T(8,128)(2,1)S(1)}, bf16[816,128]{1,0:T(8,128)(2,1)S(1)}, bf16[816,128]{1,0:T(8,128)(2,1)S(1)}, bf16[816,128]{1,0:T(8,128)(2,1)S(1)}) custom-call(s32[2]{0:T(128)S(1)} %pad_add_fusion.1.place, s32[8,128]{1,0:T(8,128)S(1)} %pad_add_fusion.meta_ref, bf16[4,704,128]{2,1,0:T(8,128)(2,1)S(1)} %bitcast.6), custom_call_target="tpu_custom_call" | custom-call | flops 1 | bytes 1 | tf_op jit(solution)/shard_map/dispatch/pallas_call | solution.py:303
  12.1 0.6 %collective-permute-start.9 = (bf16[816,128]{1,0:T(8,128)(2,1)S(1)}, bf16[816,128]{1,0:T(8,128)(2,1)S(1)}, u32[]{:S(2)}, u32[]{:S(2)}) collective-permute-start(bf16[816,128]{1,0:T(8,128)(2,1)S(1)} %get-tuple-element.71), channel_id=1, source_target_pairs={{0,8},{8,0},{16,24},{24,16},{1,9},{9,1},{17,25},{25,17},{2,10},{10... | collective-permute-start | bytes 626696 | tf_op jit(solution)/shard_map/ppermute | solution.py:336
  12.7 6.1 %collective-permute-done.6.refs_1_ = bf16[8,128]{1,0:T(8,128)(2,1)S(1)} collective-permute-done((bf16[8,128]{1,0:T(8,128)(2,1)S(1)}, bf16[8,128]{1,0:T(8,128)(2,1)S(1)}, u32[]{:S(2)}, u32[]{:S(2)}) %collective-permute-start.6) | collective-permute-done | bytes 2080 | tf_op jit(solution)/shard_map/ppermute | solution.py:336
  18.8 0.0 collective-permute-start.10
  18.9 3.8 %conditional.2 = (bf16[128,1024]{1,0:T(8,128)(2,1)}, bf16[128,1024]{1,0:T(8,128)(2,1)}, bf16[128,1024]{1,0:T(8,128)(2,1)}) conditional(s32[]{:T(128)} %convert_element_type.4, (bf16[128,1024]{1,0:T(8,128)(2,1)S(1)}, bf16[128,1024]{1,0:T(8,128)(2,1)S(1)}, bf16[128,1024]{1,0:T(8,128)(2,1)S(1)}) %tuple.36, (bf16[128,1024]{1,0:T(8,128)(2,1)S(1)}, ...), branch_computations={%region_0.0_spmd, %region_1.0_spmd} | conditional | bytes 3145872 | solution.py:373
  18.9 0.1 collective-permute-start
  18.9 0.5 collective-permute-start.1
  19.4 1.2 %collective-permute-done = bf16[128,1024]{1,0:T(8,128)(2,1)} collective-permute-done((bf16[128,1024]{1,0:T(8,128)(2,1)S(1)}, bf16[128,1024]{1,0:T(8,128)(2,1)}, u32[]{:S(2)}, u32[]{:S(2)}) %collective-permute-start) | collective-permute-done | bytes 262176 | tf_op jit(solution)/shard_map/cond/branch_1_fun/ppermute | solution.py:339
  20.6 0.4 collective-permute-done.1
  21.0 0.1 collective-permute-start.2
  21.1 1.5 %collective-permute-done.2 = bf16[128,1024]{1,0:T(8,128)(2,1)} collective-permute-done((bf16[128,1024]{1,0:T(8,128)(2,1)S(1)}, bf16[128,1024]{1,0:T(8,128)(2,1)}, u32[]{:S(2)}, u32[]{:S(2)}) %collective-permute-start.2) | collective-permute-done | bytes 262176 | tf_op jit(solution)/shard_map/cond/branch_1_fun/ppermute | solution.py:339
  22.6 2.9 %collective-permute-start.11 = (bf16[816,128]{1,0:T(8,128)(2,1)S(1)}, bf16[816,128]{1,0:T(8,128)(2,1)S(1)}, u32[]{:S(2)}, u32[]{:S(2)}) collective-permute-start(bf16[816,128]{1,0:T(8,128)(2,1)S(1)} %get-tuple-element.73), channel_id=1, source_target_pairs={{0,24},{8,16},{16,8},{24,0},{1,25},{9,17},{17,9},{25,1},{2,26},{10... | collective-permute-start | bytes 626696 | tf_op jit(solution)/shard_map/ppermute | solution.py:336
  25.5 1.7 %conditional.3 = (bf16[1032,128]{1,0:T(8,128)(2,1)}) conditional(s32[]{:T(128)} %convert_element_type.4, bf16[1032,128]{1,0:T(8,128)(2,1)S(1)} %collective-permute-done.8.refs_6_, bf16[1032,128]{1,0:T(8,128)(2,1)S(1)} %collective-permute-done.8.refs_6_), branch_computations={%region_2.0_spmd, %region_3.0_spmd} | conditional | bytes 1056816 | solution.py:375
  25.5 0.0 collective-permute-start.3
  25.5 1.7 %collective-permute-done.3 = bf16[1032,128]{1,0:T(8,128)(2,1)} collective-permute-done((bf16[1032,128]{1,0:T(8,128)(2,1)S(1)}, bf16[1032,128]{1,0:T(8,128)(2,1)}, u32[]{:S(2)}, u32[]{:S(2)}) %collective-permute-start.3) | collective-permute-done | bytes 264224 | tf_op jit(solution)/shard_map/cond/branch_1_fun/ppermute | solution.py:339
  27.2 2.2 %gather.1.x_ref = bf16[2,288,2048]{2,1,0:T(8,128)(2,1)S(1)} custom-call(s32[2]{0:T(128)S(1)} %pad_add_fusion.1.place, bf16[8,128]{1,0:T(8,128)(2,1)S(1)} %names.1.names_ref.refs_0_, bf16[8,128]{1,0:T(8,128)(2,1)S(1)} %collective-permute-done.6.refs_1_, bf16[8,128]{1,0:T(8,128)(2,1)S(1)} %collective-permute-done.7.refs_2_, bf16[128,1024]{1,0:T(8,128)(2,1)S(1)} %copy-done.4, ...), custom_call_target="tpu_custom_call" | custom-call | flops 2000000000 | bytes 1 | tf_op jit(solution)/shard_map/gather/pallas_call | solution.py:303
  29.4 0.7 %copy-done = bf16[2,704,2048]{2,1,0:T(8,128)(2,1)S(1)} copy-done((bf16[2,704,2048]{2,1,0:T(8,128)(2,1)S(1)}, bf16[2,704,2048]{2,1,0:T(8,128)(2,1)}, u32[]{:S(2)}) %copy-start) | copy-done | bytes 5767192
  30.1 2.1 %grad.1 = (bf16[800,128]{1,0:T(8,128)(2,1)S(1)}, bf16[800,128]{1,0:T(8,128)(2,1)S(1)}, bf16[800,128]{1,0:T(8,128)(2,1)S(1)}, bf16[800,128]{1,0:T(8,128)(2,1)S(1)}) custom-call(bf16[2,288,2048]{2,1,0:T(8,128)(2,1)S(1)} %gather.1.x_ref, bf16[2,704,2048]{2,1,0:T(8,128)(2,1)S(1)} %copy-done), custom_call_target="tpu_custom_call" | custom-call | flops 1 | bytes 1 | tf_op jit(solution)/shard_map/grad/pallas_call | solution.py:303
  32.2 0.6 %collective-permute-start.13 = (bf16[800,128]{1,0:T(8,128)(2,1)S(1)}, bf16[800,128]{1,0:T(8,128)(2,1)S(1)}, u32[]{:S(2)}, u32[]{:S(2)}) collective-permute-start(bf16[800,128]{1,0:T(8,128)(2,1)S(1)} %get-tuple-element.77), channel_id=1, source_target_pairs={{0,8},{8,0},{16,24},{24,16},{1,9},{9,1},{17,25},{25,17},{2,10},{10... | collective-permute-start | bytes 614408 | tf_op jit(solution)/shard_map/ppermute | solution.py:336
  32.8 0.1 collective-permute-start.14
  32.9 2.9 %collective-permute-start.21 = (bf16[800,128]{1,0:T(8,128)(2,1)S(1)}, bf16[800,128]{1,0:T(8,128)(2,1)S(1)}, u32[]{:S(2)}, u32[]{:S(2)}) collective-permute-start(bf16[800,128]{1,0:T(8,128)(2,1)S(1)} %get-tuple-element.90), channel_id=1, source_target_pairs={{0,24},{8,16},{16,8},{24,0},{1,25},{9,17},{17,9},{25,1},{2,26},{10... | collective-permute-start | bytes 614408 | tf_op jit(solution)/shard_map/ppermute | solution.py:336
  35.8 0.0 collective-permute-done.10.refs_2_
  35.8 0.0 collective-permute-done.11.refs_3_
  35.8 2.3 %mix_sibling.1 = bf16[512,1024]{1,0:T(8,128)(2,1)S(1)} custom-call(s32[2]{0:T(128)S(1)} %pad_add_fusion.1.place, bf16[816,128]{1,0:T(8,128)(2,1)S(1)} %get-tuple-element.70.refs_0_, bf16[816,128]{1,0:T(8,128)(2,1)S(1)} %collective-permute-done.9.refs_1_, bf16[816,128]{1,0:T(8,128)(2,1)S(1)} %collective-permute-done.10.refs_2_, ...), custom_call_target="tpu_custom_call" | custom-call | flops 1 | bytes 1 | tf_op jit(solution)/shard_map/mix_sibling/pallas_call | solution.py:303
  38.1 0.1 collective-permute-start.12
  38.2 2.3 %mix_own.1.own = f32[512,1024]{1,0:T(8,128)S(1)} custom-call(s32[2]{0:T(128)S(1)} %pad_add_fusion.1.place, bf16[816,128]{1,0:T(8,128)(2,1)S(1)} %get-tuple-element.70.refs_0_, bf16[816,128]{1,0:T(8,128)(2,1)S(1)} %collective-permute-done.9.refs_1_, bf16[816,128]{1,0:T(8,128)(2,1)S(1)} %collective-permute-done.10.refs_2_, ...), custom_call_target="tpu_custom_call" | custom-call | flops 99999997952 | bytes 1 | tf_op jit(solution)/shard_map/mix_own/pallas_call | solution.py:303
  40.5 0.3 collective-permute-done.12.arrived
  40.8 0.2 add.5
  41.1 0.6 %collective-permute-start.16 = (bf16[128,512]{1,0:T(8,128)(2,1)S(1)}, bf16[128,512]{1,0:T(8,128)(2,1)S(1)}, u32[]{:S(2)}, u32[]{:S(2)}) collective-permute-start(bf16[128,512]{1,0:T(8,128)(2,1)S(1)} %get-tuple-element.82), channel_id=1, source_target_pairs={{0,8},{8,0},{16,24},{24,16},{1,9},{9,1},{17,25},{25,17},{2,10},{10... | collective-permute-start | bytes 393224 | tf_op jit(solution)/shard_map/ppermute | solution.py:336
  41.7 0.1 collective-permute-start.17
  41.7 2.3 %collective-permute-done.14.refs_2_ = bf16[800,128]{1,0:T(8,128)(2,1)S(1)} collective-permute-done((bf16[800,128]{1,0:T(8,128)(2,1)S(1)}, bf16[800,128]{1,0:T(8,128)(2,1)S(1)}, u32[]{:S(2)}, u32[]{:S(2)}) %collective-permute-start.14) | collective-permute-done | bytes 204832 | tf_op jit(solution)/shard_map/ppermute | solution.py:336
  44.0 1.5 %collective-permute-start.15 = (bf16[128,512]{1,0:T(8,128)(2,1)S(1)}, bf16[128,512]{1,0:T(8,128)(2,1)S(1)}, u32[]{:S(2)}, u32[]{:S(2)}) collective-permute-start(bf16[128,512]{1,0:T(8,128)(2,1)S(1)} %get-tuple-element.79), channel_id=1, source_target_pairs={{0,8},{8,0},{16,24},{24,16},{1,9},{9,1},{17,25},{25,17},{2,10},{10... | collective-permute-start | bytes 393224 | tf_op jit(solution)/shard_map/ppermute | solution.py:336
  45.5 0.5 collective-permute-start.20
  46.0 1.4 %collective-permute-done.16.low = bf16[128,512]{1,0:T(8,128)(2,1)S(1)} collective-permute-done((bf16[128,512]{1,0:T(8,128)(2,1)S(1)}, bf16[128,512]{1,0:T(8,128)(2,1)S(1)}, u32[]{:S(2)}, u32[]{:S(2)}) %collective-permute-start.16) | collective-permute-done | bytes 131104 | tf_op jit(solution)/shard_map/ppermute | solution.py:336
  47.5 2.1 %collective-permute-start.18 = (bf16[128,512]{1,0:T(8,128)(2,1)S(1)}, bf16[128,512]{1,0:T(8,128)(2,1)S(1)}, u32[]{:S(2)}, u32[]{:S(2)}) collective-permute-start(bf16[128,512]{1,0:T(8,128)(2,1)S(1)} %get-tuple-element.84), channel_id=1, source_target_pairs={{0,8},{8,0},{16,24},{24,16},{1,9},{9,1},{17,25},{25,17},{2,10},{10... | collective-permute-start | bytes 393224 | tf_op jit(solution)/shard_map/ppermute | solution.py:336
  49.6 0.5 collective-permute-start.19
  50.2 2.3 %restore.1 = bf16[4,704,128]{2,1,0:T(8,128)(2,1)} custom-call(s32[2]{0:T(128)S(1)} %pad_add_fusion.1.place, s32[8,128]{1,0:T(8,128)S(1)} %pad_add_fusion.meta_ref, bf16[800,128]{1,0:T(8,128)(2,1)S(1)} %get-tuple-element.87.refs_0_, bf16[800,128]{1,0:T(8,128)(2,1)S(1)} %collective-permute-done.13.refs_1_, ...), custom_call_target="tpu_custom_call" | custom-call | flops 99999997952 | bytes 1 | tf_op jit(solution)/shard_map/restore/pallas_call | solution.py:303
  52.5 0.1 collective-permute-done.18.one_high
  52.6 2.0 %collective-permute-done.19.two_low = bf16[128,512]{1,0:T(8,128)(2,1)S(1)} collective-permute-done((bf16[128,512]{1,0:T(8,128)(2,1)S(1)}, bf16[128,512]{1,0:T(8,128)(2,1)S(1)}, u32[]{:S(2)}, u32[]{:S(2)}) %collective-permute-start.19) | collective-permute-done | bytes 131104 | tf_op jit(solution)/shard_map/ppermute | solution.py:336
  54.6 0.8 %finish.1 = bf16[128,1024]{1,0:T(8,128)(2,1)} custom-call(f32[128,1024]{1,0:T(8,128)S(1)} %get-tuple-element.74.mine, bf16[128,512]{1,0:T(8,128)(2,1)S(1)} %collective-permute-done.15.one_low, bf16[128,512]{1,0:T(8,128)(2,1)S(1)} %collective-permute-done.18.one_high, bf16[128,512]{1,0:T(8,128)(2,1)S(1)} %collective-permute-done.19.two_low, ...), custom_call_target="tpu_custom_call" | custom-call | flops 1 | bytes 1 | tf_op jit(solution)/shard_map/finish/pallas_call | solution.py:303
  (23 shorter events, 0.1 us)
Async XLA Ops:
  0.6 9.9 %copy-start.1 = (bf16[128,4,704]{0,2,1:T(8,128)(2,1)S(1)}, bf16[128,4,704]{0,2,1:T(8,128)(2,1)}, u32[]{:S(2)}) copy-start(bf16[128,4,704]{0,2,1:T(8,128)(2,1)} %param.9) | copy-start | bytes 2162692
  0.6 18.2 %collective-permute-start.5 = (bf16[128,1024]{1,0:T(8,128)(2,1)}, bf16[128,1024]{1,0:T(8,128)(2,1)S(1)}, u32[]{:S(2)}, u32[]{:S(2)}) collective-permute-start(bf16[128,1024]{1,0:T(8,128)(2,1)} %refs_3_.1), channel_id=1, source_target_pairs={{0,16},{8,24},{16,0},{24,8},{1,17},{9,25},{17,1},{25,9},{2,18},{10... | collective-permute-start | bytes 786440 | tf_op jit(solution)/shard_map/ppermute | solution.py:336
  3.7 15.2 %collective-permute-start.4 = (bf16[128,1024]{1,0:T(8,128)(2,1)}, bf16[128,1024]{1,0:T(8,128)(2,1)S(1)}, u32[]{:S(2)}, u32[]{:S(2)}) collective-permute-start(bf16[128,1024]{1,0:T(8,128)(2,1)} %refs_3_.1), channel_id=1, source_target_pairs={{0,8},{8,0},{16,24},{24,16},{1,9},{9,1},{17,25},{25,17},{2,10},{10... | collective-permute-start | bytes 786440 | tf_op jit(solution)/shard_map/ppermute | solution.py:336
  5.2 0.7 %copy-start.2 = (s32[128,4]{0,1:T(4,128)S(1)}, s32[128,4]{0,1:T(4,128)}, u32[]{:S(2)}) copy-start(s32[128,4]{0,1:T(4,128)} %param.10) | copy-start | bytes 6148
  5.8 0.9 %copy-start.4 = (bf16[128,1024]{1,0:T(8,128)(2,1)S(1)}, bf16[128,1024]{1,0:T(8,128)(2,1)}, u32[]{:S(2)}) copy-start(bf16[128,1024]{1,0:T(8,128)(2,1)} %refs_3_.1) | copy-start | bytes 786436
  5.8 4.6 %copy-start.3 = (s32[128,4]{0,1:T(4,128)S(1)}, s32[128,4]{0,1:T(4,128)}, u32[]{:S(2)}) copy-start(s32[128,4]{0,1:T(4,128)} %param.10) | copy-start | bytes 6148
  5.9 4.6 %copy-start.5 = (s32[128,4]{0,1:T(4,128)S(1)}, s32[128,4]{0,1:T(4,128)}, u32[]{:S(2)}) copy-start(s32[128,4]{0,1:T(4,128)} %param.11) | copy-start | bytes 6148
  6.8 18.6 %collective-permute-start.8 = (bf16[1032,128]{1,0:T(8,128)(2,1)S(1)}, bf16[1032,128]{1,0:T(8,128)(2,1)S(1)}, u32[]{:S(2)}, u32[]{:S(2)}) collective-permute-start(bf16[1032,128]{1,0:T(8,128)(2,1)S(1)} %pack.1), channel_id=1, source_target_pairs={{0,24},{8,16},{16,8},{24,0},{1,25},{9,17},{17,9},{25,1},{2,26},{10... | collective-permute-start | bytes 792584 | tf_op jit(solution)/shard_map/ppermute | solution.py:336
  7.0 5.1 %collective-permute-start.7 = (bf16[8,128]{1,0:T(8,128)(2,1)S(1)}, bf16[8,128]{1,0:T(8,128)(2,1)S(1)}, u32[]{:S(2)}, u32[]{:S(2)}) collective-permute-start(bf16[8,128]{1,0:T(8,128)(2,1)S(1)} %names.1.names_ref.refs_0_), channel_id=1, source_target_pairs={{0,16},{8,24},{16,0},{24,8},{1,17},{9,25},{17,1},{25,9},{2,18},{10... | collective-permute-start | bytes 6152 | tf_op jit(solution)/shard_map/ppermute | solution.py:336
  8.9 9.9 %collective-permute-start.6 = (bf16[8,128]{1,0:T(8,128)(2,1)S(1)}, bf16[8,128]{1,0:T(8,128)(2,1)S(1)}, u32[]{:S(2)}, u32[]{:S(2)}) collective-permute-start(bf16[8,128]{1,0:T(8,128)(2,1)S(1)} %names.1.names_ref.refs_0_), channel_id=1, source_target_pairs={{0,8},{8,0},{16,24},{24,16},{1,9},{9,1},{17,25},{25,17},{2,10},{10... | collective-permute-start | bytes 6152 | tf_op jit(solution)/shard_map/ppermute | solution.py:336
  12.1 20.8 %collective-permute-start.9 = (bf16[816,128]{1,0:T(8,128)(2,1)S(1)}, bf16[816,128]{1,0:T(8,128)(2,1)S(1)}, u32[]{:S(2)}, u32[]{:S(2)}) collective-permute-start(bf16[816,128]{1,0:T(8,128)(2,1)S(1)} %get-tuple-element.71), channel_id=1, source_target_pairs={{0,8},{8,0},{16,24},{24,16},{1,9},{9,1},{17,25},{25,17},{2,10},{10... | collective-permute-start | bytes 626696 | tf_op jit(solution)/shard_map/ppermute | solution.py:336
  18.8 17.0 %collective-permute-start.10 = (bf16[816,128]{1,0:T(8,128)(2,1)S(1)}, bf16[816,128]{1,0:T(8,128)(2,1)S(1)}, u32[]{:S(2)}, u32[]{:S(2)}) collective-permute-start(bf16[816,128]{1,0:T(8,128)(2,1)S(1)} %get-tuple-element.72), channel_id=1, source_target_pairs={{0,16},{8,24},{16,0},{24,8},{1,17},{9,25},{17,1},{25,9},{2,18},{10... | collective-permute-start | bytes 626696 | tf_op jit(solution)/shard_map/ppermute | solution.py:336
  18.9 1.7 %collective-permute-start = (bf16[128,1024]{1,0:T(8,128)(2,1)S(1)}, bf16[128,1024]{1,0:T(8,128)(2,1)}, u32[]{:S(2)}, u32[]{:S(2)}) collective-permute-start(bf16[128,1024]{1,0:T(8,128)(2,1)S(1)} %get-tuple-element.18), channel_id=1, source_target_pairs={{0,1},{1,0},{2,3},{3,2},{4,5},{5,4},{6,7},{7,6},{8,9},{9,8},{10,11... | collective-permute-start | bytes 786440 | tf_op jit(solution)/shard_map/cond/branch_1_fun/ppermute | solution.py:339
  18.9 2.0 %collective-permute-start.1 = (bf16[128,1024]{1,0:T(8,128)(2,1)S(1)}, bf16[128,1024]{1,0:T(8,128)(2,1)}, u32[]{:S(2)}, u32[]{:S(2)}) collective-permute-start(bf16[128,1024]{1,0:T(8,128)(2,1)S(1)} %get-tuple-element.19), channel_id=1, source_target_pairs={{0,1},{1,0},{2,3},{3,2},{4,5},{5,4},{6,7},{7,6},{8,9},{9,8},{10,11... | collective-permute-start | bytes 786440 | tf_op jit(solution)/shard_map/cond/branch_1_fun/ppermute | solution.py:339
  21.0 1.7 %collective-permute-start.2 = (bf16[128,1024]{1,0:T(8,128)(2,1)S(1)}, bf16[128,1024]{1,0:T(8,128)(2,1)}, u32[]{:S(2)}, u32[]{:S(2)}) collective-permute-start(bf16[128,1024]{1,0:T(8,128)(2,1)S(1)} %get-tuple-element.22), channel_id=1, source_target_pairs={{0,1},{1,0},{2,3},{3,2},{4,5},{5,4},{6,7},{7,6},{8,9},{9,8},{10,11... | collective-permute-start | bytes 786440 | tf_op jit(solution)/shard_map/cond/branch_1_fun/ppermute | solution.py:339
  22.6 13.1 %collective-permute-start.11 = (bf16[816,128]{1,0:T(8,128)(2,1)S(1)}, bf16[816,128]{1,0:T(8,128)(2,1)S(1)}, u32[]{:S(2)}, u32[]{:S(2)}) collective-permute-start(bf16[816,128]{1,0:T(8,128)(2,1)S(1)} %get-tuple-element.73), channel_id=1, source_target_pairs={{0,24},{8,16},{16,8},{24,0},{1,25},{9,17},{17,9},{25,1},{2,26},{10... | collective-permute-start | bytes 626696 | tf_op jit(solution)/shard_map/ppermute | solution.py:336
  25.5 1.7 %collective-permute-start.3 = (bf16[1032,128]{1,0:T(8,128)(2,1)S(1)}, bf16[1032,128]{1,0:T(8,128)(2,1)}, u32[]{:S(2)}, u32[]{:S(2)}) collective-permute-start(bf16[1032,128]{1,0:T(8,128)(2,1)S(1)} %param.3), channel_id=1, source_target_pairs={{0,1},{1,0},{2,3},{3,2},{4,5},{5,4},{6,7},{7,6},{8,9},{9,8},{10,11... | collective-permute-start | bytes 792584 | tf_op jit(solution)/shard_map/cond/branch_1_fun/ppermute | solution.py:339
  27.2 3.0 %copy-start = (bf16[2,704,2048]{2,1,0:T(8,128)(2,1)S(1)}, bf16[2,704,2048]{2,1,0:T(8,128)(2,1)}, u32[]{:S(2)}) copy-start(bf16[2,704,2048]{2,1,0:T(8,128)(2,1)} %refs_4_.3) | copy-start | bytes 17301508
  32.2 9.5 %collective-permute-start.13 = (bf16[800,128]{1,0:T(8,128)(2,1)S(1)}, bf16[800,128]{1,0:T(8,128)(2,1)S(1)}, u32[]{:S(2)}, u32[]{:S(2)}) collective-permute-start(bf16[800,128]{1,0:T(8,128)(2,1)S(1)} %get-tuple-element.77), channel_id=1, source_target_pairs={{0,8},{8,0},{16,24},{24,16},{1,9},{9,1},{17,25},{25,17},{2,10},{10... | collective-permute-start | bytes 614408 | tf_op jit(solution)/shard_map/ppermute | solution.py:336
  32.8 11.2 %collective-permute-start.14 = (bf16[800,128]{1,0:T(8,128)(2,1)S(1)}, bf16[800,128]{1,0:T(8,128)(2,1)S(1)}, u32[]{:S(2)}, u32[]{:S(2)}) collective-permute-start(bf16[800,128]{1,0:T(8,128)(2,1)S(1)} %get-tuple-element.78), channel_id=1, source_target_pairs={{0,16},{8,24},{16,0},{24,8},{1,17},{9,25},{17,1},{25,9},{2,18},{10... | collective-permute-start | bytes 614408 | tf_op jit(solution)/shard_map/ppermute | solution.py:336
  32.9 17.2 %collective-permute-start.21 = (bf16[800,128]{1,0:T(8,128)(2,1)S(1)}, bf16[800,128]{1,0:T(8,128)(2,1)S(1)}, u32[]{:S(2)}, u32[]{:S(2)}) collective-permute-start(bf16[800,128]{1,0:T(8,128)(2,1)S(1)} %get-tuple-element.90), channel_id=1, source_target_pairs={{0,24},{8,16},{16,8},{24,0},{1,25},{9,17},{17,9},{25,1},{2,26},{10... | collective-permute-start | bytes 614408 | tf_op jit(solution)/shard_map/ppermute | solution.py:336
  38.1 2.7 %collective-permute-start.12 = (bf16[512,1024]{1,0:T(8,128)(2,1)S(1)}, bf16[512,1024]{1,0:T(8,128)(2,1)S(1)}, u32[]{:S(2)}, u32[]{:S(2)}) collective-permute-start(bf16[512,1024]{1,0:T(8,128)(2,1)S(1)} %mix_sibling.1), channel_id=1, source_target_pairs={{0,1},{1,0},{2,3},{3,2},{4,5},{5,4},{6,7},{7,6},{8,9},{9,8},{10,11... | collective-permute-start | bytes 3145736 | tf_op jit(solution)/shard_map/ppermute | solution.py:339
  41.1 6.4 %collective-permute-start.16 = (bf16[128,512]{1,0:T(8,128)(2,1)S(1)}, bf16[128,512]{1,0:T(8,128)(2,1)S(1)}, u32[]{:S(2)}, u32[]{:S(2)}) collective-permute-start(bf16[128,512]{1,0:T(8,128)(2,1)S(1)} %get-tuple-element.82), channel_id=1, source_target_pairs={{0,8},{8,0},{16,24},{24,16},{1,9},{9,1},{17,25},{25,17},{2,10},{10... | collective-permute-start | bytes 393224 | tf_op jit(solution)/shard_map/ppermute | solution.py:336
  41.7 5.8 %collective-permute-start.17 = (bf16[128,512]{1,0:T(8,128)(2,1)S(1)}, bf16[128,512]{1,0:T(8,128)(2,1)S(1)}, u32[]{:S(2)}, u32[]{:S(2)}) collective-permute-start(bf16[128,512]{1,0:T(8,128)(2,1)S(1)} %get-tuple-element.83), channel_id=1, source_target_pairs={{0,16},{8,24},{16,0},{24,8},{1,17},{9,25},{17,1},{25,9},{2,18},{10... | collective-permute-start | bytes 393224 | tf_op jit(solution)/shard_map/ppermute | solution.py:336
  44.0 8.4 %collective-permute-start.15 = (bf16[128,512]{1,0:T(8,128)(2,1)S(1)}, bf16[128,512]{1,0:T(8,128)(2,1)S(1)}, u32[]{:S(2)}, u32[]{:S(2)}) collective-permute-start(bf16[128,512]{1,0:T(8,128)(2,1)S(1)} %get-tuple-element.79), channel_id=1, source_target_pairs={{0,8},{8,0},{16,24},{24,16},{1,9},{9,1},{17,25},{25,17},{2,10},{10... | collective-permute-start | bytes 393224 | tf_op jit(solution)/shard_map/ppermute | solution.py:336
  45.5 6.9 %collective-permute-start.20 = (bf16[128,512]{1,0:T(8,128)(2,1)S(1)}, bf16[128,512]{1,0:T(8,128)(2,1)S(1)}, u32[]{:S(2)}, u32[]{:S(2)}) collective-permute-start(bf16[128,512]{1,0:T(8,128)(2,1)S(1)} %get-tuple-element.86), channel_id=1, source_target_pairs={{0,16},{8,24},{16,0},{24,8},{1,17},{9,25},{17,1},{25,9},{2,18},{10... | collective-permute-start | bytes 393224 | tf_op jit(solution)/shard_map/ppermute | solution.py:336
  47.5 5.1 %collective-permute-start.18 = (bf16[128,512]{1,0:T(8,128)(2,1)S(1)}, bf16[128,512]{1,0:T(8,128)(2,1)S(1)}, u32[]{:S(2)}, u32[]{:S(2)}) collective-permute-start(bf16[128,512]{1,0:T(8,128)(2,1)S(1)} %get-tuple-element.84), channel_id=1, source_target_pairs={{0,8},{8,0},{16,24},{24,16},{1,9},{9,1},{17,25},{25,17},{2,10},{10... | collective-permute-start | bytes 393224 | tf_op jit(solution)/shard_map/ppermute | solution.py:336
  49.6 5.0 %collective-permute-start.19 = (bf16[128,512]{1,0:T(8,128)(2,1)S(1)}, bf16[128,512]{1,0:T(8,128)(2,1)S(1)}, u32[]{:S(2)}, u32[]{:S(2)}) collective-permute-start(bf16[128,512]{1,0:T(8,128)(2,1)S(1)} %get-tuple-element.85), channel_id=1, source_target_pairs={{0,16},{8,24},{16,0},{24,8},{1,17},{9,25},{17,1},{25,9},{2,18},{10... | collective-permute-start | bytes 393224 | tf_op jit(solution)/shard_map/ppermute | solution.py:336

commit v14 on v11

--- a/solution.py
+++ b/solution.py
@@ -355,16 +355,16 @@
     def swaps(xs):
         return [swap(x) for x in xs]
 
-    def swaps_in_turn(xs):
-        first = swap(xs[0])
-        second, first = lax.optimization_barrier((xs[1], first))
-        return [first, swap(second)]
+    def swaps_by_two(xs):
+        first = swaps(xs[:2])
+        *rest, first[0], first[1] = lax.optimization_barrier((*xs[2:], *first))
+        return first + swaps(rest)
 
     if forward:
         always = place[0] < 1000
-        last, mine = lax.cond(always, swaps_in_turn, list, [own[3], own[0]])
-        *own[1:3], last = lax.optimization_barrier((*own[1:3], last))
-        other = [mine] + lax.cond(always, swaps, list, own[1:3]) + [last]
+        one, two, mine = lax.cond(always, swaps_by_two, list, [own[1], own[2], own[0]])
+        own[3], mine = lax.optimization_barrier((own[3], mine))
+        other = [mine, one, two] + lax.cond(always, swaps, list, own[3:])
     else:
         other = swaps(own)
     (x,) = run(

time: 49.5 us -> 49.6 us (level)
  starting transfers between devices: 19.1 us -> 21.1 us
  waiting for transfers between devices: 13.8 us -> 12 us
    ppermute x15, starting transfers between devices: 18.4 us -> 20.3 us  [send(): return lax.ppermute(x, 'ctx', [(i, i ^ s) for i in range(n)]) if s else x]
    ppermute x15, waiting for transfers between devices: 8.77 us -> 6.94 us  [send(): return lax.ppermute(x, 'ctx', [(i, i ^ s) for i in range(n)]) if s else x]
  transfers between devices with their start and end apart: 20 -> 20, of which waited for: 11 -> 10; matrix products, arithmetic and copies ran while one was open for 0% -> 0% of each run, Pallas kernels for 27% -> 26%
where the time goes in v14:
time: 49.6 us; the launch traced here: 49.5 us
  starting transfers between devices  21.1 us (43%)
  Pallas kernels  14 us (28%)
  waiting for transfers between devices  12 us (24%)
  local copies, waits for them, and re-layouts  1.65 us (3%)
  between operations  0.73 us (1%)
    ppermute x15, starting transfers between devices, send(): return lax.ppermute(x, 'ctx', [(i, i ^ s) for i in range(n)]) if s else x  20.3 us
    pallas_call x11, Pallas kernels, call(): pl.pallas_call(kernel, out_shape=outs, in_specs=[pl.BlockSpec(memory_spac...  14 us
    ppermute x15, waiting for transfers between devices, send(): return lax.ppermute(x, 'ctx', [(i, i ^ s) for i in range(n)]) if s else x  6.94 us
    ppermute x5, waiting for transfers between devices, swap(): return lax.ppermute(x, 'tp', [(0, 1), (1, 0)])  5.08 us
    unnamed x12, local copies, waits for them, and re-layouts  1.65 us
  transfers between devices with their start and end apart: 20, of which 10 were waited for; matrix products, arithmetic and copies ran while one was open for 0% of the time, Pallas kernels for 26%

profile of v14, /device:TPU:0, one launch (start us, length us, event | category | flops | bytes accessed | tf_op | source)
XLA Modules:
  0.0 49.5 jit_solution(16226965812787279594)
XLA Ops:
  0.7 0.8 %copy-done.3 = s32[128,4]{0,1:T(4,128)S(1)} copy-done((s32[128,4]{0,1:T(4,128)S(1)}, s32[128,4]{0,1:T(4,128)}, u32[]{:S(2)}) %copy-start.3) | copy-done | bytes 2072
  1.4 0.2 copy-done.2
  1.6 3.0 %collective-permute-start.5 = (bf16[1032,128]{1,0:T(8,128)(2,1)S(1)}, bf16[1032,128]{1,0:T(8,128)(2,1)S(1)}, u32[]{:S(2)}, u32[]{:S(2)}) collective-permute-start(bf16[1032,128]{1,0:T(8,128)(2,1)S(1)} %pack.1.refs_0_), channel_id=1, source_target_pairs={{0,16},{8,24},{16,0},{24,8},{1,17},{9,25},{17,1},{25,9},{2,18},{10... | collective-permute-start | bytes 792584 | tf_op jit(solution)/shard_map/ppermute | solution.py:333
  4.7 1.5 %collective-permute-start.4 = (bf16[1032,128]{1,0:T(8,128)(2,1)S(1)}, bf16[1032,128]{1,0:T(8,128)(2,1)S(1)}, u32[]{:S(2)}, u32[]{:S(2)}) collective-permute-start(bf16[1032,128]{1,0:T(8,128)(2,1)S(1)} %pack.1.refs_0_), channel_id=1, source_target_pairs={{0,8},{8,0},{16,24},{24,16},{1,9},{9,1},{17,25},{25,17},{2,10},{10... | collective-permute-start | bytes 792584 | tf_op jit(solution)/shard_map/ppermute | solution.py:333
  6.2 0.0 collective-permute-start.6
  6.2 0.1 pad_add_fusion.1.place
  6.3 1.6 %dispatch.1 = (bf16[816,128]{1,0:T(8,128)(2,1)S(1)}, bf16[816,128]{1,0:T(8,128)(2,1)S(1)}, bf16[816,128]{1,0:T(8,128)(2,1)S(1)}, bf16[816,128]{1,0:T(8,128)(2,1)S(1)}) custom-call(s32[2]{0:T(128)S(1)} %pad_add_fusion.1.place, s32[8,128]{1,0:T(8,128)S(1)} %pad_add_fusion.meta_ref, bf16[4,704,128]{2,1,0:T(8,128)(2,1)S(1)} %bitcast.6), custom_call_target="tpu_custom_call" | custom-call | flops 1 | bytes 1 | tf_op jit(solution)/shard_map/dispatch/pallas_call | solution.py:300
  7.9 2.0 %collective-permute-start.7 = (bf16[816,128]{1,0:T(8,128)(2,1)S(1)}, bf16[816,128]{1,0:T(8,128)(2,1)S(1)}, u32[]{:S(2)}, u32[]{:S(2)}) collective-permute-start(bf16[816,128]{1,0:T(8,128)(2,1)S(1)} %get-tuple-element.61), channel_id=1, source_target_pairs={{0,8},{8,0},{16,24},{24,16},{1,9},{9,1},{17,25},{25,17},{2,10},{10... | collective-permute-start | bytes 626696 | tf_op jit(solution)/shard_map/ppermute | solution.py:333
  9.9 1.5 %collective-permute-start.8 = (bf16[816,128]{1,0:T(8,128)(2,1)S(1)}, bf16[816,128]{1,0:T(8,128)(2,1)S(1)}, u32[]{:S(2)}, u32[]{:S(2)}) collective-permute-start(bf16[816,128]{1,0:T(8,128)(2,1)S(1)} %get-tuple-element.62), channel_id=1, source_target_pairs={{0,16},{8,24},{16,0},{24,8},{1,17},{9,25},{17,1},{25,9},{2,18},{10... | collective-permute-start | bytes 626696 | tf_op jit(solution)/shard_map/ppermute | solution.py:333
  11.4 0.0 collective-permute-done.5.refs_2_
  11.4 2.5 %collective-permute-done.4.refs_1_ = bf16[1032,128]{1,0:T(8,128)(2,1)S(1)} collective-permute-done((bf16[1032,128]{1,0:T(8,128)(2,1)S(1)}, bf16[1032,128]{1,0:T(8,128)(2,1)S(1)}, u32[]{:S(2)}, u32[]{:S(2)}) %collective-permute-start.4) | collective-permute-done | bytes 264224 | tf_op jit(solution)/shard_map/ppermute | solution.py:333
  13.9 3.7 %conditional.2 = (bf16[1032,128]{1,0:T(8,128)(2,1)}, bf16[1032,128]{1,0:T(8,128)(2,1)}, bf16[1032,128]{1,0:T(8,128)(2,1)}) conditional(s32[]{:T(128)} %convert_element_type.4, (bf16[1032,128]{1,0:T(8,128)(2,1)S(1)}, bf16[1032,128]{1,0:T(8,128)(2,1)S(1)}, bf16[1032,128]{1,0:T(8,128)(2,1)S(1)}) %tuple.25, (bf16[1032,128]{1,0:T(8,128)(2,1)S(1)}, ...), branch_computations={%region_0.0_spmd, %region_1.0_spmd} | conditional | bytes 3170448 | solution.py:365
  13.9 0.5 %collective-permute-start.1 = (bf16[1032,128]{1,0:T(8,128)(2,1)S(1)}, bf16[1032,128]{1,0:T(8,128)(2,1)}, u32[]{:S(2)}, u32[]{:S(2)}) collective-permute-start(bf16[1032,128]{1,0:T(8,128)(2,1)S(1)} %get-tuple-element.19), channel_id=1, source_target_pairs={{0,1},{1,0},{2,3},{3,2},{4,5},{5,4},{6,7},{7,6},{8,9},{9,8},{10,11... | collective-permute-start | bytes 792584 | tf_op jit(solution)/shard_map/cond/branch_1_fun/ppermute | solution.py:336
  14.5 1.2 %collective-permute-done = bf16[1032,128]{1,0:T(8,128)(2,1)} collective-permute-done((bf16[1032,128]{1,0:T(8,128)(2,1)S(1)}, bf16[1032,128]{1,0:T(8,128)(2,1)}, u32[]{:S(2)}, u32[]{:S(2)}) %collective-permute-start) | collective-permute-done | bytes 264224 | tf_op jit(solution)/shard_map/cond/branch_1_fun/ppermute | solution.py:336
  15.6 0.4 collective-permute-done.1
  16.0 0.1 collective-permute-start.2
  16.1 1.5 %collective-permute-done.2 = bf16[1032,128]{1,0:T(8,128)(2,1)} collective-permute-done((bf16[1032,128]{1,0:T(8,128)(2,1)S(1)}, bf16[1032,128]{1,0:T(8,128)(2,1)}, u32[]{:S(2)}, u32[]{:S(2)}) %collective-permute-start.2) | collective-permute-done | bytes 264224 | tf_op jit(solution)/shard_map/cond/branch_1_fun/ppermute | solution.py:336
  17.7 1.9 %collective-permute-start.9 = (bf16[816,128]{1,0:T(8,128)(2,1)S(1)}, bf16[816,128]{1,0:T(8,128)(2,1)S(1)}, u32[]{:S(2)}, u32[]{:S(2)}) collective-permute-start(bf16[816,128]{1,0:T(8,128)(2,1)S(1)} %get-tuple-element.63), channel_id=1, source_target_pairs={{0,24},{8,16},{16,8},{24,0},{1,25},{9,17},{17,9},{25,1},{2,26},{10... | collective-permute-start | bytes 626696 | tf_op jit(solution)/shard_map/ppermute | solution.py:333
  19.6 0.0 collective-permute-done.6.refs_3_
  19.6 1.7 %conditional.3 = (bf16[1032,128]{1,0:T(8,128)(2,1)}) conditional(s32[]{:T(128)} %convert_element_type.4, bf16[1032,128]{1,0:T(8,128)(2,1)S(1)} %collective-permute-done.6.refs_3_, bf16[1032,128]{1,0:T(8,128)(2,1)S(1)} %collective-permute-done.6.refs_3_), branch_computations={%region_2.0_spmd, %region_3.0_spmd} | conditional | bytes 1056816 | solution.py:367
  19.6 0.0 collective-permute-start.3
  19.6 1.7 %collective-permute-done.3 = bf16[1032,128]{1,0:T(8,128)(2,1)} collective-permute-done((bf16[1032,128]{1,0:T(8,128)(2,1)S(1)}, bf16[1032,128]{1,0:T(8,128)(2,1)}, u32[]{:S(2)}, u32[]{:S(2)}) %collective-permute-start.3) | collective-permute-done | bytes 264224 | tf_op jit(solution)/shard_map/cond/branch_1_fun/ppermute | solution.py:336
  21.2 2.2 %gather.1.x_ref = bf16[2,288,2048]{2,1,0:T(8,128)(2,1)S(1)} custom-call(s32[2]{0:T(128)S(1)} %pad_add_fusion.1.place, bf16[1032,128]{1,0:T(8,128)(2,1)S(1)} %pack.1.refs_0_, bf16[1032,128]{1,0:T(8,128)(2,1)S(1)} %collective-permute-done.4.refs_1_, bf16[1032,128]{1,0:T(8,128)(2,1)S(1)} %collective-permute-done.5.refs_2_, ...), custom_call_target="tpu_custom_call" | custom-call | flops 2000000000 | bytes 1 | tf_op jit(solution)/shard_map/gather/pallas_call | solution.py:300
  23.5 0.7 %copy-done = bf16[2,704,2048]{2,1,0:T(8,128)(2,1)S(1)} copy-done((bf16[2,704,2048]{2,1,0:T(8,128)(2,1)S(1)}, bf16[2,704,2048]{2,1,0:T(8,128)(2,1)}, u32[]{:S(2)}) %copy-start) | copy-done | bytes 5767192
  24.2 2.1 %grad.1 = (bf16[800,128]{1,0:T(8,128)(2,1)S(1)}, bf16[800,128]{1,0:T(8,128)(2,1)S(1)}, bf16[800,128]{1,0:T(8,128)(2,1)S(1)}, bf16[800,128]{1,0:T(8,128)(2,1)S(1)}) custom-call(bf16[2,288,2048]{2,1,0:T(8,128)(2,1)S(1)} %gather.1.x_ref, bf16[2,704,2048]{2,1,0:T(8,128)(2,1)S(1)} %copy-done), custom_call_target="tpu_custom_call" | custom-call | flops 1 | bytes 1 | tf_op jit(solution)/shard_map/grad/pallas_call | solution.py:300
  26.3 1.6 %collective-permute-start.11 = (bf16[800,128]{1,0:T(8,128)(2,1)S(1)}, bf16[800,128]{1,0:T(8,128)(2,1)S(1)}, u32[]{:S(2)}, u32[]{:S(2)}) collective-permute-start(bf16[800,128]{1,0:T(8,128)(2,1)S(1)} %get-tuple-element.67), channel_id=1, source_target_pairs={{0,8},{8,0},{16,24},{24,16},{1,9},{9,1},{17,25},{25,17},{2,10},{10... | collective-permute-start | bytes 614408 | tf_op jit(solution)/shard_map/ppermute | solution.py:333
  27.9 1.5 %collective-permute-start.12 = (bf16[800,128]{1,0:T(8,128)(2,1)S(1)}, bf16[800,128]{1,0:T(8,128)(2,1)S(1)}, u32[]{:S(2)}, u32[]{:S(2)}) collective-permute-start(bf16[800,128]{1,0:T(8,128)(2,1)S(1)} %get-tuple-element.68), channel_id=1, source_target_pairs={{0,16},{8,24},{16,0},{24,8},{1,17},{9,25},{17,1},{25,9},{2,18},{10... | collective-permute-start | bytes 614408 | tf_op jit(solution)/shard_map/ppermute | solution.py:333
  29.4 0.4 collective-permute-start.19
  29.9 0.0 collective-permute-done.8.refs_2_
  29.9 0.0 collective-permute-done.9.refs_3_
  29.9 2.3 %mix_sibling.1 = bf16[512,1024]{1,0:T(8,128)(2,1)S(1)} custom-call(s32[2]{0:T(128)S(1)} %pad_add_fusion.1.place, bf16[816,128]{1,0:T(8,128)(2,1)S(1)} %get-tuple-element.60.refs_0_, bf16[816,128]{1,0:T(8,128)(2,1)S(1)} %collective-permute-done.7.refs_1_, bf16[816,128]{1,0:T(8,128)(2,1)S(1)} %collective-permute-done.8.refs_2_, ...), custom_call_target="tpu_custom_call" | custom-call | flops 1 | bytes 1 | tf_op jit(solution)/shard_map/mix_sibling/pallas_call | solution.py:300
  32.2 0.1 collective-permute-start.10
  32.2 2.3 %mix_own.1.own = f32[512,1024]{1,0:T(8,128)S(1)} custom-call(s32[2]{0:T(128)S(1)} %pad_add_fusion.1.place, bf16[816,128]{1,0:T(8,128)(2,1)S(1)} %get-tuple-element.60.refs_0_, bf16[816,128]{1,0:T(8,128)(2,1)S(1)} %collective-permute-done.7.refs_1_, bf16[816,128]{1,0:T(8,128)(2,1)S(1)} %collective-permute-done.8.refs_2_, ...), custom_call_target="tpu_custom_call" | custom-call | flops 99999997952 | bytes 1 | tf_op jit(solution)/shard_map/mix_own/pallas_call | solution.py:300
  34.6 0.3 collective-permute-done.10.arrived
  34.9 0.2 add.5
  35.1 1.6 %collective-permute-start.14 = (bf16[128,512]{1,0:T(8,128)(2,1)S(1)}, bf16[128,512]{1,0:T(8,128)(2,1)S(1)}, u32[]{:S(2)}, u32[]{:S(2)}) collective-permute-start(bf16[128,512]{1,0:T(8,128)(2,1)S(1)} %get-tuple-element.72), channel_id=1, source_target_pairs={{0,8},{8,0},{16,24},{24,16},{1,9},{9,1},{17,25},{25,17},{2,10},{10... | collective-permute-start | bytes 393224 | tf_op jit(solution)/shard_map/ppermute | solution.py:333
  36.7 1.5 %collective-permute-start.15 = (bf16[128,512]{1,0:T(8,128)(2,1)S(1)}, bf16[128,512]{1,0:T(8,128)(2,1)S(1)}, u32[]{:S(2)}, u32[]{:S(2)}) collective-permute-start(bf16[128,512]{1,0:T(8,128)(2,1)S(1)} %get-tuple-element.73), channel_id=1, source_target_pairs={{0,16},{8,24},{16,0},{24,8},{1,17},{9,25},{17,1},{25,9},{2,18},{10... | collective-permute-start | bytes 393224 | tf_op jit(solution)/shard_map/ppermute | solution.py:333
  38.2 0.0 collective-permute-done.11.refs_1_
  38.2 0.9 %collective-permute-done.12.refs_2_ = bf16[800,128]{1,0:T(8,128)(2,1)S(1)} collective-permute-done((bf16[800,128]{1,0:T(8,128)(2,1)S(1)}, bf16[800,128]{1,0:T(8,128)(2,1)S(1)}, u32[]{:S(2)}, u32[]{:S(2)}) %collective-permute-start.12) | collective-permute-done | bytes 204832 | tf_op jit(solution)/shard_map/ppermute | solution.py:333
  39.1 2.0 %collective-permute-start.18 = (bf16[128,512]{1,0:T(8,128)(2,1)S(1)}, bf16[128,512]{1,0:T(8,128)(2,1)S(1)}, u32[]{:S(2)}, u32[]{:S(2)}) collective-permute-start(bf16[128,512]{1,0:T(8,128)(2,1)S(1)} %get-tuple-element.76), channel_id=1, source_target_pairs={{0,16},{8,24},{16,0},{24,8},{1,17},{9,25},{17,1},{25,9},{2,18},{10... | collective-permute-start | bytes 393224 | tf_op jit(solution)/shard_map/ppermute | solution.py:333
  41.2 1.9 %collective-permute-done.15.high = bf16[128,512]{1,0:T(8,128)(2,1)S(1)} collective-permute-done((bf16[128,512]{1,0:T(8,128)(2,1)S(1)}, bf16[128,512]{1,0:T(8,128)(2,1)S(1)}, u32[]{:S(2)}, u32[]{:S(2)}) %collective-permute-start.15) | collective-permute-done | bytes 131104 | tf_op jit(solution)/shard_map/ppermute | solution.py:333
  43.2 0.6 %collective-permute-start.16 = (bf16[128,512]{1,0:T(8,128)(2,1)S(1)}, bf16[128,512]{1,0:T(8,128)(2,1)S(1)}, u32[]{:S(2)}, u32[]{:S(2)}) collective-permute-start(bf16[128,512]{1,0:T(8,128)(2,1)S(1)} %get-tuple-element.74), channel_id=1, source_target_pairs={{0,8},{8,0},{16,24},{24,16},{1,9},{9,1},{17,25},{25,17},{2,10},{10... | collective-permute-start | bytes 393224 | tf_op jit(solution)/shard_map/ppermute | solution.py:333
  43.7 1.1 %collective-permute-start.17 = (bf16[128,512]{1,0:T(8,128)(2,1)S(1)}, bf16[128,512]{1,0:T(8,128)(2,1)S(1)}, u32[]{:S(2)}, u32[]{:S(2)}) collective-permute-start(bf16[128,512]{1,0:T(8,128)(2,1)S(1)} %get-tuple-element.75), channel_id=1, source_target_pairs={{0,16},{8,24},{16,0},{24,8},{1,17},{9,25},{17,1},{25,9},{2,18},{10... | collective-permute-start | bytes 393224 | tf_op jit(solution)/shard_map/ppermute | solution.py:333
  44.8 0.0 collective-permute-done.19.refs_3_
  44.8 2.3 %restore.1 = bf16[4,704,128]{2,1,0:T(8,128)(2,1)} custom-call(s32[2]{0:T(128)S(1)} %pad_add_fusion.1.place, s32[8,128]{1,0:T(8,128)S(1)} %pad_add_fusion.meta_ref, bf16[800,128]{1,0:T(8,128)(2,1)S(1)} %get-tuple-element.77.refs_0_, bf16[800,128]{1,0:T(8,128)(2,1)S(1)} %collective-permute-done.11.refs_1_, ...), custom_call_target="tpu_custom_call" | custom-call | flops 99999997952 | bytes 1 | tf_op jit(solution)/shard_map/restore/pallas_call | solution.py:300
  47.1 1.1 %collective-permute-done.16.one_high = bf16[128,512]{1,0:T(8,128)(2,1)S(1)} collective-permute-done((bf16[128,512]{1,0:T(8,128)(2,1)S(1)}, bf16[128,512]{1,0:T(8,128)(2,1)S(1)}, u32[]{:S(2)}, u32[]{:S(2)}) %collective-permute-start.16) | collective-permute-done | bytes 131104 | tf_op jit(solution)/shard_map/ppermute | solution.py:333
  48.2 0.5 %collective-permute-done.17.two_low = bf16[128,512]{1,0:T(8,128)(2,1)S(1)} collective-permute-done((bf16[128,512]{1,0:T(8,128)(2,1)S(1)}, bf16[128,512]{1,0:T(8,128)(2,1)S(1)}, u32[]{:S(2)}, u32[]{:S(2)}) %collective-permute-start.17) | collective-permute-done | bytes 131104 | tf_op jit(solution)/shard_map/ppermute | solution.py:333
  48.7 0.8 %finish.1 = bf16[128,1024]{1,0:T(8,128)(2,1)} custom-call(f32[128,1024]{1,0:T(8,128)S(1)} %get-tuple-element.64.mine, bf16[128,512]{1,0:T(8,128)(2,1)S(1)} %collective-permute-done.13.one_low, bf16[128,512]{1,0:T(8,128)(2,1)S(1)} %collective-permute-done.16.one_high, bf16[128,512]{1,0:T(8,128)(2,1)S(1)} %collective-permute-done.17.two_low, ...), custom_call_target="tpu_custom_call" | custom-call | flops 1 | bytes 1 | tf_op jit(solution)/shard_map/finish/pallas_call | solution.py:300
  (19 shorter events, 0.1 us)
Async XLA Ops:
  0.6 1.0 %copy-start.2 = (bf16[128,1024]{1,0:T(8,128)(2,1)S(1)}, bf16[128,1024]{1,0:T(8,128)(2,1)}, u32[]{:S(2)}) copy-start(bf16[128,1024]{1,0:T(8,128)(2,1)} %dy_ref.1) | copy-start | bytes 786436
  0.6 5.7 %copy-start.1 = (bf16[128,4,704]{0,2,1:T(8,128)(2,1)S(1)}, bf16[128,4,704]{0,2,1:T(8,128)(2,1)}, u32[]{:S(2)}) copy-start(bf16[128,4,704]{0,2,1:T(8,128)(2,1)} %param.9) | copy-start | bytes 2162692
  0.7 0.8 %copy-start.3 = (s32[128,4]{0,1:T(4,128)S(1)}, s32[128,4]{0,1:T(4,128)}, u32[]{:S(2)}) copy-start(s32[128,4]{0,1:T(4,128)} %param.10) | copy-start | bytes 6148
  1.4 4.9 %copy-start.4 = (s32[128,4]{0,1:T(4,128)S(1)}, s32[128,4]{0,1:T(4,128)}, u32[]{:S(2)}) copy-start(s32[128,4]{0,1:T(4,128)} %param.10) | copy-start | bytes 6148
  1.4 4.9 %copy-start.5 = (s32[128,4]{0,1:T(4,128)S(1)}, s32[128,4]{0,1:T(4,128)}, u32[]{:S(2)}) copy-start(s32[128,4]{0,1:T(4,128)} %param.11) | copy-start | bytes 6148
  1.6 9.8 %collective-permute-start.5 = (bf16[1032,128]{1,0:T(8,128)(2,1)S(1)}, bf16[1032,128]{1,0:T(8,128)(2,1)S(1)}, u32[]{:S(2)}, u32[]{:S(2)}) collective-permute-start(bf16[1032,128]{1,0:T(8,128)(2,1)S(1)} %pack.1.refs_0_), channel_id=1, source_target_pairs={{0,16},{8,24},{16,0},{24,8},{1,17},{9,25},{17,1},{25,9},{2,18},{10... | collective-permute-start | bytes 792584 | tf_op jit(solution)/shard_map/ppermute | solution.py:333
  4.7 9.3 %collective-permute-start.4 = (bf16[1032,128]{1,0:T(8,128)(2,1)S(1)}, bf16[1032,128]{1,0:T(8,128)(2,1)S(1)}, u32[]{:S(2)}, u32[]{:S(2)}) collective-permute-start(bf16[1032,128]{1,0:T(8,128)(2,1)S(1)} %pack.1.refs_0_), channel_id=1, source_target_pairs={{0,8},{8,0},{16,24},{24,16},{1,9},{9,1},{17,25},{25,17},{2,10},{10... | collective-permute-start | bytes 792584 | tf_op jit(solution)/shard_map/ppermute | solution.py:333
  6.2 13.4 %collective-permute-start.6 = (bf16[1032,128]{1,0:T(8,128)(2,1)S(1)}, bf16[1032,128]{1,0:T(8,128)(2,1)S(1)}, u32[]{:S(2)}, u32[]{:S(2)}) collective-permute-start(bf16[1032,128]{1,0:T(8,128)(2,1)S(1)} %pack.1.refs_0_), channel_id=1, source_target_pairs={{0,24},{8,16},{16,8},{24,0},{1,25},{9,17},{17,9},{25,1},{2,26},{10... | collective-permute-start | bytes 792584 | tf_op jit(solution)/shard_map/ppermute | solution.py:333
  7.9 21.5 %collective-permute-start.7 = (bf16[816,128]{1,0:T(8,128)(2,1)S(1)}, bf16[816,128]{1,0:T(8,128)(2,1)S(1)}, u32[]{:S(2)}, u32[]{:S(2)}) collective-permute-start(bf16[816,128]{1,0:T(8,128)(2,1)S(1)} %get-tuple-element.61), channel_id=1, source_target_pairs={{0,8},{8,0},{16,24},{24,16},{1,9},{9,1},{17,25},{25,17},{2,10},{10... | collective-permute-start | bytes 626696 | tf_op jit(solution)/shard_map/ppermute | solution.py:333
  9.9 20.0 %collective-permute-start.8 = (bf16[816,128]{1,0:T(8,128)(2,1)S(1)}, bf16[816,128]{1,0:T(8,128)(2,1)S(1)}, u32[]{:S(2)}, u32[]{:S(2)}) collective-permute-start(bf16[816,128]{1,0:T(8,128)(2,1)S(1)} %get-tuple-element.62), channel_id=1, source_target_pairs={{0,16},{8,24},{16,0},{24,8},{1,17},{9,25},{17,1},{25,9},{2,18},{10... | collective-permute-start | bytes 626696 | tf_op jit(solution)/shard_map/ppermute | solution.py:333
  13.9 1.7 %collective-permute-start = (bf16[1032,128]{1,0:T(8,128)(2,1)S(1)}, bf16[1032,128]{1,0:T(8,128)(2,1)}, u32[]{:S(2)}, u32[]{:S(2)}) collective-permute-start(bf16[1032,128]{1,0:T(8,128)(2,1)S(1)} %get-tuple-element.18), channel_id=1, source_target_pairs={{0,1},{1,0},{2,3},{3,2},{4,5},{5,4},{6,7},{7,6},{8,9},{9,8},{10,11... | collective-permute-start | bytes 792584 | tf_op jit(solution)/shard_map/cond/branch_1_fun/ppermute | solution.py:336
  13.9 2.0 %collective-permute-start.1 = (bf16[1032,128]{1,0:T(8,128)(2,1)S(1)}, bf16[1032,128]{1,0:T(8,128)(2,1)}, u32[]{:S(2)}, u32[]{:S(2)}) collective-permute-start(bf16[1032,128]{1,0:T(8,128)(2,1)S(1)} %get-tuple-element.19), channel_id=1, source_target_pairs={{0,1},{1,0},{2,3},{3,2},{4,5},{5,4},{6,7},{7,6},{8,9},{9,8},{10,11... | collective-permute-start | bytes 792584 | tf_op jit(solution)/shard_map/cond/branch_1_fun/ppermute | solution.py:336
  16.0 1.7 %collective-permute-start.2 = (bf16[1032,128]{1,0:T(8,128)(2,1)S(1)}, bf16[1032,128]{1,0:T(8,128)(2,1)}, u32[]{:S(2)}, u32[]{:S(2)}) collective-permute-start(bf16[1032,128]{1,0:T(8,128)(2,1)S(1)} %get-tuple-element.22), channel_id=1, source_target_pairs={{0,1},{1,0},{2,3},{3,2},{4,5},{5,4},{6,7},{7,6},{8,9},{9,8},{10,11... | collective-permute-start | bytes 792584 | tf_op jit(solution)/shard_map/cond/branch_1_fun/ppermute | solution.py:336
  17.7 12.2 %collective-permute-start.9 = (bf16[816,128]{1,0:T(8,128)(2,1)S(1)}, bf16[816,128]{1,0:T(8,128)(2,1)S(1)}, u32[]{:S(2)}, u32[]{:S(2)}) collective-permute-start(bf16[816,128]{1,0:T(8,128)(2,1)S(1)} %get-tuple-element.63), channel_id=1, source_target_pairs={{0,24},{8,16},{16,8},{24,0},{1,25},{9,17},{17,9},{25,1},{2,26},{10... | collective-permute-start | bytes 626696 | tf_op jit(solution)/shard_map/ppermute | solution.py:333
  19.6 1.7 %collective-permute-start.3 = (bf16[1032,128]{1,0:T(8,128)(2,1)S(1)}, bf16[1032,128]{1,0:T(8,128)(2,1)}, u32[]{:S(2)}, u32[]{:S(2)}) collective-permute-start(bf16[1032,128]{1,0:T(8,128)(2,1)S(1)} %param.3), channel_id=1, source_target_pairs={{0,1},{1,0},{2,3},{3,2},{4,5},{5,4},{6,7},{7,6},{8,9},{9,8},{10,11... | collective-permute-start | bytes 792584 | tf_op jit(solution)/shard_map/cond/branch_1_fun/ppermute | solution.py:336
  21.2 3.0 %copy-start = (bf16[2,704,2048]{2,1,0:T(8,128)(2,1)S(1)}, bf16[2,704,2048]{2,1,0:T(8,128)(2,1)}, u32[]{:S(2)}) copy-start(bf16[2,704,2048]{2,1,0:T(8,128)(2,1)} %refs_4_.3) | copy-start | bytes 17301508
  26.3 11.9 %collective-permute-start.11 = (bf16[800,128]{1,0:T(8,128)(2,1)S(1)}, bf16[800,128]{1,0:T(8,128)(2,1)S(1)}, u32[]{:S(2)}, u32[]{:S(2)}) collective-permute-start(bf16[800,128]{1,0:T(8,128)(2,1)S(1)} %get-tuple-element.67), channel_id=1, source_target_pairs={{0,8},{8,0},{16,24},{24,16},{1,9},{9,1},{17,25},{25,17},{2,10},{10... | collective-permute-start | bytes 614408 | tf_op jit(solution)/shard_map/ppermute | solution.py:333
  27.9 11.2 %collective-permute-start.12 = (bf16[800,128]{1,0:T(8,128)(2,1)S(1)}, bf16[800,128]{1,0:T(8,128)(2,1)S(1)}, u32[]{:S(2)}, u32[]{:S(2)}) collective-permute-start(bf16[800,128]{1,0:T(8,128)(2,1)S(1)} %get-tuple-element.68), channel_id=1, source_target_pairs={{0,16},{8,24},{16,0},{24,8},{1,17},{9,25},{17,1},{25,9},{2,18},{10... | collective-permute-start | bytes 614408 | tf_op jit(solution)/shard_map/ppermute | solution.py:333
  29.4 15.4 %collective-permute-start.19 = (bf16[800,128]{1,0:T(8,128)(2,1)S(1)}, bf16[800,128]{1,0:T(8,128)(2,1)S(1)}, u32[]{:S(2)}, u32[]{:S(2)}) collective-permute-start(bf16[800,128]{1,0:T(8,128)(2,1)S(1)} %get-tuple-element.80), channel_id=1, source_target_pairs={{0,24},{8,16},{16,8},{24,0},{1,25},{9,17},{17,9},{25,1},{2,26},{10... | collective-permute-start | bytes 614408 | tf_op jit(solution)/shard_map/ppermute | solution.py:333
  32.2 2.7 %collective-permute-start.10 = (bf16[512,1024]{1,0:T(8,128)(2,1)S(1)}, bf16[512,1024]{1,0:T(8,128)(2,1)S(1)}, u32[]{:S(2)}, u32[]{:S(2)}) collective-permute-start(bf16[512,1024]{1,0:T(8,128)(2,1)S(1)} %mix_sibling.1), channel_id=1, source_target_pairs={{0,1},{1,0},{2,3},{3,2},{4,5},{5,4},{6,7},{7,6},{8,9},{9,8},{10,11... | collective-permute-start | bytes 3145736 | tf_op jit(solution)/shard_map/ppermute | solution.py:336
  35.1 6.0 %collective-permute-start.14 = (bf16[128,512]{1,0:T(8,128)(2,1)S(1)}, bf16[128,512]{1,0:T(8,128)(2,1)S(1)}, u32[]{:S(2)}, u32[]{:S(2)}) collective-permute-start(bf16[128,512]{1,0:T(8,128)(2,1)S(1)} %get-tuple-element.72), channel_id=1, source_target_pairs={{0,8},{8,0},{16,24},{24,16},{1,9},{9,1},{17,25},{25,17},{2,10},{10... | collective-permute-start | bytes 393224 | tf_op jit(solution)/shard_map/ppermute | solution.py:333
  36.7 6.4 %collective-permute-start.15 = (bf16[128,512]{1,0:T(8,128)(2,1)S(1)}, bf16[128,512]{1,0:T(8,128)(2,1)S(1)}, u32[]{:S(2)}, u32[]{:S(2)}) collective-permute-start(bf16[128,512]{1,0:T(8,128)(2,1)S(1)} %get-tuple-element.73), channel_id=1, source_target_pairs={{0,16},{8,24},{16,0},{24,8},{1,17},{9,25},{17,1},{25,9},{2,18},{10... | collective-permute-start | bytes 393224 | tf_op jit(solution)/shard_map/ppermute | solution.py:333
  39.1 8.0 %collective-permute-start.13 = (bf16[128,512]{1,0:T(8,128)(2,1)S(1)}, bf16[128,512]{1,0:T(8,128)(2,1)S(1)}, u32[]{:S(2)}, u32[]{:S(2)}) collective-permute-start(bf16[128,512]{1,0:T(8,128)(2,1)S(1)} %get-tuple-element.69), channel_id=1, source_target_pairs={{0,8},{8,0},{16,24},{24,16},{1,9},{9,1},{17,25},{25,17},{2,10},{10... | collective-permute-start | bytes 393224 | tf_op jit(solution)/shard_map/ppermute | solution.py:333
  39.1 8.0 %collective-permute-start.18 = (bf16[128,512]{1,0:T(8,128)(2,1)S(1)}, bf16[128,512]{1,0:T(8,128)(2,1)S(1)}, u32[]{:S(2)}, u32[]{:S(2)}) collective-permute-start(bf16[128,512]{1,0:T(8,128)(2,1)S(1)} %get-tuple-element.76), channel_id=1, source_target_pairs={{0,16},{8,24},{16,0},{24,8},{1,17},{9,25},{17,1},{25,9},{2,18},{10... | collective-permute-start | bytes 393224 | tf_op jit(solution)/shard_map/ppermute | solution.py:333
  43.2 5.0 %collective-permute-start.16 = (bf16[128,512]{1,0:T(8,128)(2,1)S(1)}, bf16[128,512]{1,0:T(8,128)(2,1)S(1)}, u32[]{:S(2)}, u32[]{:S(2)}) collective-permute-start(bf16[128,512]{1,0:T(8,128)(2,1)S(1)} %get-tuple-element.74), channel_id=1, source_target_pairs={{0,8},{8,0},{16,24},{24,16},{1,9},{9,1},{17,25},{25,17},{2,10},{10... | collective-permute-start | bytes 393224 | tf_op jit(solution)/shard_map/ppermute | solution.py:333
  43.7 5.0 %collective-permute-start.17 = (bf16[128,512]{1,0:T(8,128)(2,1)S(1)}, bf16[128,512]{1,0:T(8,128)(2,1)S(1)}, u32[]{:S(2)}, u32[]{:S(2)}) collective-permute-start(bf16[128,512]{1,0:T(8,128)(2,1)S(1)} %get-tuple-element.75), channel_id=1, source_target_pairs={{0,16},{8,24},{16,0},{24,8},{1,17},{9,25},{17,1},{25,9},{2,18},{10... | collective-permute-start | bytes 393224 | tf_op jit(solution)/shard_map/ppermute | solution.py:333

commit v15 on v11

--- a/solution.py
+++ b/solution.py
@@ -114,7 +114,7 @@
     ]
     sent = dot(picks, jnp.concatenate(scaled, axis=1), NT)
     tokens = hid_ref.shape[2]
-    number = jnp.bitwise_and(iota((8, picks.shape[1]), 1), tokens - 1) + 1
+    number = lax.rem(iota((8, picks.shape[1]), 1), tokens) + 1
     number = number.astype(F32).astype(BF16)
     for s, out in enumerate(outs):
         at = slice(s * width, (s + 1) * width)
@@ -156,22 +156,6 @@
         jnp.concatenate([r[s * cap : (s + 1) * cap] for r in rows], axis=0)
         for s in range(count)
     ]
-
-
-def routes(dims, top, me, packed, tokens):
-    experts, local, cap, width = dims
-    ids = packed[tokens:, :tokens].astype(F32).astype(jnp.int32)[:top]
-    return jnp.concatenate(slots_by_lane(ids, me, local, cap, width), axis=0)
-
-
-def gather_rows(dims, held, halves, x_ref):
-    experts, local, cap, width = dims
-    tokens, half = held[0].shape[1], halves[0].shape[1]
-    chunk = min(half, 512)
-    for c in range(0, half, chunk):
-        rows = [dot(h, ref[:tokens, c : c + chunk], NN) for h, ref in zip(held, halves)]
-        for l, x in enumerate(by_expert(rows, local, cap)):
-            x_ref[l, :, c : c + chunk] = x.astype(BF16)
 
 
 def gather_kernel(dims, top, tokens, place, *refs):
@@ -338,10 +322,10 @@
     meta = jnp.concatenate([expert_ids.T, gate_fix.T], axis=0)
     hid_t = hidden.transpose(1, 2, 0)
     (names,) = run(
-        names_kernel, [shaped((8, tokens))], [expert_ids.T], name="names", weight=10**9
+        names_kernel, [shaped((16, tokens))], [expert_ids.T], name="names", weight=10**9
     )
     (packed,) = run(
-        pack_kernel, [shaped((half // 128 * tokens + 8, 128))], [grad_out, names], name="pack"
+        pack_kernel, [shaped((half // 128 * tokens + 16, 128))], [grad_out, names], name="pack"
     )
     forward = n == 4
     own = [send(packed, s) for s in range(n)]

time: 49.5 us -> 49.6 us (level)
  no operation moved by 1% of the time
where the time goes in v15:
time: 49.6 us; the launch traced here: 49.4 us
  starting transfers between devices  19.1 us (39%)
  Pallas kernels  14 us (28%)
  waiting for transfers between devices  13.9 us (28%)
  local copies, waits for them, and re-layouts  1.64 us (3%)
  between operations  0.73 us (1%)
    ppermute x15, starting transfers between devices, send(): return lax.ppermute(x, 'ctx', [(i, i ^ s) for i in range(n)]) if s else x  18.4 us
    pallas_call x11, Pallas kernels, call(): pl.pallas_call(kernel, out_shape=outs, in_specs=[pl.BlockSpec(memory_spac...  14 us
    ppermute x15, waiting for transfers between devices, send(): return lax.ppermute(x, 'ctx', [(i, i ^ s) for i in range(n)]) if s else x  8.85 us
    ppermute x5, waiting for transfers between devices, swap(): return lax.ppermute(x, 'tp', [(0, 1), (1, 0)])  5.09 us
    unnamed x12, local copies, waits for them, and re-layouts  1.64 us
  transfers between devices with their start and end apart: 20, of which 11 were waited for; matrix products, arithmetic and copies ran while one was open for 0% of the time, Pallas kernels for 27%

profile of v15, /device:TPU:0, one launch (start us, length us, event | category | flops | bytes accessed | tf_op | source)
XLA Modules:
  0.0 49.4 jit_solution(12675647886334240750)
XLA Ops:
  0.7 0.8 %copy-done.3 = s32[128,4]{0,1:T(4,128)S(1)} copy-done((s32[128,4]{0,1:T(4,128)S(1)}, s32[128,4]{0,1:T(4,128)}, u32[]{:S(2)}) %copy-start.3) | copy-done | bytes 2072
  1.4 0.2 copy-done.2
  1.6 4.0 %collective-permute-start.6 = (bf16[1040,128]{1,0:T(8,128)(2,1)S(1)}, bf16[1040,128]{1,0:T(8,128)(2,1)S(1)}, u32[]{:S(2)}, u32[]{:S(2)}) collective-permute-start(bf16[1040,128]{1,0:T(8,128)(2,1)S(1)} %pack.1.refs_0_), channel_id=1, source_target_pairs={{0,24},{8,16},{16,8},{24,0},{1,25},{9,17},{17,9},{25,1},{2,26},{10... | collective-permute-start | bytes 798728 | tf_op jit(solution)/shard_map/ppermute | solution.py:317
  5.6 0.5 %collective-permute-start.5 = (bf16[1040,128]{1,0:T(8,128)(2,1)S(1)}, bf16[1040,128]{1,0:T(8,128)(2,1)S(1)}, u32[]{:S(2)}, u32[]{:S(2)}) collective-permute-start(bf16[1040,128]{1,0:T(8,128)(2,1)S(1)} %pack.1.refs_0_), channel_id=1, source_target_pairs={{0,16},{8,24},{16,0},{24,8},{1,17},{9,25},{17,1},{25,9},{2,18},{10... | collective-permute-start | bytes 798728 | tf_op jit(solution)/shard_map/ppermute | solution.py:317
  6.1 0.1 collective-permute-start.4
  6.2 0.1 pad_add_fusion.1.place
  6.3 1.6 %dispatch.1 = (bf16[816,128]{1,0:T(8,128)(2,1)S(1)}, bf16[816,128]{1,0:T(8,128)(2,1)S(1)}, bf16[816,128]{1,0:T(8,128)(2,1)S(1)}, bf16[816,128]{1,0:T(8,128)(2,1)S(1)}) custom-call(s32[2]{0:T(128)S(1)} %pad_add_fusion.1.place, s32[8,128]{1,0:T(8,128)S(1)} %pad_add_fusion.meta_ref, bf16[4,704,128]{2,1,0:T(8,128)(2,1)S(1)} %bitcast.6), custom_call_target="tpu_custom_call" | custom-call | flops 1 | bytes 1 | tf_op jit(solution)/shard_map/dispatch/pallas_call | solution.py:284
  7.9 2.0 %collective-permute-start.7 = (bf16[816,128]{1,0:T(8,128)(2,1)S(1)}, bf16[816,128]{1,0:T(8,128)(2,1)S(1)}, u32[]{:S(2)}, u32[]{:S(2)}) collective-permute-start(bf16[816,128]{1,0:T(8,128)(2,1)S(1)} %get-tuple-element.64), channel_id=1, source_target_pairs={{0,8},{8,0},{16,24},{24,16},{1,9},{9,1},{17,25},{25,17},{2,10},{10... | collective-permute-start | bytes 626696 | tf_op jit(solution)/shard_map/ppermute | solution.py:317
  9.9 1.5 %collective-permute-start.8 = (bf16[816,128]{1,0:T(8,128)(2,1)S(1)}, bf16[816,128]{1,0:T(8,128)(2,1)S(1)}, u32[]{:S(2)}, u32[]{:S(2)}) collective-permute-start(bf16[816,128]{1,0:T(8,128)(2,1)S(1)} %get-tuple-element.65), channel_id=1, source_target_pairs={{0,16},{8,24},{16,0},{24,8},{1,17},{9,25},{17,1},{25,9},{2,18},{10... | collective-permute-start | bytes 626696 | tf_op jit(solution)/shard_map/ppermute | solution.py:317
  11.4 1.5 %collective-permute-done.6.refs_3_ = bf16[1040,128]{1,0:T(8,128)(2,1)S(1)} collective-permute-done((bf16[1040,128]{1,0:T(8,128)(2,1)S(1)}, bf16[1040,128]{1,0:T(8,128)(2,1)S(1)}, u32[]{:S(2)}, u32[]{:S(2)}) %collective-permute-start.6) | collective-permute-done | bytes 266272 | tf_op jit(solution)/shard_map/ppermute | solution.py:317
  12.9 3.3 %conditional.2 = (bf16[1040,128]{1,0:T(8,128)(2,1)}, bf16[1040,128]{1,0:T(8,128)(2,1)}) conditional(s32[]{:T(128)} %convert_element_type.4, (bf16[1040,128]{1,0:T(8,128)(2,1)S(1)}, bf16[1040,128]{1,0:T(8,128)(2,1)S(1)}) %tuple.26, (bf16[1040,128]{1,0:T(8,128)(2,1)S(1)}, bf16[1040,128]{1,0:T(8,128)(2,1)S(1)}) %tuple.26), branch_computations={%region_0.0_spmd, %region_1.0_spmd} | conditional | bytes 2130016 | solution.py:349
  12.9 0.0 collective-permute-start
  12.9 1.7 %collective-permute-done = bf16[1040,128]{1,0:T(8,128)(2,1)} collective-permute-done((bf16[1040,128]{1,0:T(8,128)(2,1)S(1)}, bf16[1040,128]{1,0:T(8,128)(2,1)}, u32[]{:S(2)}, u32[]{:S(2)}) %collective-permute-start) | collective-permute-done | bytes 266272 | tf_op jit(solution)/shard_map/cond/branch_1_fun/ppermute | solution.py:320
  14.5 0.1 collective-permute-start.1
  14.7 1.5 %collective-permute-done.1 = bf16[1040,128]{1,0:T(8,128)(2,1)} collective-permute-done((bf16[1040,128]{1,0:T(8,128)(2,1)S(1)}, bf16[1040,128]{1,0:T(8,128)(2,1)}, u32[]{:S(2)}, u32[]{:S(2)}) %collective-permute-start.1) | collective-permute-done | bytes 266272 | tf_op jit(solution)/shard_map/cond/branch_1_fun/ppermute | solution.py:320
  16.2 2.9 %collective-permute-start.9 = (bf16[816,128]{1,0:T(8,128)(2,1)S(1)}, bf16[816,128]{1,0:T(8,128)(2,1)S(1)}, u32[]{:S(2)}, u32[]{:S(2)}) collective-permute-start(bf16[816,128]{1,0:T(8,128)(2,1)S(1)} %get-tuple-element.66), channel_id=1, source_target_pairs={{0,24},{8,16},{16,8},{24,0},{1,25},{9,17},{17,9},{25,1},{2,26},{10... | collective-permute-start | bytes 626696 | tf_op jit(solution)/shard_map/ppermute | solution.py:317
  19.1 0.0 collective-permute-done.5.refs_2_
  19.1 0.0 collective-permute-done.4.refs_1_
  19.1 2.1 %conditional.3 = (bf16[1040,128]{1,0:T(8,128)(2,1)}, bf16[1040,128]{1,0:T(8,128)(2,1)}) conditional(s32[]{:T(128)} %convert_element_type.4, (bf16[1040,128]{1,0:T(8,128)(2,1)S(1)}, bf16[1040,128]{1,0:T(8,128)(2,1)S(1)}) %tuple.28, (bf16[1040,128]{1,0:T(8,128)(2,1)S(1)}, bf16[1040,128]{1,0:T(8,128)(2,1)S(1)}) %tuple.28), branch_computations={%region_2.0_spmd, %region_3.0_spmd} | conditional | bytes 2130016 | solution.py:351
  19.1 0.5 %collective-permute-start.3 = (bf16[1040,128]{1,0:T(8,128)(2,1)S(1)}, bf16[1040,128]{1,0:T(8,128)(2,1)}, u32[]{:S(2)}, u32[]{:S(2)}) collective-permute-start(bf16[1040,128]{1,0:T(8,128)(2,1)S(1)} %get-tuple-element.21), channel_id=1, source_target_pairs={{0,1},{1,0},{2,3},{3,2},{4,5},{5,4},{6,7},{7,6},{8,9},{9,8},{10,11... | collective-permute-start | bytes 798728 | tf_op jit(solution)/shard_map/cond/branch_1_fun/ppermute | solution.py:320
  19.6 1.2 %collective-permute-done.2 = bf16[1040,128]{1,0:T(8,128)(2,1)} collective-permute-done((bf16[1040,128]{1,0:T(8,128)(2,1)S(1)}, bf16[1040,128]{1,0:T(8,128)(2,1)}, u32[]{:S(2)}, u32[]{:S(2)}) %collective-permute-start.2) | collective-permute-done | bytes 266272 | tf_op jit(solution)/shard_map/cond/branch_1_fun/ppermute | solution.py:320
  20.8 0.4 collective-permute-done.3
  21.2 2.2 %gather.1.x_ref = bf16[2,288,2048]{2,1,0:T(8,128)(2,1)S(1)} custom-call(s32[2]{0:T(128)S(1)} %pad_add_fusion.1.place, bf16[1040,128]{1,0:T(8,128)(2,1)S(1)} %pack.1.refs_0_, bf16[1040,128]{1,0:T(8,128)(2,1)S(1)} %collective-permute-done.4.refs_1_, bf16[1040,128]{1,0:T(8,128)(2,1)S(1)} %collective-permute-done.5.refs_2_, ...), custom_call_target="tpu_custom_call" | custom-call | flops 2000000000 | bytes 1 | tf_op jit(solution)/shard_map/gather/pallas_call | solution.py:284
  23.4 0.7 %copy-done = bf16[2,704,2048]{2,1,0:T(8,128)(2,1)S(1)} copy-done((bf16[2,704,2048]{2,1,0:T(8,128)(2,1)S(1)}, bf16[2,704,2048]{2,1,0:T(8,128)(2,1)}, u32[]{:S(2)}) %copy-start) | copy-done | bytes 5767192
  24.1 2.1 %grad.1 = (bf16[800,128]{1,0:T(8,128)(2,1)S(1)}, bf16[800,128]{1,0:T(8,128)(2,1)S(1)}, bf16[800,128]{1,0:T(8,128)(2,1)S(1)}, bf16[800,128]{1,0:T(8,128)(2,1)S(1)}) custom-call(bf16[2,288,2048]{2,1,0:T(8,128)(2,1)S(1)} %gather.1.x_ref, bf16[2,704,2048]{2,1,0:T(8,128)(2,1)S(1)} %copy-done), custom_call_target="tpu_custom_call" | custom-call | flops 1 | bytes 1 | tf_op jit(solution)/shard_map/grad/pallas_call | solution.py:284
  26.3 1.5 %collective-permute-start.11 = (bf16[800,128]{1,0:T(8,128)(2,1)S(1)}, bf16[800,128]{1,0:T(8,128)(2,1)S(1)}, u32[]{:S(2)}, u32[]{:S(2)}) collective-permute-start(bf16[800,128]{1,0:T(8,128)(2,1)S(1)} %get-tuple-element.70), channel_id=1, source_target_pairs={{0,8},{8,0},{16,24},{24,16},{1,9},{9,1},{17,25},{25,17},{2,10},{10... | collective-permute-start | bytes 614408 | tf_op jit(solution)/shard_map/ppermute | solution.py:317
  27.8 0.5 %collective-permute-start.12 = (bf16[800,128]{1,0:T(8,128)(2,1)S(1)}, bf16[800,128]{1,0:T(8,128)(2,1)S(1)}, u32[]{:S(2)}, u32[]{:S(2)}) collective-permute-start(bf16[800,128]{1,0:T(8,128)(2,1)S(1)} %get-tuple-element.71), channel_id=1, source_target_pairs={{0,16},{8,24},{16,0},{24,8},{1,17},{9,25},{17,1},{25,9},{2,18},{10... | collective-permute-start | bytes 614408 | tf_op jit(solution)/shard_map/ppermute | solution.py:317
  28.3 0.0 collective-permute-done.7.refs_1_
  28.3 1.5 %collective-permute-start.19 = (bf16[800,128]{1,0:T(8,128)(2,1)S(1)}, bf16[800,128]{1,0:T(8,128)(2,1)S(1)}, u32[]{:S(2)}, u32[]{:S(2)}) collective-permute-start(bf16[800,128]{1,0:T(8,128)(2,1)S(1)} %get-tuple-element.83), channel_id=1, source_target_pairs={{0,24},{8,16},{16,8},{24,0},{1,25},{9,17},{17,9},{25,1},{2,26},{10... | collective-permute-start | bytes 614408 | tf_op jit(solution)/shard_map/ppermute | solution.py:317
  29.8 0.0 collective-permute-done.8.refs_2_
  29.8 2.3 %mix_sibling.1 = bf16[512,1024]{1,0:T(8,128)(2,1)S(1)} custom-call(s32[2]{0:T(128)S(1)} %pad_add_fusion.1.place, bf16[816,128]{1,0:T(8,128)(2,1)S(1)} %get-tuple-element.63.refs_0_, bf16[816,128]{1,0:T(8,128)(2,1)S(1)} %collective-permute-done.7.refs_1_, bf16[816,128]{1,0:T(8,128)(2,1)S(1)} %collective-permute-done.8.refs_2_, ...), custom_call_target="tpu_custom_call" | custom-call | flops 1 | bytes 1 | tf_op jit(solution)/shard_map/mix_sibling/pallas_call | solution.py:284
  32.1 0.1 collective-permute-start.10
  32.2 2.3 %mix_own.1.own = f32[512,1024]{1,0:T(8,128)S(1)} custom-call(s32[2]{0:T(128)S(1)} %pad_add_fusion.1.place, bf16[816,128]{1,0:T(8,128)(2,1)S(1)} %get-tuple-element.63.refs_0_, bf16[816,128]{1,0:T(8,128)(2,1)S(1)} %collective-permute-done.7.refs_1_, bf16[816,128]{1,0:T(8,128)(2,1)S(1)} %collective-permute-done.8.refs_2_, ...), custom_call_target="tpu_custom_call" | custom-call | flops 99999997952 | bytes 1 | tf_op jit(solution)/shard_map/mix_own/pallas_call | solution.py:284
  34.5 0.3 collective-permute-done.10.arrived
  34.9 0.2 add.5
  35.1 1.5 %collective-permute-start.14 = (bf16[128,512]{1,0:T(8,128)(2,1)S(1)}, bf16[128,512]{1,0:T(8,128)(2,1)S(1)}, u32[]{:S(2)}, u32[]{:S(2)}) collective-permute-start(bf16[128,512]{1,0:T(8,128)(2,1)S(1)} %get-tuple-element.75), channel_id=1, source_target_pairs={{0,8},{8,0},{16,24},{24,16},{1,9},{9,1},{17,25},{25,17},{2,10},{10... | collective-permute-start | bytes 393224 | tf_op jit(solution)/shard_map/ppermute | solution.py:317
  36.6 0.5 %collective-permute-start.15 = (bf16[128,512]{1,0:T(8,128)(2,1)S(1)}, bf16[128,512]{1,0:T(8,128)(2,1)S(1)}, u32[]{:S(2)}, u32[]{:S(2)}) collective-permute-start(bf16[128,512]{1,0:T(8,128)(2,1)S(1)} %get-tuple-element.76), channel_id=1, source_target_pairs={{0,16},{8,24},{16,0},{24,8},{1,17},{9,25},{17,1},{25,9},{2,18},{10... | collective-permute-start | bytes 393224 | tf_op jit(solution)/shard_map/ppermute | solution.py:317
  37.2 0.0 collective-permute-done.11.refs_1_
  37.2 1.8 %collective-permute-done.12.refs_2_ = bf16[800,128]{1,0:T(8,128)(2,1)S(1)} collective-permute-done((bf16[800,128]{1,0:T(8,128)(2,1)S(1)}, bf16[800,128]{1,0:T(8,128)(2,1)S(1)}, u32[]{:S(2)}, u32[]{:S(2)}) %collective-permute-start.12) | collective-permute-done | bytes 204832 | tf_op jit(solution)/shard_map/ppermute | solution.py:317
  39.0 0.6 %collective-permute-start.13 = (bf16[128,512]{1,0:T(8,128)(2,1)S(1)}, bf16[128,512]{1,0:T(8,128)(2,1)S(1)}, u32[]{:S(2)}, u32[]{:S(2)}) collective-permute-start(bf16[128,512]{1,0:T(8,128)(2,1)S(1)} %get-tuple-element.72), channel_id=1, source_target_pairs={{0,8},{8,0},{16,24},{24,16},{1,9},{9,1},{17,25},{25,17},{2,10},{10... | collective-permute-start | bytes 393224 | tf_op jit(solution)/shard_map/ppermute | solution.py:317
  39.6 1.9 %collective-permute-done.14.low = bf16[128,512]{1,0:T(8,128)(2,1)S(1)} collective-permute-done((bf16[128,512]{1,0:T(8,128)(2,1)S(1)}, bf16[128,512]{1,0:T(8,128)(2,1)S(1)}, u32[]{:S(2)}, u32[]{:S(2)}) %collective-permute-start.14) | collective-permute-done | bytes 131104 | tf_op jit(solution)/shard_map/ppermute | solution.py:317
  41.5 1.5 %collective-permute-done.15.high = bf16[128,512]{1,0:T(8,128)(2,1)S(1)} collective-permute-done((bf16[128,512]{1,0:T(8,128)(2,1)S(1)}, bf16[128,512]{1,0:T(8,128)(2,1)S(1)}, u32[]{:S(2)}, u32[]{:S(2)}) %collective-permute-start.15) | collective-permute-done | bytes 131104 | tf_op jit(solution)/shard_map/ppermute | solution.py:317
  43.0 0.6 %collective-permute-start.16 = (bf16[128,512]{1,0:T(8,128)(2,1)S(1)}, bf16[128,512]{1,0:T(8,128)(2,1)S(1)}, u32[]{:S(2)}, u32[]{:S(2)}) collective-permute-start(bf16[128,512]{1,0:T(8,128)(2,1)S(1)} %get-tuple-element.77), channel_id=1, source_target_pairs={{0,8},{8,0},{16,24},{24,16},{1,9},{9,1},{17,25},{25,17},{2,10},{10... | collective-permute-start | bytes 393224 | tf_op jit(solution)/shard_map/ppermute | solution.py:317
  43.7 0.6 %collective-permute-start.17 = (bf16[128,512]{1,0:T(8,128)(2,1)S(1)}, bf16[128,512]{1,0:T(8,128)(2,1)S(1)}, u32[]{:S(2)}, u32[]{:S(2)}) collective-permute-start(bf16[128,512]{1,0:T(8,128)(2,1)S(1)} %get-tuple-element.78), channel_id=1, source_target_pairs={{0,16},{8,24},{16,0},{24,8},{1,17},{9,25},{17,1},{25,9},{2,18},{10... | collective-permute-start | bytes 393224 | tf_op jit(solution)/shard_map/ppermute | solution.py:317
  44.2 2.3 %restore.1 = bf16[4,704,128]{2,1,0:T(8,128)(2,1)} custom-call(s32[2]{0:T(128)S(1)} %pad_add_fusion.1.place, s32[8,128]{1,0:T(8,128)S(1)} %pad_add_fusion.meta_ref, bf16[800,128]{1,0:T(8,128)(2,1)S(1)} %get-tuple-element.80.refs_0_, bf16[800,128]{1,0:T(8,128)(2,1)S(1)} %collective-permute-done.11.refs_1_, ...), custom_call_target="tpu_custom_call" | custom-call | flops 99999997952 | bytes 1 | tf_op jit(solution)/shard_map/restore/pallas_call | solution.py:284
  46.5 1.5 %collective-permute-done.16.one_high = bf16[128,512]{1,0:T(8,128)(2,1)S(1)} collective-permute-done((bf16[128,512]{1,0:T(8,128)(2,1)S(1)}, bf16[128,512]{1,0:T(8,128)(2,1)S(1)}, u32[]{:S(2)}, u32[]{:S(2)}) %collective-permute-start.16) | collective-permute-done | bytes 131104 | tf_op jit(solution)/shard_map/ppermute | solution.py:317
  48.1 0.6 %collective-permute-done.17.two_low = bf16[128,512]{1,0:T(8,128)(2,1)S(1)} collective-permute-done((bf16[128,512]{1,0:T(8,128)(2,1)S(1)}, bf16[128,512]{1,0:T(8,128)(2,1)S(1)}, u32[]{:S(2)}, u32[]{:S(2)}) %collective-permute-start.17) | collective-permute-done | bytes 131104 | tf_op jit(solution)/shard_map/ppermute | solution.py:317
  48.7 0.8 %finish.1 = bf16[128,1024]{1,0:T(8,128)(2,1)} custom-call(f32[128,1024]{1,0:T(8,128)S(1)} %get-tuple-element.67.mine, bf16[128,512]{1,0:T(8,128)(2,1)S(1)} %collective-permute-done.13.one_low, bf16[128,512]{1,0:T(8,128)(2,1)S(1)} %collective-permute-done.16.one_high, bf16[128,512]{1,0:T(8,128)(2,1)S(1)} %collective-permute-done.17.two_low, ...), custom_call_target="tpu_custom_call" | custom-call | flops 1 | bytes 1 | tf_op jit(solution)/shard_map/finish/pallas_call | solution.py:284
  (19 shorter events, 0.1 us)
Async XLA Ops:
  0.6 1.0 %copy-start.2 = (bf16[128,1024]{1,0:T(8,128)(2,1)S(1)}, bf16[128,1024]{1,0:T(8,128)(2,1)}, u32[]{:S(2)}) copy-start(bf16[128,1024]{1,0:T(8,128)(2,1)} %dy_ref.1) | copy-start | bytes 786436
  0.6 5.7 %copy-start.1 = (bf16[128,4,704]{0,2,1:T(8,128)(2,1)S(1)}, bf16[128,4,704]{0,2,1:T(8,128)(2,1)}, u32[]{:S(2)}) copy-start(bf16[128,4,704]{0,2,1:T(8,128)(2,1)} %param.9) | copy-start | bytes 2162692
  0.7 0.8 %copy-start.3 = (s32[128,4]{0,1:T(4,128)S(1)}, s32[128,4]{0,1:T(4,128)}, u32[]{:S(2)}) copy-start(s32[128,4]{0,1:T(4,128)} %param.10) | copy-start | bytes 6148
  1.4 4.9 %copy-start.4 = (s32[128,4]{0,1:T(4,128)S(1)}, s32[128,4]{0,1:T(4,128)}, u32[]{:S(2)}) copy-start(s32[128,4]{0,1:T(4,128)} %param.10) | copy-start | bytes 6148
  1.4 4.9 %copy-start.5 = (s32[128,4]{0,1:T(4,128)S(1)}, s32[128,4]{0,1:T(4,128)}, u32[]{:S(2)}) copy-start(s32[128,4]{0,1:T(4,128)} %param.11) | copy-start | bytes 6148
  1.6 11.2 %collective-permute-start.6 = (bf16[1040,128]{1,0:T(8,128)(2,1)S(1)}, bf16[1040,128]{1,0:T(8,128)(2,1)S(1)}, u32[]{:S(2)}, u32[]{:S(2)}) collective-permute-start(bf16[1040,128]{1,0:T(8,128)(2,1)S(1)} %pack.1.refs_0_), channel_id=1, source_target_pairs={{0,24},{8,16},{16,8},{24,0},{1,25},{9,17},{17,9},{25,1},{2,26},{10... | collective-permute-start | bytes 798728 | tf_op jit(solution)/shard_map/ppermute | solution.py:317
  5.6 13.5 %collective-permute-start.5 = (bf16[1040,128]{1,0:T(8,128)(2,1)S(1)}, bf16[1040,128]{1,0:T(8,128)(2,1)S(1)}, u32[]{:S(2)}, u32[]{:S(2)}) collective-permute-start(bf16[1040,128]{1,0:T(8,128)(2,1)S(1)} %pack.1.refs_0_), channel_id=1, source_target_pairs={{0,16},{8,24},{16,0},{24,8},{1,17},{9,25},{17,1},{25,9},{2,18},{10... | collective-permute-start | bytes 798728 | tf_op jit(solution)/shard_map/ppermute | solution.py:317
  6.1 13.0 %collective-permute-start.4 = (bf16[1040,128]{1,0:T(8,128)(2,1)S(1)}, bf16[1040,128]{1,0:T(8,128)(2,1)S(1)}, u32[]{:S(2)}, u32[]{:S(2)}) collective-permute-start(bf16[1040,128]{1,0:T(8,128)(2,1)S(1)} %pack.1.refs_0_), channel_id=1, source_target_pairs={{0,8},{8,0},{16,24},{24,16},{1,9},{9,1},{17,25},{25,17},{2,10},{10... | collective-permute-start | bytes 798728 | tf_op jit(solution)/shard_map/ppermute | solution.py:317
  7.9 20.4 %collective-permute-start.7 = (bf16[816,128]{1,0:T(8,128)(2,1)S(1)}, bf16[816,128]{1,0:T(8,128)(2,1)S(1)}, u32[]{:S(2)}, u32[]{:S(2)}) collective-permute-start(bf16[816,128]{1,0:T(8,128)(2,1)S(1)} %get-tuple-element.64), channel_id=1, source_target_pairs={{0,8},{8,0},{16,24},{24,16},{1,9},{9,1},{17,25},{25,17},{2,10},{10... | collective-permute-start | bytes 626696 | tf_op jit(solution)/shard_map/ppermute | solution.py:317
  9.9 19.9 %collective-permute-start.8 = (bf16[816,128]{1,0:T(8,128)(2,1)S(1)}, bf16[816,128]{1,0:T(8,128)(2,1)S(1)}, u32[]{:S(2)}, u32[]{:S(2)}) collective-permute-start(bf16[816,128]{1,0:T(8,128)(2,1)S(1)} %get-tuple-element.65), channel_id=1, source_target_pairs={{0,16},{8,24},{16,0},{24,8},{1,17},{9,25},{17,1},{25,9},{2,18},{10... | collective-permute-start | bytes 626696 | tf_op jit(solution)/shard_map/ppermute | solution.py:317
  12.9 1.7 %collective-permute-start = (bf16[1040,128]{1,0:T(8,128)(2,1)S(1)}, bf16[1040,128]{1,0:T(8,128)(2,1)}, u32[]{:S(2)}, u32[]{:S(2)}) collective-permute-start(bf16[1040,128]{1,0:T(8,128)(2,1)S(1)} %get-tuple-element.17), channel_id=1, source_target_pairs={{0,1},{1,0},{2,3},{3,2},{4,5},{5,4},{6,7},{7,6},{8,9},{9,8},{10,11... | collective-permute-start | bytes 798728 | tf_op jit(solution)/shard_map/cond/branch_1_fun/ppermute | solution.py:320
  14.5 1.7 %collective-permute-start.1 = (bf16[1040,128]{1,0:T(8,128)(2,1)S(1)}, bf16[1040,128]{1,0:T(8,128)(2,1)}, u32[]{:S(2)}, u32[]{:S(2)}) collective-permute-start(bf16[1040,128]{1,0:T(8,128)(2,1)S(1)} %get-tuple-element.19), channel_id=1, source_target_pairs={{0,1},{1,0},{2,3},{3,2},{4,5},{5,4},{6,7},{7,6},{8,9},{9,8},{10,11... | collective-permute-start | bytes 798728 | tf_op jit(solution)/shard_map/cond/branch_1_fun/ppermute | solution.py:320
  16.2 13.6 %collective-permute-start.9 = (bf16[816,128]{1,0:T(8,128)(2,1)S(1)}, bf16[816,128]{1,0:T(8,128)(2,1)S(1)}, u32[]{:S(2)}, u32[]{:S(2)}) collective-permute-start(bf16[816,128]{1,0:T(8,128)(2,1)S(1)} %get-tuple-element.66), channel_id=1, source_target_pairs={{0,24},{8,16},{16,8},{24,0},{1,25},{9,17},{17,9},{25,1},{2,26},{10... | collective-permute-start | bytes 626696 | tf_op jit(solution)/shard_map/ppermute | solution.py:317
  19.1 1.7 %collective-permute-start.2 = (bf16[1040,128]{1,0:T(8,128)(2,1)S(1)}, bf16[1040,128]{1,0:T(8,128)(2,1)}, u32[]{:S(2)}, u32[]{:S(2)}) collective-permute-start(bf16[1040,128]{1,0:T(8,128)(2,1)S(1)} %get-tuple-element.20), channel_id=1, source_target_pairs={{0,1},{1,0},{2,3},{3,2},{4,5},{5,4},{6,7},{7,6},{8,9},{9,8},{10,11... | collective-permute-start | bytes 798728 | tf_op jit(solution)/shard_map/cond/branch_1_fun/ppermute | solution.py:320
  19.1 2.0 %collective-permute-start.3 = (bf16[1040,128]{1,0:T(8,128)(2,1)S(1)}, bf16[1040,128]{1,0:T(8,128)(2,1)}, u32[]{:S(2)}, u32[]{:S(2)}) collective-permute-start(bf16[1040,128]{1,0:T(8,128)(2,1)S(1)} %get-tuple-element.21), channel_id=1, source_target_pairs={{0,1},{1,0},{2,3},{3,2},{4,5},{5,4},{6,7},{7,6},{8,9},{9,8},{10,11... | collective-permute-start | bytes 798728 | tf_op jit(solution)/shard_map/cond/branch_1_fun/ppermute | solution.py:320
  21.2 3.0 %copy-start = (bf16[2,704,2048]{2,1,0:T(8,128)(2,1)S(1)}, bf16[2,704,2048]{2,1,0:T(8,128)(2,1)}, u32[]{:S(2)}) copy-start(bf16[2,704,2048]{2,1,0:T(8,128)(2,1)} %refs_4_.3) | copy-start | bytes 17301508
  26.3 10.9 %collective-permute-start.11 = (bf16[800,128]{1,0:T(8,128)(2,1)S(1)}, bf16[800,128]{1,0:T(8,128)(2,1)S(1)}, u32[]{:S(2)}, u32[]{:S(2)}) collective-permute-start(bf16[800,128]{1,0:T(8,128)(2,1)S(1)} %get-tuple-element.70), channel_id=1, source_target_pairs={{0,8},{8,0},{16,24},{24,16},{1,9},{9,1},{17,25},{25,17},{2,10},{10... | collective-permute-start | bytes 614408 | tf_op jit(solution)/shard_map/ppermute | solution.py:317
  27.8 11.2 %collective-permute-start.12 = (bf16[800,128]{1,0:T(8,128)(2,1)S(1)}, bf16[800,128]{1,0:T(8,128)(2,1)S(1)}, u32[]{:S(2)}, u32[]{:S(2)}) collective-permute-start(bf16[800,128]{1,0:T(8,128)(2,1)S(1)} %get-tuple-element.71), channel_id=1, source_target_pairs={{0,16},{8,24},{16,0},{24,8},{1,17},{9,25},{17,1},{25,9},{2,18},{10... | collective-permute-start | bytes 614408 | tf_op jit(solution)/shard_map/ppermute | solution.py:317
  28.3 15.9 %collective-permute-start.19 = (bf16[800,128]{1,0:T(8,128)(2,1)S(1)}, bf16[800,128]{1,0:T(8,128)(2,1)S(1)}, u32[]{:S(2)}, u32[]{:S(2)}) collective-permute-start(bf16[800,128]{1,0:T(8,128)(2,1)S(1)} %get-tuple-element.83), channel_id=1, source_target_pairs={{0,24},{8,16},{16,8},{24,0},{1,25},{9,17},{17,9},{25,1},{2,26},{10... | collective-permute-start | bytes 614408 | tf_op jit(solution)/shard_map/ppermute | solution.py:317
  32.1 2.7 %collective-permute-start.10 = (bf16[512,1024]{1,0:T(8,128)(2,1)S(1)}, bf16[512,1024]{1,0:T(8,128)(2,1)S(1)}, u32[]{:S(2)}, u32[]{:S(2)}) collective-permute-start(bf16[512,1024]{1,0:T(8,128)(2,1)S(1)} %mix_sibling.1), channel_id=1, source_target_pairs={{0,1},{1,0},{2,3},{3,2},{4,5},{5,4},{6,7},{7,6},{8,9},{9,8},{10,11... | collective-permute-start | bytes 3145736 | tf_op jit(solution)/shard_map/ppermute | solution.py:320
  35.1 6.4 %collective-permute-start.14 = (bf16[128,512]{1,0:T(8,128)(2,1)S(1)}, bf16[128,512]{1,0:T(8,128)(2,1)S(1)}, u32[]{:S(2)}, u32[]{:S(2)}) collective-permute-start(bf16[128,512]{1,0:T(8,128)(2,1)S(1)} %get-tuple-element.75), channel_id=1, source_target_pairs={{0,8},{8,0},{16,24},{24,16},{1,9},{9,1},{17,25},{25,17},{2,10},{10... | collective-permute-start | bytes 393224 | tf_op jit(solution)/shard_map/ppermute | solution.py:317
  36.6 6.4 %collective-permute-start.15 = (bf16[128,512]{1,0:T(8,128)(2,1)S(1)}, bf16[128,512]{1,0:T(8,128)(2,1)S(1)}, u32[]{:S(2)}, u32[]{:S(2)}) collective-permute-start(bf16[128,512]{1,0:T(8,128)(2,1)S(1)} %get-tuple-element.76), channel_id=1, source_target_pairs={{0,16},{8,24},{16,0},{24,8},{1,17},{9,25},{17,1},{25,9},{2,18},{10... | collective-permute-start | bytes 393224 | tf_op jit(solution)/shard_map/ppermute | solution.py:317
  39.0 7.5 %collective-permute-start.13 = (bf16[128,512]{1,0:T(8,128)(2,1)S(1)}, bf16[128,512]{1,0:T(8,128)(2,1)S(1)}, u32[]{:S(2)}, u32[]{:S(2)}) collective-permute-start(bf16[128,512]{1,0:T(8,128)(2,1)S(1)} %get-tuple-element.72), channel_id=1, source_target_pairs={{0,8},{8,0},{16,24},{24,16},{1,9},{9,1},{17,25},{25,17},{2,10},{10... | collective-permute-start | bytes 393224 | tf_op jit(solution)/shard_map/ppermute | solution.py:317
  39.6 6.9 %collective-permute-start.18 = (bf16[128,512]{1,0:T(8,128)(2,1)S(1)}, bf16[128,512]{1,0:T(8,128)(2,1)S(1)}, u32[]{:S(2)}, u32[]{:S(2)}) collective-permute-start(bf16[128,512]{1,0:T(8,128)(2,1)S(1)} %get-tuple-element.79), channel_id=1, source_target_pairs={{0,16},{8,24},{16,0},{24,8},{1,17},{9,25},{17,1},{25,9},{2,18},{10... | collective-permute-start | bytes 393224 | tf_op jit(solution)/shard_map/ppermute | solution.py:317
  43.0 5.0 %collective-permute-start.16 = (bf16[128,512]{1,0:T(8,128)(2,1)S(1)}, bf16[128,512]{1,0:T(8,128)(2,1)S(1)}, u32[]{:S(2)}, u32[]{:S(2)}) collective-permute-start(bf16[128,512]{1,0:T(8,128)(2,1)S(1)} %get-tuple-element.77), channel_id=1, source_target_pairs={{0,8},{8,0},{16,24},{24,16},{1,9},{9,1},{17,25},{25,17},{2,10},{10... | collective-permute-start | bytes 393224 | tf_op jit(solution)/shard_map/ppermute | solution.py:317
  43.7 5.0 %collective-permute-start.17 = (bf16[128,512]{1,0:T(8,128)(2,1)S(1)}, bf16[128,512]{1,0:T(8,128)(2,1)S(1)}, u32[]{:S(2)}, u32[]{:S(2)}) collective-permute-start(bf16[128,512]{1,0:T(8,128)(2,1)S(1)} %get-tuple-element.78), channel_id=1, source_target_pairs={{0,16},{8,24},{16,0},{24,8},{1,17},{9,25},{17,1},{25,9},{2,18},{10... | collective-permute-start | bytes 393224 | tf_op jit(solution)/shard_map/ppermute | solution.py:317

commit v16 on v15

--- a/solution.py
+++ b/solution.py
@@ -380,8 +380,8 @@
             [mine, arrived], name="add",
         )
         low, high = send(low, 1), send(high, 2)
-        one_low, two_high, *grad_back[1:3] = lax.optimization_barrier(
-            (one_low, two_high, *grad_back[1:3])
+        one_low, two_high, *grad_back[2:] = lax.optimization_barrier(
+            (one_low, two_high, *grad_back[2:])
         )
         one_low, two_high = send(one_low, 1), send(two_high, 2)
         to_one, to_two = run(

time: 49.6 us -> 50.4 us (1.016)
  starting transfers between devices: 19.1 us -> 21.4 us
  waiting for transfers between devices: 13.9 us -> 12.5 us
    ppermute x15, starting transfers between devices: 18.4 us -> 20.7 us  [send(): return lax.ppermute(x, 'ctx', [(i, i ^ s) for i in range(n)]) if s else x]
    ppermute x15, waiting for transfers between devices: 8.85 us -> 7.4 us  [send(): return lax.ppermute(x, 'ctx', [(i, i ^ s) for i in range(n)]) if s else x]
  transfers between devices with their start and end apart: 20 -> 20, of which waited for: 11 -> 10; matrix products, arithmetic and copies ran while one was open for 0% -> 0% of each run, Pallas kernels for 27% -> 26%
where the time goes in v16:
time: 50.4 us; the launch traced here: 50.3 us
  starting transfers between devices  21.4 us (42%)
  Pallas kernels  14 us (28%)
  waiting for transfers between devices  12.5 us (25%)
  local copies, waits for them, and re-layouts  1.64 us (3%)
  between operations  0.73 us (1%)
    ppermute x15, starting transfers between devices, send(): return lax.ppermute(x, 'ctx', [(i, i ^ s) for i in range(n)]) if s else x  20.7 us
    pallas_call x11, Pallas kernels, call(): pl.pallas_call(kernel, out_shape=outs, in_specs=[pl.BlockSpec(memory_spac...  14 us
    ppermute x15, waiting for transfers between devices, send(): return lax.ppermute(x, 'ctx', [(i, i ^ s) for i in range(n)]) if s else x  7.4 us
    ppermute x5, waiting for transfers between devices, swap(): return lax.ppermute(x, 'tp', [(0, 1), (1, 0)])  5.09 us
    unnamed x12, local copies, waits for them, and re-layouts  1.64 us
  transfers between devices with their start and end apart: 20, of which 10 were waited for; matrix products, arithmetic and copies ran while one was open for 0% of the time, Pallas kernels for 26%

profile of v16, /device:TPU:0, one launch (start us, length us, event | category | flops | bytes accessed | tf_op | source)
XLA Modules:
  0.0 50.3 jit_solution(270890931588246903)
XLA Ops:
  0.7 0.8 %copy-done.3 = s32[128,4]{0,1:T(4,128)S(1)} copy-done((s32[128,4]{0,1:T(4,128)S(1)}, s32[128,4]{0,1:T(4,128)}, u32[]{:S(2)}) %copy-start.3) | copy-done | bytes 2072
  1.4 0.2 copy-done.2
  1.6 4.0 %collective-permute-start.6 = (bf16[1040,128]{1,0:T(8,128)(2,1)S(1)}, bf16[1040,128]{1,0:T(8,128)(2,1)S(1)}, u32[]{:S(2)}, u32[]{:S(2)}) collective-permute-start(bf16[1040,128]{1,0:T(8,128)(2,1)S(1)} %pack.1.refs_0_), channel_id=1, source_target_pairs={{0,24},{8,16},{16,8},{24,0},{1,25},{9,17},{17,9},{25,1},{2,26},{10... | collective-permute-start | bytes 798728 | tf_op jit(solution)/shard_map/ppermute | solution.py:317
  5.6 0.5 %collective-permute-start.5 = (bf16[1040,128]{1,0:T(8,128)(2,1)S(1)}, bf16[1040,128]{1,0:T(8,128)(2,1)S(1)}, u32[]{:S(2)}, u32[]{:S(2)}) collective-permute-start(bf16[1040,128]{1,0:T(8,128)(2,1)S(1)} %pack.1.refs_0_), channel_id=1, source_target_pairs={{0,16},{8,24},{16,0},{24,8},{1,17},{9,25},{17,1},{25,9},{2,18},{10... | collective-permute-start | bytes 798728 | tf_op jit(solution)/shard_map/ppermute | solution.py:317
  6.1 0.1 collective-permute-start.4
  6.2 0.1 pad_add_fusion.1.place
  6.3 1.6 %dispatch.1 = (bf16[816,128]{1,0:T(8,128)(2,1)S(1)}, bf16[816,128]{1,0:T(8,128)(2,1)S(1)}, bf16[816,128]{1,0:T(8,128)(2,1)S(1)}, bf16[816,128]{1,0:T(8,128)(2,1)S(1)}) custom-call(s32[2]{0:T(128)S(1)} %pad_add_fusion.1.place, s32[8,128]{1,0:T(8,128)S(1)} %pad_add_fusion.meta_ref, bf16[4,704,128]{2,1,0:T(8,128)(2,1)S(1)} %bitcast.6), custom_call_target="tpu_custom_call" | custom-call | flops 1 | bytes 1 | tf_op jit(solution)/shard_map/dispatch/pallas_call | solution.py:284
  7.9 2.0 %collective-permute-start.7 = (bf16[816,128]{1,0:T(8,128)(2,1)S(1)}, bf16[816,128]{1,0:T(8,128)(2,1)S(1)}, u32[]{:S(2)}, u32[]{:S(2)}) collective-permute-start(bf16[816,128]{1,0:T(8,128)(2,1)S(1)} %get-tuple-element.64), channel_id=1, source_target_pairs={{0,8},{8,0},{16,24},{24,16},{1,9},{9,1},{17,25},{25,17},{2,10},{10... | collective-permute-start | bytes 626696 | tf_op jit(solution)/shard_map/ppermute | solution.py:317
  9.9 1.5 %collective-permute-start.8 = (bf16[816,128]{1,0:T(8,128)(2,1)S(1)}, bf16[816,128]{1,0:T(8,128)(2,1)S(1)}, u32[]{:S(2)}, u32[]{:S(2)}) collective-permute-start(bf16[816,128]{1,0:T(8,128)(2,1)S(1)} %get-tuple-element.65), channel_id=1, source_target_pairs={{0,16},{8,24},{16,0},{24,8},{1,17},{9,25},{17,1},{25,9},{2,18},{10... | collective-permute-start | bytes 626696 | tf_op jit(solution)/shard_map/ppermute | solution.py:317
  11.4 1.5 %collective-permute-done.6.refs_3_ = bf16[1040,128]{1,0:T(8,128)(2,1)S(1)} collective-permute-done((bf16[1040,128]{1,0:T(8,128)(2,1)S(1)}, bf16[1040,128]{1,0:T(8,128)(2,1)S(1)}, u32[]{:S(2)}, u32[]{:S(2)}) %collective-permute-start.6) | collective-permute-done | bytes 266272 | tf_op jit(solution)/shard_map/ppermute | solution.py:317
  12.9 3.3 %conditional.2 = (bf16[1040,128]{1,0:T(8,128)(2,1)}, bf16[1040,128]{1,0:T(8,128)(2,1)}) conditional(s32[]{:T(128)} %convert_element_type.4, (bf16[1040,128]{1,0:T(8,128)(2,1)S(1)}, bf16[1040,128]{1,0:T(8,128)(2,1)S(1)}) %tuple.26, (bf16[1040,128]{1,0:T(8,128)(2,1)S(1)}, bf16[1040,128]{1,0:T(8,128)(2,1)S(1)}) %tuple.26), branch_computations={%region_0.0_spmd, %region_1.0_spmd} | conditional | bytes 2130016 | solution.py:349
  12.9 0.0 collective-permute-start
  12.9 1.7 %collective-permute-done = bf16[1040,128]{1,0:T(8,128)(2,1)} collective-permute-done((bf16[1040,128]{1,0:T(8,128)(2,1)S(1)}, bf16[1040,128]{1,0:T(8,128)(2,1)}, u32[]{:S(2)}, u32[]{:S(2)}) %collective-permute-start) | collective-permute-done | bytes 266272 | tf_op jit(solution)/shard_map/cond/branch_1_fun/ppermute | solution.py:320
  14.5 0.1 collective-permute-start.1
  14.7 1.5 %collective-permute-done.1 = bf16[1040,128]{1,0:T(8,128)(2,1)} collective-permute-done((bf16[1040,128]{1,0:T(8,128)(2,1)S(1)}, bf16[1040,128]{1,0:T(8,128)(2,1)}, u32[]{:S(2)}, u32[]{:S(2)}) %collective-permute-start.1) | collective-permute-done | bytes 266272 | tf_op jit(solution)/shard_map/cond/branch_1_fun/ppermute | solution.py:320
  16.2 2.9 %collective-permute-start.9 = (bf16[816,128]{1,0:T(8,128)(2,1)S(1)}, bf16[816,128]{1,0:T(8,128)(2,1)S(1)}, u32[]{:S(2)}, u32[]{:S(2)}) collective-permute-start(bf16[816,128]{1,0:T(8,128)(2,1)S(1)} %get-tuple-element.66), channel_id=1, source_target_pairs={{0,24},{8,16},{16,8},{24,0},{1,25},{9,17},{17,9},{25,1},{2,26},{10... | collective-permute-start | bytes 626696 | tf_op jit(solution)/shard_map/ppermute | solution.py:317
  19.1 0.0 collective-permute-done.5.refs_2_
  19.1 0.0 collective-permute-done.4.refs_1_
  19.1 2.1 %conditional.3 = (bf16[1040,128]{1,0:T(8,128)(2,1)}, bf16[1040,128]{1,0:T(8,128)(2,1)}) conditional(s32[]{:T(128)} %convert_element_type.4, (bf16[1040,128]{1,0:T(8,128)(2,1)S(1)}, bf16[1040,128]{1,0:T(8,128)(2,1)S(1)}) %tuple.28, (bf16[1040,128]{1,0:T(8,128)(2,1)S(1)}, bf16[1040,128]{1,0:T(8,128)(2,1)S(1)}) %tuple.28), branch_computations={%region_2.0_spmd, %region_3.0_spmd} | conditional | bytes 2130016 | solution.py:351
  19.1 0.5 collective-permute-start.3
  19.6 1.2 %collective-permute-done.2 = bf16[1040,128]{1,0:T(8,128)(2,1)} collective-permute-done((bf16[1040,128]{1,0:T(8,128)(2,1)S(1)}, bf16[1040,128]{1,0:T(8,128)(2,1)}, u32[]{:S(2)}, u32[]{:S(2)}) %collective-permute-start.2) | collective-permute-done | bytes 266272 | tf_op jit(solution)/shard_map/cond/branch_1_fun/ppermute | solution.py:320
  20.8 0.4 collective-permute-done.3
  21.2 2.2 %gather.1.x_ref = bf16[2,288,2048]{2,1,0:T(8,128)(2,1)S(1)} custom-call(s32[2]{0:T(128)S(1)} %pad_add_fusion.1.place, bf16[1040,128]{1,0:T(8,128)(2,1)S(1)} %pack.1.refs_0_, bf16[1040,128]{1,0:T(8,128)(2,1)S(1)} %collective-permute-done.4.refs_1_, bf16[1040,128]{1,0:T(8,128)(2,1)S(1)} %collective-permute-done.5.refs_2_, ...), custom_call_target="tpu_custom_call" | custom-call | flops 2000000000 | bytes 1 | tf_op jit(solution)/shard_map/gather/pallas_call | solution.py:284
  23.4 0.7 %copy-done = bf16[2,704,2048]{2,1,0:T(8,128)(2,1)S(1)} copy-done((bf16[2,704,2048]{2,1,0:T(8,128)(2,1)S(1)}, bf16[2,704,2048]{2,1,0:T(8,128)(2,1)}, u32[]{:S(2)}) %copy-start) | copy-done | bytes 5767192
  24.1 2.1 %grad.1 = (bf16[800,128]{1,0:T(8,128)(2,1)S(1)}, bf16[800,128]{1,0:T(8,128)(2,1)S(1)}, bf16[800,128]{1,0:T(8,128)(2,1)S(1)}, bf16[800,128]{1,0:T(8,128)(2,1)S(1)}) custom-call(bf16[2,288,2048]{2,1,0:T(8,128)(2,1)S(1)} %gather.1.x_ref, bf16[2,704,2048]{2,1,0:T(8,128)(2,1)S(1)} %copy-done), custom_call_target="tpu_custom_call" | custom-call | flops 1 | bytes 1 | tf_op jit(solution)/shard_map/grad/pallas_call | solution.py:284
  26.3 0.6 %collective-permute-start.11 = (bf16[800,128]{1,0:T(8,128)(2,1)S(1)}, bf16[800,128]{1,0:T(8,128)(2,1)S(1)}, u32[]{:S(2)}, u32[]{:S(2)}) collective-permute-start(bf16[800,128]{1,0:T(8,128)(2,1)S(1)} %get-tuple-element.70), channel_id=1, source_target_pairs={{0,16},{8,24},{16,0},{24,8},{1,17},{9,25},{17,1},{25,9},{2,18},{10... | collective-permute-start | bytes 614408 | tf_op jit(solution)/shard_map/ppermute | solution.py:317
  26.9 2.4 %collective-permute-start.12 = (bf16[800,128]{1,0:T(8,128)(2,1)S(1)}, bf16[800,128]{1,0:T(8,128)(2,1)S(1)}, u32[]{:S(2)}, u32[]{:S(2)}) collective-permute-start(bf16[800,128]{1,0:T(8,128)(2,1)S(1)} %get-tuple-element.71), channel_id=1, source_target_pairs={{0,24},{8,16},{16,8},{24,0},{1,25},{9,17},{17,9},{25,1},{2,26},{10... | collective-permute-start | bytes 614408 | tf_op jit(solution)/shard_map/ppermute | solution.py:317
  29.2 0.6 %collective-permute-start.19 = (bf16[800,128]{1,0:T(8,128)(2,1)S(1)}, bf16[800,128]{1,0:T(8,128)(2,1)S(1)}, u32[]{:S(2)}, u32[]{:S(2)}) collective-permute-start(bf16[800,128]{1,0:T(8,128)(2,1)S(1)} %get-tuple-element.81), channel_id=1, source_target_pairs={{0,8},{8,0},{16,24},{24,16},{1,9},{9,1},{17,25},{25,17},{2,10},{10... | collective-permute-start | bytes 614408 | tf_op jit(solution)/shard_map/ppermute | solution.py:317
  29.8 0.0 collective-permute-done.8.refs_2_
  29.8 0.0 collective-permute-done.9.refs_3_
  29.8 2.3 %mix_sibling.1 = bf16[512,1024]{1,0:T(8,128)(2,1)S(1)} custom-call(s32[2]{0:T(128)S(1)} %pad_add_fusion.1.place, bf16[816,128]{1,0:T(8,128)(2,1)S(1)} %get-tuple-element.63.refs_0_, bf16[816,128]{1,0:T(8,128)(2,1)S(1)} %collective-permute-done.7.refs_1_, bf16[816,128]{1,0:T(8,128)(2,1)S(1)} %collective-permute-done.8.refs_2_, ...), custom_call_target="tpu_custom_call" | custom-call | flops 1 | bytes 1 | tf_op jit(solution)/shard_map/mix_sibling/pallas_call | solution.py:284
  32.1 0.1 collective-permute-start.10
  32.2 2.3 %mix_own.1.own = f32[512,1024]{1,0:T(8,128)S(1)} custom-call(s32[2]{0:T(128)S(1)} %pad_add_fusion.1.place, bf16[816,128]{1,0:T(8,128)(2,1)S(1)} %get-tuple-element.63.refs_0_, bf16[816,128]{1,0:T(8,128)(2,1)S(1)} %collective-permute-done.7.refs_1_, bf16[816,128]{1,0:T(8,128)(2,1)S(1)} %collective-permute-done.8.refs_2_, ...), custom_call_target="tpu_custom_call" | custom-call | flops 99999997952 | bytes 1 | tf_op jit(solution)/shard_map/mix_own/pallas_call | solution.py:284
  34.5 0.3 collective-permute-done.10.arrived
  34.9 0.2 add.5
  35.1 1.5 %collective-permute-start.14 = (bf16[128,512]{1,0:T(8,128)(2,1)S(1)}, bf16[128,512]{1,0:T(8,128)(2,1)S(1)}, u32[]{:S(2)}, u32[]{:S(2)}) collective-permute-start(bf16[128,512]{1,0:T(8,128)(2,1)S(1)} %get-tuple-element.75), channel_id=1, source_target_pairs={{0,8},{8,0},{16,24},{24,16},{1,9},{9,1},{17,25},{25,17},{2,10},{10... | collective-permute-start | bytes 393224 | tf_op jit(solution)/shard_map/ppermute | solution.py:317
  36.6 0.5 %collective-permute-start.15 = (bf16[128,512]{1,0:T(8,128)(2,1)S(1)}, bf16[128,512]{1,0:T(8,128)(2,1)S(1)}, u32[]{:S(2)}, u32[]{:S(2)}) collective-permute-start(bf16[128,512]{1,0:T(8,128)(2,1)S(1)} %get-tuple-element.76), channel_id=1, source_target_pairs={{0,16},{8,24},{16,0},{24,8},{1,17},{9,25},{17,1},{25,9},{2,18},{10... | collective-permute-start | bytes 393224 | tf_op jit(solution)/shard_map/ppermute | solution.py:317
  37.2 0.7 %collective-permute-done.11.refs_2_ = bf16[800,128]{1,0:T(8,128)(2,1)S(1)} collective-permute-done((bf16[800,128]{1,0:T(8,128)(2,1)S(1)}, bf16[800,128]{1,0:T(8,128)(2,1)S(1)}, u32[]{:S(2)}, u32[]{:S(2)}) %collective-permute-start.11) | collective-permute-done | bytes 204832 | tf_op jit(solution)/shard_map/ppermute | solution.py:317
  37.8 1.4 %collective-permute-start.13 = (bf16[128,512]{1,0:T(8,128)(2,1)S(1)}, bf16[128,512]{1,0:T(8,128)(2,1)S(1)}, u32[]{:S(2)}, u32[]{:S(2)}) collective-permute-start(bf16[128,512]{1,0:T(8,128)(2,1)S(1)} %get-tuple-element.72), channel_id=1, source_target_pairs={{0,8},{8,0},{16,24},{24,16},{1,9},{9,1},{17,25},{25,17},{2,10},{10... | collective-permute-start | bytes 393224 | tf_op jit(solution)/shard_map/ppermute | solution.py:317
  39.3 0.5 %collective-permute-start.18 = (bf16[128,512]{1,0:T(8,128)(2,1)S(1)}, bf16[128,512]{1,0:T(8,128)(2,1)S(1)}, u32[]{:S(2)}, u32[]{:S(2)}) collective-permute-start(bf16[128,512]{1,0:T(8,128)(2,1)S(1)} %get-tuple-element.79), channel_id=1, source_target_pairs={{0,16},{8,24},{16,0},{24,8},{1,17},{9,25},{17,1},{25,9},{2,18},{10... | collective-permute-start | bytes 393224 | tf_op jit(solution)/shard_map/ppermute | solution.py:317
  39.8 3.1 %collective-permute-done.14.low = bf16[128,512]{1,0:T(8,128)(2,1)S(1)} collective-permute-done((bf16[128,512]{1,0:T(8,128)(2,1)S(1)}, bf16[128,512]{1,0:T(8,128)(2,1)S(1)}, u32[]{:S(2)}, u32[]{:S(2)}) %collective-permute-start.14) | collective-permute-done | bytes 131104 | tf_op jit(solution)/shard_map/ppermute | solution.py:317
  43.0 0.0 collective-permute-done.15.high
  43.0 1.5 %collective-permute-start.16 = (bf16[128,512]{1,0:T(8,128)(2,1)S(1)}, bf16[128,512]{1,0:T(8,128)(2,1)S(1)}, u32[]{:S(2)}, u32[]{:S(2)}) collective-permute-start(bf16[128,512]{1,0:T(8,128)(2,1)S(1)} %get-tuple-element.77), channel_id=1, source_target_pairs={{0,8},{8,0},{16,24},{24,16},{1,9},{9,1},{17,25},{25,17},{2,10},{10... | collective-permute-start | bytes 393224 | tf_op jit(solution)/shard_map/ppermute | solution.py:317
  44.5 0.5 %collective-permute-start.17 = (bf16[128,512]{1,0:T(8,128)(2,1)S(1)}, bf16[128,512]{1,0:T(8,128)(2,1)S(1)}, u32[]{:S(2)}, u32[]{:S(2)}) collective-permute-start(bf16[128,512]{1,0:T(8,128)(2,1)S(1)} %get-tuple-element.78), channel_id=1, source_target_pairs={{0,16},{8,24},{16,0},{24,8},{1,17},{9,25},{17,1},{25,9},{2,18},{10... | collective-permute-start | bytes 393224 | tf_op jit(solution)/shard_map/ppermute | solution.py:317
  45.1 2.3 %restore.1 = bf16[4,704,128]{2,1,0:T(8,128)(2,1)} custom-call(s32[2]{0:T(128)S(1)} %pad_add_fusion.1.place, s32[8,128]{1,0:T(8,128)S(1)} %pad_add_fusion.meta_ref, bf16[800,128]{1,0:T(8,128)(2,1)S(1)} %get-tuple-element.80.refs_0_, bf16[800,128]{1,0:T(8,128)(2,1)S(1)} %collective-permute-done.19.refs_1_, ...), custom_call_target="tpu_custom_call" | custom-call | flops 99999997952 | bytes 1 | tf_op jit(solution)/shard_map/restore/pallas_call | solution.py:284
  47.4 0.7 %collective-permute-done.16.one_high = bf16[128,512]{1,0:T(8,128)(2,1)S(1)} collective-permute-done((bf16[128,512]{1,0:T(8,128)(2,1)S(1)}, bf16[128,512]{1,0:T(8,128)(2,1)S(1)}, u32[]{:S(2)}, u32[]{:S(2)}) %collective-permute-start.16) | collective-permute-done | bytes 131104 | tf_op jit(solution)/shard_map/ppermute | solution.py:317
  48.0 1.4 %collective-permute-done.17.two_low = bf16[128,512]{1,0:T(8,128)(2,1)S(1)} collective-permute-done((bf16[128,512]{1,0:T(8,128)(2,1)S(1)}, bf16[128,512]{1,0:T(8,128)(2,1)S(1)}, u32[]{:S(2)}, u32[]{:S(2)}) %collective-permute-start.17) | collective-permute-done | bytes 131104 | tf_op jit(solution)/shard_map/ppermute | solution.py:317
  49.5 0.8 %finish.1 = bf16[128,1024]{1,0:T(8,128)(2,1)} custom-call(f32[128,1024]{1,0:T(8,128)S(1)} %get-tuple-element.67.mine, bf16[128,512]{1,0:T(8,128)(2,1)S(1)} %collective-permute-done.13.one_low, bf16[128,512]{1,0:T(8,128)(2,1)S(1)} %collective-permute-done.16.one_high, bf16[128,512]{1,0:T(8,128)(2,1)S(1)} %collective-permute-done.17.two_low, ...), custom_call_target="tpu_custom_call" | custom-call | flops 1 | bytes 1 | tf_op jit(solution)/shard_map/finish/pallas_call | solution.py:284
  (19 shorter events, 0.1 us)
Async XLA Ops:
  0.6 1.0 %copy-start.2 = (bf16[128,1024]{1,0:T(8,128)(2,1)S(1)}, bf16[128,1024]{1,0:T(8,128)(2,1)}, u32[]{:S(2)}) copy-start(bf16[128,1024]{1,0:T(8,128)(2,1)} %dy_ref.1) | copy-start | bytes 786436
  0.6 5.7 %copy-start.1 = (bf16[128,4,704]{0,2,1:T(8,128)(2,1)S(1)}, bf16[128,4,704]{0,2,1:T(8,128)(2,1)}, u32[]{:S(2)}) copy-start(bf16[128,4,704]{0,2,1:T(8,128)(2,1)} %param.9) | copy-start | bytes 2162692
  0.7 0.8 %copy-start.3 = (s32[128,4]{0,1:T(4,128)S(1)}, s32[128,4]{0,1:T(4,128)}, u32[]{:S(2)}) copy-start(s32[128,4]{0,1:T(4,128)} %param.10) | copy-start | bytes 6148
  1.4 4.9 %copy-start.4 = (s32[128,4]{0,1:T(4,128)S(1)}, s32[128,4]{0,1:T(4,128)}, u32[]{:S(2)}) copy-start(s32[128,4]{0,1:T(4,128)} %param.10) | copy-start | bytes 6148
  1.4 4.9 %copy-start.5 = (s32[128,4]{0,1:T(4,128)S(1)}, s32[128,4]{0,1:T(4,128)}, u32[]{:S(2)}) copy-start(s32[128,4]{0,1:T(4,128)} %param.11) | copy-start | bytes 6148
  1.6 11.2 %collective-permute-start.6 = (bf16[1040,128]{1,0:T(8,128)(2,1)S(1)}, bf16[1040,128]{1,0:T(8,128)(2,1)S(1)}, u32[]{:S(2)}, u32[]{:S(2)}) collective-permute-start(bf16[1040,128]{1,0:T(8,128)(2,1)S(1)} %pack.1.refs_0_), channel_id=1, source_target_pairs={{0,24},{8,16},{16,8},{24,0},{1,25},{9,17},{17,9},{25,1},{2,26},{10... | collective-permute-start | bytes 798728 | tf_op jit(solution)/shard_map/ppermute | solution.py:317
  5.6 13.5 %collective-permute-start.5 = (bf16[1040,128]{1,0:T(8,128)(2,1)S(1)}, bf16[1040,128]{1,0:T(8,128)(2,1)S(1)}, u32[]{:S(2)}, u32[]{:S(2)}) collective-permute-start(bf16[1040,128]{1,0:T(8,128)(2,1)S(1)} %pack.1.refs_0_), channel_id=1, source_target_pairs={{0,16},{8,24},{16,0},{24,8},{1,17},{9,25},{17,1},{25,9},{2,18},{10... | collective-permute-start | bytes 798728 | tf_op jit(solution)/shard_map/ppermute | solution.py:317
  6.1 13.0 %collective-permute-start.4 = (bf16[1040,128]{1,0:T(8,128)(2,1)S(1)}, bf16[1040,128]{1,0:T(8,128)(2,1)S(1)}, u32[]{:S(2)}, u32[]{:S(2)}) collective-permute-start(bf16[1040,128]{1,0:T(8,128)(2,1)S(1)} %pack.1.refs_0_), channel_id=1, source_target_pairs={{0,8},{8,0},{16,24},{24,16},{1,9},{9,1},{17,25},{25,17},{2,10},{10... | collective-permute-start | bytes 798728 | tf_op jit(solution)/shard_map/ppermute | solution.py:317
  7.9 21.3 %collective-permute-start.7 = (bf16[816,128]{1,0:T(8,128)(2,1)S(1)}, bf16[816,128]{1,0:T(8,128)(2,1)S(1)}, u32[]{:S(2)}, u32[]{:S(2)}) collective-permute-start(bf16[816,128]{1,0:T(8,128)(2,1)S(1)} %get-tuple-element.64), channel_id=1, source_target_pairs={{0,8},{8,0},{16,24},{24,16},{1,9},{9,1},{17,25},{25,17},{2,10},{10... | collective-permute-start | bytes 626696 | tf_op jit(solution)/shard_map/ppermute | solution.py:317
  9.9 19.9 %collective-permute-start.8 = (bf16[816,128]{1,0:T(8,128)(2,1)S(1)}, bf16[816,128]{1,0:T(8,128)(2,1)S(1)}, u32[]{:S(2)}, u32[]{:S(2)}) collective-permute-start(bf16[816,128]{1,0:T(8,128)(2,1)S(1)} %get-tuple-element.65), channel_id=1, source_target_pairs={{0,16},{8,24},{16,0},{24,8},{1,17},{9,25},{17,1},{25,9},{2,18},{10... | collective-permute-start | bytes 626696 | tf_op jit(solution)/shard_map/ppermute | solution.py:317
  12.9 1.7 %collective-permute-start = (bf16[1040,128]{1,0:T(8,128)(2,1)S(1)}, bf16[1040,128]{1,0:T(8,128)(2,1)}, u32[]{:S(2)}, u32[]{:S(2)}) collective-permute-start(bf16[1040,128]{1,0:T(8,128)(2,1)S(1)} %get-tuple-element.17), channel_id=1, source_target_pairs={{0,1},{1,0},{2,3},{3,2},{4,5},{5,4},{6,7},{7,6},{8,9},{9,8},{10,11... | collective-permute-start | bytes 798728 | tf_op jit(solution)/shard_map/cond/branch_1_fun/ppermute | solution.py:320
  14.5 1.7 %collective-permute-start.1 = (bf16[1040,128]{1,0:T(8,128)(2,1)S(1)}, bf16[1040,128]{1,0:T(8,128)(2,1)}, u32[]{:S(2)}, u32[]{:S(2)}) collective-permute-start(bf16[1040,128]{1,0:T(8,128)(2,1)S(1)} %get-tuple-element.19), channel_id=1, source_target_pairs={{0,1},{1,0},{2,3},{3,2},{4,5},{5,4},{6,7},{7,6},{8,9},{9,8},{10,11... | collective-permute-start | bytes 798728 | tf_op jit(solution)/shard_map/cond/branch_1_fun/ppermute | solution.py:320
  16.2 13.6 %collective-permute-start.9 = (bf16[816,128]{1,0:T(8,128)(2,1)S(1)}, bf16[816,128]{1,0:T(8,128)(2,1)S(1)}, u32[]{:S(2)}, u32[]{:S(2)}) collective-permute-start(bf16[816,128]{1,0:T(8,128)(2,1)S(1)} %get-tuple-element.66), channel_id=1, source_target_pairs={{0,24},{8,16},{16,8},{24,0},{1,25},{9,17},{17,9},{25,1},{2,26},{10... | collective-permute-start | bytes 626696 | tf_op jit(solution)/shard_map/ppermute | solution.py:317
  19.1 1.7 %collective-permute-start.2 = (bf16[1040,128]{1,0:T(8,128)(2,1)S(1)}, bf16[1040,128]{1,0:T(8,128)(2,1)}, u32[]{:S(2)}, u32[]{:S(2)}) collective-permute-start(bf16[1040,128]{1,0:T(8,128)(2,1)S(1)} %get-tuple-element.20), channel_id=1, source_target_pairs={{0,1},{1,0},{2,3},{3,2},{4,5},{5,4},{6,7},{7,6},{8,9},{9,8},{10,11... | collective-permute-start | bytes 798728 | tf_op jit(solution)/shard_map/cond/branch_1_fun/ppermute | solution.py:320
  19.1 2.0 %collective-permute-start.3 = (bf16[1040,128]{1,0:T(8,128)(2,1)S(1)}, bf16[1040,128]{1,0:T(8,128)(2,1)}, u32[]{:S(2)}, u32[]{:S(2)}) collective-permute-start(bf16[1040,128]{1,0:T(8,128)(2,1)S(1)} %get-tuple-element.21), channel_id=1, source_target_pairs={{0,1},{1,0},{2,3},{3,2},{4,5},{5,4},{6,7},{7,6},{8,9},{9,8},{10,11... | collective-permute-start | bytes 798728 | tf_op jit(solution)/shard_map/cond/branch_1_fun/ppermute | solution.py:320
  21.2 3.0 %copy-start = (bf16[2,704,2048]{2,1,0:T(8,128)(2,1)S(1)}, bf16[2,704,2048]{2,1,0:T(8,128)(2,1)}, u32[]{:S(2)}) copy-start(bf16[2,704,2048]{2,1,0:T(8,128)(2,1)} %refs_4_.3) | copy-start | bytes 17301508
  26.3 11.6 %collective-permute-start.11 = (bf16[800,128]{1,0:T(8,128)(2,1)S(1)}, bf16[800,128]{1,0:T(8,128)(2,1)S(1)}, u32[]{:S(2)}, u32[]{:S(2)}) collective-permute-start(bf16[800,128]{1,0:T(8,128)(2,1)S(1)} %get-tuple-element.70), channel_id=1, source_target_pairs={{0,16},{8,24},{16,0},{24,8},{1,17},{9,25},{17,1},{25,9},{2,18},{10... | collective-permute-start | bytes 614408 | tf_op jit(solution)/shard_map/ppermute | solution.py:317
  26.9 11.0 %collective-permute-start.12 = (bf16[800,128]{1,0:T(8,128)(2,1)S(1)}, bf16[800,128]{1,0:T(8,128)(2,1)S(1)}, u32[]{:S(2)}, u32[]{:S(2)}) collective-permute-start(bf16[800,128]{1,0:T(8,128)(2,1)S(1)} %get-tuple-element.71), channel_id=1, source_target_pairs={{0,24},{8,16},{16,8},{24,0},{1,25},{9,17},{17,9},{25,1},{2,26},{10... | collective-permute-start | bytes 614408 | tf_op jit(solution)/shard_map/ppermute | solution.py:317
  29.2 15.8 %collective-permute-start.19 = (bf16[800,128]{1,0:T(8,128)(2,1)S(1)}, bf16[800,128]{1,0:T(8,128)(2,1)S(1)}, u32[]{:S(2)}, u32[]{:S(2)}) collective-permute-start(bf16[800,128]{1,0:T(8,128)(2,1)S(1)} %get-tuple-element.81), channel_id=1, source_target_pairs={{0,8},{8,0},{16,24},{24,16},{1,9},{9,1},{17,25},{25,17},{2,10},{10... | collective-permute-start | bytes 614408 | tf_op jit(solution)/shard_map/ppermute | solution.py:317
  32.1 2.7 %collective-permute-start.10 = (bf16[512,1024]{1,0:T(8,128)(2,1)S(1)}, bf16[512,1024]{1,0:T(8,128)(2,1)S(1)}, u32[]{:S(2)}, u32[]{:S(2)}) collective-permute-start(bf16[512,1024]{1,0:T(8,128)(2,1)S(1)} %mix_sibling.1), channel_id=1, source_target_pairs={{0,1},{1,0},{2,3},{3,2},{4,5},{5,4},{6,7},{7,6},{8,9},{9,8},{10,11... | collective-permute-start | bytes 3145736 | tf_op jit(solution)/shard_map/ppermute | solution.py:320
  35.1 7.9 %collective-permute-start.14 = (bf16[128,512]{1,0:T(8,128)(2,1)S(1)}, bf16[128,512]{1,0:T(8,128)(2,1)S(1)}, u32[]{:S(2)}, u32[]{:S(2)}) collective-permute-start(bf16[128,512]{1,0:T(8,128)(2,1)S(1)} %get-tuple-element.75), channel_id=1, source_target_pairs={{0,8},{8,0},{16,24},{24,16},{1,9},{9,1},{17,25},{25,17},{2,10},{10... | collective-permute-start | bytes 393224 | tf_op jit(solution)/shard_map/ppermute | solution.py:317
  36.6 6.3 %collective-permute-start.15 = (bf16[128,512]{1,0:T(8,128)(2,1)S(1)}, bf16[128,512]{1,0:T(8,128)(2,1)S(1)}, u32[]{:S(2)}, u32[]{:S(2)}) collective-permute-start(bf16[128,512]{1,0:T(8,128)(2,1)S(1)} %get-tuple-element.76), channel_id=1, source_target_pairs={{0,16},{8,24},{16,0},{24,8},{1,17},{9,25},{17,1},{25,9},{2,18},{10... | collective-permute-start | bytes 393224 | tf_op jit(solution)/shard_map/ppermute | solution.py:317
  37.8 9.5 %collective-permute-start.13 = (bf16[128,512]{1,0:T(8,128)(2,1)S(1)}, bf16[128,512]{1,0:T(8,128)(2,1)S(1)}, u32[]{:S(2)}, u32[]{:S(2)}) collective-permute-start(bf16[128,512]{1,0:T(8,128)(2,1)S(1)} %get-tuple-element.72), channel_id=1, source_target_pairs={{0,8},{8,0},{16,24},{24,16},{1,9},{9,1},{17,25},{25,17},{2,10},{10... | collective-permute-start | bytes 393224 | tf_op jit(solution)/shard_map/ppermute | solution.py:317
  39.3 8.1 %collective-permute-start.18 = (bf16[128,512]{1,0:T(8,128)(2,1)S(1)}, bf16[128,512]{1,0:T(8,128)(2,1)S(1)}, u32[]{:S(2)}, u32[]{:S(2)}) collective-permute-start(bf16[128,512]{1,0:T(8,128)(2,1)S(1)} %get-tuple-element.79), channel_id=1, source_target_pairs={{0,16},{8,24},{16,0},{24,8},{1,17},{9,25},{17,1},{25,9},{2,18},{10... | collective-permute-start | bytes 393224 | tf_op jit(solution)/shard_map/ppermute | solution.py:317
  43.0 5.0 %collective-permute-start.16 = (bf16[128,512]{1,0:T(8,128)(2,1)S(1)}, bf16[128,512]{1,0:T(8,128)(2,1)S(1)}, u32[]{:S(2)}, u32[]{:S(2)}) collective-permute-start(bf16[128,512]{1,0:T(8,128)(2,1)S(1)} %get-tuple-element.77), channel_id=1, source_target_pairs={{0,8},{8,0},{16,24},{24,16},{1,9},{9,1},{17,25},{25,17},{2,10},{10... | collective-permute-start | bytes 393224 | tf_op jit(solution)/shard_map/ppermute | solution.py:317
  44.5 5.0 %collective-permute-start.17 = (bf16[128,512]{1,0:T(8,128)(2,1)S(1)}, bf16[128,512]{1,0:T(8,128)(2,1)S(1)}, u32[]{:S(2)}, u32[]{:S(2)}) collective-permute-start(bf16[128,512]{1,0:T(8,128)(2,1)S(1)} %get-tuple-element.78), channel_id=1, source_target_pairs={{0,16},{8,24},{16,0},{24,8},{1,17},{9,25},{17,1},{25,9},{2,18},{10... | collective-permute-start | bytes 393224 | tf_op jit(solution)/shard_map/ppermute | solution.py:317

commit v17 on v15

--- a/solution.py
+++ b/solution.py
@@ -68,7 +68,22 @@
     return ff // 128 * width + (first if ff % 128 else 0), first
 
 
-def pack_slots(rows, out):
+def lines_of(names, lines):
+    width, lanes = names.shape[1], lines.shape[1]
+    if width % lanes:
+        names = jnp.concatenate([names, jnp.zeros((1, -width % lanes), F32)], axis=1)
+    for i in range(names.shape[1] // lanes):
+        line = names[:, i * lanes : (i + 1) * lanes]
+        lines = jnp.where(iota(lines.shape, 0) == i, line, lines)
+    return lines
+
+
+def spare_fits(width, ff):
+    rest, first = ff % 128, packed_rows(width, ff)[1]
+    return bool(rest) and (2 * first - width) * rest >= -(-width // rest) * rest
+
+
+def pack_slots(rows, out, names=None):
     width, ff = rows.shape
     full, rest = ff // 128, ff % 128
     for c in range(full):
@@ -79,6 +94,8 @@
         right = tail[first:]
         if right.shape[0] < first:
             spare = jnp.zeros((first - right.shape[0], rest), F32)
+            if names is not None:
+                spare = lines_of(names, spare)
             right = jnp.concatenate([right, spare], axis=0)
         pair = jnp.concatenate([tail[:first], right], axis=1)
         out[full * width : end, :] = pair.astype(BF16)
@@ -118,16 +135,13 @@
     number = number.astype(F32).astype(BF16)
     for s, out in enumerate(outs):
         at = slice(s * width, (s + 1) * width)
-        pack_slots(sent[at], out)
         names = dot(number, picks[at], NT)[:1]
-        if width % 128:
-            spare = jnp.zeros((1, -width % 128), F32)
-            names = jnp.concatenate([names, spare], axis=1)
-        lines = jnp.zeros((16, 128), F32)
-        for i in range(names.shape[1] // 128):
-            line = names[:, i * 128 : (i + 1) * 128]
-            lines = jnp.where(iota((16, 128), 0) == i, line, lines)
-        out[out.shape[0] - 16 :, :] = lines.astype(BF16)
+        if spare_fits(width, sent.shape[1]):
+            pack_slots(sent[at], out, names)
+        else:
+            pack_slots(sent[at], out)
+            lines = lines_of(names, jnp.zeros((16, 128), F32))
+            out[out.shape[0] - 16 :, :] = lines.astype(BF16)
 
 
 def names_kernel(ids_ref, out):
@@ -197,11 +211,17 @@
     chunk = min(half, 256)
     held, rows = [], []
     for h in hid:
-        lines = h[h.shape[0] - 16 :, :].astype(F32)
-        names = jnp.concatenate(
-            [lines[i // 128 : i // 128 + 1, : min(128, width - i)] for i in range(0, width, 128)],
-            axis=1,
-        )
+        if spare_fits(width, ff):
+            end, first = packed_rows(width, ff)
+            lines = h[end - first : end, :].astype(F32)[width - first :, ff % 128 :]
+        else:
+            lines = h[h.shape[0] - 16 :, :].astype(F32)
+        lanes = lines.shape[1]
+        names = [
+            lines[i // lanes : i // lanes + 1, : min(lanes, width - i)]
+            for i in range(0, width, lanes)
+        ]
+        names = jnp.concatenate(names, axis=1)
         held.append(ones_where(iota((tokens, width), 0) == names.astype(jnp.int32) - 1))
         rows.append(unpack_slots(h, width, ff))
     x = [r.astype(BF16) for r in by_expert(rows, local, cap)]
@@ -329,8 +349,9 @@
     )
     forward = n == 4
     own = [send(packed, s) for s in range(n)]
+    tail = 0 if spare_fits(width, ff) else 16
     hid_sent = run(
-        functools.partial(dispatch_kernel, dims), [shaped((packed_rows(width, ff)[0] + 16, 128))] * n,
+        functools.partial(dispatch_kernel, dims), [shaped((packed_rows(width, ff)[0] + tail, 128))] * n,
         [place, meta, hid_t], where=placed, name="dispatch",
     )
     hid = [send(hid_sent[s], s) for s in range(n)]

time: 49.6 us -> 49.6 us (level)
  no operation moved by 1% of the time
where the time goes in v17:
time: 49.6 us; the launch traced here: 49.5 us
  starting transfers between devices  19.1 us (39%)
  Pallas kernels  14.1 us (28%)
  waiting for transfers between devices  13.9 us (28%)
  local copies, waits for them, and re-layouts  1.64 us (3%)
  between operations  0.73 us (1%)
    ppermute x15, starting transfers between devices, send(): return lax.ppermute(x, 'ctx', [(i, i ^ s) for i in range(n)]) if s else x  18.3 us
    pallas_call x11, Pallas kernels, call(): pl.pallas_call(kernel, out_shape=outs, in_specs=[pl.BlockSpec(memory_spac...  14.1 us
    ppermute x15, waiting for transfers between devices, send(): return lax.ppermute(x, 'ctx', [(i, i ^ s) for i in range(n)]) if s else x  8.79 us
    ppermute x5, waiting for transfers between devices, swap(): return lax.ppermute(x, 'tp', [(0, 1), (1, 0)])  5.1 us
    unnamed x12, local copies, waits for them, and re-layouts  1.64 us
  transfers between devices with their start and end apart: 20, of which 11 were waited for; matrix products, arithmetic and copies ran while one was open for 0% of the time, Pallas kernels for 27%

profile of v17, /device:TPU:0, one launch (start us, length us, event | category | flops | bytes accessed | tf_op | source)
XLA Modules:
  0.0 49.5 jit_solution(8875100990990351223)
XLA Ops:
  0.7 0.8 %copy-done.3 = s32[128,4]{0,1:T(4,128)S(1)} copy-done((s32[128,4]{0,1:T(4,128)S(1)}, s32[128,4]{0,1:T(4,128)}, u32[]{:S(2)}) %copy-start.3) | copy-done | bytes 2072
  1.4 0.2 copy-done.2
  1.6 4.0 %collective-permute-start.6 = (bf16[1040,128]{1,0:T(8,128)(2,1)S(1)}, bf16[1040,128]{1,0:T(8,128)(2,1)S(1)}, u32[]{:S(2)}, u32[]{:S(2)}) collective-permute-start(bf16[1040,128]{1,0:T(8,128)(2,1)S(1)} %pack.1.refs_0_), channel_id=1, source_target_pairs={{0,24},{8,16},{16,8},{24,0},{1,25},{9,17},{17,9},{25,1},{2,26},{10... | collective-permute-start | bytes 798728 | tf_op jit(solution)/shard_map/ppermute | solution.py:337
  5.6 0.5 %collective-permute-start.5 = (bf16[1040,128]{1,0:T(8,128)(2,1)S(1)}, bf16[1040,128]{1,0:T(8,128)(2,1)S(1)}, u32[]{:S(2)}, u32[]{:S(2)}) collective-permute-start(bf16[1040,128]{1,0:T(8,128)(2,1)S(1)} %pack.1.refs_0_), channel_id=1, source_target_pairs={{0,16},{8,24},{16,0},{24,8},{1,17},{9,25},{17,1},{25,9},{2,18},{10... | collective-permute-start | bytes 798728 | tf_op jit(solution)/shard_map/ppermute | solution.py:337
  6.1 0.1 collective-permute-start.4
  6.2 0.1 pad_add_fusion.1.place
  6.3 1.7 %dispatch.1 = (bf16[800,128]{1,0:T(8,128)(2,1)S(1)}, bf16[800,128]{1,0:T(8,128)(2,1)S(1)}, bf16[800,128]{1,0:T(8,128)(2,1)S(1)}, bf16[800,128]{1,0:T(8,128)(2,1)S(1)}) custom-call(s32[2]{0:T(128)S(1)} %pad_add_fusion.1.place, s32[8,128]{1,0:T(8,128)S(1)} %pad_add_fusion.meta_ref, bf16[4,704,128]{2,1,0:T(8,128)(2,1)S(1)} %bitcast.6), custom_call_target="tpu_custom_call" | custom-call | flops 1 | bytes 1 | tf_op jit(solution)/shard_map/dispatch/pallas_call | solution.py:304
  8.0 1.9 %collective-permute-start.7 = (bf16[800,128]{1,0:T(8,128)(2,1)S(1)}, bf16[800,128]{1,0:T(8,128)(2,1)S(1)}, u32[]{:S(2)}, u32[]{:S(2)}) collective-permute-start(bf16[800,128]{1,0:T(8,128)(2,1)S(1)} %get-tuple-element.64), channel_id=1, source_target_pairs={{0,8},{8,0},{16,24},{24,16},{1,9},{9,1},{17,25},{25,17},{2,10},{10... | collective-permute-start | bytes 614408 | tf_op jit(solution)/shard_map/ppermute | solution.py:337
  9.9 1.5 %collective-permute-start.8 = (bf16[800,128]{1,0:T(8,128)(2,1)S(1)}, bf16[800,128]{1,0:T(8,128)(2,1)S(1)}, u32[]{:S(2)}, u32[]{:S(2)}) collective-permute-start(bf16[800,128]{1,0:T(8,128)(2,1)S(1)} %get-tuple-element.65), channel_id=1, source_target_pairs={{0,16},{8,24},{16,0},{24,8},{1,17},{9,25},{17,1},{25,9},{2,18},{10... | collective-permute-start | bytes 614408 | tf_op jit(solution)/shard_map/ppermute | solution.py:337
  11.5 1.4 %collective-permute-done.6.refs_3_ = bf16[1040,128]{1,0:T(8,128)(2,1)S(1)} collective-permute-done((bf16[1040,128]{1,0:T(8,128)(2,1)S(1)}, bf16[1040,128]{1,0:T(8,128)(2,1)S(1)}, u32[]{:S(2)}, u32[]{:S(2)}) %collective-permute-start.6) | collective-permute-done | bytes 266272 | tf_op jit(solution)/shard_map/ppermute | solution.py:337
  12.9 3.3 %conditional.2 = (bf16[1040,128]{1,0:T(8,128)(2,1)}, bf16[1040,128]{1,0:T(8,128)(2,1)}) conditional(s32[]{:T(128)} %convert_element_type.4, (bf16[1040,128]{1,0:T(8,128)(2,1)S(1)}, bf16[1040,128]{1,0:T(8,128)(2,1)S(1)}) %tuple.26, (bf16[1040,128]{1,0:T(8,128)(2,1)S(1)}, bf16[1040,128]{1,0:T(8,128)(2,1)S(1)}) %tuple.26), branch_computations={%region_0.0_spmd, %region_1.0_spmd} | conditional | bytes 2130016 | solution.py:370
  12.9 0.0 collective-permute-start
  12.9 1.7 %collective-permute-done = bf16[1040,128]{1,0:T(8,128)(2,1)} collective-permute-done((bf16[1040,128]{1,0:T(8,128)(2,1)S(1)}, bf16[1040,128]{1,0:T(8,128)(2,1)}, u32[]{:S(2)}, u32[]{:S(2)}) %collective-permute-start) | collective-permute-done | bytes 266272 | tf_op jit(solution)/shard_map/cond/branch_1_fun/ppermute | solution.py:340
  14.5 0.1 collective-permute-start.1
  14.7 1.5 %collective-permute-done.1 = bf16[1040,128]{1,0:T(8,128)(2,1)} collective-permute-done((bf16[1040,128]{1,0:T(8,128)(2,1)S(1)}, bf16[1040,128]{1,0:T(8,128)(2,1)}, u32[]{:S(2)}, u32[]{:S(2)}) %collective-permute-start.1) | collective-permute-done | bytes 266272 | tf_op jit(solution)/shard_map/cond/branch_1_fun/ppermute | solution.py:340
  16.2 2.9 %collective-permute-start.9 = (bf16[800,128]{1,0:T(8,128)(2,1)S(1)}, bf16[800,128]{1,0:T(8,128)(2,1)S(1)}, u32[]{:S(2)}, u32[]{:S(2)}) collective-permute-start(bf16[800,128]{1,0:T(8,128)(2,1)S(1)} %get-tuple-element.66), channel_id=1, source_target_pairs={{0,24},{8,16},{16,8},{24,0},{1,25},{9,17},{17,9},{25,1},{2,26},{10... | collective-permute-start | bytes 614408 | tf_op jit(solution)/shard_map/ppermute | solution.py:337
  19.1 0.0 collective-permute-done.4.refs_1_
  19.1 2.1 %conditional.3 = (bf16[1040,128]{1,0:T(8,128)(2,1)}, bf16[1040,128]{1,0:T(8,128)(2,1)}) conditional(s32[]{:T(128)} %convert_element_type.4, (bf16[1040,128]{1,0:T(8,128)(2,1)S(1)}, bf16[1040,128]{1,0:T(8,128)(2,1)S(1)}) %tuple.28, (bf16[1040,128]{1,0:T(8,128)(2,1)S(1)}, bf16[1040,128]{1,0:T(8,128)(2,1)S(1)}) %tuple.28), branch_computations={%region_2.0_spmd, %region_3.0_spmd} | conditional | bytes 2130016 | solution.py:372
  19.1 0.0 collective-permute-start.2
  19.1 0.5 %collective-permute-start.3 = (bf16[1040,128]{1,0:T(8,128)(2,1)S(1)}, bf16[1040,128]{1,0:T(8,128)(2,1)}, u32[]{:S(2)}, u32[]{:S(2)}) collective-permute-start(bf16[1040,128]{1,0:T(8,128)(2,1)S(1)} %get-tuple-element.21), channel_id=1, source_target_pairs={{0,1},{1,0},{2,3},{3,2},{4,5},{5,4},{6,7},{7,6},{8,9},{9,8},{10,11... | collective-permute-start | bytes 798728 | tf_op jit(solution)/shard_map/cond/branch_1_fun/ppermute | solution.py:340
  19.6 1.2 %collective-permute-done.2 = bf16[1040,128]{1,0:T(8,128)(2,1)} collective-permute-done((bf16[1040,128]{1,0:T(8,128)(2,1)S(1)}, bf16[1040,128]{1,0:T(8,128)(2,1)}, u32[]{:S(2)}, u32[]{:S(2)}) %collective-permute-start.2) | collective-permute-done | bytes 266272 | tf_op jit(solution)/shard_map/cond/branch_1_fun/ppermute | solution.py:340
  20.8 0.4 collective-permute-done.3
  21.2 2.2 %gather.1.x_ref = bf16[2,288,2048]{2,1,0:T(8,128)(2,1)S(1)} custom-call(s32[2]{0:T(128)S(1)} %pad_add_fusion.1.place, bf16[1040,128]{1,0:T(8,128)(2,1)S(1)} %pack.1.refs_0_, bf16[1040,128]{1,0:T(8,128)(2,1)S(1)} %collective-permute-done.4.refs_1_, bf16[1040,128]{1,0:T(8,128)(2,1)S(1)} %collective-permute-done.5.refs_2_, ...), custom_call_target="tpu_custom_call" | custom-call | flops 2000000000 | bytes 1 | tf_op jit(solution)/shard_map/gather/pallas_call | solution.py:304
  23.4 0.7 %copy-done = bf16[2,704,2048]{2,1,0:T(8,128)(2,1)S(1)} copy-done((bf16[2,704,2048]{2,1,0:T(8,128)(2,1)S(1)}, bf16[2,704,2048]{2,1,0:T(8,128)(2,1)}, u32[]{:S(2)}) %copy-start) | copy-done | bytes 5767192
  24.1 2.1 %grad.1 = (bf16[800,128]{1,0:T(8,128)(2,1)S(1)}, bf16[800,128]{1,0:T(8,128)(2,1)S(1)}, bf16[800,128]{1,0:T(8,128)(2,1)S(1)}, bf16[800,128]{1,0:T(8,128)(2,1)S(1)}) custom-call(bf16[2,288,2048]{2,1,0:T(8,128)(2,1)S(1)} %gather.1.x_ref, bf16[2,704,2048]{2,1,0:T(8,128)(2,1)S(1)} %copy-done), custom_call_target="tpu_custom_call" | custom-call | flops 1 | bytes 1 | tf_op jit(solution)/shard_map/grad/pallas_call | solution.py:304
  26.3 1.5 %collective-permute-start.11 = (bf16[800,128]{1,0:T(8,128)(2,1)S(1)}, bf16[800,128]{1,0:T(8,128)(2,1)S(1)}, u32[]{:S(2)}, u32[]{:S(2)}) collective-permute-start(bf16[800,128]{1,0:T(8,128)(2,1)S(1)} %get-tuple-element.70), channel_id=1, source_target_pairs={{0,8},{8,0},{16,24},{24,16},{1,9},{9,1},{17,25},{25,17},{2,10},{10... | collective-permute-start | bytes 614408 | tf_op jit(solution)/shard_map/ppermute | solution.py:337
  27.8 0.5 %collective-permute-start.12 = (bf16[800,128]{1,0:T(8,128)(2,1)S(1)}, bf16[800,128]{1,0:T(8,128)(2,1)S(1)}, u32[]{:S(2)}, u32[]{:S(2)}) collective-permute-start(bf16[800,128]{1,0:T(8,128)(2,1)S(1)} %get-tuple-element.71), channel_id=1, source_target_pairs={{0,16},{8,24},{16,0},{24,8},{1,17},{9,25},{17,1},{25,9},{2,18},{10... | collective-permute-start | bytes 614408 | tf_op jit(solution)/shard_map/ppermute | solution.py:337
  28.3 0.0 collective-permute-done.7.refs_1_
  28.3 1.5 %collective-permute-start.19 = (bf16[800,128]{1,0:T(8,128)(2,1)S(1)}, bf16[800,128]{1,0:T(8,128)(2,1)S(1)}, u32[]{:S(2)}, u32[]{:S(2)}) collective-permute-start(bf16[800,128]{1,0:T(8,128)(2,1)S(1)} %get-tuple-element.83), channel_id=1, source_target_pairs={{0,24},{8,16},{16,8},{24,0},{1,25},{9,17},{17,9},{25,1},{2,26},{10... | collective-permute-start | bytes 614408 | tf_op jit(solution)/shard_map/ppermute | solution.py:337
  29.8 2.3 %mix_sibling.1 = bf16[512,1024]{1,0:T(8,128)(2,1)S(1)} custom-call(s32[2]{0:T(128)S(1)} %pad_add_fusion.1.place, bf16[800,128]{1,0:T(8,128)(2,1)S(1)} %get-tuple-element.63.refs_0_, bf16[800,128]{1,0:T(8,128)(2,1)S(1)} %collective-permute-done.7.refs_1_, bf16[800,128]{1,0:T(8,128)(2,1)S(1)} %collective-permute-done.8.refs_2_, ...), custom_call_target="tpu_custom_call" | custom-call | flops 1 | bytes 1 | tf_op jit(solution)/shard_map/mix_sibling/pallas_call | solution.py:304
  32.1 0.1 collective-permute-start.10
  32.2 2.3 %mix_own.1.own = f32[512,1024]{1,0:T(8,128)S(1)} custom-call(s32[2]{0:T(128)S(1)} %pad_add_fusion.1.place, bf16[800,128]{1,0:T(8,128)(2,1)S(1)} %get-tuple-element.63.refs_0_, bf16[800,128]{1,0:T(8,128)(2,1)S(1)} %collective-permute-done.7.refs_1_, bf16[800,128]{1,0:T(8,128)(2,1)S(1)} %collective-permute-done.8.refs_2_, ...), custom_call_target="tpu_custom_call" | custom-call | flops 99999997952 | bytes 1 | tf_op jit(solution)/shard_map/mix_own/pallas_call | solution.py:304
  34.5 0.4 collective-permute-done.10.arrived
  34.9 0.2 add.5
  35.1 1.5 %collective-permute-start.14 = (bf16[128,512]{1,0:T(8,128)(2,1)S(1)}, bf16[128,512]{1,0:T(8,128)(2,1)S(1)}, u32[]{:S(2)}, u32[]{:S(2)}) collective-permute-start(bf16[128,512]{1,0:T(8,128)(2,1)S(1)} %get-tuple-element.75), channel_id=1, source_target_pairs={{0,8},{8,0},{16,24},{24,16},{1,9},{9,1},{17,25},{25,17},{2,10},{10... | collective-permute-start | bytes 393224 | tf_op jit(solution)/shard_map/ppermute | solution.py:337
  36.6 0.5 %collective-permute-start.15 = (bf16[128,512]{1,0:T(8,128)(2,1)S(1)}, bf16[128,512]{1,0:T(8,128)(2,1)S(1)}, u32[]{:S(2)}, u32[]{:S(2)}) collective-permute-start(bf16[128,512]{1,0:T(8,128)(2,1)S(1)} %get-tuple-element.76), channel_id=1, source_target_pairs={{0,16},{8,24},{16,0},{24,8},{1,17},{9,25},{17,1},{25,9},{2,18},{10... | collective-permute-start | bytes 393224 | tf_op jit(solution)/shard_map/ppermute | solution.py:337
  37.2 1.8 %collective-permute-done.12.refs_2_ = bf16[800,128]{1,0:T(8,128)(2,1)S(1)} collective-permute-done((bf16[800,128]{1,0:T(8,128)(2,1)S(1)}, bf16[800,128]{1,0:T(8,128)(2,1)S(1)}, u32[]{:S(2)}, u32[]{:S(2)}) %collective-permute-start.12) | collective-permute-done | bytes 204832 | tf_op jit(solution)/shard_map/ppermute | solution.py:337
  39.0 0.6 %collective-permute-start.13 = (bf16[128,512]{1,0:T(8,128)(2,1)S(1)}, bf16[128,512]{1,0:T(8,128)(2,1)S(1)}, u32[]{:S(2)}, u32[]{:S(2)}) collective-permute-start(bf16[128,512]{1,0:T(8,128)(2,1)S(1)} %get-tuple-element.72), channel_id=1, source_target_pairs={{0,8},{8,0},{16,24},{24,16},{1,9},{9,1},{17,25},{25,17},{2,10},{10... | collective-permute-start | bytes 393224 | tf_op jit(solution)/shard_map/ppermute | solution.py:337
  39.6 1.9 %collective-permute-done.14.low = bf16[128,512]{1,0:T(8,128)(2,1)S(1)} collective-permute-done((bf16[128,512]{1,0:T(8,128)(2,1)S(1)}, bf16[128,512]{1,0:T(8,128)(2,1)S(1)}, u32[]{:S(2)}, u32[]{:S(2)}) %collective-permute-start.14) | collective-permute-done | bytes 131104 | tf_op jit(solution)/shard_map/ppermute | solution.py:337
  41.5 1.5 %collective-permute-done.15.high = bf16[128,512]{1,0:T(8,128)(2,1)S(1)} collective-permute-done((bf16[128,512]{1,0:T(8,128)(2,1)S(1)}, bf16[128,512]{1,0:T(8,128)(2,1)S(1)}, u32[]{:S(2)}, u32[]{:S(2)}) %collective-permute-start.15) | collective-permute-done | bytes 131104 | tf_op jit(solution)/shard_map/ppermute | solution.py:337
  43.0 0.6 %collective-permute-start.16 = (bf16[128,512]{1,0:T(8,128)(2,1)S(1)}, bf16[128,512]{1,0:T(8,128)(2,1)S(1)}, u32[]{:S(2)}, u32[]{:S(2)}) collective-permute-start(bf16[128,512]{1,0:T(8,128)(2,1)S(1)} %get-tuple-element.77), channel_id=1, source_target_pairs={{0,8},{8,0},{16,24},{24,16},{1,9},{9,1},{17,25},{25,17},{2,10},{10... | collective-permute-start | bytes 393224 | tf_op jit(solution)/shard_map/ppermute | solution.py:337
  43.7 0.5 %collective-permute-start.17 = (bf16[128,512]{1,0:T(8,128)(2,1)S(1)}, bf16[128,512]{1,0:T(8,128)(2,1)S(1)}, u32[]{:S(2)}, u32[]{:S(2)}) collective-permute-start(bf16[128,512]{1,0:T(8,128)(2,1)S(1)} %get-tuple-element.78), channel_id=1, source_target_pairs={{0,16},{8,24},{16,0},{24,8},{1,17},{9,25},{17,1},{25,9},{2,18},{10... | collective-permute-start | bytes 393224 | tf_op jit(solution)/shard_map/ppermute | solution.py:337
  44.2 0.0 collective-permute-done.19.refs_3_
  44.2 2.3 %restore.1 = bf16[4,704,128]{2,1,0:T(8,128)(2,1)} custom-call(s32[2]{0:T(128)S(1)} %pad_add_fusion.1.place, s32[8,128]{1,0:T(8,128)S(1)} %pad_add_fusion.meta_ref, bf16[800,128]{1,0:T(8,128)(2,1)S(1)} %get-tuple-element.80.refs_0_, bf16[800,128]{1,0:T(8,128)(2,1)S(1)} %collective-permute-done.11.refs_1_, ...), custom_call_target="tpu_custom_call" | custom-call | flops 99999997952 | bytes 1 | tf_op jit(solution)/shard_map/restore/pallas_call | solution.py:304
  46.5 0.0 collective-permute-done.13.one_low
  46.5 1.5 %collective-permute-done.16.one_high = bf16[128,512]{1,0:T(8,128)(2,1)S(1)} collective-permute-done((bf16[128,512]{1,0:T(8,128)(2,1)S(1)}, bf16[128,512]{1,0:T(8,128)(2,1)S(1)}, u32[]{:S(2)}, u32[]{:S(2)}) %collective-permute-start.16) | collective-permute-done | bytes 131104 | tf_op jit(solution)/shard_map/ppermute | solution.py:337
  48.1 0.6 %collective-permute-done.17.two_low = bf16[128,512]{1,0:T(8,128)(2,1)S(1)} collective-permute-done((bf16[128,512]{1,0:T(8,128)(2,1)S(1)}, bf16[128,512]{1,0:T(8,128)(2,1)S(1)}, u32[]{:S(2)}, u32[]{:S(2)}) %collective-permute-start.17) | collective-permute-done | bytes 131104 | tf_op jit(solution)/shard_map/ppermute | solution.py:337
  48.7 0.8 %finish.1 = bf16[128,1024]{1,0:T(8,128)(2,1)} custom-call(f32[128,1024]{1,0:T(8,128)S(1)} %get-tuple-element.67.mine, bf16[128,512]{1,0:T(8,128)(2,1)S(1)} %collective-permute-done.13.one_low, bf16[128,512]{1,0:T(8,128)(2,1)S(1)} %collective-permute-done.16.one_high, bf16[128,512]{1,0:T(8,128)(2,1)S(1)} %collective-permute-done.17.two_low, ...), custom_call_target="tpu_custom_call" | custom-call | flops 1 | bytes 1 | tf_op jit(solution)/shard_map/finish/pallas_call | solution.py:304
  (19 shorter events, 0.1 us)
Async XLA Ops:
  0.6 1.0 %copy-start.2 = (bf16[128,1024]{1,0:T(8,128)(2,1)S(1)}, bf16[128,1024]{1,0:T(8,128)(2,1)}, u32[]{:S(2)}) copy-start(bf16[128,1024]{1,0:T(8,128)(2,1)} %dy_ref.1) | copy-start | bytes 786436
  0.6 5.7 %copy-start.1 = (bf16[128,4,704]{0,2,1:T(8,128)(2,1)S(1)}, bf16[128,4,704]{0,2,1:T(8,128)(2,1)}, u32[]{:S(2)}) copy-start(bf16[128,4,704]{0,2,1:T(8,128)(2,1)} %param.9) | copy-start | bytes 2162692
  0.7 0.8 %copy-start.3 = (s32[128,4]{0,1:T(4,128)S(1)}, s32[128,4]{0,1:T(4,128)}, u32[]{:S(2)}) copy-start(s32[128,4]{0,1:T(4,128)} %param.10) | copy-start | bytes 6148
  1.4 4.9 %copy-start.4 = (s32[128,4]{0,1:T(4,128)S(1)}, s32[128,4]{0,1:T(4,128)}, u32[]{:S(2)}) copy-start(s32[128,4]{0,1:T(4,128)} %param.10) | copy-start | bytes 6148
  1.4 4.9 %copy-start.5 = (s32[128,4]{0,1:T(4,128)S(1)}, s32[128,4]{0,1:T(4,128)}, u32[]{:S(2)}) copy-start(s32[128,4]{0,1:T(4,128)} %param.11) | copy-start | bytes 6148
  1.6 11.2 %collective-permute-start.6 = (bf16[1040,128]{1,0:T(8,128)(2,1)S(1)}, bf16[1040,128]{1,0:T(8,128)(2,1)S(1)}, u32[]{:S(2)}, u32[]{:S(2)}) collective-permute-start(bf16[1040,128]{1,0:T(8,128)(2,1)S(1)} %pack.1.refs_0_), channel_id=1, source_target_pairs={{0,24},{8,16},{16,8},{24,0},{1,25},{9,17},{17,9},{25,1},{2,26},{10... | collective-permute-start | bytes 798728 | tf_op jit(solution)/shard_map/ppermute | solution.py:337
  5.6 13.5 %collective-permute-start.5 = (bf16[1040,128]{1,0:T(8,128)(2,1)S(1)}, bf16[1040,128]{1,0:T(8,128)(2,1)S(1)}, u32[]{:S(2)}, u32[]{:S(2)}) collective-permute-start(bf16[1040,128]{1,0:T(8,128)(2,1)S(1)} %pack.1.refs_0_), channel_id=1, source_target_pairs={{0,16},{8,24},{16,0},{24,8},{1,17},{9,25},{17,1},{25,9},{2,18},{10... | collective-permute-start | bytes 798728 | tf_op jit(solution)/shard_map/ppermute | solution.py:337
  6.1 13.0 %collective-permute-start.4 = (bf16[1040,128]{1,0:T(8,128)(2,1)S(1)}, bf16[1040,128]{1,0:T(8,128)(2,1)S(1)}, u32[]{:S(2)}, u32[]{:S(2)}) collective-permute-start(bf16[1040,128]{1,0:T(8,128)(2,1)S(1)} %pack.1.refs_0_), channel_id=1, source_target_pairs={{0,8},{8,0},{16,24},{24,16},{1,9},{9,1},{17,25},{25,17},{2,10},{10... | collective-permute-start | bytes 798728 | tf_op jit(solution)/shard_map/ppermute | solution.py:337
  8.0 20.3 %collective-permute-start.7 = (bf16[800,128]{1,0:T(8,128)(2,1)S(1)}, bf16[800,128]{1,0:T(8,128)(2,1)S(1)}, u32[]{:S(2)}, u32[]{:S(2)}) collective-permute-start(bf16[800,128]{1,0:T(8,128)(2,1)S(1)} %get-tuple-element.64), channel_id=1, source_target_pairs={{0,8},{8,0},{16,24},{24,16},{1,9},{9,1},{17,25},{25,17},{2,10},{10... | collective-permute-start | bytes 614408 | tf_op jit(solution)/shard_map/ppermute | solution.py:337
  9.9 19.9 %collective-permute-start.8 = (bf16[800,128]{1,0:T(8,128)(2,1)S(1)}, bf16[800,128]{1,0:T(8,128)(2,1)S(1)}, u32[]{:S(2)}, u32[]{:S(2)}) collective-permute-start(bf16[800,128]{1,0:T(8,128)(2,1)S(1)} %get-tuple-element.65), channel_id=1, source_target_pairs={{0,16},{8,24},{16,0},{24,8},{1,17},{9,25},{17,1},{25,9},{2,18},{10... | collective-permute-start | bytes 614408 | tf_op jit(solution)/shard_map/ppermute | solution.py:337
  12.9 1.7 %collective-permute-start = (bf16[1040,128]{1,0:T(8,128)(2,1)S(1)}, bf16[1040,128]{1,0:T(8,128)(2,1)}, u32[]{:S(2)}, u32[]{:S(2)}) collective-permute-start(bf16[1040,128]{1,0:T(8,128)(2,1)S(1)} %get-tuple-element.17), channel_id=1, source_target_pairs={{0,1},{1,0},{2,3},{3,2},{4,5},{5,4},{6,7},{7,6},{8,9},{9,8},{10,11... | collective-permute-start | bytes 798728 | tf_op jit(solution)/shard_map/cond/branch_1_fun/ppermute | solution.py:340
  14.5 1.7 %collective-permute-start.1 = (bf16[1040,128]{1,0:T(8,128)(2,1)S(1)}, bf16[1040,128]{1,0:T(8,128)(2,1)}, u32[]{:S(2)}, u32[]{:S(2)}) collective-permute-start(bf16[1040,128]{1,0:T(8,128)(2,1)S(1)} %get-tuple-element.19), channel_id=1, source_target_pairs={{0,1},{1,0},{2,3},{3,2},{4,5},{5,4},{6,7},{7,6},{8,9},{9,8},{10,11... | collective-permute-start | bytes 798728 | tf_op jit(solution)/shard_map/cond/branch_1_fun/ppermute | solution.py:340
  16.2 13.6 %collective-permute-start.9 = (bf16[800,128]{1,0:T(8,128)(2,1)S(1)}, bf16[800,128]{1,0:T(8,128)(2,1)S(1)}, u32[]{:S(2)}, u32[]{:S(2)}) collective-permute-start(bf16[800,128]{1,0:T(8,128)(2,1)S(1)} %get-tuple-element.66), channel_id=1, source_target_pairs={{0,24},{8,16},{16,8},{24,0},{1,25},{9,17},{17,9},{25,1},{2,26},{10... | collective-permute-start | bytes 614408 | tf_op jit(solution)/shard_map/ppermute | solution.py:337
  19.1 1.7 %collective-permute-start.2 = (bf16[1040,128]{1,0:T(8,128)(2,1)S(1)}, bf16[1040,128]{1,0:T(8,128)(2,1)}, u32[]{:S(2)}, u32[]{:S(2)}) collective-permute-start(bf16[1040,128]{1,0:T(8,128)(2,1)S(1)} %get-tuple-element.20), channel_id=1, source_target_pairs={{0,1},{1,0},{2,3},{3,2},{4,5},{5,4},{6,7},{7,6},{8,9},{9,8},{10,11... | collective-permute-start | bytes 798728 | tf_op jit(solution)/shard_map/cond/branch_1_fun/ppermute | solution.py:340
  19.1 2.0 %collective-permute-start.3 = (bf16[1040,128]{1,0:T(8,128)(2,1)S(1)}, bf16[1040,128]{1,0:T(8,128)(2,1)}, u32[]{:S(2)}, u32[]{:S(2)}) collective-permute-start(bf16[1040,128]{1,0:T(8,128)(2,1)S(1)} %get-tuple-element.21), channel_id=1, source_target_pairs={{0,1},{1,0},{2,3},{3,2},{4,5},{5,4},{6,7},{7,6},{8,9},{9,8},{10,11... | collective-permute-start | bytes 798728 | tf_op jit(solution)/shard_map/cond/branch_1_fun/ppermute | solution.py:340
  21.2 3.0 %copy-start = (bf16[2,704,2048]{2,1,0:T(8,128)(2,1)S(1)}, bf16[2,704,2048]{2,1,0:T(8,128)(2,1)}, u32[]{:S(2)}) copy-start(bf16[2,704,2048]{2,1,0:T(8,128)(2,1)} %refs_4_.3) | copy-start | bytes 17301508
  26.3 10.9 %collective-permute-start.11 = (bf16[800,128]{1,0:T(8,128)(2,1)S(1)}, bf16[800,128]{1,0:T(8,128)(2,1)S(1)}, u32[]{:S(2)}, u32[]{:S(2)}) collective-permute-start(bf16[800,128]{1,0:T(8,128)(2,1)S(1)} %get-tuple-element.70), channel_id=1, source_target_pairs={{0,8},{8,0},{16,24},{24,16},{1,9},{9,1},{17,25},{25,17},{2,10},{10... | collective-permute-start | bytes 614408 | tf_op jit(solution)/shard_map/ppermute | solution.py:337
  27.8 11.2 %collective-permute-start.12 = (bf16[800,128]{1,0:T(8,128)(2,1)S(1)}, bf16[800,128]{1,0:T(8,128)(2,1)S(1)}, u32[]{:S(2)}, u32[]{:S(2)}) collective-permute-start(bf16[800,128]{1,0:T(8,128)(2,1)S(1)} %get-tuple-element.71), channel_id=1, source_target_pairs={{0,16},{8,24},{16,0},{24,8},{1,17},{9,25},{17,1},{25,9},{2,18},{10... | collective-permute-start | bytes 614408 | tf_op jit(solution)/shard_map/ppermute | solution.py:337
  28.3 15.9 %collective-permute-start.19 = (bf16[800,128]{1,0:T(8,128)(2,1)S(1)}, bf16[800,128]{1,0:T(8,128)(2,1)S(1)}, u32[]{:S(2)}, u32[]{:S(2)}) collective-permute-start(bf16[800,128]{1,0:T(8,128)(2,1)S(1)} %get-tuple-element.83), channel_id=1, source_target_pairs={{0,24},{8,16},{16,8},{24,0},{1,25},{9,17},{17,9},{25,1},{2,26},{10... | collective-permute-start | bytes 614408 | tf_op jit(solution)/shard_map/ppermute | solution.py:337
  32.1 2.7 %collective-permute-start.10 = (bf16[512,1024]{1,0:T(8,128)(2,1)S(1)}, bf16[512,1024]{1,0:T(8,128)(2,1)S(1)}, u32[]{:S(2)}, u32[]{:S(2)}) collective-permute-start(bf16[512,1024]{1,0:T(8,128)(2,1)S(1)} %mix_sibling.1), channel_id=1, source_target_pairs={{0,1},{1,0},{2,3},{3,2},{4,5},{5,4},{6,7},{7,6},{8,9},{9,8},{10,11... | collective-permute-start | bytes 3145736 | tf_op jit(solution)/shard_map/ppermute | solution.py:340
  35.1 6.4 %collective-permute-start.14 = (bf16[128,512]{1,0:T(8,128)(2,1)S(1)}, bf16[128,512]{1,0:T(8,128)(2,1)S(1)}, u32[]{:S(2)}, u32[]{:S(2)}) collective-permute-start(bf16[128,512]{1,0:T(8,128)(2,1)S(1)} %get-tuple-element.75), channel_id=1, source_target_pairs={{0,8},{8,0},{16,24},{24,16},{1,9},{9,1},{17,25},{25,17},{2,10},{10... | collective-permute-start | bytes 393224 | tf_op jit(solution)/shard_map/ppermute | solution.py:337
  36.6 6.4 %collective-permute-start.15 = (bf16[128,512]{1,0:T(8,128)(2,1)S(1)}, bf16[128,512]{1,0:T(8,128)(2,1)S(1)}, u32[]{:S(2)}, u32[]{:S(2)}) collective-permute-start(bf16[128,512]{1,0:T(8,128)(2,1)S(1)} %get-tuple-element.76), channel_id=1, source_target_pairs={{0,16},{8,24},{16,0},{24,8},{1,17},{9,25},{17,1},{25,9},{2,18},{10... | collective-permute-start | bytes 393224 | tf_op jit(solution)/shard_map/ppermute | solution.py:337
  39.0 7.5 %collective-permute-start.13 = (bf16[128,512]{1,0:T(8,128)(2,1)S(1)}, bf16[128,512]{1,0:T(8,128)(2,1)S(1)}, u32[]{:S(2)}, u32[]{:S(2)}) collective-permute-start(bf16[128,512]{1,0:T(8,128)(2,1)S(1)} %get-tuple-element.72), channel_id=1, source_target_pairs={{0,8},{8,0},{16,24},{24,16},{1,9},{9,1},{17,25},{25,17},{2,10},{10... | collective-permute-start | bytes 393224 | tf_op jit(solution)/shard_map/ppermute | solution.py:337
  39.6 6.9 %collective-permute-start.18 = (bf16[128,512]{1,0:T(8,128)(2,1)S(1)}, bf16[128,512]{1,0:T(8,128)(2,1)S(1)}, u32[]{:S(2)}, u32[]{:S(2)}) collective-permute-start(bf16[128,512]{1,0:T(8,128)(2,1)S(1)} %get-tuple-element.79), channel_id=1, source_target_pairs={{0,16},{8,24},{16,0},{24,8},{1,17},{9,25},{17,1},{25,9},{2,18},{10... | collective-permute-start | bytes 393224 | tf_op jit(solution)/shard_map/ppermute | solution.py:337
  43.0 5.0 %collective-permute-start.16 = (bf16[128,512]{1,0:T(8,128)(2,1)S(1)}, bf16[128,512]{1,0:T(8,128)(2,1)S(1)}, u32[]{:S(2)}, u32[]{:S(2)}) collective-permute-start(bf16[128,512]{1,0:T(8,128)(2,1)S(1)} %get-tuple-element.77), channel_id=1, source_target_pairs={{0,8},{8,0},{16,24},{24,16},{1,9},{9,1},{17,25},{25,17},{2,10},{10... | collective-permute-start | bytes 393224 | tf_op jit(solution)/shard_map/ppermute | solution.py:337
  43.7 5.0 %collective-permute-start.17 = (bf16[128,512]{1,0:T(8,128)(2,1)S(1)}, bf16[128,512]{1,0:T(8,128)(2,1)S(1)}, u32[]{:S(2)}, u32[]{:S(2)}) collective-permute-start(bf16[128,512]{1,0:T(8,128)(2,1)S(1)} %get-tuple-element.78), channel_id=1, source_target_pairs={{0,16},{8,24},{16,0},{24,8},{1,17},{9,25},{17,1},{25,9},{2,18},{10... | collective-permute-start | bytes 393224 | tf_op jit(solution)/shard_map/ppermute | solution.py:337

commit v18 on v17

--- a/solution.py
+++ b/solution.py
@@ -271,12 +271,12 @@
     high[...] = parts[3][:, cut:].astype(BF16)
 
 
-def join_kernel(one_high, two_low, low, high, to_one, to_two):
+def join_kernel(high, low, one_high, two_low, to_one, to_two):
     to_one[...] = (one_high[...] + high[...].astype(F32)).astype(BF16)
     to_two[...] = (two_low[...] + low[...].astype(F32)).astype(BF16)
 
 
-def finish_kernel(mine, one_low, one_high, two_low, two_high, out):
+def finish_kernel(two_high, two_low, one_low, one_high, mine, out):
     cut = one_low.shape[1]
     for at, one, two in ((0, one_low, two_low), (cut, one_high, two_high)):
         total = mine[:, at : at + cut] + one[...].astype(F32) + two[...].astype(F32)
@@ -400,17 +400,18 @@
             add_split_kernel, [kept, piece, wide, wide, piece, piece, piece],
             [mine, arrived], name="add",
         )
-        low, high = send(low, 1), send(high, 2)
+        high, low = send(high, 2), send(low, 1)
         one_low, two_high, *grad_back[1:3] = lax.optimization_barrier(
             (one_low, two_high, *grad_back[1:3])
         )
-        one_low, two_high = send(one_low, 1), send(two_high, 2)
+        two_high, one_low = send(two_high, 2), send(one_low, 1)
         to_one, to_two = run(
-            join_kernel, [piece] * 2, [one_high, two_low, low, high], name="join"
-        )
+            join_kernel, [piece] * 2, [high, low, one_high, two_low], name="join"
+        )
+        to_two, to_one = send(to_two, 2), send(to_one, 1)
         (mixed,) = run(
             finish_kernel, [shaped((tokens, half))],
-            [kept, one_low, send(to_one, 1), send(to_two, 2), two_high], name="finish",
+            [two_high, to_two, one_low, to_one, kept], name="finish",
         )
     else:
         sums = run(

time: 49.6 us -> 49.6 us (level)
  waiting for transfers between devices: 13.9 us -> 13.4 us
  transfers between devices with their start and end apart: 20 -> 20, of which waited for: 11 -> 10; matrix products, arithmetic and copies ran while one was open for 0% -> 0% of each run, Pallas kernels for 27% -> 27%
where the time goes in v18:
time: 49.6 us; the launch traced here: 49.5 us
  starting transfers between devices  19.5 us (39%)
  Pallas kernels  14.1 us (28%)
  waiting for transfers between devices  13.4 us (27%)
  local copies, waits for them, and re-layouts  1.64 us (3%)
  between operations  0.73 us (1%)
    ppermute x15, starting transfers between devices, send(): return lax.ppermute(x, 'ctx', [(i, i ^ s) for i in range(n)]) if s else x  18.8 us
    pallas_call x11, Pallas kernels, call(): pl.pallas_call(kernel, out_shape=outs, in_specs=[pl.BlockSpec(memory_spac...  14.1 us
    ppermute x15, waiting for transfers between devices, send(): return lax.ppermute(x, 'ctx', [(i, i ^ s) for i in range(n)]) if s else x  8.3 us
    ppermute x5, waiting for transfers between devices, swap(): return lax.ppermute(x, 'tp', [(0, 1), (1, 0)])  5.1 us
    unnamed x12, local copies, waits for them, and re-layouts  1.64 us
  transfers between devices with their start and end apart: 20, of which 10 were waited for; matrix products, arithmetic and copies ran while one was open for 0% of the time, Pallas kernels for 27%

profile of v18, /device:TPU:0, one launch (start us, length us, event | category | flops | bytes accessed | tf_op | source)
XLA Modules:
  0.0 49.5 jit_solution(1331914876776194385)
XLA Ops:
  0.7 0.8 %copy-done.3 = s32[128,4]{0,1:T(4,128)S(1)} copy-done((s32[128,4]{0,1:T(4,128)S(1)}, s32[128,4]{0,1:T(4,128)}, u32[]{:S(2)}) %copy-start.3) | copy-done | bytes 2072
  1.4 0.2 copy-done.2
  1.6 4.0 %collective-permute-start.6 = (bf16[1040,128]{1,0:T(8,128)(2,1)S(1)}, bf16[1040,128]{1,0:T(8,128)(2,1)S(1)}, u32[]{:S(2)}, u32[]{:S(2)}) collective-permute-start(bf16[1040,128]{1,0:T(8,128)(2,1)S(1)} %pack.1.refs_0_), channel_id=1, source_target_pairs={{0,24},{8,16},{16,8},{24,0},{1,25},{9,17},{17,9},{25,1},{2,26},{10... | collective-permute-start | bytes 798728 | tf_op jit(solution)/shard_map/ppermute | solution.py:337
  5.6 0.5 %collective-permute-start.5 = (bf16[1040,128]{1,0:T(8,128)(2,1)S(1)}, bf16[1040,128]{1,0:T(8,128)(2,1)S(1)}, u32[]{:S(2)}, u32[]{:S(2)}) collective-permute-start(bf16[1040,128]{1,0:T(8,128)(2,1)S(1)} %pack.1.refs_0_), channel_id=1, source_target_pairs={{0,16},{8,24},{16,0},{24,8},{1,17},{9,25},{17,1},{25,9},{2,18},{10... | collective-permute-start | bytes 798728 | tf_op jit(solution)/shard_map/ppermute | solution.py:337
  6.1 0.1 collective-permute-start.4
  6.2 0.1 pad_add_fusion.1.place
  6.3 1.7 %dispatch.1 = (bf16[800,128]{1,0:T(8,128)(2,1)S(1)}, bf16[800,128]{1,0:T(8,128)(2,1)S(1)}, bf16[800,128]{1,0:T(8,128)(2,1)S(1)}, bf16[800,128]{1,0:T(8,128)(2,1)S(1)}) custom-call(s32[2]{0:T(128)S(1)} %pad_add_fusion.1.place, s32[8,128]{1,0:T(8,128)S(1)} %pad_add_fusion.meta_ref, bf16[4,704,128]{2,1,0:T(8,128)(2,1)S(1)} %bitcast.6), custom_call_target="tpu_custom_call" | custom-call | flops 1 | bytes 1 | tf_op jit(solution)/shard_map/dispatch/pallas_call | solution.py:304
  8.0 1.9 %collective-permute-start.7 = (bf16[800,128]{1,0:T(8,128)(2,1)S(1)}, bf16[800,128]{1,0:T(8,128)(2,1)S(1)}, u32[]{:S(2)}, u32[]{:S(2)}) collective-permute-start(bf16[800,128]{1,0:T(8,128)(2,1)S(1)} %get-tuple-element.64), channel_id=1, source_target_pairs={{0,8},{8,0},{16,24},{24,16},{1,9},{9,1},{17,25},{25,17},{2,10},{10... | collective-permute-start | bytes 614408 | tf_op jit(solution)/shard_map/ppermute | solution.py:337
  9.9 1.5 %collective-permute-start.8 = (bf16[800,128]{1,0:T(8,128)(2,1)S(1)}, bf16[800,128]{1,0:T(8,128)(2,1)S(1)}, u32[]{:S(2)}, u32[]{:S(2)}) collective-permute-start(bf16[800,128]{1,0:T(8,128)(2,1)S(1)} %get-tuple-element.65), channel_id=1, source_target_pairs={{0,16},{8,24},{16,0},{24,8},{1,17},{9,25},{17,1},{25,9},{2,18},{10... | collective-permute-start | bytes 614408 | tf_op jit(solution)/shard_map/ppermute | solution.py:337
  11.5 1.4 %collective-permute-done.6.refs_3_ = bf16[1040,128]{1,0:T(8,128)(2,1)S(1)} collective-permute-done((bf16[1040,128]{1,0:T(8,128)(2,1)S(1)}, bf16[1040,128]{1,0:T(8,128)(2,1)S(1)}, u32[]{:S(2)}, u32[]{:S(2)}) %collective-permute-start.6) | collective-permute-done | bytes 266272 | tf_op jit(solution)/shard_map/ppermute | solution.py:337
  12.9 3.3 %conditional.2 = (bf16[1040,128]{1,0:T(8,128)(2,1)}, bf16[1040,128]{1,0:T(8,128)(2,1)}) conditional(s32[]{:T(128)} %convert_element_type.4, (bf16[1040,128]{1,0:T(8,128)(2,1)S(1)}, bf16[1040,128]{1,0:T(8,128)(2,1)S(1)}) %tuple.26, (bf16[1040,128]{1,0:T(8,128)(2,1)S(1)}, bf16[1040,128]{1,0:T(8,128)(2,1)S(1)}) %tuple.26), branch_computations={%region_0.0_spmd, %region_1.0_spmd} | conditional | bytes 2130016 | solution.py:370
  12.9 0.0 collective-permute-start
  12.9 1.7 %collective-permute-done = bf16[1040,128]{1,0:T(8,128)(2,1)} collective-permute-done((bf16[1040,128]{1,0:T(8,128)(2,1)S(1)}, bf16[1040,128]{1,0:T(8,128)(2,1)}, u32[]{:S(2)}, u32[]{:S(2)}) %collective-permute-start) | collective-permute-done | bytes 266272 | tf_op jit(solution)/shard_map/cond/branch_1_fun/ppermute | solution.py:340
  14.5 0.1 collective-permute-start.1
  14.7 1.5 %collective-permute-done.1 = bf16[1040,128]{1,0:T(8,128)(2,1)} collective-permute-done((bf16[1040,128]{1,0:T(8,128)(2,1)S(1)}, bf16[1040,128]{1,0:T(8,128)(2,1)}, u32[]{:S(2)}, u32[]{:S(2)}) %collective-permute-start.1) | collective-permute-done | bytes 266272 | tf_op jit(solution)/shard_map/cond/branch_1_fun/ppermute | solution.py:340
  16.2 2.9 %collective-permute-start.9 = (bf16[800,128]{1,0:T(8,128)(2,1)S(1)}, bf16[800,128]{1,0:T(8,128)(2,1)S(1)}, u32[]{:S(2)}, u32[]{:S(2)}) collective-permute-start(bf16[800,128]{1,0:T(8,128)(2,1)S(1)} %get-tuple-element.66), channel_id=1, source_target_pairs={{0,24},{8,16},{16,8},{24,0},{1,25},{9,17},{17,9},{25,1},{2,26},{10... | collective-permute-start | bytes 614408 | tf_op jit(solution)/shard_map/ppermute | solution.py:337
  19.1 0.0 collective-permute-done.4.refs_1_
  19.1 2.1 %conditional.3 = (bf16[1040,128]{1,0:T(8,128)(2,1)}, bf16[1040,128]{1,0:T(8,128)(2,1)}) conditional(s32[]{:T(128)} %convert_element_type.4, (bf16[1040,128]{1,0:T(8,128)(2,1)S(1)}, bf16[1040,128]{1,0:T(8,128)(2,1)S(1)}) %tuple.28, (bf16[1040,128]{1,0:T(8,128)(2,1)S(1)}, bf16[1040,128]{1,0:T(8,128)(2,1)S(1)}) %tuple.28), branch_computations={%region_2.0_spmd, %region_3.0_spmd} | conditional | bytes 2130016 | solution.py:372
  19.1 0.0 collective-permute-start.2
  19.1 0.5 %collective-permute-start.3 = (bf16[1040,128]{1,0:T(8,128)(2,1)S(1)}, bf16[1040,128]{1,0:T(8,128)(2,1)}, u32[]{:S(2)}, u32[]{:S(2)}) collective-permute-start(bf16[1040,128]{1,0:T(8,128)(2,1)S(1)} %get-tuple-element.21), channel_id=1, source_target_pairs={{0,1},{1,0},{2,3},{3,2},{4,5},{5,4},{6,7},{7,6},{8,9},{9,8},{10,11... | collective-permute-start | bytes 798728 | tf_op jit(solution)/shard_map/cond/branch_1_fun/ppermute | solution.py:340
  19.6 1.2 %collective-permute-done.2 = bf16[1040,128]{1,0:T(8,128)(2,1)} collective-permute-done((bf16[1040,128]{1,0:T(8,128)(2,1)S(1)}, bf16[1040,128]{1,0:T(8,128)(2,1)}, u32[]{:S(2)}, u32[]{:S(2)}) %collective-permute-start.2) | collective-permute-done | bytes 266272 | tf_op jit(solution)/shard_map/cond/branch_1_fun/ppermute | solution.py:340
  20.8 0.4 collective-permute-done.3
  21.2 2.2 %gather.1.x_ref = bf16[2,288,2048]{2,1,0:T(8,128)(2,1)S(1)} custom-call(s32[2]{0:T(128)S(1)} %pad_add_fusion.1.place, bf16[1040,128]{1,0:T(8,128)(2,1)S(1)} %pack.1.refs_0_, bf16[1040,128]{1,0:T(8,128)(2,1)S(1)} %collective-permute-done.4.refs_1_, bf16[1040,128]{1,0:T(8,128)(2,1)S(1)} %collective-permute-done.5.refs_2_, ...), custom_call_target="tpu_custom_call" | custom-call | flops 2000000000 | bytes 1 | tf_op jit(solution)/shard_map/gather/pallas_call | solution.py:304
  23.4 0.7 %copy-done = bf16[2,704,2048]{2,1,0:T(8,128)(2,1)S(1)} copy-done((bf16[2,704,2048]{2,1,0:T(8,128)(2,1)S(1)}, bf16[2,704,2048]{2,1,0:T(8,128)(2,1)}, u32[]{:S(2)}) %copy-start) | copy-done | bytes 5767192
  24.1 2.1 %grad.1 = (bf16[800,128]{1,0:T(8,128)(2,1)S(1)}, bf16[800,128]{1,0:T(8,128)(2,1)S(1)}, bf16[800,128]{1,0:T(8,128)(2,1)S(1)}, bf16[800,128]{1,0:T(8,128)(2,1)S(1)}) custom-call(bf16[2,288,2048]{2,1,0:T(8,128)(2,1)S(1)} %gather.1.x_ref, bf16[2,704,2048]{2,1,0:T(8,128)(2,1)S(1)} %copy-done), custom_call_target="tpu_custom_call" | custom-call | flops 1 | bytes 1 | tf_op jit(solution)/shard_map/grad/pallas_call | solution.py:304
  26.3 1.5 %collective-permute-start.11 = (bf16[800,128]{1,0:T(8,128)(2,1)S(1)}, bf16[800,128]{1,0:T(8,128)(2,1)S(1)}, u32[]{:S(2)}, u32[]{:S(2)}) collective-permute-start(bf16[800,128]{1,0:T(8,128)(2,1)S(1)} %get-tuple-element.69), channel_id=1, source_target_pairs={{0,8},{8,0},{16,24},{24,16},{1,9},{9,1},{17,25},{25,17},{2,10},{10... | collective-permute-start | bytes 614408 | tf_op jit(solution)/shard_map/ppermute | solution.py:337
  27.8 0.5 %collective-permute-start.12 = (bf16[800,128]{1,0:T(8,128)(2,1)S(1)}, bf16[800,128]{1,0:T(8,128)(2,1)S(1)}, u32[]{:S(2)}, u32[]{:S(2)}) collective-permute-start(bf16[800,128]{1,0:T(8,128)(2,1)S(1)} %get-tuple-element.70), channel_id=1, source_target_pairs={{0,16},{8,24},{16,0},{24,8},{1,17},{9,25},{17,1},{25,9},{2,18},{10... | collective-permute-start | bytes 614408 | tf_op jit(solution)/shard_map/ppermute | solution.py:337
  28.3 0.0 collective-permute-done.7.refs_1_
  28.3 1.5 %collective-permute-start.19 = (bf16[800,128]{1,0:T(8,128)(2,1)S(1)}, bf16[800,128]{1,0:T(8,128)(2,1)S(1)}, u32[]{:S(2)}, u32[]{:S(2)}) collective-permute-start(bf16[800,128]{1,0:T(8,128)(2,1)S(1)} %get-tuple-element.83), channel_id=1, source_target_pairs={{0,24},{8,16},{16,8},{24,0},{1,25},{9,17},{17,9},{25,1},{2,26},{10... | collective-permute-start | bytes 614408 | tf_op jit(solution)/shard_map/ppermute | solution.py:337
  29.8 2.3 %mix_sibling.1 = bf16[512,1024]{1,0:T(8,128)(2,1)S(1)} custom-call(s32[2]{0:T(128)S(1)} %pad_add_fusion.1.place, bf16[800,128]{1,0:T(8,128)(2,1)S(1)} %get-tuple-element.63.refs_0_, bf16[800,128]{1,0:T(8,128)(2,1)S(1)} %collective-permute-done.7.refs_1_, bf16[800,128]{1,0:T(8,128)(2,1)S(1)} %collective-permute-done.8.refs_2_, ...), custom_call_target="tpu_custom_call" | custom-call | flops 1 | bytes 1 | tf_op jit(solution)/shard_map/mix_sibling/pallas_call | solution.py:304
  32.1 0.1 collective-permute-start.10
  32.2 2.3 %mix_own.1.own = f32[512,1024]{1,0:T(8,128)S(1)} custom-call(s32[2]{0:T(128)S(1)} %pad_add_fusion.1.place, bf16[800,128]{1,0:T(8,128)(2,1)S(1)} %get-tuple-element.63.refs_0_, bf16[800,128]{1,0:T(8,128)(2,1)S(1)} %collective-permute-done.7.refs_1_, bf16[800,128]{1,0:T(8,128)(2,1)S(1)} %collective-permute-done.8.refs_2_, ...), custom_call_target="tpu_custom_call" | custom-call | flops 99999997952 | bytes 1 | tf_op jit(solution)/shard_map/mix_own/pallas_call | solution.py:304
  34.5 0.4 collective-permute-done.10.arrived
  34.9 0.2 add.5
  35.1 0.6 %collective-permute-start.14 = (bf16[128,512]{1,0:T(8,128)(2,1)S(1)}, bf16[128,512]{1,0:T(8,128)(2,1)S(1)}, u32[]{:S(2)}, u32[]{:S(2)}) collective-permute-start(bf16[128,512]{1,0:T(8,128)(2,1)S(1)} %get-tuple-element.72), channel_id=1, source_target_pairs={{0,16},{8,24},{16,0},{24,8},{1,17},{9,25},{17,1},{25,9},{2,18},{10... | collective-permute-start | bytes 393224 | tf_op jit(solution)/shard_map/ppermute | solution.py:337
  35.7 1.5 %collective-permute-start.15 = (bf16[128,512]{1,0:T(8,128)(2,1)S(1)}, bf16[128,512]{1,0:T(8,128)(2,1)S(1)}, u32[]{:S(2)}, u32[]{:S(2)}) collective-permute-start(bf16[128,512]{1,0:T(8,128)(2,1)S(1)} %get-tuple-element.73), channel_id=1, source_target_pairs={{0,8},{8,0},{16,24},{24,16},{1,9},{9,1},{17,25},{25,17},{2,10},{10... | collective-permute-start | bytes 393224 | tf_op jit(solution)/shard_map/ppermute | solution.py:337
  37.2 2.9 %collective-permute-done.12.refs_2_ = bf16[800,128]{1,0:T(8,128)(2,1)S(1)} collective-permute-done((bf16[800,128]{1,0:T(8,128)(2,1)S(1)}, bf16[800,128]{1,0:T(8,128)(2,1)S(1)}, u32[]{:S(2)}, u32[]{:S(2)}) %collective-permute-start.12) | collective-permute-done | bytes 204832 | tf_op jit(solution)/shard_map/ppermute | solution.py:337
  40.0 0.0 collective-permute-start.17
  40.0 2.8 %collective-permute-done.14.high = bf16[128,512]{1,0:T(8,128)(2,1)S(1)} collective-permute-done((bf16[128,512]{1,0:T(8,128)(2,1)S(1)}, bf16[128,512]{1,0:T(8,128)(2,1)S(1)}, u32[]{:S(2)}, u32[]{:S(2)}) %collective-permute-start.14) | collective-permute-done | bytes 131104 | tf_op jit(solution)/shard_map/ppermute | solution.py:337
  42.8 0.0 collective-permute-done.15.low
  42.9 0.8 %collective-permute-start.16 = (bf16[128,512]{1,0:T(8,128)(2,1)S(1)}, bf16[128,512]{1,0:T(8,128)(2,1)S(1)}, u32[]{:S(2)}, u32[]{:S(2)}) collective-permute-start(bf16[128,512]{1,0:T(8,128)(2,1)S(1)} %get-tuple-element.76), channel_id=1, source_target_pairs={{0,16},{8,24},{16,0},{24,8},{1,17},{9,25},{17,1},{25,9},{2,18},{10... | collective-permute-start | bytes 393224 | tf_op jit(solution)/shard_map/ppermute | solution.py:337
  43.7 1.4 %collective-permute-start.18 = (bf16[128,512]{1,0:T(8,128)(2,1)S(1)}, bf16[128,512]{1,0:T(8,128)(2,1)S(1)}, u32[]{:S(2)}, u32[]{:S(2)}) collective-permute-start(bf16[128,512]{1,0:T(8,128)(2,1)S(1)} %get-tuple-element.78), channel_id=1, source_target_pairs={{0,8},{8,0},{16,24},{24,16},{1,9},{9,1},{17,25},{25,17},{2,10},{10... | collective-permute-start | bytes 393224 | tf_op jit(solution)/shard_map/ppermute | solution.py:337
  45.1 2.3 %restore.1 = bf16[4,704,128]{2,1,0:T(8,128)(2,1)} custom-call(s32[2]{0:T(128)S(1)} %pad_add_fusion.1.place, s32[8,128]{1,0:T(8,128)S(1)} %pad_add_fusion.meta_ref, bf16[800,128]{1,0:T(8,128)(2,1)S(1)} %get-tuple-element.80.refs_0_, bf16[800,128]{1,0:T(8,128)(2,1)S(1)} %collective-permute-done.11.refs_1_, ...), custom_call_target="tpu_custom_call" | custom-call | flops 99999997952 | bytes 1 | tf_op jit(solution)/shard_map/restore/pallas_call | solution.py:304
  47.4 0.0 collective-permute-done.13.two_high
  47.4 0.0 collective-permute-done.17.one_low
  47.4 0.5 collective-permute-done.16.two_low
  47.9 0.7 %collective-permute-done.18.one_high = bf16[128,512]{1,0:T(8,128)(2,1)S(1)} collective-permute-done((bf16[128,512]{1,0:T(8,128)(2,1)S(1)}, bf16[128,512]{1,0:T(8,128)(2,1)S(1)}, u32[]{:S(2)}, u32[]{:S(2)}) %collective-permute-start.18) | collective-permute-done | bytes 131104 | tf_op jit(solution)/shard_map/ppermute | solution.py:337
  48.7 0.8 %finish.1 = bf16[128,1024]{1,0:T(8,128)(2,1)} custom-call(bf16[128,512]{1,0:T(8,128)(2,1)S(1)} %collective-permute-done.13.two_high, bf16[128,512]{1,0:T(8,128)(2,1)S(1)} %collective-permute-done.16.two_low, bf16[128,512]{1,0:T(8,128)(2,1)S(1)} %collective-permute-done.17.one_low, bf16[128,512]{1,0:T(8,128)(2,1)S(1)} %collective-permute-done.18.one_high, ...), custom_call_target="tpu_custom_call" | custom-call | flops 1 | bytes 1 | tf_op jit(solution)/shard_map/finish/pallas_call | solution.py:304
  (19 shorter events, 0.1 us)
Async XLA Ops:
  0.6 1.0 %copy-start.2 = (bf16[128,1024]{1,0:T(8,128)(2,1)S(1)}, bf16[128,1024]{1,0:T(8,128)(2,1)}, u32[]{:S(2)}) copy-start(bf16[128,1024]{1,0:T(8,128)(2,1)} %dy_ref.1) | copy-start | bytes 786436
  0.6 5.7 %copy-start.1 = (bf16[128,4,704]{0,2,1:T(8,128)(2,1)S(1)}, bf16[128,4,704]{0,2,1:T(8,128)(2,1)}, u32[]{:S(2)}) copy-start(bf16[128,4,704]{0,2,1:T(8,128)(2,1)} %param.9) | copy-start | bytes 2162692
  0.7 0.8 %copy-start.3 = (s32[128,4]{0,1:T(4,128)S(1)}, s32[128,4]{0,1:T(4,128)}, u32[]{:S(2)}) copy-start(s32[128,4]{0,1:T(4,128)} %param.10) | copy-start | bytes 6148
  1.4 4.9 %copy-start.4 = (s32[128,4]{0,1:T(4,128)S(1)}, s32[128,4]{0,1:T(4,128)}, u32[]{:S(2)}) copy-start(s32[128,4]{0,1:T(4,128)} %param.10) | copy-start | bytes 6148
  1.4 4.9 %copy-start.5 = (s32[128,4]{0,1:T(4,128)S(1)}, s32[128,4]{0,1:T(4,128)}, u32[]{:S(2)}) copy-start(s32[128,4]{0,1:T(4,128)} %param.11) | copy-start | bytes 6148
  1.6 11.2 %collective-permute-start.6 = (bf16[1040,128]{1,0:T(8,128)(2,1)S(1)}, bf16[1040,128]{1,0:T(8,128)(2,1)S(1)}, u32[]{:S(2)}, u32[]{:S(2)}) collective-permute-start(bf16[1040,128]{1,0:T(8,128)(2,1)S(1)} %pack.1.refs_0_), channel_id=1, source_target_pairs={{0,24},{8,16},{16,8},{24,0},{1,25},{9,17},{17,9},{25,1},{2,26},{10... | collective-permute-start | bytes 798728 | tf_op jit(solution)/shard_map/ppermute | solution.py:337
  5.6 13.5 %collective-permute-start.5 = (bf16[1040,128]{1,0:T(8,128)(2,1)S(1)}, bf16[1040,128]{1,0:T(8,128)(2,1)S(1)}, u32[]{:S(2)}, u32[]{:S(2)}) collective-permute-start(bf16[1040,128]{1,0:T(8,128)(2,1)S(1)} %pack.1.refs_0_), channel_id=1, source_target_pairs={{0,16},{8,24},{16,0},{24,8},{1,17},{9,25},{17,1},{25,9},{2,18},{10... | collective-permute-start | bytes 798728 | tf_op jit(solution)/shard_map/ppermute | solution.py:337
  6.1 13.0 %collective-permute-start.4 = (bf16[1040,128]{1,0:T(8,128)(2,1)S(1)}, bf16[1040,128]{1,0:T(8,128)(2,1)S(1)}, u32[]{:S(2)}, u32[]{:S(2)}) collective-permute-start(bf16[1040,128]{1,0:T(8,128)(2,1)S(1)} %pack.1.refs_0_), channel_id=1, source_target_pairs={{0,8},{8,0},{16,24},{24,16},{1,9},{9,1},{17,25},{25,17},{2,10},{10... | collective-permute-start | bytes 798728 | tf_op jit(solution)/shard_map/ppermute | solution.py:337
  8.0 20.3 %collective-permute-start.7 = (bf16[800,128]{1,0:T(8,128)(2,1)S(1)}, bf16[800,128]{1,0:T(8,128)(2,1)S(1)}, u32[]{:S(2)}, u32[]{:S(2)}) collective-permute-start(bf16[800,128]{1,0:T(8,128)(2,1)S(1)} %get-tuple-element.64), channel_id=1, source_target_pairs={{0,8},{8,0},{16,24},{24,16},{1,9},{9,1},{17,25},{25,17},{2,10},{10... | collective-permute-start | bytes 614408 | tf_op jit(solution)/shard_map/ppermute | solution.py:337
  9.9 19.9 %collective-permute-start.8 = (bf16[800,128]{1,0:T(8,128)(2,1)S(1)}, bf16[800,128]{1,0:T(8,128)(2,1)S(1)}, u32[]{:S(2)}, u32[]{:S(2)}) collective-permute-start(bf16[800,128]{1,0:T(8,128)(2,1)S(1)} %get-tuple-element.65), channel_id=1, source_target_pairs={{0,16},{8,24},{16,0},{24,8},{1,17},{9,25},{17,1},{25,9},{2,18},{10... | collective-permute-start | bytes 614408 | tf_op jit(solution)/shard_map/ppermute | solution.py:337
  12.9 1.7 %collective-permute-start = (bf16[1040,128]{1,0:T(8,128)(2,1)S(1)}, bf16[1040,128]{1,0:T(8,128)(2,1)}, u32[]{:S(2)}, u32[]{:S(2)}) collective-permute-start(bf16[1040,128]{1,0:T(8,128)(2,1)S(1)} %get-tuple-element.17), channel_id=1, source_target_pairs={{0,1},{1,0},{2,3},{3,2},{4,5},{5,4},{6,7},{7,6},{8,9},{9,8},{10,11... | collective-permute-start | bytes 798728 | tf_op jit(solution)/shard_map/cond/branch_1_fun/ppermute | solution.py:340
  14.5 1.7 %collective-permute-start.1 = (bf16[1040,128]{1,0:T(8,128)(2,1)S(1)}, bf16[1040,128]{1,0:T(8,128)(2,1)}, u32[]{:S(2)}, u32[]{:S(2)}) collective-permute-start(bf16[1040,128]{1,0:T(8,128)(2,1)S(1)} %get-tuple-element.19), channel_id=1, source_target_pairs={{0,1},{1,0},{2,3},{3,2},{4,5},{5,4},{6,7},{7,6},{8,9},{9,8},{10,11... | collective-permute-start | bytes 798728 | tf_op jit(solution)/shard_map/cond/branch_1_fun/ppermute | solution.py:340
  16.2 13.6 %collective-permute-start.9 = (bf16[800,128]{1,0:T(8,128)(2,1)S(1)}, bf16[800,128]{1,0:T(8,128)(2,1)S(1)}, u32[]{:S(2)}, u32[]{:S(2)}) collective-permute-start(bf16[800,128]{1,0:T(8,128)(2,1)S(1)} %get-tuple-element.66), channel_id=1, source_target_pairs={{0,24},{8,16},{16,8},{24,0},{1,25},{9,17},{17,9},{25,1},{2,26},{10... | collective-permute-start | bytes 614408 | tf_op jit(solution)/shard_map/ppermute | solution.py:337
  19.1 1.7 %collective-permute-start.2 = (bf16[1040,128]{1,0:T(8,128)(2,1)S(1)}, bf16[1040,128]{1,0:T(8,128)(2,1)}, u32[]{:S(2)}, u32[]{:S(2)}) collective-permute-start(bf16[1040,128]{1,0:T(8,128)(2,1)S(1)} %get-tuple-element.20), channel_id=1, source_target_pairs={{0,1},{1,0},{2,3},{3,2},{4,5},{5,4},{6,7},{7,6},{8,9},{9,8},{10,11... | collective-permute-start | bytes 798728 | tf_op jit(solution)/shard_map/cond/branch_1_fun/ppermute | solution.py:340
  19.1 2.0 %collective-permute-start.3 = (bf16[1040,128]{1,0:T(8,128)(2,1)S(1)}, bf16[1040,128]{1,0:T(8,128)(2,1)}, u32[]{:S(2)}, u32[]{:S(2)}) collective-permute-start(bf16[1040,128]{1,0:T(8,128)(2,1)S(1)} %get-tuple-element.21), channel_id=1, source_target_pairs={{0,1},{1,0},{2,3},{3,2},{4,5},{5,4},{6,7},{7,6},{8,9},{9,8},{10,11... | collective-permute-start | bytes 798728 | tf_op jit(solution)/shard_map/cond/branch_1_fun/ppermute | solution.py:340
  21.2 3.0 %copy-start = (bf16[2,704,2048]{2,1,0:T(8,128)(2,1)S(1)}, bf16[2,704,2048]{2,1,0:T(8,128)(2,1)}, u32[]{:S(2)}) copy-start(bf16[2,704,2048]{2,1,0:T(8,128)(2,1)} %refs_4_.3) | copy-start | bytes 17301508
  26.3 10.9 %collective-permute-start.11 = (bf16[800,128]{1,0:T(8,128)(2,1)S(1)}, bf16[800,128]{1,0:T(8,128)(2,1)S(1)}, u32[]{:S(2)}, u32[]{:S(2)}) collective-permute-start(bf16[800,128]{1,0:T(8,128)(2,1)S(1)} %get-tuple-element.69), channel_id=1, source_target_pairs={{0,8},{8,0},{16,24},{24,16},{1,9},{9,1},{17,25},{25,17},{2,10},{10... | collective-permute-start | bytes 614408 | tf_op jit(solution)/shard_map/ppermute | solution.py:337
  27.8 12.2 %collective-permute-start.12 = (bf16[800,128]{1,0:T(8,128)(2,1)S(1)}, bf16[800,128]{1,0:T(8,128)(2,1)S(1)}, u32[]{:S(2)}, u32[]{:S(2)}) collective-permute-start(bf16[800,128]{1,0:T(8,128)(2,1)S(1)} %get-tuple-element.70), channel_id=1, source_target_pairs={{0,16},{8,24},{16,0},{24,8},{1,17},{9,25},{17,1},{25,9},{2,18},{10... | collective-permute-start | bytes 614408 | tf_op jit(solution)/shard_map/ppermute | solution.py:337
  28.3 16.8 %collective-permute-start.19 = (bf16[800,128]{1,0:T(8,128)(2,1)S(1)}, bf16[800,128]{1,0:T(8,128)(2,1)S(1)}, u32[]{:S(2)}, u32[]{:S(2)}) collective-permute-start(bf16[800,128]{1,0:T(8,128)(2,1)S(1)} %get-tuple-element.83), channel_id=1, source_target_pairs={{0,24},{8,16},{16,8},{24,0},{1,25},{9,17},{17,9},{25,1},{2,26},{10... | collective-permute-start | bytes 614408 | tf_op jit(solution)/shard_map/ppermute | solution.py:337
  32.1 2.7 %collective-permute-start.10 = (bf16[512,1024]{1,0:T(8,128)(2,1)S(1)}, bf16[512,1024]{1,0:T(8,128)(2,1)S(1)}, u32[]{:S(2)}, u32[]{:S(2)}) collective-permute-start(bf16[512,1024]{1,0:T(8,128)(2,1)S(1)} %mix_sibling.1), channel_id=1, source_target_pairs={{0,1},{1,0},{2,3},{3,2},{4,5},{5,4},{6,7},{7,6},{8,9},{9,8},{10,11... | collective-permute-start | bytes 3145736 | tf_op jit(solution)/shard_map/ppermute | solution.py:340
  35.1 7.7 %collective-permute-start.14 = (bf16[128,512]{1,0:T(8,128)(2,1)S(1)}, bf16[128,512]{1,0:T(8,128)(2,1)S(1)}, u32[]{:S(2)}, u32[]{:S(2)}) collective-permute-start(bf16[128,512]{1,0:T(8,128)(2,1)S(1)} %get-tuple-element.72), channel_id=1, source_target_pairs={{0,16},{8,24},{16,0},{24,8},{1,17},{9,25},{17,1},{25,9},{2,18},{10... | collective-permute-start | bytes 393224 | tf_op jit(solution)/shard_map/ppermute | solution.py:337
  35.7 7.1 %collective-permute-start.15 = (bf16[128,512]{1,0:T(8,128)(2,1)S(1)}, bf16[128,512]{1,0:T(8,128)(2,1)S(1)}, u32[]{:S(2)}, u32[]{:S(2)}) collective-permute-start(bf16[128,512]{1,0:T(8,128)(2,1)S(1)} %get-tuple-element.73), channel_id=1, source_target_pairs={{0,8},{8,0},{16,24},{24,16},{1,9},{9,1},{17,25},{25,17},{2,10},{10... | collective-permute-start | bytes 393224 | tf_op jit(solution)/shard_map/ppermute | solution.py:337
  40.0 7.4 %collective-permute-start.13 = (bf16[128,512]{1,0:T(8,128)(2,1)S(1)}, bf16[128,512]{1,0:T(8,128)(2,1)S(1)}, u32[]{:S(2)}, u32[]{:S(2)}) collective-permute-start(bf16[128,512]{1,0:T(8,128)(2,1)S(1)} %get-tuple-element.71), channel_id=1, source_target_pairs={{0,16},{8,24},{16,0},{24,8},{1,17},{9,25},{17,1},{25,9},{2,18},{10... | collective-permute-start | bytes 393224 | tf_op jit(solution)/shard_map/ppermute | solution.py:337
  40.0 7.4 %collective-permute-start.17 = (bf16[128,512]{1,0:T(8,128)(2,1)S(1)}, bf16[128,512]{1,0:T(8,128)(2,1)S(1)}, u32[]{:S(2)}, u32[]{:S(2)}) collective-permute-start(bf16[128,512]{1,0:T(8,128)(2,1)S(1)} %get-tuple-element.77), channel_id=1, source_target_pairs={{0,8},{8,0},{16,24},{24,16},{1,9},{9,1},{17,25},{25,17},{2,10},{10... | collective-permute-start | bytes 393224 | tf_op jit(solution)/shard_map/ppermute | solution.py:337
  42.9 5.0 %collective-permute-start.16 = (bf16[128,512]{1,0:T(8,128)(2,1)S(1)}, bf16[128,512]{1,0:T(8,128)(2,1)S(1)}, u32[]{:S(2)}, u32[]{:S(2)}) collective-permute-start(bf16[128,512]{1,0:T(8,128)(2,1)S(1)} %get-tuple-element.76), channel_id=1, source_target_pairs={{0,16},{8,24},{16,0},{24,8},{1,17},{9,25},{17,1},{25,9},{2,18},{10... | collective-permute-start | bytes 393224 | tf_op jit(solution)/shard_map/ppermute | solution.py:337
  43.7 5.0 %collective-permute-start.18 = (bf16[128,512]{1,0:T(8,128)(2,1)S(1)}, bf16[128,512]{1,0:T(8,128)(2,1)S(1)}, u32[]{:S(2)}, u32[]{:S(2)}) collective-permute-start(bf16[128,512]{1,0:T(8,128)(2,1)S(1)} %get-tuple-element.78), channel_id=1, source_target_pairs={{0,8},{8,0},{16,24},{24,16},{1,9},{9,1},{17,25},{25,17},{2,10},{10... | collective-permute-start | bytes 393224 | tf_op jit(solution)/shard_map/ppermute | solution.py:337
